TPU v7x, 256 devices: a whole 4x4x8 slice. The times are simulated.
256 devices in a mesh: clus: 32 (over y, x, core), col: 8 (over z).
Axes of the slice: x: 4, y: 4, z: 8, core: 2. Of those that a mesh axis runs over, the one named last changes fastest.
Arguments:
- embeds: bfloat16 [98304, 1024], P('clus', 'col')
- cluster_ids: int32 [98304], P('clus'), may hold values from 0 to 31, as said below
- orders: int32 [98304], P('clus'), may hold values from 0 to 98303, each once
Outputs:
- maxima: float32 [98304], P('clus')
Inputs may be any that keep to these rules, and one draw needn't show every extreme that they name: `cluster_ids`: within each device's block of 3072 rows no cluster is named more than 192 times, and one cluster, the same for every block, is named exactly 192 times in each block.
All inputs are finite; a program needn't handle non-finite values.
Results may differ from a plain program's by a relative error of at most 0.0003.
Values may be sent and summed in bfloat16 or wider, within the bound.
No kernel may reach another device: no remote copies, remote signals or barrier semaphores. Data moves between devices by JAX's collectives and lax.ppermute only.
A program may use at most 128 MiB of HBM per device.

v0:
```python
import jax
import jax.numpy as jnp
from jax import lax
from jax.sharding import PartitionSpec as P

never_order = 2**30


def masked_largest(scores, query_squares, key_squares, query_orders, key_orders):
    similar = scores / (
        jnp.sqrt(query_squares + 1e-06)[:, None] * jnp.sqrt(key_squares + 1e-06)[None, :]
    )
    earlier = key_orders[None, :] < query_orders[:, None]
    return jnp.max(jnp.where(earlier, similar, jnp.float32(-1.0)), axis=1)


def shards(embeds, cluster_ids, orders):
    rows_dev = embeds.shape[0]
    groups = lax.axis_size("clus")
    blocks = lax.axis_size("col")
    capacity = 2 * rows_dev // groups
    members = groups * capacity
    block_rows = members // blocks
    first_row = lax.axis_index("col") * block_rows
    one_hot = (cluster_ids[:, None] == jnp.arange(groups, dtype=jnp.int32)[None, :]).astype(
        jnp.int32
    )
    running = jnp.cumsum(one_hot, axis=0) - one_hot
    within = jnp.sum(running * one_hot, axis=1)
    slot_index = cluster_ids * capacity + within
    order_slots = jnp.full((members,), never_order, jnp.int32).at[slot_index].set(orders)
    order_slots = order_slots.reshape(groups, capacity)
    full_rows = lax.all_gather(embeds, "col", axis=1, tiled=True)
    placed = jnp.zeros((members, full_rows.shape[1]), full_rows.dtype).at[slot_index].set(full_rows)
    arrived = lax.all_to_all(
        placed.reshape(groups, capacity, full_rows.shape[1]),
        "clus",
        split_axis=0,
        concat_axis=0,
        tiled=True,
    )
    key_orders = lax.all_to_all(order_slots, "clus", split_axis=0, concat_axis=0, tiled=True)
    key_orders = key_orders.reshape(members)
    key_rows = arrived.reshape(members, full_rows.shape[1])
    query_rows = lax.dynamic_slice_in_dim(key_rows, first_row, block_rows, 0)
    scores = lax.dot_general(
        query_rows, key_rows, (((1,), (1,)), ((), ())), preferred_element_type=jnp.float32
    )
    squares = jnp.einsum("md,md->m", key_rows, key_rows, preferred_element_type=jnp.float32)
    largest = masked_largest(
        scores,
        lax.dynamic_slice_in_dim(squares, first_row, block_rows, 0),
        squares,
        lax.dynamic_slice_in_dim(key_orders, first_row, block_rows, 0),
        key_orders,
    )
    gathered = lax.all_gather(largest, "col", axis=0, tiled=True).reshape(groups, capacity)
    returned = lax.all_to_all(gathered, "clus", split_axis=0, concat_axis=0, tiled=True).reshape(
        members
    )
    return returned[slot_index]


def solution(mesh):
    return jax.shard_map(
        shards,
        mesh=mesh,
        in_specs=(P("clus", "col"), P("clus"), P("clus")),
        out_specs=P("clus"),
        check_vma=False,
    )
```

profile of v0, /device:TPU:1, one launch (start us, length us, event | category | flops | bytes accessed | tf_op | source)
XLA Modules:
  0.0 380.2 jit_solution(17366549843339361773)
XLA Ops:
  6.5 0.7 all-gather.3.cloned.1.call-update
  7.3 0.7 fusion.7
  8.0 9.2 %reduce-window.6 = s32[32,24,128]{2,1,0:T(8,128)S(1)} reduce-window(s32[32,24,128]{2,1,0:T(8,128)S(1)} %fusion.7, s32[]{:T(128)} %constant.12.clone.1), window={size=1x1x128 pad=0_0x0_0x127_0}, to_apply=%region_0.0 | reduce-window | flops 12484608 | bytes 786436 | tf_op jit(solution)/shard_map/reduce-window
  17.2 0.2 slice.10
  17.3 0.2 copy.12
  17.6 0.2 reduce-window.9
  17.8 0.2 broadcast_add_fusion
  18.0 0.8 fusion.6
  18.8 0.7 broadcast_clamp_fusion
  19.5 12.0 %scatter_custom_fusion = s32[6144]{0:T(1024)S(1)} fusion(s32[3072]{0:T(1024)S(1)} %get-tuple-element.6, s32[3072]{0:T(1024)} %param.5, s32[]{:T(128)} %constant.10.clone.1), kind=kCustom, calls=%fused_computation.19 | custom fusion | bytes 25088 | tf_op jit(solution)/shard_map/scatter | solution.py:31
  31.5 0.7 all_to_all.15
  32.2 8.6 %all-to-all-start = ((s32[32,1,192]{2,1,0:T(1,128)}), s32[32,1,192]{2,1,0:T(1,128)S(1)}, u32[]{:S(2)}, u32[]{:S(2)}) async-start(s32[32,1,192]{2,1,0:T(1,128)} %all_to_all.15), calls=%async_computation | async-start | bytes 65536 | tf_op jit(solution)/shard_map/all_to_all | solution.py:42
  40.8 50.1 %all-gather.3.cloned.1.call-done = bf16[3072,1024]{1,0:T(8,128)(2,1)} async-done(((bf16[3072,128]{1,0:T(8,128)(2,1)}), bf16[3072,1024]{1,0:T(8,128)(2,1)}) %all-gather.3.cloned.1.call-update) | async-done | bytes 6291472 | tf_op jit(solution)/shard_map/all_gather | solution.py:33
  90.9 22.0 %scatter_custom_fusion.1 = bf16[6144,1024]{1,0:T(8,128)(2,1)} fusion(s32[3072]{0:T(1024)S(1)} %get-tuple-element.6, bf16[3072,1024]{1,0:T(8,128)(2,1)} %all-gather.3.cloned.1.call-done, bf16[]{:T(256)} %constant.5.clone.1), kind=kCustom, calls=%fused_computation.6 | custom fusion | bytes 12583424 | tf_op jit(solution)/shard_map/scatter | solution.py:34
  112.9 10.8 %all-to-all-start.1 = ((bf16[32,192,1024]{2,1,0:T(8,128)(2,1)}), bf16[32,192,1024]{2,1,0:T(8,128)(2,1)}, u32[]{:S(2)}, u32[]{:S(2)}) async-start(bf16[32,192,1024]{2,1,0:T(8,128)(2,1)} %bitcast.25), calls=%async_computation.1 | async-start | bytes 25165824 | tf_op jit(solution)/shard_map/all_to_all | solution.py:35
  124.0 151.3 %all-to-all-done.1 = bf16[32,192,1024]{2,1,0:T(8,128)(2,1)} async-done(((bf16[32,192,1024]{2,1,0:T(8,128)(2,1)}), bf16[32,192,1024]{2,1,0:T(8,128)(2,1)}, u32[]{:S(2)}, u32[]{:S(2)}) %all-to-all-start.1) | async-done | bytes 12582944 | tf_op jit(solution)/shard_map/all_to_all | solution.py:35
  275.3 7.1 %fusion = f32[6144]{0:T(1024)S(1)} fusion(bf16[32,192,1024]{2,1,0:T(8,128)(2,1)} %all-to-all-done.1), kind=kLoop, calls=%fused_computation.4 | loop fusion | flops 18868224 | bytes 12607488 | tf_op jit(solution)/shard_map/md,md->m/dot_general | solution.py:49
  282.5 0.1 add_sqrt_fusion.1
  282.6 16.0 %select_reduce_fusion = f32[768]{0:T(1024)S(1)} fusion(f32[6144]{0:T(1024)S(1)} %add_sqrt_fusion, f32[768]{0:T(1024)S(1)} %add_sqrt_fusion.1, s32[6144]{0:T(1024)S(1)} %lt.26, s32[768]{0:T(1024)S(1)} %dynamic_slice.9, bf16[6144,1024]{1,0:T(8,128)(2,1)} %bitcast.5, s32[]{:T(128)S(6)} %select_n.15), kind=kOutput, calls=%fused_computation.5 | convolution fusion | flops 9687268352 | bytes 14214148 | tf_op jit(solution)/shard_map/dot_general | solution.py:46
  298.6 18.0 %all-gather = f32[8,1,768]{2,1,0:T(1,128)S(1)} all-gather(f32[1,1,768]{2,1,0:T(1,128)S(1)} %reshape.72), channel_id=1, replica_groups=mesh['clus'=32,'col'=8] {'col'}, dimensions={0}, use_global_device_ids=true | all-gather | bytes 27648 | tf_op jit(solution)/shard_map/all_gather | solution.py:57
  316.7 0.1 all_to_all.20
  316.8 25.9 %all_to_all.24 = f32[32,1,192]{2,1,0:T(1,128)S(1)} all-to-all(f32[32,1,192]{2,1,0:T(1,128)S(1)} %all_to_all.20), channel_id=1, replica_groups=mesh['clus'=32,'col'=8] {'clus'}, dimensions={0} | all-to-all | bytes 49152 | tf_op jit(solution)/shard_map/all_to_all | solution.py:58
  342.8 0.1 reshape.44
  342.9 30.5 %gather_fusion = f32[3072]{0:T(1024)} fusion(f32[6144]{0:T(1024)S(1)} %reshape.44, s32[3072]{0:T(1024)S(1)} %get-tuple-element.5), kind=kCustom, calls=%fused_computation | custom fusion | bytes 36864 | tf_op jit(solution)/shard_map/gather | solution.py:61
  (9 shorter events, 0.4 us)
Async XLA Ops:
  6.5 84.4 %all-gather.3.cloned.1.call-start = ((), (), s32[]{:S(2)}) async-start(), calls=%async_computation.3 | async-start | bytes 7077888 | tf_op jit(solution)/shard_map/all_gather | solution.py:33
  32.2 80.7 %all-to-all-start = ((s32[32,1,192]{2,1,0:T(1,128)}), s32[32,1,192]{2,1,0:T(1,128)S(1)}, u32[]{:S(2)}, u32[]{:S(2)}) async-start(s32[32,1,192]{2,1,0:T(1,128)} %all_to_all.15), calls=%async_computation | async-start | bytes 65536 | tf_op jit(solution)/shard_map/all_to_all | solution.py:42
  112.9 162.4 %all-to-all-start.1 = ((bf16[32,192,1024]{2,1,0:T(8,128)(2,1)}), bf16[32,192,1024]{2,1,0:T(8,128)(2,1)}, u32[]{:S(2)}, u32[]{:S(2)}) async-start(bf16[32,192,1024]{2,1,0:T(8,128)(2,1)} %bitcast.25), calls=%async_computation.1 | async-start | bytes 25165824 | tf_op jit(solution)/shard_map/all_to_all | solution.py:35
Sparse Core Ops, SparseCore 0:
  9.1 81.7 all-gather.2
where the time goes:
time: 381 us; the launch traced here: 380 us
  waiting for transfers between devices  202 us (53%)
  local copies, waits for them, and re-layouts  66 us (17%)
  blocking collectives  43.9 us (12%)
  starting transfers between devices  19.4 us (5%)
  other arithmetic  19.2 us (5%)
  matrix products  16 us (4%)
  between operations  13.5 us (4%)
    all_to_all x1, waiting for transfers between devices, shards(): lax.all_to_all(placed.reshape(groups, capacity, full_rows.shape[1]), 'clu...  151 us
    all_gather x1, waiting for transfers between devices, shards(): full_rows = lax.all_gather(embeds, 'col', axis=1, tiled=True)  50.1 us
    gather x1, local copies, waits for them, and re-layouts, shards(): return returned[slot_index]  30.5 us
    all_to_all x1, blocking collectives, shards(): lax.all_to_all(gathered, 'clus', split_axis=0, concat_axis=0, tiled=True)  25.9 us
    scatter x1, local copies, waits for them, and re-layouts, shards(): jnp.zeros((members, full_rows.shape[1]), full_rows.dtype).at[slot_index]  22 us
    all_gather x1, blocking collectives, shards(): lax.all_gather(largest, 'col', axis=0, tiled=True).reshape(groups, capacity)  18 us
    dot_general x1, matrix products, shards(): lax.dot_general(query_rows, key_rows, (((1,), (1,)), ((), ())), preferred...  16 us
    scatter x1, local copies, waits for them, and re-layouts, shards(): jnp.full((members,), never_order, jnp.int32).at[slot_index].set(orders)  12 us
  transfers between devices with their start and end apart: 3, of which 2 were waited for; matrix products, arithmetic and copies ran while one was open for 12% of the time, Pallas kernels for 0%

commit v1 on v0

v1 whole, which is shorter than its diff:
```python
import functools

import jax
import jax.numpy as jnp
from jax import lax
from jax.experimental import pallas as pl
from jax.experimental.pallas import tpu as pltpu
from jax.sharding import Mesh, PartitionSpec as P

never_order = 2**30
low = -3e38
Y, X, C, Z = 4, 4, 2, 8
ROWS = 3072
GROUPS = 32
CAP = 192
WIDTH = 128
BLOCK = Y * CAP
HALF = BLOCK // 2
LINES = ROWS // 128
ALL = ("y", "x", "core", "z")
PARAMS = pltpu.CompilerParams(vmem_limit_bytes=40 * 2**20)
VMEM = pl.BlockSpec(memory_space=pltpu.VMEM)
SMEM = pl.BlockSpec(memory_space=pltpu.SMEM)


def routes(move):
    pairs = []
    for y in range(Y):
        for x in range(X):
            for c in range(C):
                for z in range(Z):
                    y2, x2, c2, z2 = move(y, x, c, z)
                    to = (((y2 % Y) * X + x2 % X) * C + c2 % C) * Z + z2 % Z
                    pairs.append((((y * X + x) * C + c) * Z + z, to))
    return pairs


def place_kernel(ids_ref, rows_ref, placed_ref, slot_ref, member_ref, wide_ref, out_ref, slot_sm, sem):
    r = lax.broadcasted_iota(jnp.int32, (128, 256), 0)
    c = lax.broadcasted_iota(jnp.int32, (128, 256), 1)
    weights = ((r < c) | (c >= 128)).astype(jnp.float32).astype(jnp.bfloat16)
    group = lax.broadcasted_iota(jnp.int32, (GROUPS, 128), 0)
    for i in range(LINES):
        hit = group == ids_ref[pl.ds(i, 1), :]
        member_ref[pl.ds(i * GROUPS, GROUPS), :] = hit.astype(jnp.float32).astype(jnp.bfloat16)
    counts = jnp.dot(member_ref[...], weights, preferred_element_type=jnp.float32)
    carry = jnp.zeros((GROUPS, 128), jnp.float32)
    for i in range(LINES):
        part = counts[i * GROUPS : (i + 1) * GROUPS]
        line = ids_ref[pl.ds(i, 1), :]
        within = jnp.sum(jnp.where(group == line, part[:, :128] + carry, 0.0), axis=0, keepdims=True)
        slot_ref[pl.ds(i, 1), :] = line * CAP + within.astype(jnp.int32)
        carry = carry + part[:, 128:]
    copy = pltpu.make_async_copy(slot_ref, slot_sm, sem)
    copy.start()
    wide_ref[...] = rows_ref[...].astype(jnp.float32)
    out_ref[...] = jnp.zeros_like(out_ref)
    copy.wait()

    @pl.loop(0, LINES)
    def _(i):
        for lane in range(128):
            slot = slot_sm[i, lane]
            out_ref[pl.ds(slot, 1), :] = wide_ref[pl.ds(i * 128 + lane, 1), :]

    placed_ref[...] = out_ref[...].astype(jnp.bfloat16)


def place(ids, rows):
    return pl.pallas_call(
        place_kernel,
        out_shape=(
            jax.ShapeDtypeStruct((GROUPS * CAP, WIDTH), jnp.bfloat16),
            jax.ShapeDtypeStruct((LINES, 128), jnp.int32),
        ),
        in_specs=[VMEM, VMEM],
        out_specs=(VMEM, VMEM),
        scratch_shapes=[
            pltpu.VMEM((LINES * GROUPS, 128), jnp.bfloat16),
            pltpu.VMEM((ROWS, WIDTH), jnp.float32),
            pltpu.VMEM((GROUPS * CAP, WIDTH), jnp.float32),
            pltpu.SMEM((LINES, 128), jnp.int32),
            pltpu.SemaphoreType.DMA,
        ],
        compiler_params=PARAMS,
        name="place",
    )(ids, rows)


def col_inverse(ref):
    pieces = []
    for i in range(BLOCK // 128):
        wide = ref[pl.ds(i * 128, 128), :].astype(jnp.float32)
        pieces.append(lax.rsqrt(jnp.sum(wide * wide, axis=1, keepdims=True) + 1e-06))
    return jnp.concatenate(pieces, axis=0)


def to_row(col):
    eye = lax.broadcasted_iota(jnp.int32, (128, 128), 0) == lax.broadcasted_iota(
        jnp.int32, (128, 128), 1
    )
    pieces = []
    for i in range(BLOCK // 128):
        piece = jnp.broadcast_to(col[i * 128 : (i + 1) * 128], (128, 128))
        pieces.append(jnp.max(jnp.where(eye, piece, low), axis=0, keepdims=True))
    return jnp.concatenate(pieces, axis=1)


def dot_rows(p, q):
    return lax.dot_general(p, q, (((1,), (1,)), ((), ())), preferred_element_type=jnp.float32)


def cross(p_ref, q_ref, inv_p, inv_q_ref, order_p, order_q_ref, flip, q_best_ref):
    p_parts = []
    for h in range(2):
        start = pl.multiple_of(jnp.where(flip == 0, h, 1 - h) * HALF, HALF)
        q = q_ref[pl.ds(start, HALF), :]
        inv_q = inv_q_ref[:, pl.ds(start, HALF)]
        order_q = order_q_ref[:, pl.ds(start, HALF)]
        q_best = jnp.full((1, HALF), low, jnp.float32)
        for t in range(HALF // 128):
            at = h * HALF + t * 128
            s = dot_rows(p_ref[pl.ds(at, 128), :], q)
            earlier = order_q < order_p[at : at + 128]
            inv = inv_p[at : at + 128]
            p_best = jnp.max(jnp.where(earlier, s * inv_q, low), axis=1, keepdims=True)
            p_parts.append(p_best * inv)
            q_best = jnp.maximum(
                q_best, jnp.max(jnp.where(earlier, low, s * inv), axis=0, keepdims=True)
            )
        q_best_ref[:, pl.ds(start, HALF)] = jnp.maximum(
            q_best_ref[:, pl.ds(start, HALF)], q_best * inv_q
        )
    return jnp.concatenate(p_parts, axis=0)


def first_kernel(place_ref, a0, e0, order_rows, order_cols, best, inv_rows, row_a, row_b):
    core = place_ref[1]
    inv_p = col_inverse(a0)
    inv_rows[...] = jnp.zeros_like(inv_rows)
    inv_rows[pl.ds(0, 1), :] = to_row(inv_p)
    row_a[pl.ds(0, 1), :] = to_row(col_inverse(e0))
    row_b[...] = jnp.full_like(row_b, low)
    order_p = order_cols[:, 0:1]
    order_q = order_rows[0:1, :]
    inv_q = inv_rows[0:1, :]
    parts = []
    for t in range(BLOCK // 128):
        s = dot_rows(a0[pl.ds(t * 128, 128), :], a0[...])
        earlier = order_q < order_p[t * 128 : (t + 1) * 128]
        p_best = jnp.max(jnp.where(earlier, s * inv_q, low), axis=1, keepdims=True)
        parts.append(p_best * inv_p[t * 128 : (t + 1) * 128])
    own = jnp.concatenate(parts, axis=0)
    other = cross(
        a0, e0, inv_p, row_a.at[pl.ds(0, 1)], order_p, order_rows.at[pl.ds(3, 1)], core,
        row_b.at[pl.ds(0, 1)],
    )
    best[...] = jnp.full_like(best, -1.0)
    best[pl.ds(0, 1), :] = to_row(jnp.maximum(own, other))
    best[pl.ds(3, 1), :] = row_b[pl.ds(0, 1), :]


def second_kernel(
    place_ref, a0, a1, e1, order_rows, order_cols, before, inv_before, best, inv_rows, inv_e1, row_b
):
    core = place_ref[1]
    inv_p = col_inverse(a0)
    inv_rows[...] = inv_before[...]
    inv_rows[pl.ds(1, 1), :] = to_row(col_inverse(a1))
    inv_e = col_inverse(e1)
    inv_e1[...] = jnp.broadcast_to(inv_e, inv_e1.shape)
    row_b[...] = jnp.full_like(row_b, low)
    order_p = order_cols[:, 0:1]
    order_e = order_cols[:, 4:5]
    own = cross(
        a0, a1, inv_p, inv_rows.at[pl.ds(1, 1)], order_p, order_rows.at[pl.ds(1, 1)], 0,
        row_b.at[pl.ds(1, 1)],
    )
    own_b = cross(
        a0, a1, inv_p, inv_rows.at[pl.ds(1, 1)], order_p, order_rows.at[pl.ds(1, 1)], 1,
        row_b.at[pl.ds(1, 1)],
    )
    other = cross(
        e1, a0, inv_e, inv_rows.at[pl.ds(0, 1)], order_e, order_rows.at[pl.ds(0, 1)], core,
        row_b.at[pl.ds(0, 1)],
    )
    other_b = cross(
        e1, a1, inv_e, inv_rows.at[pl.ds(1, 1)], order_e, order_rows.at[pl.ds(1, 1)], core,
        row_b.at[pl.ds(1, 1)],
    )
    best[...] = before[...]
    best[pl.ds(0, 1), :] = jnp.maximum(
        jnp.maximum(before[pl.ds(0, 1), :], row_b[pl.ds(0, 1), :]), to_row(jnp.maximum(own, own_b))
    )
    best[pl.ds(1, 1), :] = jnp.maximum(before[pl.ds(1, 1), :], row_b[pl.ds(1, 1), :])
    best[pl.ds(4, 1), :] = jnp.maximum(
        before[pl.ds(4, 1), :], to_row(jnp.maximum(other, other_b))
    )


def third_kernel(
    place_ref, a0, a2, e1, order_rows, order_cols, before, inv_rows, inv_e1, best, row_a, row_b
):
    core = place_ref[1]
    far = place_ref[2]
    row_a[pl.ds(0, 1), :] = to_row(col_inverse(a2))
    row_b[...] = jnp.full_like(row_b, low)
    inv_p = col_inverse(a0)
    own = cross(
        a0, a2, inv_p, row_a.at[pl.ds(0, 1)], order_cols[:, 0:1], order_rows.at[pl.ds(2, 1)], far,
        row_b.at[pl.ds(0, 1)],
    )
    other = cross(
        e1, a2, inv_e1[:, 0:1], row_a.at[pl.ds(0, 1)], order_cols[:, 4:5],
        order_rows.at[pl.ds(2, 1)], core, row_b.at[pl.ds(0, 1)],
    )
    best[...] = jnp.full_like(best, -1.0)
    best[pl.ds(place_ref[3], 1), :] = jnp.maximum(before[pl.ds(0, 1), :], to_row(own))
    best[pl.ds(place_ref[4], 1), :] = before[pl.ds(1, 1), :]
    best[pl.ds(place_ref[5], 1), :] = jnp.maximum(before[pl.ds(2, 1), :], row_b[pl.ds(0, 1), :])
    best[pl.ds(place_ref[6], 1), :] = before[pl.ds(3, 1), :]
    best[pl.ds(place_ref[7], 1), :] = jnp.maximum(before[pl.ds(4, 1), :], to_row(other))


def shape(*dims):
    return jax.ShapeDtypeStruct(dims, jnp.float32)


def scores_call(kernel, units, inputs, outs, scratch, name):
    return pl.pallas_call(
        kernel,
        out_shape=outs,
        in_specs=[SMEM] + [VMEM] * (len(inputs) - 1),
        out_specs=jax.tree.map(lambda _: VMEM, outs),
        scratch_shapes=scratch,
        compiler_params=PARAMS,
        cost_estimate=pl.CostEstimate(
            flops=int(units * 2 * BLOCK * BLOCK * 1024), bytes_accessed=4 * 2**20, transcendentals=0
        ),
        name=name,
    )(*inputs)


def answer_kernel(ids_ref, slot_ref, table_ref, out_ref):
    table = table_ref[...]
    high = table.astype(jnp.bfloat16)
    rest = table - high.astype(jnp.float32)
    middle = rest.astype(jnp.bfloat16)
    small = (rest - middle.astype(jnp.float32)).astype(jnp.bfloat16)
    pieces = jnp.concatenate([high, middle, small], axis=0)
    group = lax.broadcasted_iota(jnp.int32, (3 * GROUPS, 128), 0) & (GROUPS - 1)
    place_in = lax.broadcasted_iota(jnp.int32, (CAP, 128), 0)
    for i in range(LINES):
        ids = ids_ref[pl.ds(i, 1), :]
        within = slot_ref[pl.ds(i, 1), :] - ids * CAP
        where = (ids & (Z - 1)) * Y + (ids >> 3)
        member = (group == where).astype(jnp.float32).astype(jnp.bfloat16)
        found = lax.dot_general(
            pieces, member, (((0,), (0,)), ((), ())), preferred_element_type=jnp.float32
        )
        out_ref[pl.ds(i, 1), :] = jnp.sum(
            jnp.where(place_in == within, found, 0.0), axis=0, keepdims=True
        )


def answer(ids, slots, table):
    return pl.pallas_call(
        answer_kernel,
        out_shape=jax.ShapeDtypeStruct((LINES, 128), jnp.float32),
        in_specs=[VMEM] * 3,
        out_specs=VMEM,
        compiler_params=PARAMS,
        name="answer",
    )(ids, slots, table)


def shards(embeds, cluster_ids, orders):
    x, core, z = lax.axis_index("x"), lax.axis_index("core"), lax.axis_index("z")
    ids = cluster_ids.reshape(LINES, 128)
    placed, slots = place(ids, embeds)
    arrived = lax.all_to_all(
        placed.reshape(GROUPS, CAP, WIDTH), ("y", "z"), split_axis=0, concat_axis=0, tiled=True
    )
    a0 = arrived.reshape(Y, Z, CAP, WIDTH).transpose(0, 2, 1, 3).reshape(BLOCK, Z * WIDTH)

    order_slots = jnp.full((GROUPS * CAP,), never_order, jnp.int32).at[slots.reshape(ROWS)].set(orders)
    order_slots = order_slots.reshape(Y, Z, CAP)
    mine = lax.dynamic_slice_in_dim(order_slots, z, 1, 1).reshape(1, Y, CAP)
    spread = jnp.broadcast_to(mine, (X * C, Y, CAP)).reshape(GROUPS, CAP)
    member_orders = lax.all_to_all(
        spread, ("x", "core", "y"), split_axis=0, concat_axis=0, tiled=True
    ).reshape(X * C, BLOCK)
    step = jnp.where(core == 0, -1, 1)
    spots = jnp.stack(
        [
            x * 2 + core,
            ((x + step) % X) * 2 + core,
            ((x + 2) % X) * 2 + core,
            x * 2 + 1 - core,
            ((x - step) % X) * 2 + 1 - core,
        ]
    )
    place_in = jnp.concatenate([jnp.stack([x, core, x // 2]), spots]).astype(jnp.int32)
    order_rows = member_orders.astype(jnp.float32)[spots]
    order_rows = jnp.concatenate([order_rows, jnp.zeros((3, BLOCK), jnp.float32)])
    order_cols = order_rows.T

    swap = routes(lambda y, x, c, z: (y, x, 1 - c, z))
    ring = routes(lambda y, x, c, z: (y, x + (1 if c == 0 else -1), c, z))
    a1 = lax.ppermute(a0, ALL, ring)
    e0 = lax.ppermute(a0, ALL, swap)
    a2 = lax.ppermute(a1, ALL, ring)
    e1 = lax.ppermute(a1, ALL, swap)
    vector = pltpu.VMEM((8, BLOCK), jnp.float32)
    best, inv_rows = scores_call(
        first_kernel, 1.5, (place_in, a0, e0, order_rows, order_cols),
        (shape(8, BLOCK), shape(8, BLOCK)), [vector, vector], "first",
    )
    best, inv_rows, inv_e1 = scores_call(
        second_kernel, 2, (place_in, a0, a1, e1, order_rows, order_cols, best, inv_rows),
        (shape(8, BLOCK), shape(8, BLOCK), shape(BLOCK, 128)), [vector], "second",
    )
    best = scores_call(
        third_kernel, 1, (place_in, a0, a2, e1, order_rows, order_cols, best, inv_rows, inv_e1),
        shape(8, BLOCK), [vector, vector], "third",
    )
    back = lax.all_to_all(
        best.reshape(GROUPS, CAP), ("x", "core", "y"), split_axis=0, concat_axis=0, tiled=True
    )
    merged = jnp.max(back.reshape(X * C, Y, CAP), axis=0)
    table = lax.all_to_all(
        jnp.broadcast_to(merged[None], (Z, Y, CAP)), "z", split_axis=0, concat_axis=0, tiled=True
    )
    return answer(ids, slots, table.reshape(GROUPS, CAP)).reshape(ROWS)


def solution(mesh):
    fine = Mesh(mesh.devices.reshape(Y, X, C, Z), ALL)
    clus = ("y", "x", "core")
    return jax.shard_map(
        shards,
        mesh=fine,
        in_specs=(P(clus, "z"), P(clus), P(clus)),
        out_specs=P(clus),
        check_vma=False,
    )
```

time: 381 us -> 154 us (0.40)
  waiting for transfers between devices: 202 us -> 21.5 us
  local copies, waits for them, and re-layouts: 66 us -> 20 us
  blocking collectives: 43.9 us -> 69.9 us
  Pallas kernels: 0 us -> 24.6 us
  other arithmetic: 19.2 us -> 0.21 us
  matrix products: 16 us -> 0 us
  between operations: 13.5 us -> 0.22 us
    all_to_all x2 -> x1, waiting for transfers between devices: 151 us -> 6.76 us  [shards(): lax.all_to_all(spread, ('x', 'core', 'y'), split_axis=0, concat_axis=0, t...]
    all_gather x1 -> x0, waiting for transfers between devices: 50.1 us -> none  [shards(): full_rows = lax.all_gather(embeds, 'col', axis=1, tiled=True)]
    all_to_all x1 -> x3, blocking collectives: 25.9 us -> 69.9 us  [the longest x1 48.5 us: shards(): lax.all_to_all(placed.reshape(GROUPS, CAP, WIDTH), ('y', 'z'), split_axis...]
    gather x1 -> x2, local copies, waits for them, and re-layouts: 30.5 us -> 2.07 us  [shards(): order_rows = member_orders.astype(jnp.float32)[spots]]
    pallas_call x0 -> x5, Pallas kernels: none -> 24.6 us  [the longest x3 19.5 us: scores_call(): pl.pallas_call(kernel, out_shape=outs, in_specs=[SMEM] + [VMEM] * (len(in...]
    scatter x2 -> x1, local copies, waits for them, and re-layouts: 34 us -> 12 us  [shards(): jnp.full((GROUPS * CAP,), never_order, jnp.int32).at[slots.reshape(ROWS)]]
    all_gather x1 -> x0, blocking collectives: 18 us -> none  [shards(): lax.all_gather(largest, 'col', axis=0, tiled=True).reshape(groups, capacity)]
    dot_general x1 -> x0, matrix products: 16 us -> none  [shards(): lax.dot_general(query_rows, key_rows, (((1,), (1,)), ((), ())), preferred...]
  transfers between devices with their start and end apart: 3 -> 5, of which waited for: 2 -> 2; matrix products, arithmetic and copies ran while one was open for 12% -> 10% of each run, Pallas kernels for 0% -> 9%
where the time goes in v1:
time: 154 us; the launch traced here: 153 us
  blocking collectives  69.9 us (45%)
  Pallas kernels  24.6 us (16%)
  waiting for transfers between devices  21.5 us (14%)
  local copies, waits for them, and re-layouts  20 us (13%)
  starting transfers between devices  16.7 us (11%)
    all_to_all x1, blocking collectives, shards(): lax.all_to_all(placed.reshape(GROUPS, CAP, WIDTH), ('y', 'z'), split_axis...  48.5 us
    pallas_call x3, Pallas kernels, scores_call(): pl.pallas_call(kernel, out_shape=outs, in_specs=[SMEM] + [VMEM] * (len(in...  19.5 us
    ppermute x1, waiting for transfers between devices, shards(): a1 = lax.ppermute(a0, ALL, ring)  14.7 us
    scatter x1, local copies, waits for them, and re-layouts, shards(): jnp.full((GROUPS * CAP,), never_order, jnp.int32).at[slots.reshape(ROWS)]  12 us
    all_to_all x1, blocking collectives, shards(): lax.all_to_all(best.reshape(GROUPS, CAP), ('x', 'core', 'y'), split_axis=...  10.8 us
    all_to_all x1, blocking collectives, shards(): lax.all_to_all(jnp.broadcast_to(merged[None], (Z, Y, CAP)), 'z', split_ax...  10.6 us
    all_to_all x1, waiting for transfers between devices, shards(): lax.all_to_all(spread, ('x', 'core', 'y'), split_axis=0, concat_axis=0, t...  6.76 us
    ppermute x1, starting transfers between devices, shards(): e1 = lax.ppermute(a1, ALL, swap)  5.51 us
  transfers between devices with their start and end apart: 5, of which 2 were waited for; matrix products, arithmetic and copies ran while one was open for 10% of the time, Pallas kernels for 9%

profile of v1, /device:TPU:1, one launch (start us, length us, event | category | flops | bytes accessed | tf_op | source)
XLA Modules:
  0.0 153.1 jit_solution(11088967107055239092)
XLA Ops:
  0.0 1.1 copy-done
  1.1 0.7 copy-done.1
  1.8 4.0 %place.1 = (bf16[6144,128]{1,0:T(8,128)(2,1)S(1)}, s32[24,128]{1,0:T(8,128)S(1)}) custom-call(s32[24,128]{1,0:T(8,128)S(1)} %bitcast.41, bf16[3072,128]{1,0:T(8,128)(2,1)S(1)} %copy-done), custom_call_target="tpu_custom_call" | custom-call | tf_op jit(solution)/shard_map/place/pallas_call | solution.py:70
  5.8 48.5 %all_to_all.29 = bf16[32,192,128]{2,1,0:T(8,128)(2,1)S(1)} all-to-all(bf16[32,192,128]{2,1,0:T(8,128)(2,1)S(1)} %bitcast.39), channel_id=1, replica_groups=mesh['y'=4,'x'=4,'core'=2,'z'=8] {'y','z'}, dimensions={0} | all-to-all | bytes 3145728 | tf_op jit(solution)/shard_map/all_to_all | solution.py:281
  54.3 1.0 copy.13
  55.8 2.6 %collective-permute-start = (bf16[768,1024]{1,0:T(8,128)(2,1)S(1)}, bf16[768,1024]{1,0:T(8,128)(2,1)}, u32[]{:S(2)}, u32[]{:S(2)}) collective-permute-start(bf16[768,1024]{1,0:T(8,128)(2,1)S(1)} %bitcast.34), channel_id=1, source_target_pairs={{0,16},{1,17},{2,18},{3,19},{4,20},{5,21},{6,22},{7,23},{8,56},{9,... | collective-permute-start | bytes 4718600 | tf_op jit(solution)/shard_map/ppermute | solution.py:310
  58.3 2.6 %collective-permute-start.3 = (bf16[768,1024]{1,0:T(8,128)(2,1)S(1)}, bf16[768,1024]{1,0:T(8,128)(2,1)}, u32[]{:S(2)}, u32[]{:S(2)}) collective-permute-start(bf16[768,1024]{1,0:T(8,128)(2,1)S(1)} %bitcast.35), channel_id=1, source_target_pairs={{0,8},{1,9},{2,10},{3,11},{4,12},{5,13},{6,14},{7,15},{8,0},{9,1},... | collective-permute-start | bytes 4718600 | tf_op jit(solution)/shard_map/ppermute | solution.py:311
  61.0 14.7 %collective-permute-done.a1 = bf16[768,1024]{1,0:T(8,128)(2,1)} collective-permute-done((bf16[768,1024]{1,0:T(8,128)(2,1)S(1)}, bf16[768,1024]{1,0:T(8,128)(2,1)}, u32[]{:S(2)}, u32[]{:S(2)}) %collective-permute-start) | collective-permute-done | bytes 1572896 | tf_op jit(solution)/shard_map/ppermute | solution.py:310
  75.7 5.5 %collective-permute-start.2 = (bf16[768,1024]{1,0:T(8,128)(2,1)}, bf16[768,1024]{1,0:T(8,128)(2,1)S(1)}, u32[]{:S(2)}, u32[]{:S(2)}) collective-permute-start(bf16[768,1024]{1,0:T(8,128)(2,1)} %collective-permute-done.a1), channel_id=1, source_target_pairs={{0,8},{1,9},{2,10},{3,11},{4,12},{5,13},{6,14},{7,15},{8,0},{9,1},... | collective-permute-start | bytes 4718600 | tf_op jit(solution)/shard_map/ppermute | solution.py:313
  81.2 1.3 collective-permute-start.1
  82.5 12.0 %scatter_custom_fusion = s32[6144]{0:T(1024)S(1)} fusion(s32[3072]{0:T(1024)S(1)} %bitcast.46, s32[3072]{0:T(1024)} %param.5, s32[]{:T(128)} %constant.59.clone.1), kind=kCustom, calls=%fused_computation.5 | custom fusion | bytes 25088 | tf_op jit(solution)/shard_map/scatter | solution.py:286
  94.6 0.6 all_to_all.19
  95.2 4.7 %all-to-all-start.1 = ((s32[32,1,192]{2,1,0:T(1,128)}), s32[32,1,192]{2,1,0:T(1,128)S(1)}, u32[]{:S(2)}, u32[]{:S(2)}) async-start(s32[32,1,192]{2,1,0:T(1,128)} %all_to_all.19), calls=%async_computation.1 | async-start | bytes 65536 | tf_op jit(solution)/shard_map/all_to_all | solution.py:290
  100.2 6.8 %all-to-all-done.1 = s32[32,1,192]{2,1,0:T(1,128)S(1)} async-done(((s32[32,1,192]{2,1,0:T(1,128)}), s32[32,1,192]{2,1,0:T(1,128)S(1)}, u32[]{:S(2)}, u32[]{:S(2)}) %all-to-all-start.1) | async-done | bytes 24608 | tf_op jit(solution)/shard_map/all_to_all | solution.py:290
  107.1 1.2 gather_fusion
  108.3 0.9 copy.14
  109.2 0.8 copy.24
  109.9 0.7 concatenate.27.clone.order_rows
  110.7 6.7 %first.1 = (f32[8,768]{1,0:T(8,128)S(1)}, f32[8,768]{1,0:T(8,128)S(1)}) custom-call(s32[8]{0:T(128)S(1)} %concatenate.26.place_ref, bf16[768,1024]{1,0:T(8,128)(2,1)S(1)} %bitcast.36, bf16[768,1024]{1,0:T(8,128)(2,1)} %collective-permute-done.3.e0, f32[8,768]{1,0:T(8,128)S(1)} %concatenate.27.clone.order_rows, f32[768,8]{1,0:T(8,128)S(1)} %pad_bitcast_fusion.order_cols), custom_call_target="tpu_custom_call" | custom-call | flops 1811939328 | bytes 4194304 | tf_op jit(solution)/shard_map/first/pallas_call | solution.py:230
  117.4 7.7 %second.1 = (f32[8,768]{1,0:T(8,128)S(1)}, f32[8,768]{1,0:T(8,128)S(1)}, f32[768,128]{1,0:T(8,128)S(1)}) custom-call(s32[8]{0:T(128)S(1)} %concatenate.26.place_ref, bf16[768,1024]{1,0:T(8,128)(2,1)S(1)} %bitcast.37, bf16[768,1024]{1,0:T(8,128)(2,1)} %collective-permute-done.a1, bf16[768,1024]{1,0:T(8,128)(2,1)S(1)} %collective-permute-done.2.e1, ...), custom_call_target="tpu_custom_call" | custom-call | flops 2415919104 | bytes 4194304 | tf_op jit(solution)/shard_map/second/pallas_call | solution.py:230
  125.1 5.1 %third.1 = f32[8,768]{1,0:T(8,128)S(1)} custom-call(s32[8]{0:T(128)S(1)} %concatenate.26.place_ref, bf16[768,1024]{1,0:T(8,128)(2,1)S(1)} %bitcast.38, bf16[768,1024]{1,0:T(8,128)(2,1)} %collective-permute-done.1.a2, bf16[768,1024]{1,0:T(8,128)(2,1)S(1)} %collective-permute-done.2.e1, f32[8,768]{1,0:T(8,128)S(1)} %concatenate.27.clone.order_rows, ...), custom_call_target="tpu_custom_call" | custom-call | flops 1207959552 | bytes 4194304 | tf_op jit(solution)/shard_map/third/pallas_call | solution.py:230
  130.3 10.8 %all_to_all.30 = f32[32,1,192]{2,1,0:T(1,128)S(1)} all-to-all(f32[32,1,192]{2,1,0:T(1,128)S(1)} %all_to_all.24), channel_id=1, replica_groups=mesh['y'=4,'x'=4,'core'=2,'z'=8] {'x','core','y'}, dimensions={0} | all-to-all | bytes 49152 | tf_op jit(solution)/shard_map/all_to_all | solution.py:327
  141.2 10.6 %all_to_all.31 = f32[8,4,192]{2,1,0:T(4,128)S(1)} all-to-all(f32[8,4,192]{2,1,0:T(4,128)S(1)} %broadcast_in_dim.22), channel_id=1, replica_groups=mesh['y'=4,'x'=4,'core'=2,'z'=8] {'z'}, dimensions={0} | all-to-all | bytes 49152 | tf_op jit(solution)/shard_map/all_to_all | solution.py:331
  151.9 1.2 answer.1
  (26 shorter events, 1.2 us)
Async XLA Ops:
  0.0 1.1 copy-start
  1.1 0.7 copy-start.1
  55.8 19.9 %collective-permute-start = (bf16[768,1024]{1,0:T(8,128)(2,1)S(1)}, bf16[768,1024]{1,0:T(8,128)(2,1)}, u32[]{:S(2)}, u32[]{:S(2)}) collective-permute-start(bf16[768,1024]{1,0:T(8,128)(2,1)S(1)} %bitcast.34), channel_id=1, source_target_pairs={{0,16},{1,17},{2,18},{3,19},{4,20},{5,21},{6,22},{7,23},{8,56},{9,... | collective-permute-start | bytes 4718600 | tf_op jit(solution)/shard_map/ppermute | solution.py:310
  58.3 52.4 %collective-permute-start.3 = (bf16[768,1024]{1,0:T(8,128)(2,1)S(1)}, bf16[768,1024]{1,0:T(8,128)(2,1)}, u32[]{:S(2)}, u32[]{:S(2)}) collective-permute-start(bf16[768,1024]{1,0:T(8,128)(2,1)S(1)} %bitcast.35), channel_id=1, source_target_pairs={{0,8},{1,9},{2,10},{3,11},{4,12},{5,13},{6,14},{7,15},{8,0},{9,1},... | collective-permute-start | bytes 4718600 | tf_op jit(solution)/shard_map/ppermute | solution.py:311
  75.7 41.7 %collective-permute-start.2 = (bf16[768,1024]{1,0:T(8,128)(2,1)}, bf16[768,1024]{1,0:T(8,128)(2,1)S(1)}, u32[]{:S(2)}, u32[]{:S(2)}) collective-permute-start(bf16[768,1024]{1,0:T(8,128)(2,1)} %collective-permute-done.a1), channel_id=1, source_target_pairs={{0,8},{1,9},{2,10},{3,11},{4,12},{5,13},{6,14},{7,15},{8,0},{9,1},... | collective-permute-start | bytes 4718600 | tf_op jit(solution)/shard_map/ppermute | solution.py:313
  81.2 43.9 %collective-permute-start.1 = (bf16[768,1024]{1,0:T(8,128)(2,1)}, bf16[768,1024]{1,0:T(8,128)(2,1)}, u32[]{:S(2)}, u32[]{:S(2)}) collective-permute-start(bf16[768,1024]{1,0:T(8,128)(2,1)} %collective-permute-done.a1), channel_id=1, source_target_pairs={{0,16},{1,17},{2,18},{3,19},{4,20},{5,21},{6,22},{7,23},{8,56},{9,... | collective-permute-start | bytes 4718600 | tf_op jit(solution)/shard_map/ppermute | solution.py:312
  95.2 11.7 %all-to-all-start.1 = ((s32[32,1,192]{2,1,0:T(1,128)}), s32[32,1,192]{2,1,0:T(1,128)S(1)}, u32[]{:S(2)}, u32[]{:S(2)}) async-start(s32[32,1,192]{2,1,0:T(1,128)} %all_to_all.19), calls=%async_computation.1 | async-start | bytes 65536 | tf_op jit(solution)/shard_map/all_to_all | solution.py:290
  125.1 26.8 %copy-start.2 = (s32[3072]{0:T(1024)S(1)}, s32[3072]{0:T(1024)}, u32[]{:S(2)}) copy-start(s32[3072]{0:T(1024)} %param.4) | copy-start | bytes 36868

commit v2 on v1

--- a/solution.py
+++ b/solution.py
@@ -281,8 +281,6 @@
     arrived = lax.all_to_all(
         placed.reshape(GROUPS, CAP, WIDTH), ("y", "z"), split_axis=0, concat_axis=0, tiled=True
     )
-    a0 = arrived.reshape(Y, Z, CAP, WIDTH).transpose(0, 2, 1, 3).reshape(BLOCK, Z * WIDTH)
-
     order_slots = jnp.full((GROUPS * CAP,), never_order, jnp.int32).at[slots.reshape(ROWS)].set(orders)
     order_slots = order_slots.reshape(Y, Z, CAP)
     mine = lax.dynamic_slice_in_dim(order_slots, z, 1, 1).reshape(1, Y, CAP)
@@ -304,6 +302,8 @@
     order_rows = member_orders.astype(jnp.float32)[spots]
     order_rows = jnp.concatenate([order_rows, jnp.zeros((3, BLOCK), jnp.float32)])
     order_cols = order_rows.T
+    arrived, order_rows, order_cols = lax.optimization_barrier((arrived, order_rows, order_cols))
+    a0 = arrived.reshape(Y, Z, CAP, WIDTH).transpose(0, 2, 1, 3).reshape(BLOCK, Z * WIDTH)
 
     swap = routes(lambda y, x, c, z: (y, x, 1 - c, z))
     ring = routes(lambda y, x, c, z: (y, x + (1 if c == 0 else -1), c, z))

time: 154 us -> 159 us (1.032)
  waiting for transfers between devices: 21.5 us -> 53.2 us
  blocking collectives: 69.9 us -> 38.4 us
  starting transfers between devices: 16.7 us -> 18.8 us
  local copies, waits for them, and re-layouts: 20 us -> 21.9 us
    all_to_all x1, blocking collectives: 48.5 us -> 15.6 us  [shards(): lax.all_to_all(spread, ('x', 'core', 'y'), split_axis=0, concat_axis=0, t...]
    all_to_all x1, waiting for transfers between devices: 6.76 us -> 34.8 us  [shards(): lax.all_to_all(placed.reshape(GROUPS, CAP, WIDTH), ('y', 'z'), split_axis...]
    all_to_all x1, starting transfers between devices: 4.66 us -> 8.91 us  [shards(): lax.all_to_all(placed.reshape(GROUPS, CAP, WIDTH), ('y', 'z'), split_axis...]
    ppermute x1, waiting for transfers between devices: 0.01 us -> 2.9 us  [shards(): a2 = lax.ppermute(a1, ALL, ring)]
    optimization_barrier x0 -> x1, local copies, waits for them, and re-layouts: none -> 1.73 us  [shards(): lax.optimization_barrier((arrived, order_rows, order_cols))]
    ppermute x1, starting transfers between devices: 2.57 us -> 0.92 us  [shards(): a1 = lax.ppermute(a0, ALL, ring)]
    unnamed x9 -> x14, local copies, waits for them, and re-layouts: 3.04 us -> 4.33 us
  transfers between devices with their start and end apart: 5 -> 5, of which waited for: 2 -> 3; matrix products, arithmetic and copies ran while one was open for 10% -> 2% of each run, Pallas kernels for 9% -> 9%
where the time goes in v2:
time: 159 us; the launch traced here: 158 us
  waiting for transfers between devices  53.2 us (33%)
  blocking collectives  38.4 us (24%)
  Pallas kernels  25.8 us (16%)
  local copies, waits for them, and re-layouts  21.9 us (14%)
  starting transfers between devices  18.8 us (12%)
    all_to_all x1, waiting for transfers between devices, shards(): lax.all_to_all(placed.reshape(GROUPS, CAP, WIDTH), ('y', 'z'), split_axis...  34.8 us
    pallas_call x3, Pallas kernels, scores_call(): pl.pallas_call(kernel, out_shape=outs, in_specs=[SMEM] + [VMEM] * (len(in...  19.5 us
    all_to_all x1, blocking collectives, shards(): lax.all_to_all(spread, ('x', 'core', 'y'), split_axis=0, concat_axis=0, t...  15.6 us
    ppermute x1, waiting for transfers between devices, shards(): a1 = lax.ppermute(a0, ALL, ring)  15.5 us
    all_to_all x1, blocking collectives, shards(): lax.all_to_all(best.reshape(GROUPS, CAP), ('x', 'core', 'y'), split_axis=...  12 us
    scatter x1, local copies, waits for them, and re-layouts, shards(): jnp.full((GROUPS * CAP,), never_order, jnp.int32).at[slots.reshape(ROWS)]  12 us
    all_to_all x1, blocking collectives, shards(): lax.all_to_all(jnp.broadcast_to(merged[None], (Z, Y, CAP)), 'z', split_ax...  10.8 us
    all_to_all x1, starting transfers between devices, shards(): lax.all_to_all(placed.reshape(GROUPS, CAP, WIDTH), ('y', 'z'), split_axis...  8.91 us
  transfers between devices with their start and end apart: 5, of which 3 were waited for; matrix products, arithmetic and copies ran while one was open for 2% of the time, Pallas kernels for 9%

profile of v2, /device:TPU:1, one launch (start us, length us, event | category | flops | bytes accessed | tf_op | source)
XLA Modules:
  0.0 158.5 jit_solution(15718278598823782822)
XLA Ops:
  0.0 1.1 copy-done
  1.1 0.7 copy-done.4
  1.8 5.1 %place.1 = (bf16[6144,128]{1,0:T(8,128)(2,1)}, s32[24,128]{1,0:T(8,128)S(1)}) custom-call(s32[24,128]{1,0:T(8,128)S(1)} %bitcast.40, bf16[3072,128]{1,0:T(8,128)(2,1)S(1)} %copy-done), custom_call_target="tpu_custom_call" | custom-call | tf_op jit(solution)/shard_map/place/pallas_call | solution.py:70
  7.0 12.0 %scatter_custom_fusion = s32[6144]{0:T(1024)S(1)} fusion(s32[3072]{0:T(1024)S(1)} %bitcast.45, s32[3072]{0:T(1024)} %param.5, s32[]{:T(128)} %constant.59.clone.1), kind=kCustom, calls=%fused_computation.5 | custom fusion | bytes 25088 | tf_op jit(solution)/shard_map/scatter | solution.py:284
  19.1 15.6 %all_to_all.29 = s32[32,1,192]{2,1,0:T(1,128)S(1)} all-to-all(s32[32,1,192]{2,1,0:T(1,128)S(1)} %all_to_all.19), channel_id=1, replica_groups=mesh['y'=4,'x'=4,'core'=2,'z'=8] {'x','core','y'}, dimensions={0} | all-to-all | bytes 49152 | tf_op jit(solution)/shard_map/all_to_all | solution.py:288
  34.8 8.9 %all-to-all-start = ((bf16[32,192,128]{2,1,0:T(8,128)(2,1)}), bf16[32,192,128]{2,1,0:T(8,128)(2,1)S(1)}, u32[]{:S(2)}, u32[]{:S(2)}) async-start(bf16[32,192,128]{2,1,0:T(8,128)(2,1)} %bitcast.9), calls=%async_computation | async-start | bytes 3145728 | tf_op jit(solution)/shard_map/all_to_all | solution.py:281
  44.8 0.8 pad_bitcast_fusion
  45.6 34.8 %all-to-all-done = bf16[32,192,128]{2,1,0:T(8,128)(2,1)S(1)} async-done(((bf16[32,192,128]{2,1,0:T(8,128)(2,1)}), bf16[32,192,128]{2,1,0:T(8,128)(2,1)S(1)}, u32[]{:S(2)}, u32[]{:S(2)}) %all-to-all-start) | async-done | bytes 1572896 | tf_op jit(solution)/shard_map/all_to_all | solution.py:281
  80.4 1.0 copy.14
  81.9 0.9 collective-permute-start
  82.8 3.4 %collective-permute-start.3 = (bf16[768,1024]{1,0:T(8,128)(2,1)S(1)}, bf16[768,1024]{1,0:T(8,128)(2,1)}, u32[]{:S(2)}, u32[]{:S(2)}) collective-permute-start(bf16[768,1024]{1,0:T(8,128)(2,1)S(1)} %bitcast.35), channel_id=1, source_target_pairs={{0,8},{1,9},{2,10},{3,11},{4,12},{5,13},{6,14},{7,15},{8,0},{9,1},... | collective-permute-start | bytes 4718600 | tf_op jit(solution)/shard_map/ppermute | solution.py:311
  86.1 15.5 %collective-permute-done.a1 = bf16[768,1024]{1,0:T(8,128)(2,1)} collective-permute-done((bf16[768,1024]{1,0:T(8,128)(2,1)S(1)}, bf16[768,1024]{1,0:T(8,128)(2,1)}, u32[]{:S(2)}, u32[]{:S(2)}) %collective-permute-start) | collective-permute-done | bytes 1572896 | tf_op jit(solution)/shard_map/ppermute | solution.py:310
  101.6 5.7 %collective-permute-start.2 = (bf16[768,1024]{1,0:T(8,128)(2,1)}, bf16[768,1024]{1,0:T(8,128)(2,1)S(1)}, u32[]{:S(2)}, u32[]{:S(2)}) collective-permute-start(bf16[768,1024]{1,0:T(8,128)(2,1)} %collective-permute-done.a1), channel_id=1, source_target_pairs={{0,8},{1,9},{2,10},{3,11},{4,12},{5,13},{6,14},{7,15},{8,0},{9,1},... | collective-permute-start | bytes 4718600 | tf_op jit(solution)/shard_map/ppermute | solution.py:313
  107.3 1.7 %copy.17.order_rows = f32[8,768]{1,0:T(8,128)} copy(f32[8,768]{0,1:T(8,128)} %get-tuple-element.18) | data formatting | bytes 49152 | tf_op jit(solution)/shard_map/optimization_barrier | solution.py:305
  109.1 0.7 copy-done.1
  109.8 6.7 %first.1 = (f32[8,768]{1,0:T(8,128)S(1)}, f32[8,768]{1,0:T(8,128)S(1)}) custom-call(s32[8]{0:T(128)S(1)} %concatenate.26.place_ref, bf16[768,1024]{1,0:T(8,128)(2,1)S(1)} %bitcast.36, bf16[768,1024]{1,0:T(8,128)(2,1)} %collective-permute-done.3.e0, f32[8,768]{1,0:T(8,128)S(1)} %copy-done.1, f32[768,8]{1,0:T(8,128)S(1)} %get-tuple-element.19.order_cols), custom_call_target="tpu_custom_call" | custom-call | flops 1811939328 | bytes 4194304 | tf_op jit(solution)/shard_map/first/pallas_call | solution.py:230
  116.5 7.7 %second.1 = (f32[8,768]{1,0:T(8,128)S(1)}, f32[8,768]{1,0:T(8,128)S(1)}, f32[768,128]{1,0:T(8,128)S(1)}) custom-call(s32[8]{0:T(128)S(1)} %concatenate.26.place_ref, bf16[768,1024]{1,0:T(8,128)(2,1)S(1)} %bitcast.37, bf16[768,1024]{1,0:T(8,128)(2,1)} %collective-permute-done.a1, bf16[768,1024]{1,0:T(8,128)(2,1)S(1)} %collective-permute-done.2.e1, ...), custom_call_target="tpu_custom_call" | custom-call | flops 2415919104 | bytes 4194304 | tf_op jit(solution)/shard_map/second/pallas_call | solution.py:230
  124.2 2.9 %collective-permute-done.1.a2 = bf16[768,1024]{1,0:T(8,128)(2,1)} collective-permute-done((bf16[768,1024]{1,0:T(8,128)(2,1)}, bf16[768,1024]{1,0:T(8,128)(2,1)}, u32[]{:S(2)}, u32[]{:S(2)}) %collective-permute-start.1) | collective-permute-done | bytes 1572896 | tf_op jit(solution)/shard_map/ppermute | solution.py:312
  127.1 5.1 %third.1 = f32[8,768]{1,0:T(8,128)S(1)} custom-call(s32[8]{0:T(128)S(1)} %concatenate.26.place_ref, bf16[768,1024]{1,0:T(8,128)(2,1)S(1)} %bitcast.38, bf16[768,1024]{1,0:T(8,128)(2,1)} %collective-permute-done.1.a2, bf16[768,1024]{1,0:T(8,128)(2,1)S(1)} %collective-permute-done.2.e1, f32[8,768]{1,0:T(8,128)S(1)} %copy-done.2, ...), custom_call_target="tpu_custom_call" | custom-call | flops 1207959552 | bytes 4194304 | tf_op jit(solution)/shard_map/third/pallas_call | solution.py:230
  132.8 0.8 all_to_all.24
  133.6 12.0 %all_to_all.30 = f32[32,1,192]{2,1,0:T(1,128)S(1)} all-to-all(f32[32,1,192]{2,1,0:T(1,128)S(1)} %all_to_all.24), channel_id=1, replica_groups=mesh['y'=4,'x'=4,'core'=2,'z'=8] {'x','core','y'}, dimensions={0} | all-to-all | bytes 49152 | tf_op jit(solution)/shard_map/all_to_all | solution.py:327
  145.8 10.8 %all_to_all.31 = f32[8,4,192]{2,1,0:T(4,128)S(1)} all-to-all(f32[8,4,192]{2,1,0:T(4,128)S(1)} %broadcast_in_dim.22), channel_id=1, replica_groups=mesh['y'=4,'x'=4,'core'=2,'z'=8] {'z'}, dimensions={0} | all-to-all | bytes 49152 | tf_op jit(solution)/shard_map/all_to_all | solution.py:331
  156.6 0.7 copy-done.5
  157.3 1.2 answer.1
  (31 shorter events, 2.5 us)
Async XLA Ops:
  0.0 1.1 copy-start
  1.1 0.7 copy-start.4
  34.8 45.6 %all-to-all-start = ((bf16[32,192,128]{2,1,0:T(8,128)(2,1)}), bf16[32,192,128]{2,1,0:T(8,128)(2,1)S(1)}, u32[]{:S(2)}, u32[]{:S(2)}) async-start(bf16[32,192,128]{2,1,0:T(8,128)(2,1)} %bitcast.9), calls=%async_computation | async-start | bytes 3145728 | tf_op jit(solution)/shard_map/all_to_all | solution.py:281
  81.9 19.7 %collective-permute-start = (bf16[768,1024]{1,0:T(8,128)(2,1)S(1)}, bf16[768,1024]{1,0:T(8,128)(2,1)}, u32[]{:S(2)}, u32[]{:S(2)}) collective-permute-start(bf16[768,1024]{1,0:T(8,128)(2,1)S(1)} %bitcast.34), channel_id=1, source_target_pairs={{0,16},{1,17},{2,18},{3,19},{4,20},{5,21},{6,22},{7,23},{8,56},{9,... | collective-permute-start | bytes 4718600 | tf_op jit(solution)/shard_map/ppermute | solution.py:310
  82.8 26.3 %collective-permute-start.3 = (bf16[768,1024]{1,0:T(8,128)(2,1)S(1)}, bf16[768,1024]{1,0:T(8,128)(2,1)}, u32[]{:S(2)}, u32[]{:S(2)}) collective-permute-start(bf16[768,1024]{1,0:T(8,128)(2,1)S(1)} %bitcast.35), channel_id=1, source_target_pairs={{0,8},{1,9},{2,10},{3,11},{4,12},{5,13},{6,14},{7,15},{8,0},{9,1},... | collective-permute-start | bytes 4718600 | tf_op jit(solution)/shard_map/ppermute | solution.py:311
  101.6 14.9 %collective-permute-start.2 = (bf16[768,1024]{1,0:T(8,128)(2,1)}, bf16[768,1024]{1,0:T(8,128)(2,1)S(1)}, u32[]{:S(2)}, u32[]{:S(2)}) collective-permute-start(bf16[768,1024]{1,0:T(8,128)(2,1)} %collective-permute-done.a1), channel_id=1, source_target_pairs={{0,8},{1,9},{2,10},{3,11},{4,12},{5,13},{6,14},{7,15},{8,0},{9,1},... | collective-permute-start | bytes 4718600 | tf_op jit(solution)/shard_map/ppermute | solution.py:313
  107.3 19.9 %collective-permute-start.1 = (bf16[768,1024]{1,0:T(8,128)(2,1)}, bf16[768,1024]{1,0:T(8,128)(2,1)}, u32[]{:S(2)}, u32[]{:S(2)}) collective-permute-start(bf16[768,1024]{1,0:T(8,128)(2,1)} %collective-permute-done.a1), channel_id=1, source_target_pairs={{0,16},{1,17},{2,18},{3,19},{4,20},{5,21},{6,22},{7,23},{8,56},{9,... | collective-permute-start | bytes 4718600 | tf_op jit(solution)/shard_map/ppermute | solution.py:312
  109.1 0.7 copy-start.1
  109.8 6.7 %copy-start.2 = (f32[8,768]{1,0:T(8,128)S(1)}, f32[8,768]{1,0:T(8,128)}, u32[]{:S(2)}) copy-start(f32[8,768]{1,0:T(8,128)} %copy.17.order_rows) | copy-start | bytes 73732
  132.2 0.6 copy-start.3
  156.6 0.7 copy-start.5

commit v3 on v2

--- a/solution.py
+++ b/solution.py
@@ -7,7 +7,7 @@
 from jax.experimental.pallas import tpu as pltpu
 from jax.sharding import Mesh, PartitionSpec as P
 
-never_order = 2**30
+never_order = 2.0**30
 low = -3e38
 Y, X, C, Z = 4, 4, 2, 8
 ROWS = 3072
@@ -85,6 +85,37 @@
         compiler_params=PARAMS,
         name="place",
     )(ids, rows)
+
+
+def ranks_kernel(ids_ref, slot_ref, orders_ref, table_ref):
+    group = lax.broadcasted_iota(jnp.int32, (GROUPS, 128), 0)
+    spot = lax.broadcasted_iota(jnp.int32, (CAP, 128), 0)
+    total = jnp.zeros((3 * GROUPS, CAP), jnp.float32)
+    for i in range(LINES):
+        ids = ids_ref[pl.ds(i, 1), :]
+        within = slot_ref[pl.ds(i, 1), :] - ids * CAP
+        value = orders_ref[pl.ds(i, 1), :] + 1
+        hit = group == ids
+        digits = [
+            jnp.where(hit, digit.astype(jnp.float32), 0.0)
+            for digit in (value & 255, (value >> 8) & 255, value >> 16)
+        ]
+        left = jnp.concatenate(digits, axis=0).astype(jnp.bfloat16)
+        right = (spot == within).astype(jnp.float32).astype(jnp.bfloat16)
+        total = total + dot_rows(left, right)
+    value = total[:GROUPS] + 256.0 * total[GROUPS : 2 * GROUPS] + 65536.0 * total[2 * GROUPS :]
+    table_ref[...] = jnp.where(value > 0, value - 1.0, never_order)
+
+
+def ranks(ids, slots, orders):
+    return pl.pallas_call(
+        ranks_kernel,
+        out_shape=jax.ShapeDtypeStruct((GROUPS, CAP), jnp.float32),
+        in_specs=[VMEM] * 3,
+        out_specs=VMEM,
+        compiler_params=PARAMS,
+        name="ranks",
+    )(ids, slots, orders)
 
 
 def col_inverse(ref):
@@ -275,19 +306,15 @@
 
 
 def shards(embeds, cluster_ids, orders):
-    x, core, z = lax.axis_index("x"), lax.axis_index("core"), lax.axis_index("z")
+    y, x, core, z = (lax.axis_index(name) for name in ALL)
     ids = cluster_ids.reshape(LINES, 128)
     placed, slots = place(ids, embeds)
     arrived = lax.all_to_all(
         placed.reshape(GROUPS, CAP, WIDTH), ("y", "z"), split_axis=0, concat_axis=0, tiled=True
     )
-    order_slots = jnp.full((GROUPS * CAP,), never_order, jnp.int32).at[slots.reshape(ROWS)].set(orders)
-    order_slots = order_slots.reshape(Y, Z, CAP)
-    mine = lax.dynamic_slice_in_dim(order_slots, z, 1, 1).reshape(1, Y, CAP)
-    spread = jnp.broadcast_to(mine, (X * C, Y, CAP)).reshape(GROUPS, CAP)
-    member_orders = lax.all_to_all(
-        spread, ("x", "core", "y"), split_axis=0, concat_axis=0, tiled=True
-    ).reshape(X * C, BLOCK)
+    tables = lax.all_gather(ranks(ids, slots, orders.reshape(LINES, 128)), ("y", "x", "core"))
+    mine = lax.dynamic_index_in_dim(tables, y * Z + z, 1, keepdims=False)
+    member_orders = mine.reshape(Y, X * C, CAP).transpose(1, 0, 2).reshape(X * C, BLOCK)
     step = jnp.where(core == 0, -1, 1)
     spots = jnp.stack(
         [
@@ -299,7 +326,7 @@
         ]
     )
     place_in = jnp.concatenate([jnp.stack([x, core, x // 2]), spots]).astype(jnp.int32)
-    order_rows = member_orders.astype(jnp.float32)[spots]
+    order_rows = member_orders[spots]
     order_rows = jnp.concatenate([order_rows, jnp.zeros((3, BLOCK), jnp.float32)])
     order_cols = order_rows.T
     arrived, order_rows, order_cols = lax.optimization_barrier((arrived, order_rows, order_cols))

time: 159 us -> 135 us (0.85)
  waiting for transfers between devices: 53.2 us -> 22.3 us
  blocking collectives: 38.4 us -> 51 us
  local copies, waits for them, and re-layouts: 21.9 us -> 9.83 us
  starting transfers between devices: 18.8 us -> 23.7 us
    all_to_all x1, waiting for transfers between devices: 34.8 us -> 5.83 us  [shards(): lax.all_to_all(placed.reshape(GROUPS, CAP, WIDTH), ('y', 'z'), split_axis...]
    all_gather x0 -> x1, blocking collectives: none -> 28.1 us  [shards(): lax.all_gather(ranks(ids, slots, orders.reshape(LINES, 128)), ('y', 'x',...]
    all_to_all x1 -> x0, blocking collectives: 15.6 us -> none  [shards(): lax.all_to_all(spread, ('x', 'core', 'y'), split_axis=0, concat_axis=0, t...]
    scatter x1 -> x0, local copies, waits for them, and re-layouts: 12 us -> none  [shards(): jnp.full((GROUPS * CAP,), never_order, jnp.int32).at[slots.reshape(ROWS)]]
    all_to_all x1, starting transfers between devices: 8.91 us -> 12 us  [shards(): lax.all_to_all(placed.reshape(GROUPS, CAP, WIDTH), ('y', 'z'), split_axis...]
    ppermute x1, starting transfers between devices: 0.92 us -> 2.57 us  [shards(): a1 = lax.ppermute(a0, ALL, ring)]
    unnamed x14 -> x20, local copies, waits for them, and re-layouts: 4.33 us -> 4.34 us
  transfers between devices with their start and end apart: 5 -> 5, of which waited for: 3 -> 3; matrix products, arithmetic and copies ran while one was open for 2% -> 3% of each run, Pallas kernels for 9% -> 11%
where the time goes in v3:
time: 135 us; the launch traced here: 134 us
  blocking collectives  51 us (38%)
  Pallas kernels  26.7 us (20%)
  starting transfers between devices  23.7 us (18%)
  waiting for transfers between devices  22.3 us (17%)
  local copies, waits for them, and re-layouts  9.83 us (7%)
    all_gather x1, blocking collectives, shards(): lax.all_gather(ranks(ids, slots, orders.reshape(LINES, 128)), ('y', 'x',...  28.1 us
    pallas_call x3, Pallas kernels, scores_call(): pl.pallas_call(kernel, out_shape=outs, in_specs=[SMEM] + [VMEM] * (len(in...  19.4 us
    ppermute x1, waiting for transfers between devices, shards(): a1 = lax.ppermute(a0, ALL, ring)  14.9 us
    all_to_all x1, starting transfers between devices, shards(): lax.all_to_all(placed.reshape(GROUPS, CAP, WIDTH), ('y', 'z'), split_axis...  12 us
    all_to_all x1, blocking collectives, shards(): lax.all_to_all(best.reshape(GROUPS, CAP), ('x', 'core', 'y'), split_axis=...  12 us
    all_to_all x1, blocking collectives, shards(): lax.all_to_all(jnp.broadcast_to(merged[None], (Z, Y, CAP)), 'z', split_ax...  10.8 us
    all_to_all x1, waiting for transfers between devices, shards(): lax.all_to_all(placed.reshape(GROUPS, CAP, WIDTH), ('y', 'z'), split_axis...  5.83 us
    ppermute x1, starting transfers between devices, shards(): e1 = lax.ppermute(a1, ALL, swap)  5.37 us
  transfers between devices with their start and end apart: 5, of which 3 were waited for; matrix products, arithmetic and copies ran while one was open for 3% of the time, Pallas kernels for 11%

profile of v3, /device:TPU:1, one launch (start us, length us, event | category | flops | bytes accessed | tf_op | source)
XLA Modules:
  0.0 133.9 jit_solution(7599711316899752796)
XLA Ops:
  0.0 1.1 copy-done
  1.1 0.7 copy-done.1
  1.8 5.1 %place.1 = (bf16[6144,128]{1,0:T(8,128)(2,1)}, s32[24,128]{1,0:T(8,128)S(1)}) custom-call(s32[24,128]{1,0:T(8,128)S(1)} %bitcast.40, bf16[3072,128]{1,0:T(8,128)(2,1)S(1)} %copy-done), custom_call_target="tpu_custom_call" | custom-call | tf_op jit(solution)/shard_map/place/pallas_call | solution.py:70
  7.0 12.0 %all-to-all-start = ((bf16[32,192,128]{2,1,0:T(8,128)(2,1)}), bf16[32,192,128]{2,1,0:T(8,128)(2,1)S(1)}, u32[]{:S(2)}, u32[]{:S(2)}) async-start(bf16[32,192,128]{2,1,0:T(8,128)(2,1)} %bitcast.9), calls=%async_computation | async-start | bytes 3145728 | tf_op jit(solution)/shard_map/all_to_all | solution.py:312
  19.1 0.9 ranks.1
  20.0 28.1 %all-gather = f32[1024,192]{1,0:T(8,128)S(1)} all-gather(f32[32,192]{1,0:T(8,128)S(1)} %ranks.1), channel_id=2, replica_groups=mesh['y'=4,'x'=4,'core'=2,'z'=8] {'y','x','core'}, dimensions={0}, use_global_device_ids=true | all-gather | bytes 811008 | tf_op jit(solution)/shard_map/all_gather | solution.py:315
  49.2 0.8 pad_bitcast_fusion
  50.0 5.8 %all-to-all-done = bf16[32,192,128]{2,1,0:T(8,128)(2,1)S(1)} async-done(((bf16[32,192,128]{2,1,0:T(8,128)(2,1)}), bf16[32,192,128]{2,1,0:T(8,128)(2,1)S(1)}, u32[]{:S(2)}, u32[]{:S(2)}) %all-to-all-start) | async-done | bytes 1572896 | tf_op jit(solution)/shard_map/all_to_all | solution.py:312
  55.9 1.0 copy.18
  57.3 2.6 %collective-permute-start = (bf16[768,1024]{1,0:T(8,128)(2,1)S(1)}, bf16[768,1024]{1,0:T(8,128)(2,1)}, u32[]{:S(2)}, u32[]{:S(2)}) collective-permute-start(bf16[768,1024]{1,0:T(8,128)(2,1)S(1)} %bitcast.35), channel_id=1, source_target_pairs={{0,16},{1,17},{2,18},{3,19},{4,20},{5,21},{6,22},{7,23},{8,56},{9,... | collective-permute-start | bytes 4718600 | tf_op jit(solution)/shard_map/ppermute | solution.py:337
  59.9 2.5 %collective-permute-start.3 = (bf16[768,1024]{1,0:T(8,128)(2,1)S(1)}, bf16[768,1024]{1,0:T(8,128)(2,1)}, u32[]{:S(2)}, u32[]{:S(2)}) collective-permute-start(bf16[768,1024]{1,0:T(8,128)(2,1)S(1)} %bitcast.36), channel_id=1, source_target_pairs={{0,8},{1,9},{2,10},{3,11},{4,12},{5,13},{6,14},{7,15},{8,0},{9,1},... | collective-permute-start | bytes 4718600 | tf_op jit(solution)/shard_map/ppermute | solution.py:338
  62.4 14.9 %collective-permute-done.a1 = bf16[768,1024]{1,0:T(8,128)(2,1)} collective-permute-done((bf16[768,1024]{1,0:T(8,128)(2,1)S(1)}, bf16[768,1024]{1,0:T(8,128)(2,1)}, u32[]{:S(2)}, u32[]{:S(2)}) %collective-permute-start) | collective-permute-done | bytes 1572896 | tf_op jit(solution)/shard_map/ppermute | solution.py:337
  77.2 5.4 %collective-permute-start.2 = (bf16[768,1024]{1,0:T(8,128)(2,1)}, bf16[768,1024]{1,0:T(8,128)(2,1)S(1)}, u32[]{:S(2)}, u32[]{:S(2)}) collective-permute-start(bf16[768,1024]{1,0:T(8,128)(2,1)} %collective-permute-done.a1), channel_id=1, source_target_pairs={{0,8},{1,9},{2,10},{3,11},{4,12},{5,13},{6,14},{7,15},{8,0},{9,1},... | collective-permute-start | bytes 4718600 | tf_op jit(solution)/shard_map/ppermute | solution.py:340
  82.6 1.3 collective-permute-start.1
  84.0 1.7 %copy.21.order_rows = f32[8,768]{1,0:T(8,128)} copy(f32[8,768]{0,1:T(8,128)} %get-tuple-element.18) | data formatting | bytes 49152 | tf_op jit(solution)/shard_map/optimization_barrier | solution.py:332
  85.7 0.7 copy-done.3
  86.4 6.7 %first.1 = (f32[8,768]{1,0:T(8,128)S(1)}, f32[8,768]{1,0:T(8,128)S(1)}) custom-call(s32[8]{0:T(128)S(1)} %concatenate.26.place_ref, bf16[768,1024]{1,0:T(8,128)(2,1)S(1)} %bitcast.37, bf16[768,1024]{1,0:T(8,128)(2,1)} %collective-permute-done.3.e0, f32[8,768]{1,0:T(8,128)S(1)} %copy-done.3, f32[768,8]{1,0:T(8,128)S(1)} %get-tuple-element.19.order_cols), custom_call_target="tpu_custom_call" | custom-call | flops 1811939328 | bytes 4194304 | tf_op jit(solution)/shard_map/first/pallas_call | solution.py:261
  93.1 7.7 %second.1 = (f32[8,768]{1,0:T(8,128)S(1)}, f32[8,768]{1,0:T(8,128)S(1)}, f32[768,128]{1,0:T(8,128)S(1)}) custom-call(s32[8]{0:T(128)S(1)} %concatenate.26.place_ref, bf16[768,1024]{1,0:T(8,128)(2,1)S(1)} %bitcast.38, bf16[768,1024]{1,0:T(8,128)(2,1)} %collective-permute-done.a1, bf16[768,1024]{1,0:T(8,128)(2,1)S(1)} %collective-permute-done.2.e1, ...), custom_call_target="tpu_custom_call" | custom-call | flops 2415919104 | bytes 4194304 | tf_op jit(solution)/shard_map/second/pallas_call | solution.py:261
  100.9 1.6 %collective-permute-done.1.a2 = bf16[768,1024]{1,0:T(8,128)(2,1)} collective-permute-done((bf16[768,1024]{1,0:T(8,128)(2,1)}, bf16[768,1024]{1,0:T(8,128)(2,1)}, u32[]{:S(2)}, u32[]{:S(2)}) %collective-permute-start.1) | collective-permute-done | bytes 1572896 | tf_op jit(solution)/shard_map/ppermute | solution.py:339
  102.5 5.1 %third.1 = f32[8,768]{1,0:T(8,128)S(1)} custom-call(s32[8]{0:T(128)S(1)} %concatenate.26.place_ref, bf16[768,1024]{1,0:T(8,128)(2,1)S(1)} %bitcast.39, bf16[768,1024]{1,0:T(8,128)(2,1)} %collective-permute-done.1.a2, bf16[768,1024]{1,0:T(8,128)(2,1)S(1)} %collective-permute-done.2.e1, f32[8,768]{1,0:T(8,128)S(1)} %copy-done.4, ...), custom_call_target="tpu_custom_call" | custom-call | flops 1207959552 | bytes 4194304 | tf_op jit(solution)/shard_map/third/pallas_call | solution.py:261
  108.2 0.8 all_to_all.16
  109.0 12.0 %all_to_all.20 = f32[32,1,192]{2,1,0:T(1,128)S(1)} all-to-all(f32[32,1,192]{2,1,0:T(1,128)S(1)} %all_to_all.16), channel_id=1, replica_groups=mesh['y'=4,'x'=4,'core'=2,'z'=8] {'x','core','y'}, dimensions={0} | all-to-all | bytes 49152 | tf_op jit(solution)/shard_map/all_to_all | solution.py:354
  121.2 10.8 %all_to_all.21 = f32[8,4,192]{2,1,0:T(4,128)S(1)} all-to-all(f32[8,4,192]{2,1,0:T(4,128)S(1)} %broadcast_in_dim.2), channel_id=1, replica_groups=mesh['y'=4,'x'=4,'core'=2,'z'=8] {'z'}, dimensions={0} | all-to-all | bytes 49152 | tf_op jit(solution)/shard_map/all_to_all | solution.py:358
  132.7 1.2 answer.1
  (33 shorter events, 3.0 us)
Async XLA Ops:
  0.0 1.1 copy-start
  1.1 0.7 copy-start.1
  7.0 12.1 %copy-start.6 = (s32[24,128]{1,0:T(8,128)}, s32[24,128]{1,0:T(8,128)S(1)}, u32[]{:S(2)}) copy-start(s32[24,128]{1,0:T(8,128)S(1)} %get-tuple-element.15.slot_ref) | copy-start | bytes 36868
  7.0 12.1 %copy-start.2 = (s32[3072]{0:T(1024)S(1)}, s32[3072]{0:T(1024)}, u32[]{:S(2)}) copy-start(s32[3072]{0:T(1024)} %param.4) | copy-start | bytes 36868
  7.0 12.1 %copy-start.8 = (s32[3072]{0:T(1024)S(1)}, s32[3072]{0:T(1024)}, u32[]{:S(2)}) copy-start(s32[3072]{0:T(1024)} %param.5) | copy-start | bytes 36868
  7.0 48.8 %all-to-all-start = ((bf16[32,192,128]{2,1,0:T(8,128)(2,1)}), bf16[32,192,128]{2,1,0:T(8,128)(2,1)S(1)}, u32[]{:S(2)}, u32[]{:S(2)}) async-start(bf16[32,192,128]{2,1,0:T(8,128)(2,1)} %bitcast.9), calls=%async_computation | async-start | bytes 3145728 | tf_op jit(solution)/shard_map/all_to_all | solution.py:312
  57.3 19.9 %collective-permute-start = (bf16[768,1024]{1,0:T(8,128)(2,1)S(1)}, bf16[768,1024]{1,0:T(8,128)(2,1)}, u32[]{:S(2)}, u32[]{:S(2)}) collective-permute-start(bf16[768,1024]{1,0:T(8,128)(2,1)S(1)} %bitcast.35), channel_id=1, source_target_pairs={{0,16},{1,17},{2,18},{3,19},{4,20},{5,21},{6,22},{7,23},{8,56},{9,... | collective-permute-start | bytes 4718600 | tf_op jit(solution)/shard_map/ppermute | solution.py:337
  59.9 25.8 %collective-permute-start.3 = (bf16[768,1024]{1,0:T(8,128)(2,1)S(1)}, bf16[768,1024]{1,0:T(8,128)(2,1)}, u32[]{:S(2)}, u32[]{:S(2)}) collective-permute-start(bf16[768,1024]{1,0:T(8,128)(2,1)S(1)} %bitcast.36), channel_id=1, source_target_pairs={{0,8},{1,9},{2,10},{3,11},{4,12},{5,13},{6,14},{7,15},{8,0},{9,1},... | collective-permute-start | bytes 4718600 | tf_op jit(solution)/shard_map/ppermute | solution.py:338
  77.2 15.9 %collective-permute-start.2 = (bf16[768,1024]{1,0:T(8,128)(2,1)}, bf16[768,1024]{1,0:T(8,128)(2,1)S(1)}, u32[]{:S(2)}, u32[]{:S(2)}) collective-permute-start(bf16[768,1024]{1,0:T(8,128)(2,1)} %collective-permute-done.a1), channel_id=1, source_target_pairs={{0,8},{1,9},{2,10},{3,11},{4,12},{5,13},{6,14},{7,15},{8,0},{9,1},... | collective-permute-start | bytes 4718600 | tf_op jit(solution)/shard_map/ppermute | solution.py:340
  82.6 19.9 %collective-permute-start.1 = (bf16[768,1024]{1,0:T(8,128)(2,1)}, bf16[768,1024]{1,0:T(8,128)(2,1)}, u32[]{:S(2)}, u32[]{:S(2)}) collective-permute-start(bf16[768,1024]{1,0:T(8,128)(2,1)} %collective-permute-done.a1), channel_id=1, source_target_pairs={{0,16},{1,17},{2,18},{3,19},{4,20},{5,21},{6,22},{7,23},{8,56},{9,... | collective-permute-start | bytes 4718600 | tf_op jit(solution)/shard_map/ppermute | solution.py:339
  85.7 0.7 copy-start.3
  86.4 6.7 %copy-start.4 = (f32[8,768]{1,0:T(8,128)S(1)}, f32[8,768]{1,0:T(8,128)}, u32[]{:S(2)}) copy-start(f32[8,768]{1,0:T(8,128)} %copy.21.order_rows) | copy-start | bytes 73732
  107.6 0.6 copy-start.5
  132.0 0.7 copy-start.7

commit v4 on v3

v4 whole, which is shorter than its diff:
```python
import functools

import jax
import jax.numpy as jnp
from jax import lax
from jax.experimental import pallas as pl
from jax.experimental.pallas import tpu as pltpu
from jax.sharding import Mesh, PartitionSpec as P

never_order = 2.0**30
low = -3e38
Y, X, C, Z = 4, 4, 2, 8
ROWS = 3072
GROUPS = 32
CAP = 192
WIDTH = 128
PARTS = (128, 64)
SIZES = (Y * 128, Y * 64)
META = 16
LINES = ROWS // 128
ALL = ("y", "x", "core", "z")
PARAMS = pltpu.CompilerParams(vmem_limit_bytes=40 * 2**20)
VMEM = pl.BlockSpec(memory_space=pltpu.VMEM)
SMEM = pl.BlockSpec(memory_space=pltpu.SMEM)


def routes(move):
    pairs = []
    for y in range(Y):
        for x in range(X):
            for c in range(C):
                for z in range(Z):
                    y2, x2, c2, z2 = move(y, x, c, z)
                    to = (((y2 % Y) * X + x2 % X) * C + c2 % C) * Z + z2 % Z
                    pairs.append((((y * X + x) * C + c) * Z + z, to))
    return pairs


def place_kernel(
    ids_any, rows_any, first_ref, second_ref, slot_ref,
    ids_ref, rows_ref, member_ref, wide_ref, out_ref, spot_ref, spot_sm, sems,
):
    ids_copy = pltpu.make_async_copy(ids_any, ids_ref, sems.at[0])
    rows_copy = pltpu.make_async_copy(rows_any, rows_ref, sems.at[1])
    ids_copy.start()
    rows_copy.start()
    out_ref[...] = jnp.zeros_like(out_ref)
    r = lax.broadcasted_iota(jnp.int32, (128, 256), 0)
    c = lax.broadcasted_iota(jnp.int32, (128, 256), 1)
    weights = ((r < c) | (c >= 128)).astype(jnp.float32).astype(jnp.bfloat16)
    group = lax.broadcasted_iota(jnp.int32, (GROUPS, 128), 0)
    ids_copy.wait()
    for i in range(LINES):
        hit = group == ids_ref[pl.ds(i, 1), :]
        member_ref[pl.ds(i * GROUPS, GROUPS), :] = hit.astype(jnp.float32).astype(jnp.bfloat16)
    counts = jnp.dot(member_ref[...], weights, preferred_element_type=jnp.float32)
    carry = jnp.zeros((GROUPS, 128), jnp.float32)
    for i in range(LINES):
        part = counts[i * GROUPS : (i + 1) * GROUPS]
        line = ids_ref[pl.ds(i, 1), :]
        within = jnp.sum(jnp.where(group == line, part[:, :128] + carry, 0.0), axis=0, keepdims=True)
        within = within.astype(jnp.int32)
        slot_ref[pl.ds(i, 1), :] = line * CAP + within
        spot_ref[pl.ds(i, 1), :] = jnp.where(
            within < PARTS[0],
            line * PARTS[0] + within,
            GROUPS * PARTS[0] + line * PARTS[1] + within - PARTS[0],
        )
        carry = carry + part[:, 128:]
    copy = pltpu.make_async_copy(spot_ref, spot_sm, sems.at[2])
    copy.start()
    rows_copy.wait()
    wide_ref[...] = rows_ref[...].astype(jnp.float32)
    copy.wait()

    @pl.loop(0, LINES)
    def _(i):
        for lane in range(128):
            spot = spot_sm[i, lane]
            out_ref[pl.ds(spot, 1), :] = wide_ref[pl.ds(i * 128 + lane, 1), :]

    split = GROUPS * PARTS[0]
    first_ref[...] = out_ref[pl.ds(0, split), :].astype(jnp.bfloat16)
    second_ref[...] = out_ref[pl.ds(split, GROUPS * PARTS[1]), :].astype(jnp.bfloat16)


def place(ids, rows):
    return pl.pallas_call(
        place_kernel,
        out_shape=(
            jax.ShapeDtypeStruct((GROUPS * PARTS[0], WIDTH), jnp.bfloat16),
            jax.ShapeDtypeStruct((GROUPS * PARTS[1], WIDTH), jnp.bfloat16),
            jax.ShapeDtypeStruct((LINES, 128), jnp.int32),
        ),
        in_specs=[pl.BlockSpec(memory_space=pl.ANY)] * 2,
        out_specs=(VMEM, VMEM, VMEM),
        scratch_shapes=[
            pltpu.VMEM((LINES, 128), jnp.int32),
            pltpu.VMEM((ROWS, WIDTH), jnp.bfloat16),
            pltpu.VMEM((LINES * GROUPS, 128), jnp.bfloat16),
            pltpu.VMEM((ROWS, WIDTH), jnp.float32),
            pltpu.VMEM((GROUPS * CAP, WIDTH), jnp.float32),
            pltpu.VMEM((LINES, 128), jnp.int32),
            pltpu.SMEM((LINES, 128), jnp.int32),
            pltpu.SemaphoreType.DMA((3,)),
        ],
        compiler_params=PARAMS,
        name="place",
    )(ids, rows)


def ranks_kernel(ids_ref, slot_ref, orders_ref, table_ref):
    group = lax.broadcasted_iota(jnp.int32, (GROUPS, 128), 0)
    spot = lax.broadcasted_iota(jnp.int32, (CAP, 128), 0)
    total = jnp.zeros((3 * GROUPS, CAP), jnp.float32)
    for i in range(LINES):
        ids = ids_ref[pl.ds(i, 1), :]
        within = slot_ref[pl.ds(i, 1), :] - ids * CAP
        value = orders_ref[pl.ds(i, 1), :] + 1
        hit = group == ids
        digits = [
            jnp.where(hit, digit.astype(jnp.float32), 0.0)
            for digit in (value & 255, (value >> 8) & 255, value >> 16)
        ]
        left = jnp.concatenate(digits, axis=0).astype(jnp.bfloat16)
        right = (spot == within).astype(jnp.float32).astype(jnp.bfloat16)
        total = total + dot_rows(left, right)
    value = total[:GROUPS] + 256.0 * total[GROUPS : 2 * GROUPS] + 65536.0 * total[2 * GROUPS :]
    table_ref[...] = value


def ranks(ids, slots, orders):
    return pl.pallas_call(
        ranks_kernel,
        out_shape=jax.ShapeDtypeStruct((GROUPS, CAP), jnp.float32),
        in_specs=[VMEM] * 3,
        out_specs=VMEM,
        compiler_params=PARAMS,
        name="ranks",
    )(ids, slots, orders)


def dot_rows(p, q):
    return lax.dot_general(p, q, (((1,), (1,)), ((), ())), preferred_element_type=jnp.float32)


def eye():
    r = lax.broadcasted_iota(jnp.int32, (128, 128), 0)
    return r == lax.broadcasted_iota(jnp.int32, (128, 128), 1)


def to_row(col):
    pieces = []
    for i in range(col.shape[0] // 128):
        piece = jnp.broadcast_to(col[i * 128 : (i + 1) * 128], (128, 128))
        pieces.append(jnp.max(jnp.where(eye(), piece, low), axis=0, keepdims=True))
    return jnp.concatenate(pieces, axis=1)


def to_col(row):
    pieces = []
    for i in range(row.shape[1] // 128):
        piece = jnp.broadcast_to(row[:, i * 128 : (i + 1) * 128], (128, 128))
        pieces.append(jnp.max(jnp.where(eye(), piece, low), axis=1, keepdims=True))
    return jnp.concatenate(pieces, axis=0)


def gather_kernel(size, in_ref, rank_ref, out_ref, meta_ref):
    part = size // Y
    cols = []
    for y in range(Y):
        total = jnp.zeros((part, WIDTH), jnp.float32)
        for z in range(Z):
            piece = in_ref[pl.ds((y * Z + z) * part, part), :]
            out_ref[pl.ds(y * part, part), pl.ds(z * WIDTH, WIDTH)] = piece
            wide = piece.astype(jnp.float32)
            total = total + wide * wide
        cols.append(lax.rsqrt(jnp.sum(total, axis=1, keepdims=True) + 1e-06))
    inverse = to_row(jnp.concatenate(cols, axis=0))
    high = inverse.astype(jnp.bfloat16).astype(jnp.float32)
    middle = (inverse - high).astype(jnp.bfloat16).astype(jnp.float32)
    rank = rank_ref[...].astype(jnp.int32)
    lines = (high, middle, inverse - high - middle, rank & 255, (rank >> 8) & 255, rank >> 16)
    meta_ref[...] = jnp.zeros_like(meta_ref)
    for i, line in enumerate(lines):
        meta_ref[pl.ds(i, 1), pl.ds(0, size)] = line.astype(jnp.float32)
    out_ref[pl.ds(size, META), :] = meta_ref[...].astype(jnp.bfloat16)


def gather(size, arrived, rank):
    return pl.pallas_call(
        functools.partial(gather_kernel, size),
        out_shape=jax.ShapeDtypeStruct((size + META, Z * WIDTH), jnp.bfloat16),
        in_specs=[VMEM] * 2,
        out_specs=VMEM,
        scratch_shapes=[pltpu.VMEM((META, Z * WIDTH), jnp.float32)],
        compiler_params=PARAMS,
        name="gather",
    )(arrived, rank)


def size_of(ref):
    return ref.shape[0] - META


def row_meta(ref):
    size = size_of(ref)
    meta = ref[pl.ds(size, META), pl.ds(0, size)].astype(jnp.float32)
    rank = meta[3:4] + 256.0 * meta[4:5] + 65536.0 * meta[5:6]
    return meta[0:1] + meta[1:2] + meta[2:3], jnp.where(rank > 0, rank, never_order)


def meet(best, p_name, p_ref, others):
    size = size_of(p_ref)
    inv_p, rank_p = (to_col(row) for row in row_meta(p_ref))
    p_best = jnp.full((size, 128), low, jnp.float32)
    for q_name, q_ref in others:
        inv_q, rank_q = row_meta(q_ref)
        q_best = []
        for j in range(0, size_of(q_ref), 256):
            s = dot_rows(p_ref[pl.ds(0, size), :], q_ref[pl.ds(j, 256), :])
            s = s * inv_p * inv_q[:, j : j + 256]
            earlier = rank_q[:, j : j + 256] < rank_p
            mine = jnp.where(earlier, s, low)
            p_best = jnp.maximum(p_best, jnp.maximum(mine[:, :128], mine[:, 128:]))
            if q_name != p_name:
                q_best.append(jnp.max(jnp.where(earlier, low, s), axis=0, keepdims=True))
        if q_best:
            record(best, q_name, jnp.concatenate(q_best, axis=1))
    record(best, p_name, to_row(jnp.max(p_best, axis=1, keepdims=True)))


def record(best, name, row):
    at = (pl.ds(name, 1), pl.ds(0, row.shape[1]))
    best[at] = jnp.maximum(best[at], row)


O1, O2, U1, U2, V1, V2, E1, E2, W1, W2 = range(10)


def first_kernel(spots, o1, u1, v1, e1, w1, best):
    best[...] = jnp.full_like(best, -1.0)
    meet(best, O1, o1, [(O1, o1), (U1, u1)])

    @pl.when(spots[0] == 0)
    def _():
        meet(best, E1, e1, [(V1, v1)])

    @pl.when(spots[0] != 0)
    def _():
        meet(best, E1, e1, [(U1, u1)])

    @pl.when(spots[1] != 0)
    def _():
        meet(best, U1, u1, [(V1, v1)])

    @pl.when(spots[1] == 0)
    def _():
        meet(best, U1, u1, [(W1, w1)])


def second_kernel(spots, o1, o2, u1, v1, e1, e2, before, best):
    best[...] = before[...]
    meet(best, O2, o2, [(O1, o1), (O2, o2), (U1, u1), (V1, v1)])
    meet(best, E2, e2, [(O1, o1), (U1, u1), (V1, v1)])

    @pl.when(spots[0] == 0)
    def _():
        meet(best, O1, o1, [(E1, e1)])

    @pl.when(spots[0] != 0)
    def _():
        meet(best, O2, o2, [(E2, e2)])


def third_kernel(spots, o2, u2, v2, e2, before, best):
    best[...] = before[...]
    meet(best, O2, o2, [(U2, u2)])

    @pl.when(spots[0] == 0)
    def _():
        meet(best, E2, e2, [(V2, v2)])

    @pl.when(spots[0] != 0)
    def _():
        meet(best, E2, e2, [(U2, u2)])


def fourth_kernel(spots, u1, u2, v1, v2, w1, w2, before, out, best, long, short):
    best[...] = before[...]

    @pl.when(spots[1] != 0)
    def _():
        meet(best, U1, u1, [(V2, v2)])
        meet(best, U2, u2, [(V1, v1), (V2, v2)])

    @pl.when(spots[1] == 0)
    def _():
        meet(best, U1, u1, [(W2, w2)])
        meet(best, U2, u2, [(W1, w1), (W2, w2)])

    long[...] = jnp.full_like(long, -1.0)
    short[...] = jnp.full_like(short, -1.0)
    for i in range(5):
        for y in range(Y):
            at = pl.ds(spots[2 + i] * Y + y, 1)
            long[at, :] = best[pl.ds(2 * i, 1), pl.ds(y * PARTS[0], PARTS[0])]
            pair = best[pl.ds(2 * i + 1, 1), pl.ds(y // 2 * 128, 128)]
            short[at, :] = pltpu.roll(pair, 64, 1) if y % 2 else pair
    out[:, pl.ds(0, PARTS[0])] = long[...]
    out[:, pl.ds(PARTS[0], PARTS[1])] = short[:, pl.ds(0, PARTS[1])]


def scores_call(kernel, units, inputs, out, scratch, name):
    return pl.pallas_call(
        kernel,
        out_shape=jax.ShapeDtypeStruct(out, jnp.float32),
        in_specs=[SMEM] + [VMEM] * (len(inputs) - 1),
        out_specs=VMEM,
        scratch_shapes=scratch,
        compiler_params=PARAMS,
        cost_estimate=pl.CostEstimate(
            flops=int(units * 2 * 256 * 256 * 1024), bytes_accessed=4 * 2**20, transcendentals=0
        ),
        name=name,
    )(*inputs)


def answer_kernel(ids_ref, slot_ref, table_ref, out_ref):
    table = table_ref[...]
    high = table.astype(jnp.bfloat16)
    rest = table - high.astype(jnp.float32)
    middle = rest.astype(jnp.bfloat16)
    small = (rest - middle.astype(jnp.float32)).astype(jnp.bfloat16)
    pieces = jnp.concatenate([high, middle, small], axis=0)
    group = lax.broadcasted_iota(jnp.int32, (3 * GROUPS, 128), 0) & (GROUPS - 1)
    place_in = lax.broadcasted_iota(jnp.int32, (CAP, 128), 0)
    for i in range(LINES):
        ids = ids_ref[pl.ds(i, 1), :]
        within = slot_ref[pl.ds(i, 1), :] - ids * CAP
        where = (ids & (Z - 1)) * Y + (ids >> 3)
        member = (group == where).astype(jnp.float32).astype(jnp.bfloat16)
        found = lax.dot_general(
            pieces, member, (((0,), (0,)), ((), ())), preferred_element_type=jnp.float32
        )
        out_ref[pl.ds(i, 1), :] = jnp.sum(
            jnp.where(place_in == within, found, 0.0), axis=0, keepdims=True
        )


def answer(ids, slots, table):
    return pl.pallas_call(
        answer_kernel,
        out_shape=jax.ShapeDtypeStruct((LINES, 128), jnp.float32),
        in_specs=[VMEM] * 3,
        out_specs=VMEM,
        compiler_params=PARAMS,
        name="answer",
    )(ids, slots, table)


def shards(embeds, cluster_ids, orders):
    y, x, core, z = (lax.axis_index(name) for name in ALL)
    ids = cluster_ids.reshape(LINES, 128)
    *placed, slots = place(ids, embeds)
    arrived = [
        lax.all_to_all(
            rows.reshape(GROUPS, part, WIDTH), ("y", "z"), split_axis=0, concat_axis=0, tiled=True
        ).reshape(GROUPS * part, WIDTH)
        for rows, part in zip(placed, PARTS)
    ]

    table = ranks(ids, slots, orders.reshape(LINES, 128)).reshape(Y, Z, CAP)
    table = lax.dynamic_index_in_dim(table, z, 1, keepdims=False)
    rank_parts = []
    for j in range(Y):
        row = lax.dynamic_slice_in_dim(table, (y + j) % Y, 1, 0)
        if j:
            row = lax.ppermute(row, ALL, routes(lambda y, x, c, z: (y + j, x, c, z)))
        rank_parts.append(row)
    member_ranks = jnp.concatenate(rank_parts)[(y - jnp.arange(Y)) % Y]
    rank1 = member_ranks[:, : PARTS[0]].reshape(1, SIZES[0])
    rank2 = member_ranks[:, PARTS[0] :].reshape(1, SIZES[1])

    step = 1 - 2 * core
    near, far = (x - step) % X, (x + step) % X
    spots = jnp.stack(
        [
            core,
            ((x < X // 2) == (core == 0)).astype(jnp.int32),
            x * C + core,
            near * C + core,
            far * C + core,
            x * C + 1 - core,
            far * C + 1 - core,
        ]
    ).astype(jnp.int32)

    swap = routes(lambda y, x, c, z: (y, x, 1 - c, z))
    ahead = routes(lambda y, x, c, z: (y, x + 1 - 2 * c, c, z))
    behind = routes(lambda y, x, c, z: (y, x - 1 + 2 * c, c, z))

    def share(own, after=()):
        u = lax.ppermute(own, ALL, ahead)
        v = lax.ppermute(own, ALL, behind)
        e = lax.ppermute(own, ALL, swap)
        u, *after = lax.optimization_barrier((u, *after))
        return (u, v, e, lax.ppermute(u, ALL, swap), *after)

    o1 = gather(SIZES[0], arrived[0], rank1)
    u1, v1, e1, w1, later = share(o1, (arrived[1],))
    o2 = gather(SIZES[1], later, rank2)
    u2, v2, e2, w2 = share(o2)
    best = scores_call(first_kernel, 16, (spots, o1, u1, v1, e1, w1), (16, SIZES[0]), [], "first")
    best = scores_call(
        second_kernel, 17, (spots, o1, o2, u1, v1, e1, e2, best), (16, SIZES[0]), [], "second"
    )
    best = scores_call(third_kernel, 2, (spots, o2, u2, v2, e2, best), (16, SIZES[0]), [], "third")
    best = scores_call(
        fourth_kernel, 5, (spots, u1, u2, v1, v2, w1, w2, best), (GROUPS, CAP),
        [pltpu.VMEM(size, jnp.float32) for size in ((16, SIZES[0]), (GROUPS, 128), (GROUPS, 128))],
        "fourth",
    )
    back = lax.all_to_all(best, ("x", "core", "y"), split_axis=0, concat_axis=0, tiled=True)
    merged = jnp.max(back.reshape(X * C, Y, CAP), axis=0)
    table = lax.all_to_all(
        jnp.broadcast_to(merged[None], (Z, Y, CAP)), "z", split_axis=0, concat_axis=0, tiled=True
    )
    return answer(ids, slots, table.reshape(GROUPS, CAP)).reshape(ROWS)


def solution(mesh):
    fine = Mesh(mesh.devices.reshape(Y, X, C, Z), ALL)
    clus = ("y", "x", "core")
    return jax.shard_map(
        shards,
        mesh=fine,
        in_specs=(P(clus, "z"), P(clus), P(clus)),
        out_specs=P(clus),
        check_vma=False,
    )
```

time: 135 us -> 126 us (0.933)
  blocking collectives: 51 us -> 22.2 us
  waiting for transfers between devices: 22.3 us -> 38.5 us
  starting transfers between devices: 23.7 us -> 36.8 us
  local copies, waits for them, and re-layouts: 9.83 us -> 2.68 us
  Pallas kernels: 26.7 us -> 25 us
    all_gather x1 -> x0, blocking collectives: 28.1 us -> none  [shards(): lax.all_gather(ranks(ids, slots, orders.reshape(LINES, 128)), ('y', 'x',...]
    all_to_all x1 -> x2, waiting for transfers between devices: 5.83 us -> 29.4 us  [shards(): lax.all_to_all(rows.reshape(GROUPS, part, WIDTH), ('y', 'z'), split_axis=...]
    all_to_all x1 -> x2, starting transfers between devices: 12 us -> 20.6 us  [shards(): lax.all_to_all(rows.reshape(GROUPS, part, WIDTH), ('y', 'z'), split_axis=...]
    ppermute x4 -> x11, waiting for transfers between devices: 16.5 us -> 9.06 us  [the longest x2 7.51 us: share(): u = lax.ppermute(own, ALL, ahead)]
    ppermute x4 -> x11, starting transfers between devices: 11.7 us -> 16.2 us  [the longest x2 5.77 us: share(): return (u, v, e, lax.ppermute(u, ALL, swap), *after)]
    unnamed x20 -> x8, local copies, waits for them, and re-layouts: 4.34 us -> 1.85 us
    transpose x3 -> x0, local copies, waits for them, and re-layouts: 1.85 us -> none  [the longest x1 1.02 us: shards(): arrived.reshape(Y, Z, CAP, WIDTH).transpose(0, 2, 1, 3)]
    optimization_barrier x1 -> x0, local copies, waits for them, and re-layouts: 1.73 us -> none  [shards(): lax.optimization_barrier((arrived, order_rows, order_cols))]
  transfers between devices with their start and end apart: 5 -> 13, of which waited for: 3 -> 5; matrix products, arithmetic and copies ran while one was open for 3% -> 1% of each run, Pallas kernels for 11% -> 11%
where the time goes in v4:
time: 126 us; the launch traced here: 125 us
  waiting for transfers between devices  38.5 us (31%)
  starting transfers between devices  36.8 us (29%)
  Pallas kernels  25 us (20%)
  blocking collectives  22.2 us (18%)
  local copies, waits for them, and re-layouts  2.68 us (2%)
    all_to_all x2, waiting for transfers between devices, shards(): lax.all_to_all(rows.reshape(GROUPS, part, WIDTH), ('y', 'z'), split_axis=...  29.4 us
    all_to_all x2, starting transfers between devices, shards(): lax.all_to_all(rows.reshape(GROUPS, part, WIDTH), ('y', 'z'), split_axis=...  20.6 us
    pallas_call x4, Pallas kernels, scores_call(): pl.pallas_call(kernel, out_shape=jax.ShapeDtypeStruct(out, jnp.float32),...  15.9 us
    all_to_all x1, blocking collectives, shards(): lax.all_to_all(best, ('x', 'core', 'y'), split_axis=0, concat_axis=0, til...  11.4 us
    all_to_all x1, blocking collectives, shards(): lax.all_to_all(jnp.broadcast_to(merged[None], (Z, Y, CAP)), 'z', split_ax...  10.8 us
    ppermute x2, waiting for transfers between devices, share(): u = lax.ppermute(own, ALL, ahead)  7.51 us
    ppermute x2, starting transfers between devices, share(): return (u, v, e, lax.ppermute(u, ALL, swap), *after)  5.77 us
    pallas_call x1, Pallas kernels, place(): pl.pallas_call(place_kernel, out_shape=(jax.ShapeDtypeStruct((GROUPS * PA...  5.16 us
  transfers between devices with their start and end apart: 13, of which 5 were waited for; matrix products, arithmetic and copies ran while one was open for 1% of the time, Pallas kernels for 11%

profile of v4, /device:TPU:1, one launch (start us, length us, event | category | flops | bytes accessed | tf_op | source)
XLA Modules:
  0.0 125.5 jit_solution(6564672287852508308)
XLA Ops:
  0.0 1.1 copy-done
  1.8 5.2 %place.1 = (bf16[4096,128]{1,0:T(8,128)(2,1)}, bf16[2048,128]{1,0:T(8,128)(2,1)}, s32[24,128]{1,0:T(8,128)S(1)}) custom-call(s32[24,128]{1,0:T(8,128)S(1)} %bitcast.30, bf16[3072,128]{1,0:T(8,128)(2,1)S(1)} %copy-done), custom_call_target="tpu_custom_call" | custom-call | tf_op jit(solution)/shard_map/place/pallas_call | solution.py:88
  7.0 12.0 %all-to-all-start = ((bf16[32,128,128]{2,1,0:T(8,128)(2,1)}), bf16[32,128,128]{2,1,0:T(8,128)(2,1)S(1)}, u32[]{:S(2)}, u32[]{:S(2)}) async-start(bf16[32,128,128]{2,1,0:T(8,128)(2,1)} %bitcast.8), calls=%async_computation | async-start | bytes 2097152 | tf_op jit(solution)/shard_map/all_to_all | solution.py:367
  20.1 1.3 %collective-permute-start = (f32[1,192]{1,0:T(1,128)S(1)}, f32[1,192]{1,0:T(1,128)S(1)}, u32[]{:S(2)}, u32[]{:S(2)}) collective-permute-start(f32[1,192]{1,0:T(1,128)S(1)} %get-tuple-element.18), channel_id=1, source_target_pairs={{0,64},{1,65},{2,66},{3,67},{4,68},{5,69},{6,70},{7,71},{8,72},{9,... | collective-permute-start | bytes 2312 | tf_op jit(solution)/shard_map/ppermute | solution.py:379
  21.4 2.4 %collective-permute-start.1 = (f32[1,192]{1,0:T(1,128)S(1)}, f32[1,192]{1,0:T(1,128)S(1)}, u32[]{:S(2)}, u32[]{:S(2)}) collective-permute-start(f32[1,192]{1,0:T(1,128)S(1)} %get-tuple-element.17), channel_id=1, source_target_pairs={{0,128},{1,129},{2,130},{3,131},{4,132},{5,133},{6,134},{7,135},{8... | collective-permute-start | bytes 2312 | tf_op jit(solution)/shard_map/ppermute | solution.py:379
  23.8 1.1 collective-permute-start.2
  25.6 1.0 collective-permute-done.2
  27.1 16.6 %all-to-all-done = bf16[32,128,128]{2,1,0:T(8,128)(2,1)S(1)} async-done(((bf16[32,128,128]{2,1,0:T(8,128)(2,1)}), bf16[32,128,128]{2,1,0:T(8,128)(2,1)S(1)}, u32[]{:S(2)}, u32[]{:S(2)}) %all-to-all-start) | async-done | bytes 1048608 | tf_op jit(solution)/shard_map/all_to_all | solution.py:367
  43.7 1.5 %gather.8.o1 = bf16[528,1024]{1,0:T(8,128)(2,1)} custom-call(bf16[4096,128]{1,0:T(8,128)(2,1)S(1)} %bitcast.27, f32[1,512]{1,0:T(1,128)S(1)} %bitcast.35), custom_call_target="tpu_custom_call" | custom-call | tf_op jit(solution)/shard_map/gather/pallas_call | solution.py:191
  45.2 2.5 %collective-permute-start.3 = (bf16[528,1024]{1,0:T(8,128)(2,1)}, bf16[528,1024]{1,0:T(8,128)(2,1)S(1)}, u32[]{:S(2)}, u32[]{:S(2)}) collective-permute-start(bf16[528,1024]{1,0:T(8,128)(2,1)} %gather.8.o1), channel_id=1, source_target_pairs={{0,16},{1,17},{2,18},{3,19},{4,20},{5,21},{6,22},{7,23},{8,56},{9,... | collective-permute-start | bytes 3244040 | tf_op jit(solution)/shard_map/ppermute | solution.py:404
  47.7 8.6 %all-to-all-start.1 = ((bf16[32,64,128]{2,1,0:T(8,128)(2,1)}), bf16[32,64,128]{2,1,0:T(8,128)(2,1)S(1)}, u32[]{:S(2)}, u32[]{:S(2)}) async-start(bf16[32,64,128]{2,1,0:T(8,128)(2,1)} %bitcast.18), calls=%async_computation.1 | async-start | bytes 1048576 | tf_op jit(solution)/shard_map/all_to_all | solution.py:367
  56.9 1.2 collective-permute-start.5
  58.1 12.8 %all-to-all-done.1 = bf16[32,64,128]{2,1,0:T(8,128)(2,1)S(1)} async-done(((bf16[32,64,128]{2,1,0:T(8,128)(2,1)}), bf16[32,64,128]{2,1,0:T(8,128)(2,1)S(1)}, u32[]{:S(2)}, u32[]{:S(2)}) %all-to-all-start.1) | async-done | bytes 524320 | tf_op jit(solution)/shard_map/all_to_all | solution.py:367
  70.9 3.1 %collective-permute-start.7 = (bf16[528,1024]{1,0:T(8,128)(2,1)S(1)}, bf16[528,1024]{1,0:T(8,128)(2,1)}, u32[]{:S(2)}, u32[]{:S(2)}) collective-permute-start(bf16[528,1024]{1,0:T(8,128)(2,1)S(1)} %collective-permute-done.3.u1), channel_id=1, source_target_pairs={{0,8},{1,9},{2,10},{3,11},{4,12},{5,13},{6,14},{7,15},{8,0},{9,1},... | collective-permute-start | bytes 3244040 | tf_op jit(solution)/shard_map/ppermute | solution.py:408
  74.4 1.2 collective-permute-start.4
  75.7 7.5 %collective-permute-done.4.u2 = bf16[272,1024]{1,0:T(8,128)(2,1)S(1)} collective-permute-done((bf16[272,1024]{1,0:T(8,128)(2,1)S(1)}, bf16[272,1024]{1,0:T(8,128)(2,1)S(1)}, u32[]{:S(2)}, u32[]{:S(2)}) %collective-permute-start.4) | collective-permute-done | bytes 557088 | tf_op jit(solution)/shard_map/ppermute | solution.py:404
  83.2 2.7 %collective-permute-start.8 = (bf16[272,1024]{1,0:T(8,128)(2,1)S(1)}, bf16[272,1024]{1,0:T(8,128)(2,1)S(1)}, u32[]{:S(2)}, u32[]{:S(2)}) collective-permute-start(bf16[272,1024]{1,0:T(8,128)(2,1)S(1)} %collective-permute-done.4.u2), channel_id=1, source_target_pairs={{0,8},{1,9},{2,10},{3,11},{4,12},{5,13},{6,14},{7,15},{8,0},{9,1},... | collective-permute-start | bytes 1671176 | tf_op jit(solution)/shard_map/ppermute | solution.py:408
  86.0 6.0 %first.1.before = f32[16,512]{1,0:T(8,128)S(1)} custom-call(s32[7]{0:T(128)S(1)} %stack.35.spots, bf16[528,1024]{1,0:T(8,128)(2,1)} %gather.8.o1, bf16[528,1024]{1,0:T(8,128)(2,1)S(1)} %collective-permute-done.3.u1, bf16[528,1024]{1,0:T(8,128)(2,1)} %collective-permute-done.5.v1, bf16[528,1024]{1,0:T(8,128)(2,1)} %collective-permute-done.10.e1, ...), custom_call_target="tpu_custom_call" | custom-call | flops 2147483648 | bytes 4194304 | tf_op jit(solution)/shard_map/first/pallas_call | solution.py:315
  91.9 5.0 %second.1.before = f32[16,512]{1,0:T(8,128)S(1)} custom-call(s32[7]{0:T(128)S(1)} %stack.35.spots, bf16[528,1024]{1,0:T(8,128)(2,1)} %gather.8.o1, bf16[272,1024]{1,0:T(8,128)(2,1)S(1)} %gather.9.o2, bf16[528,1024]{1,0:T(8,128)(2,1)S(1)} %collective-permute-done.3.u1, bf16[528,1024]{1,0:T(8,128)(2,1)} %collective-permute-done.5.v1, ...), custom_call_target="tpu_custom_call" | custom-call | flops 2281701376 | bytes 4194304 | tf_op jit(solution)/shard_map/second/pallas_call | solution.py:315
  97.0 2.0 %third.1.before = f32[16,512]{1,0:T(8,128)S(1)} custom-call(s32[7]{0:T(128)S(1)} %stack.35.spots, bf16[272,1024]{1,0:T(8,128)(2,1)S(1)} %gather.9.o2, bf16[272,1024]{1,0:T(8,128)(2,1)S(1)} %collective-permute-done.4.u2, bf16[272,1024]{1,0:T(8,128)(2,1)S(1)} %collective-permute-done.6.v2, bf16[272,1024]{1,0:T(8,128)(2,1)} %collective-permute-done.9.e2, ...), custom_call_target="tpu_custom_call" | custom-call | flops 268435456 | bytes 4194304 | tf_op jit(solution)/shard_map/third/pallas_call | solution.py:315
  99.0 2.9 %fourth.1 = f32[32,192]{1,0:T(8,128)S(1)} custom-call(s32[7]{0:T(128)S(1)} %stack.35.spots, bf16[528,1024]{1,0:T(8,128)(2,1)S(1)} %collective-permute-done.3.u1, bf16[272,1024]{1,0:T(8,128)(2,1)S(1)} %collective-permute-done.4.u2, bf16[528,1024]{1,0:T(8,128)(2,1)} %collective-permute-done.5.v1, bf16[272,1024]{1,0:T(8,128)(2,1)S(1)} %collective-permute-done.6.v2, ...), custom_call_target="tpu_custom_call" | custom-call | flops 671088640 | bytes 4194304 | tf_op jit(solution)/shard_map/fourth/pallas_call | solution.py:315
  101.9 11.4 %all_to_all.24 = f32[32,1,192]{2,1,0:T(1,128)S(1)} all-to-all(f32[32,1,192]{2,1,0:T(1,128)S(1)} %copy.4), channel_id=1, replica_groups=mesh['y'=4,'x'=4,'core'=2,'z'=8] {'x','core','y'}, dimensions={0} | all-to-all | bytes 49152 | tf_op jit(solution)/shard_map/all_to_all | solution.py:424
  113.5 10.8 %all_to_all.25 = f32[8,4,192]{2,1,0:T(4,128)S(1)} all-to-all(f32[8,4,192]{2,1,0:T(4,128)S(1)} %broadcast_in_dim.2), channel_id=1, replica_groups=mesh['y'=4,'x'=4,'core'=2,'z'=8] {'z'}, dimensions={0} | all-to-all | bytes 49152 | tf_op jit(solution)/shard_map/all_to_all | solution.py:426
  124.3 1.2 answer.1
  (36 shorter events, 4.1 us)
Async XLA Ops:
  0.0 1.1 copy-start
  1.1 0.7 copy-start.1
  7.0 12.1 %copy-start.2 = (s32[3072]{0:T(1024)S(1)}, s32[3072]{0:T(1024)}, u32[]{:S(2)}) copy-start(s32[3072]{0:T(1024)} %param.4) | copy-start | bytes 36868
  7.0 12.1 %copy-start.3 = (s32[3072]{0:T(1024)S(1)}, s32[3072]{0:T(1024)}, u32[]{:S(2)}) copy-start(s32[3072]{0:T(1024)} %param.5) | copy-start | bytes 36868
  7.0 36.7 %all-to-all-start = ((bf16[32,128,128]{2,1,0:T(8,128)(2,1)}), bf16[32,128,128]{2,1,0:T(8,128)(2,1)S(1)}, u32[]{:S(2)}, u32[]{:S(2)}) async-start(bf16[32,128,128]{2,1,0:T(8,128)(2,1)} %bitcast.8), calls=%async_computation | async-start | bytes 2097152 | tf_op jit(solution)/shard_map/all_to_all | solution.py:367
  20.1 4.9 %collective-permute-start = (f32[1,192]{1,0:T(1,128)S(1)}, f32[1,192]{1,0:T(1,128)S(1)}, u32[]{:S(2)}, u32[]{:S(2)}) collective-permute-start(f32[1,192]{1,0:T(1,128)S(1)} %get-tuple-element.18), channel_id=1, source_target_pairs={{0,64},{1,65},{2,66},{3,67},{4,68},{5,69},{6,70},{7,71},{8,72},{9,... | collective-permute-start | bytes 2312 | tf_op jit(solution)/shard_map/ppermute | solution.py:379
  21.4 4.2 %collective-permute-start.1 = (f32[1,192]{1,0:T(1,128)S(1)}, f32[1,192]{1,0:T(1,128)S(1)}, u32[]{:S(2)}, u32[]{:S(2)}) collective-permute-start(f32[1,192]{1,0:T(1,128)S(1)} %get-tuple-element.17), channel_id=1, source_target_pairs={{0,128},{1,129},{2,130},{3,131},{4,132},{5,133},{6,134},{7,135},{8... | collective-permute-start | bytes 2312 | tf_op jit(solution)/shard_map/ppermute | solution.py:379
  23.8 2.7 %collective-permute-start.2 = (f32[1,192]{1,0:T(1,128)S(1)}, f32[1,192]{1,0:T(1,128)S(1)}, u32[]{:S(2)}, u32[]{:S(2)}) collective-permute-start(f32[1,192]{1,0:T(1,128)S(1)} %get-tuple-element.16), channel_id=1, source_target_pairs={{0,192},{1,193},{2,194},{3,195},{4,196},{5,197},{6,198},{7,199},{8... | collective-permute-start | bytes 2312 | tf_op jit(solution)/shard_map/ppermute | solution.py:379
  45.2 25.7 %collective-permute-start.3 = (bf16[528,1024]{1,0:T(8,128)(2,1)}, bf16[528,1024]{1,0:T(8,128)(2,1)S(1)}, u32[]{:S(2)}, u32[]{:S(2)}) collective-permute-start(bf16[528,1024]{1,0:T(8,128)(2,1)} %gather.8.o1), channel_id=1, source_target_pairs={{0,16},{1,17},{2,18},{3,19},{4,20},{5,21},{6,22},{7,23},{8,56},{9,... | collective-permute-start | bytes 3244040 | tf_op jit(solution)/shard_map/ppermute | solution.py:404
  47.7 23.2 %all-to-all-start.1 = ((bf16[32,64,128]{2,1,0:T(8,128)(2,1)}), bf16[32,64,128]{2,1,0:T(8,128)(2,1)S(1)}, u32[]{:S(2)}, u32[]{:S(2)}) async-start(bf16[32,64,128]{2,1,0:T(8,128)(2,1)} %bitcast.18), calls=%async_computation.1 | async-start | bytes 1048576 | tf_op jit(solution)/shard_map/all_to_all | solution.py:367
  56.3 26.9 %collective-permute-start.10 = (bf16[528,1024]{1,0:T(8,128)(2,1)}, bf16[528,1024]{1,0:T(8,128)(2,1)}, u32[]{:S(2)}, u32[]{:S(2)}) collective-permute-start(bf16[528,1024]{1,0:T(8,128)(2,1)} %gather.8.o1), channel_id=1, source_target_pairs={{0,8},{1,9},{2,10},{3,11},{4,12},{5,13},{6,14},{7,15},{8,0},{9,1},... | collective-permute-start | bytes 3244040 | tf_op jit(solution)/shard_map/ppermute | solution.py:406
  56.9 29.1 %collective-permute-start.5 = (bf16[528,1024]{1,0:T(8,128)(2,1)}, bf16[528,1024]{1,0:T(8,128)(2,1)}, u32[]{:S(2)}, u32[]{:S(2)}) collective-permute-start(bf16[528,1024]{1,0:T(8,128)(2,1)} %gather.8.o1), channel_id=1, source_target_pairs={{0,48},{1,49},{2,50},{3,51},{4,52},{5,53},{6,54},{7,55},{8,24},{9,... | collective-permute-start | bytes 3244040 | tf_op jit(solution)/shard_map/ppermute | solution.py:405
  70.9 15.1 %collective-permute-start.7 = (bf16[528,1024]{1,0:T(8,128)(2,1)S(1)}, bf16[528,1024]{1,0:T(8,128)(2,1)}, u32[]{:S(2)}, u32[]{:S(2)}) collective-permute-start(bf16[528,1024]{1,0:T(8,128)(2,1)S(1)} %collective-permute-done.3.u1), channel_id=1, source_target_pairs={{0,8},{1,9},{2,10},{3,11},{4,12},{5,13},{6,14},{7,15},{8,0},{9,1},... | collective-permute-start | bytes 3244040 | tf_op jit(solution)/shard_map/ppermute | solution.py:408
  74.4 8.8 %collective-permute-start.4 = (bf16[272,1024]{1,0:T(8,128)(2,1)S(1)}, bf16[272,1024]{1,0:T(8,128)(2,1)S(1)}, u32[]{:S(2)}, u32[]{:S(2)}) collective-permute-start(bf16[272,1024]{1,0:T(8,128)(2,1)S(1)} %gather.9.o2), channel_id=1, source_target_pairs={{0,16},{1,17},{2,18},{3,19},{4,20},{5,21},{6,22},{7,23},{8,56},{9,... | collective-permute-start | bytes 1671176 | tf_op jit(solution)/shard_map/ppermute | solution.py:404
  75.7 16.2 %collective-permute-start.9 = (bf16[272,1024]{1,0:T(8,128)(2,1)S(1)}, bf16[272,1024]{1,0:T(8,128)(2,1)}, u32[]{:S(2)}, u32[]{:S(2)}) collective-permute-start(bf16[272,1024]{1,0:T(8,128)(2,1)S(1)} %gather.9.o2), channel_id=1, source_target_pairs={{0,8},{1,9},{2,10},{3,11},{4,12},{5,13},{6,14},{7,15},{8,0},{9,1},... | collective-permute-start | bytes 1671176 | tf_op jit(solution)/shard_map/ppermute | solution.py:406
  83.2 13.8 %collective-permute-start.6 = (bf16[272,1024]{1,0:T(8,128)(2,1)S(1)}, bf16[272,1024]{1,0:T(8,128)(2,1)S(1)}, u32[]{:S(2)}, u32[]{:S(2)}) collective-permute-start(bf16[272,1024]{1,0:T(8,128)(2,1)S(1)} %gather.9.o2), channel_id=1, source_target_pairs={{0,48},{1,49},{2,50},{3,51},{4,52},{5,53},{6,54},{7,55},{8,24},{9,... | collective-permute-start | bytes 1671176 | tf_op jit(solution)/shard_map/ppermute | solution.py:405
  83.2 15.8 %collective-permute-start.8 = (bf16[272,1024]{1,0:T(8,128)(2,1)S(1)}, bf16[272,1024]{1,0:T(8,128)(2,1)S(1)}, u32[]{:S(2)}, u32[]{:S(2)}) collective-permute-start(bf16[272,1024]{1,0:T(8,128)(2,1)S(1)} %collective-permute-done.4.u2), channel_id=1, source_target_pairs={{0,8},{1,9},{2,10},{3,11},{4,12},{5,13},{6,14},{7,15},{8,0},{9,1},... | collective-permute-start | bytes 1671176 | tf_op jit(solution)/shard_map/ppermute | solution.py:408

commit v5 on v4

--- a/solution.py
+++ b/solution.py
@@ -92,7 +92,7 @@
             jax.ShapeDtypeStruct((GROUPS * PARTS[1], WIDTH), jnp.bfloat16),
             jax.ShapeDtypeStruct((LINES, 128), jnp.int32),
         ),
-        in_specs=[pl.BlockSpec(memory_space=pl.ANY)] * 2,
+        in_specs=[pl.BlockSpec(memory_space=pltpu.HBM)] * 2,
         out_specs=(VMEM, VMEM, VMEM),
         scratch_shapes=[
             pltpu.VMEM((LINES, 128), jnp.int32),
@@ -238,9 +238,18 @@
 O1, O2, U1, U2, V1, V2, E1, E2, W1, W2 = range(10)
 
 
-def first_kernel(spots, o1, u1, v1, e1, w1, best):
+def own_kernel(spots, o1, e1, best):
     best[...] = jnp.full_like(best, -1.0)
-    meet(best, O1, o1, [(O1, o1), (U1, u1)])
+    meet(best, O1, o1, [(O1, o1)])
+
+    @pl.when(spots[0] == 0)
+    def _():
+        meet(best, O1, o1, [(E1, e1)])
+
+
+def first_kernel(spots, o1, u1, v1, e1, w1, before, best):
+    best[...] = before[...]
+    meet(best, O1, o1, [(U1, u1)])
 
     @pl.when(spots[0] == 0)
     def _():
@@ -264,10 +273,6 @@
     meet(best, O2, o2, [(O1, o1), (O2, o2), (U1, u1), (V1, v1)])
     meet(best, E2, e2, [(O1, o1), (U1, u1), (V1, v1)])
 
-    @pl.when(spots[0] == 0)
-    def _():
-        meet(best, O1, o1, [(E1, e1)])
-
     @pl.when(spots[0] != 0)
     def _():
         meet(best, O2, o2, [(E2, e2)])
@@ -291,12 +296,12 @@
 
     @pl.when(spots[1] != 0)
     def _():
-        meet(best, U1, u1, [(V2, v2)])
+        meet(best, V2, v2, [(U1, u1)])
         meet(best, U2, u2, [(V1, v1), (V2, v2)])
 
     @pl.when(spots[1] == 0)
     def _():
-        meet(best, U1, u1, [(W2, w2)])
+        meet(best, W2, w2, [(U1, u1)])
         meet(best, U2, u2, [(W1, w1), (W2, w2)])
 
     long[...] = jnp.full_like(long, -1.0)
@@ -400,25 +405,31 @@
     ahead = routes(lambda y, x, c, z: (y, x + 1 - 2 * c, c, z))
     behind = routes(lambda y, x, c, z: (y, x - 1 + 2 * c, c, z))
 
-    def share(own, after=()):
+    def share(own, after):
         u = lax.ppermute(own, ALL, ahead)
         v = lax.ppermute(own, ALL, behind)
         e = lax.ppermute(own, ALL, swap)
-        u, *after = lax.optimization_barrier((u, *after))
+        u, *after = lax.optimization_barrier((u, *after(e)))
         return (u, v, e, lax.ppermute(u, ALL, swap), *after)
 
+    wide = (16, SIZES[0])
     o1 = gather(SIZES[0], arrived[0], rank1)
-    u1, v1, e1, w1, later = share(o1, (arrived[1],))
+    u1, v1, e1, w1, best, later = share(
+        o1,
+        lambda e: (scores_call(own_kernel, 8, (spots, o1, e), wide, [], "own"), arrived[1]),
+    )
     o2 = gather(SIZES[1], later, rank2)
-    u2, v2, e2, w2 = share(o2)
-    best = scores_call(first_kernel, 16, (spots, o1, u1, v1, e1, w1), (16, SIZES[0]), [], "first")
-    best = scores_call(
-        second_kernel, 17, (spots, o1, o2, u1, v1, e1, e2, best), (16, SIZES[0]), [], "second"
+    u2, v2, e2, w2, best = share(
+        o2,
+        lambda e: (
+            scores_call(first_kernel, 12, (spots, o1, u1, v1, e1, w1, best), wide, [], "first"),
+        ),
     )
-    best = scores_call(third_kernel, 2, (spots, o2, u2, v2, e2, best), (16, SIZES[0]), [], "third")
+    best = scores_call(second_kernel, 14, (spots, o1, o2, u1, v1, e1, e2, best), wide, [], "second")
+    best = scores_call(third_kernel, 2, (spots, o2, u2, v2, e2, best), wide, [], "third")
     best = scores_call(
         fourth_kernel, 5, (spots, u1, u2, v1, v2, w1, w2, best), (GROUPS, CAP),
-        [pltpu.VMEM(size, jnp.float32) for size in ((16, SIZES[0]), (GROUPS, 128), (GROUPS, 128))],
+        [pltpu.VMEM(size, jnp.float32) for size in (wide, (GROUPS, 128), (GROUPS, 128))],
         "fourth",
     )
     back = lax.all_to_all(best, ("x", "core", "y"), split_axis=0, concat_axis=0, tiled=True)

time: 126 us -> 123 us (0.976)
    ppermute x2, starting transfers between devices: 0.56 us -> 4.97 us  [share(): e = lax.ppermute(own, ALL, swap)]
    all_to_all x2, starting transfers between devices: 20.6 us -> 16.8 us  [shards(): lax.all_to_all(rows.reshape(GROUPS, part, WIDTH), ('y', 'z'), split_axis=...]
    ppermute x2, waiting for transfers between devices: 7.51 us -> 4.32 us  [share(): u = lax.ppermute(own, ALL, ahead)]
    ppermute x2, starting transfers between devices: 5.77 us -> 4.41 us  [share(): return (u, v, e, lax.ppermute(u, ALL, swap), *after)]
    pallas_call x4 -> x5, Pallas kernels: 15.9 us -> 16.1 us  [scores_call(): pl.pallas_call(kernel, out_shape=jax.ShapeDtypeStruct(out, jnp.float32),...]
  transfers between devices with their start and end apart: 13 -> 13, of which waited for: 5 -> 6; matrix products, arithmetic and copies ran while one was open for 1% -> 1% of each run, Pallas kernels for 11% -> 12%
where the time goes in v5:
time: 123 us
  waiting for transfers between devices  37.4 us (30%)
  starting transfers between devices  35.6 us (29%)
  Pallas kernels  25.2 us (20%)
  blocking collectives  21.7 us (18%)
  local copies, waits for them, and re-layouts  2.68 us (2%)
    all_to_all x2, waiting for transfers between devices, shards(): lax.all_to_all(rows.reshape(GROUPS, part, WIDTH), ('y', 'z'), split_axis=...  30.5 us
    all_to_all x2, starting transfers between devices, shards(): lax.all_to_all(rows.reshape(GROUPS, part, WIDTH), ('y', 'z'), split_axis=...  16.8 us
    pallas_call x5, Pallas kernels, scores_call(): pl.pallas_call(kernel, out_shape=jax.ShapeDtypeStruct(out, jnp.float32),...  16.1 us
    all_to_all x1, blocking collectives, shards(): lax.all_to_all(jnp.broadcast_to(merged[None], (Z, Y, CAP)), 'z', split_ax...  11.2 us
    all_to_all x1, blocking collectives, shards(): lax.all_to_all(best, ('x', 'core', 'y'), split_axis=0, concat_axis=0, til...  10.5 us
    pallas_call x1, Pallas kernels, place(): pl.pallas_call(place_kernel, out_shape=(jax.ShapeDtypeStruct((GROUPS * PA...  5.16 us
    ppermute x2, starting transfers between devices, share(): e = lax.ppermute(own, ALL, swap)  4.97 us
    ppermute x3, starting transfers between devices, shards(): row = lax.ppermute(row, ALL, routes(lambda y, x, c, z: (y + j, x, c, z)))  4.89 us
  transfers between devices with their start and end apart: 13, of which 6 were waited for; matrix products, arithmetic and copies ran while one was open for 1% of the time, Pallas kernels for 12%

profile of v5, /device:TPU:1, one launch (start us, length us, event | category | flops | bytes accessed | tf_op | source)
XLA Modules:
  0.0 122.9 jit_solution(16624546522079900278)
XLA Ops:
  0.0 1.1 copy-done
  1.8 5.2 %place.1 = (bf16[4096,128]{1,0:T(8,128)(2,1)}, bf16[2048,128]{1,0:T(8,128)(2,1)}, s32[24,128]{1,0:T(8,128)S(1)}) custom-call(s32[24,128]{1,0:T(8,128)S(1)} %bitcast.30, bf16[3072,128]{1,0:T(8,128)(2,1)S(1)} %copy-done), custom_call_target="tpu_custom_call" | custom-call | tf_op jit(solution)/shard_map/place/pallas_call | solution.py:88
  7.0 12.0 %all-to-all-start = ((bf16[32,128,128]{2,1,0:T(8,128)(2,1)}), bf16[32,128,128]{2,1,0:T(8,128)(2,1)S(1)}, u32[]{:S(2)}, u32[]{:S(2)}) async-start(bf16[32,128,128]{2,1,0:T(8,128)(2,1)} %bitcast.8), calls=%async_computation | async-start | bytes 2097152 | tf_op jit(solution)/shard_map/all_to_all | solution.py:372
  20.1 1.3 %collective-permute-start = (f32[1,192]{1,0:T(1,128)S(1)}, f32[1,192]{1,0:T(1,128)S(1)}, u32[]{:S(2)}, u32[]{:S(2)}) collective-permute-start(f32[1,192]{1,0:T(1,128)S(1)} %get-tuple-element.24), channel_id=1, source_target_pairs={{0,64},{1,65},{2,66},{3,67},{4,68},{5,69},{6,70},{7,71},{8,72},{9,... | collective-permute-start | bytes 2312 | tf_op jit(solution)/shard_map/ppermute | solution.py:384
  21.4 2.4 %collective-permute-start.1 = (f32[1,192]{1,0:T(1,128)S(1)}, f32[1,192]{1,0:T(1,128)S(1)}, u32[]{:S(2)}, u32[]{:S(2)}) collective-permute-start(f32[1,192]{1,0:T(1,128)S(1)} %get-tuple-element.23), channel_id=1, source_target_pairs={{0,128},{1,129},{2,130},{3,131},{4,132},{5,133},{6,134},{7,135},{8... | collective-permute-start | bytes 2312 | tf_op jit(solution)/shard_map/ppermute | solution.py:384
  23.8 1.1 collective-permute-start.2
  27.1 16.6 %all-to-all-done = bf16[32,128,128]{2,1,0:T(8,128)(2,1)S(1)} async-done(((bf16[32,128,128]{2,1,0:T(8,128)(2,1)}), bf16[32,128,128]{2,1,0:T(8,128)(2,1)S(1)}, u32[]{:S(2)}, u32[]{:S(2)}) %all-to-all-start) | async-done | bytes 1048608 | tf_op jit(solution)/shard_map/all_to_all | solution.py:372
  43.7 1.5 %gather.8.o1 = bf16[528,1024]{1,0:T(8,128)(2,1)} custom-call(bf16[4096,128]{1,0:T(8,128)(2,1)S(1)} %bitcast.27, f32[1,512]{1,0:T(1,128)S(1)} %bitcast.35), custom_call_target="tpu_custom_call" | custom-call | tf_op jit(solution)/shard_map/gather/pallas_call | solution.py:191
  45.2 5.0 %collective-permute-start.4 = (bf16[528,1024]{1,0:T(8,128)(2,1)}, bf16[528,1024]{1,0:T(8,128)(2,1)}, u32[]{:S(2)}, u32[]{:S(2)}) collective-permute-start(bf16[528,1024]{1,0:T(8,128)(2,1)} %gather.8.o1), channel_id=1, source_target_pairs={{0,8},{1,9},{2,10},{3,11},{4,12},{5,13},{6,14},{7,15},{8,0},{9,1},... | collective-permute-start | bytes 3244040 | tf_op jit(solution)/shard_map/ppermute | solution.py:411
  50.2 2.5 %collective-permute-start.3 = (bf16[528,1024]{1,0:T(8,128)(2,1)}, bf16[528,1024]{1,0:T(8,128)(2,1)S(1)}, u32[]{:S(2)}, u32[]{:S(2)}) collective-permute-start(bf16[528,1024]{1,0:T(8,128)(2,1)} %gather.8.o1), channel_id=1, source_target_pairs={{0,16},{1,17},{2,18},{3,19},{4,20},{5,21},{6,22},{7,23},{8,56},{9,... | collective-permute-start | bytes 3244040 | tf_op jit(solution)/shard_map/ppermute | solution.py:409
  52.7 4.8 %all-to-all-start.1 = ((bf16[32,64,128]{2,1,0:T(8,128)(2,1)}), bf16[32,64,128]{2,1,0:T(8,128)(2,1)S(1)}, u32[]{:S(2)}, u32[]{:S(2)}) async-start(bf16[32,64,128]{2,1,0:T(8,128)(2,1)} %bitcast.18), calls=%async_computation.1 | async-start | bytes 1048576 | tf_op jit(solution)/shard_map/all_to_all | solution.py:372
  57.6 2.5 %own.1.before = f32[16,512]{1,0:T(8,128)S(1)} custom-call(s32[7]{0:T(128)S(1)} %stack.35.spots, bf16[528,1024]{1,0:T(8,128)(2,1)} %gather.8.o1, bf16[528,1024]{1,0:T(8,128)(2,1)} %collective-permute-done.4.e1), custom_call_target="tpu_custom_call" | custom-call | flops 1073741824 | bytes 4194304 | tf_op jit(solution)/shard_map/own/pallas_call | solution.py:320
  60.1 13.9 %all-to-all-done.1 = bf16[32,64,128]{2,1,0:T(8,128)(2,1)S(1)} async-done(((bf16[32,64,128]{2,1,0:T(8,128)(2,1)}), bf16[32,64,128]{2,1,0:T(8,128)(2,1)S(1)}, u32[]{:S(2)}, u32[]{:S(2)}) %all-to-all-start.1) | async-done | bytes 524320 | tf_op jit(solution)/shard_map/all_to_all | solution.py:372
  74.7 1.6 %collective-permute-start.5 = (bf16[272,1024]{1,0:T(8,128)(2,1)S(1)}, bf16[272,1024]{1,0:T(8,128)(2,1)S(1)}, u32[]{:S(2)}, u32[]{:S(2)}) collective-permute-start(bf16[272,1024]{1,0:T(8,128)(2,1)S(1)} %gather.9.o2), channel_id=1, source_target_pairs={{0,16},{1,17},{2,18},{3,19},{4,20},{5,21},{6,22},{7,23},{8,56},{9,... | collective-permute-start | bytes 1671176 | tf_op jit(solution)/shard_map/ppermute | solution.py:409
  76.7 1.0 collective-permute-done.6.v1
  77.7 4.9 %first.1.before = f32[16,512]{1,0:T(8,128)S(1)} custom-call(s32[7]{0:T(128)S(1)} %stack.35.spots, bf16[528,1024]{1,0:T(8,128)(2,1)} %gather.8.o1, bf16[528,1024]{1,0:T(8,128)(2,1)S(1)} %collective-permute-done.3.u1, bf16[528,1024]{1,0:T(8,128)(2,1)S(1)} %collective-permute-done.6.v1, bf16[528,1024]{1,0:T(8,128)(2,1)} %collective-permute-done.4.e1, ...), custom_call_target="tpu_custom_call" | custom-call | flops 1610612736 | bytes 4194304 | tf_op jit(solution)/shard_map/first/pallas_call | solution.py:320
  82.6 4.3 %collective-permute-done.5.u2 = bf16[272,1024]{1,0:T(8,128)(2,1)S(1)} collective-permute-done((bf16[272,1024]{1,0:T(8,128)(2,1)S(1)}, bf16[272,1024]{1,0:T(8,128)(2,1)S(1)}, u32[]{:S(2)}, u32[]{:S(2)}) %collective-permute-start.5) | collective-permute-done | bytes 557088 | tf_op jit(solution)/shard_map/ppermute | solution.py:409
  86.9 4.2 %collective-permute-start.9 = (bf16[272,1024]{1,0:T(8,128)(2,1)S(1)}, bf16[272,1024]{1,0:T(8,128)(2,1)S(1)}, u32[]{:S(2)}, u32[]{:S(2)}) collective-permute-start(bf16[272,1024]{1,0:T(8,128)(2,1)S(1)} %collective-permute-done.5.u2), channel_id=1, source_target_pairs={{0,8},{1,9},{2,10},{3,11},{4,12},{5,13},{6,14},{7,15},{8,0},{9,1},... | collective-permute-start | bytes 1671176 | tf_op jit(solution)/shard_map/ppermute | solution.py:413
  91.1 4.6 %second.1.before = f32[16,512]{1,0:T(8,128)S(1)} custom-call(s32[7]{0:T(128)S(1)} %stack.35.spots, bf16[528,1024]{1,0:T(8,128)(2,1)} %gather.8.o1, bf16[272,1024]{1,0:T(8,128)(2,1)S(1)} %gather.9.o2, bf16[528,1024]{1,0:T(8,128)(2,1)S(1)} %collective-permute-done.3.u1, bf16[528,1024]{1,0:T(8,128)(2,1)S(1)} %collective-permute-done.6.v1, ...), custom_call_target="tpu_custom_call" | custom-call | flops 1879048192 | bytes 4194304 | tf_op jit(solution)/shard_map/second/pallas_call | solution.py:320
  95.7 1.5 %third.1.before = f32[16,512]{1,0:T(8,128)S(1)} custom-call(s32[7]{0:T(128)S(1)} %stack.35.spots, bf16[272,1024]{1,0:T(8,128)(2,1)S(1)} %gather.9.o2, bf16[272,1024]{1,0:T(8,128)(2,1)S(1)} %collective-permute-done.5.u2, bf16[272,1024]{1,0:T(8,128)(2,1)S(1)} %collective-permute-done.8.v2, bf16[272,1024]{1,0:T(8,128)(2,1)S(1)} %collective-permute-done.10.e2, ...), custom_call_target="tpu_custom_call" | custom-call | flops 268435456 | bytes 4194304 | tf_op jit(solution)/shard_map/third/pallas_call | solution.py:320
  97.2 2.5 %fourth.1 = f32[32,192]{1,0:T(8,128)S(1)} custom-call(s32[7]{0:T(128)S(1)} %stack.35.spots, bf16[528,1024]{1,0:T(8,128)(2,1)S(1)} %collective-permute-done.3.u1, bf16[272,1024]{1,0:T(8,128)(2,1)S(1)} %collective-permute-done.5.u2, bf16[528,1024]{1,0:T(8,128)(2,1)S(1)} %collective-permute-done.6.v1, bf16[272,1024]{1,0:T(8,128)(2,1)S(1)} %collective-permute-done.8.v2, ...), custom_call_target="tpu_custom_call" | custom-call | flops 671088640 | bytes 4194304 | tf_op jit(solution)/shard_map/fourth/pallas_call | solution.py:320
  99.8 10.5 %all_to_all.24 = f32[32,1,192]{2,1,0:T(1,128)S(1)} all-to-all(f32[32,1,192]{2,1,0:T(1,128)S(1)} %copy.4), channel_id=1, replica_groups=mesh['y'=4,'x'=4,'core'=2,'z'=8] {'x','core','y'}, dimensions={0} | all-to-all | bytes 49152 | tf_op jit(solution)/shard_map/all_to_all | solution.py:435
  110.5 11.2 %all_to_all.25 = f32[8,4,192]{2,1,0:T(4,128)S(1)} all-to-all(f32[8,4,192]{2,1,0:T(4,128)S(1)} %broadcast_in_dim.2), channel_id=1, replica_groups=mesh['y'=4,'x'=4,'core'=2,'z'=8] {'z'}, dimensions={0} | all-to-all | bytes 49152 | tf_op jit(solution)/shard_map/all_to_all | solution.py:437
  121.7 1.2 answer.1
  (37 shorter events, 5.1 us)
Async XLA Ops:
  0.0 1.1 copy-start
  1.1 0.7 copy-start.1
  7.0 12.1 %copy-start.2 = (s32[3072]{0:T(1024)S(1)}, s32[3072]{0:T(1024)}, u32[]{:S(2)}) copy-start(s32[3072]{0:T(1024)} %param.4) | copy-start | bytes 36868
  7.0 12.1 %copy-start.3 = (s32[3072]{0:T(1024)S(1)}, s32[3072]{0:T(1024)}, u32[]{:S(2)}) copy-start(s32[3072]{0:T(1024)} %param.5) | copy-start | bytes 36868
  7.0 36.7 %all-to-all-start = ((bf16[32,128,128]{2,1,0:T(8,128)(2,1)}), bf16[32,128,128]{2,1,0:T(8,128)(2,1)S(1)}, u32[]{:S(2)}, u32[]{:S(2)}) async-start(bf16[32,128,128]{2,1,0:T(8,128)(2,1)} %bitcast.8), calls=%async_computation | async-start | bytes 2097152 | tf_op jit(solution)/shard_map/all_to_all | solution.py:372
  20.1 4.9 %collective-permute-start = (f32[1,192]{1,0:T(1,128)S(1)}, f32[1,192]{1,0:T(1,128)S(1)}, u32[]{:S(2)}, u32[]{:S(2)}) collective-permute-start(f32[1,192]{1,0:T(1,128)S(1)} %get-tuple-element.24), channel_id=1, source_target_pairs={{0,64},{1,65},{2,66},{3,67},{4,68},{5,69},{6,70},{7,71},{8,72},{9,... | collective-permute-start | bytes 2312 | tf_op jit(solution)/shard_map/ppermute | solution.py:384
  21.4 4.2 %collective-permute-start.1 = (f32[1,192]{1,0:T(1,128)S(1)}, f32[1,192]{1,0:T(1,128)S(1)}, u32[]{:S(2)}, u32[]{:S(2)}) collective-permute-start(f32[1,192]{1,0:T(1,128)S(1)} %get-tuple-element.23), channel_id=1, source_target_pairs={{0,128},{1,129},{2,130},{3,131},{4,132},{5,133},{6,134},{7,135},{8... | collective-permute-start | bytes 2312 | tf_op jit(solution)/shard_map/ppermute | solution.py:384
  23.8 2.7 %collective-permute-start.2 = (f32[1,192]{1,0:T(1,128)S(1)}, f32[1,192]{1,0:T(1,128)S(1)}, u32[]{:S(2)}, u32[]{:S(2)}) collective-permute-start(f32[1,192]{1,0:T(1,128)S(1)} %get-tuple-element.22), channel_id=1, source_target_pairs={{0,192},{1,193},{2,194},{3,195},{4,196},{5,197},{6,198},{7,199},{8... | collective-permute-start | bytes 2312 | tf_op jit(solution)/shard_map/ppermute | solution.py:384
  45.2 12.4 %collective-permute-start.4 = (bf16[528,1024]{1,0:T(8,128)(2,1)}, bf16[528,1024]{1,0:T(8,128)(2,1)}, u32[]{:S(2)}, u32[]{:S(2)}) collective-permute-start(bf16[528,1024]{1,0:T(8,128)(2,1)} %gather.8.o1), channel_id=1, source_target_pairs={{0,8},{1,9},{2,10},{3,11},{4,12},{5,13},{6,14},{7,15},{8,0},{9,1},... | collective-permute-start | bytes 3244040 | tf_op jit(solution)/shard_map/ppermute | solution.py:411
  50.2 23.9 %collective-permute-start.3 = (bf16[528,1024]{1,0:T(8,128)(2,1)}, bf16[528,1024]{1,0:T(8,128)(2,1)S(1)}, u32[]{:S(2)}, u32[]{:S(2)}) collective-permute-start(bf16[528,1024]{1,0:T(8,128)(2,1)} %gather.8.o1), channel_id=1, source_target_pairs={{0,16},{1,17},{2,18},{3,19},{4,20},{5,21},{6,22},{7,23},{8,56},{9,... | collective-permute-start | bytes 3244040 | tf_op jit(solution)/shard_map/ppermute | solution.py:409
  52.7 21.4 %all-to-all-start.1 = ((bf16[32,64,128]{2,1,0:T(8,128)(2,1)}), bf16[32,64,128]{2,1,0:T(8,128)(2,1)S(1)}, u32[]{:S(2)}, u32[]{:S(2)}) async-start(bf16[32,64,128]{2,1,0:T(8,128)(2,1)} %bitcast.18), calls=%async_computation.1 | async-start | bytes 1048576 | tf_op jit(solution)/shard_map/all_to_all | solution.py:372
  57.6 20.1 %collective-permute-start.6 = (bf16[528,1024]{1,0:T(8,128)(2,1)}, bf16[528,1024]{1,0:T(8,128)(2,1)S(1)}, u32[]{:S(2)}, u32[]{:S(2)}) collective-permute-start(bf16[528,1024]{1,0:T(8,128)(2,1)} %gather.8.o1), channel_id=1, source_target_pairs={{0,48},{1,49},{2,50},{3,51},{4,52},{5,53},{6,54},{7,55},{8,24},{9,... | collective-permute-start | bytes 3244040 | tf_op jit(solution)/shard_map/ppermute | solution.py:410
  74.0 3.6 %collective-permute-start.7 = (bf16[528,1024]{1,0:T(8,128)(2,1)S(1)}, bf16[528,1024]{1,0:T(8,128)(2,1)}, u32[]{:S(2)}, u32[]{:S(2)}) collective-permute-start(bf16[528,1024]{1,0:T(8,128)(2,1)S(1)} %collective-permute-done.3.u1), channel_id=1, source_target_pairs={{0,8},{1,9},{2,10},{3,11},{4,12},{5,13},{6,14},{7,15},{8,0},{9,1},... | collective-permute-start | bytes 3244040 | tf_op jit(solution)/shard_map/ppermute | solution.py:413
  74.7 12.2 %collective-permute-start.5 = (bf16[272,1024]{1,0:T(8,128)(2,1)S(1)}, bf16[272,1024]{1,0:T(8,128)(2,1)S(1)}, u32[]{:S(2)}, u32[]{:S(2)}) collective-permute-start(bf16[272,1024]{1,0:T(8,128)(2,1)S(1)} %gather.9.o2), channel_id=1, source_target_pairs={{0,16},{1,17},{2,18},{3,19},{4,20},{5,21},{6,22},{7,23},{8,56},{9,... | collective-permute-start | bytes 1671176 | tf_op jit(solution)/shard_map/ppermute | solution.py:409
  76.3 14.8 %collective-permute-start.10 = (bf16[272,1024]{1,0:T(8,128)(2,1)S(1)}, bf16[272,1024]{1,0:T(8,128)(2,1)S(1)}, u32[]{:S(2)}, u32[]{:S(2)}) collective-permute-start(bf16[272,1024]{1,0:T(8,128)(2,1)S(1)} %gather.9.o2), channel_id=1, source_target_pairs={{0,8},{1,9},{2,10},{3,11},{4,12},{5,13},{6,14},{7,15},{8,0},{9,1},... | collective-permute-start | bytes 1671176 | tf_op jit(solution)/shard_map/ppermute | solution.py:411
  76.3 19.5 %collective-permute-start.8 = (bf16[272,1024]{1,0:T(8,128)(2,1)S(1)}, bf16[272,1024]{1,0:T(8,128)(2,1)S(1)}, u32[]{:S(2)}, u32[]{:S(2)}) collective-permute-start(bf16[272,1024]{1,0:T(8,128)(2,1)S(1)} %gather.9.o2), channel_id=1, source_target_pairs={{0,48},{1,49},{2,50},{3,51},{4,52},{5,53},{6,54},{7,55},{8,24},{9,... | collective-permute-start | bytes 1671176 | tf_op jit(solution)/shard_map/ppermute | solution.py:410
  86.9 10.3 %collective-permute-start.9 = (bf16[272,1024]{1,0:T(8,128)(2,1)S(1)}, bf16[272,1024]{1,0:T(8,128)(2,1)S(1)}, u32[]{:S(2)}, u32[]{:S(2)}) collective-permute-start(bf16[272,1024]{1,0:T(8,128)(2,1)S(1)} %collective-permute-done.5.u2), channel_id=1, source_target_pairs={{0,8},{1,9},{2,10},{3,11},{4,12},{5,13},{6,14},{7,15},{8,0},{9,1},... | collective-permute-start | bytes 1671176 | tf_op jit(solution)/shard_map/ppermute | solution.py:413

commit v6 on v5

--- a/solution.py
+++ b/solution.py
@@ -104,7 +104,7 @@
             pltpu.SMEM((LINES, 128), jnp.int32),
             pltpu.SemaphoreType.DMA((3,)),
         ],
-        compiler_params=PARAMS,
+        compiler_params=pltpu.CompilerParams(vmem_limit_bytes=60 * 2**20),
         name="place",
     )(ids, rows)
 
@@ -291,7 +291,8 @@
         meet(best, E2, e2, [(U2, u2)])
 
 
-def fourth_kernel(spots, u1, u2, v1, v2, w1, w2, before, out, best, long, short):
+def fourth_kernel(spots, u1, u2, v1, v2, w1, w2, before, *refs):
+    *outs, best = refs
     best[...] = before[...]
 
     @pl.when(spots[1] != 0)
@@ -304,24 +305,25 @@
         meet(best, W2, w2, [(U1, u1)])
         meet(best, U2, u2, [(W1, w1), (W2, w2)])
 
-    long[...] = jnp.full_like(long, -1.0)
-    short[...] = jnp.full_like(short, -1.0)
-    for i in range(5):
+    for i, out in enumerate(outs):
         for y in range(Y):
-            at = pl.ds(spots[2 + i] * Y + y, 1)
-            long[at, :] = best[pl.ds(2 * i, 1), pl.ds(y * PARTS[0], PARTS[0])]
+            at = pl.ds(y, 1)
+            out[at, pl.ds(0, PARTS[0])] = best[pl.ds(2 * i, 1), pl.ds(y * PARTS[0], PARTS[0])]
             pair = best[pl.ds(2 * i + 1, 1), pl.ds(y // 2 * 128, 128)]
-            short[at, :] = pltpu.roll(pair, 64, 1) if y % 2 else pair
-    out[:, pl.ds(0, PARTS[0])] = long[...]
-    out[:, pl.ds(PARTS[0], PARTS[1])] = short[:, pl.ds(0, PARTS[1])]
+            pair = pltpu.roll(pair, 64, 1) if y % 2 else pair
+            out[at, pl.ds(PARTS[0], PARTS[1])] = pair[:, : PARTS[1]]
+
+
+def is_dims(item):
+    return isinstance(item, tuple) and isinstance(item[0], int)
 
 
 def scores_call(kernel, units, inputs, out, scratch, name):
     return pl.pallas_call(
         kernel,
-        out_shape=jax.ShapeDtypeStruct(out, jnp.float32),
+        out_shape=jax.tree.map(lambda dims: jax.ShapeDtypeStruct(dims, jnp.float32), out, is_leaf=is_dims),
         in_specs=[SMEM] + [VMEM] * (len(inputs) - 1),
-        out_specs=VMEM,
+        out_specs=jax.tree.map(lambda _: VMEM, out, is_leaf=is_dims),
         scratch_shapes=scratch,
         compiler_params=PARAMS,
         cost_estimate=pl.CostEstimate(
@@ -343,8 +345,7 @@
     for i in range(LINES):
         ids = ids_ref[pl.ds(i, 1), :]
         within = slot_ref[pl.ds(i, 1), :] - ids * CAP
-        where = (ids & (Z - 1)) * Y + (ids >> 3)
-        member = (group == where).astype(jnp.float32).astype(jnp.bfloat16)
+        member = (group == ids).astype(jnp.float32).astype(jnp.bfloat16)
         found = lax.dot_general(
             pieces, member, (((0,), (0,)), ((), ())), preferred_element_type=jnp.float32
         )
@@ -387,19 +388,7 @@
     rank1 = member_ranks[:, : PARTS[0]].reshape(1, SIZES[0])
     rank2 = member_ranks[:, PARTS[0] :].reshape(1, SIZES[1])
 
-    step = 1 - 2 * core
-    near, far = (x - step) % X, (x + step) % X
-    spots = jnp.stack(
-        [
-            core,
-            ((x < X // 2) == (core == 0)).astype(jnp.int32),
-            x * C + core,
-            near * C + core,
-            far * C + core,
-            x * C + 1 - core,
-            far * C + 1 - core,
-        ]
-    ).astype(jnp.int32)
+    spots = jnp.stack([core, ((x < X // 2) == (core == 0)).astype(jnp.int32)]).astype(jnp.int32)
 
     swap = routes(lambda y, x, c, z: (y, x, 1 - c, z))
     ahead = routes(lambda y, x, c, z: (y, x + 1 - 2 * c, c, z))
@@ -419,25 +408,28 @@
         lambda e: (scores_call(own_kernel, 8, (spots, o1, e), wide, [], "own"), arrived[1]),
     )
     o2 = gather(SIZES[1], later, rank2)
-    u2, v2, e2, w2, best = share(
-        o2,
-        lambda e: (
-            scores_call(first_kernel, 12, (spots, o1, u1, v1, e1, w1, best), wide, [], "first"),
-        ),
+
+    def before_arrival(e2):
+        first = scores_call(
+            first_kernel, 12, (spots, o1, u1, v1, e1, w1, best), wide, [], "first"
+        )
+        inputs = (spots, o1, o2, u1, v1, e1, e2, first)
+        return (scores_call(second_kernel, 14, inputs, wide, [], "second"),)
+
+    u2, v2, e2, w2, best = share(o2, before_arrival)
+    best = scores_call(third_kernel, 2, (spots, o2, u2, v2, e2, best), wide, [], "third")
+    own, *others = scores_call(
+        fourth_kernel, 5, (spots, u1, u2, v1, v2, w1, w2, best), [(Y, CAP)] * 5,
+        [pltpu.VMEM(wide, jnp.float32)], "fourth",
     )
-    best = scores_call(second_kernel, 14, (spots, o1, o2, u1, v1, e1, e2, best), wide, [], "second")
-    best = scores_call(third_kernel, 2, (spots, o2, u2, v2, e2, best), wide, [], "third")
-    best = scores_call(
-        fourth_kernel, 5, (spots, u1, u2, v1, v2, w1, w2, best), (GROUPS, CAP),
-        [pltpu.VMEM(size, jnp.float32) for size in (wide, (GROUPS, 128), (GROUPS, 128))],
-        "fourth",
+    across = routes(lambda y, x, c, z: (y, x + 1 - 2 * c, 1 - c, z))
+    for part, way in zip(others, (behind, ahead, swap, across)):
+        own = jnp.maximum(own, lax.ppermute(part, ALL, way))
+    table = lax.all_to_all(
+        jnp.broadcast_to(own[:, None], (Y, Z, CAP)).reshape(GROUPS, CAP),
+        ("y", "z"), split_axis=0, concat_axis=0, tiled=True,
     )
-    back = lax.all_to_all(best, ("x", "core", "y"), split_axis=0, concat_axis=0, tiled=True)
-    merged = jnp.max(back.reshape(X * C, Y, CAP), axis=0)
-    table = lax.all_to_all(
-        jnp.broadcast_to(merged[None], (Z, Y, CAP)), "z", split_axis=0, concat_axis=0, tiled=True
-    )
-    return answer(ids, slots, table.reshape(GROUPS, CAP)).reshape(ROWS)
+    return answer(ids, slots, table).reshape(ROWS)
 
 
 def solution(mesh):

time: 123 us -> 118 us (0.959)
  blocking collectives: 21.7 us -> 15.2 us
  starting transfers between devices: 35.6 us -> 38.9 us
  local copies, waits for them, and re-layouts: 2.68 us -> 0.74 us
    all_to_all x2 -> x1, blocking collectives: 21.7 us -> 15.2 us  [shards(): lax.all_to_all(jnp.broadcast_to(own[:, None], (Y, Z, CAP)).reshape(GROUPS...]
    ppermute x0 -> x4, starting transfers between devices: none -> 4.3 us  [shards(): own = jnp.maximum(own, lax.ppermute(part, ALL, way))]
    ppermute x2, waiting for transfers between devices: 4.32 us -> 1.13 us  [share(): u = lax.ppermute(own, ALL, ahead)]
    ppermute x0 -> x4, waiting for transfers between devices: none -> 2.69 us  [shards(): own = jnp.maximum(own, lax.ppermute(part, ALL, way))]
    unnamed x8 -> x7, local copies, waits for them, and re-layouts: 1.85 us -> 0.02 us
  transfers between devices with their start and end apart: 13 -> 17, of which waited for: 6 -> 8; matrix products, arithmetic and copies ran while one was open for 1% -> 1% of each run, Pallas kernels for 12% -> 12%
where the time goes in v6:
time: 118 us
  starting transfers between devices  38.9 us (33%)
  waiting for transfers between devices  37.1 us (31%)
  Pallas kernels  25.5 us (22%)
  blocking collectives  15.2 us (13%)
    all_to_all x2, waiting for transfers between devices, shards(): lax.all_to_all(rows.reshape(GROUPS, part, WIDTH), ('y', 'z'), split_axis=...  30.5 us
    all_to_all x2, starting transfers between devices, shards(): lax.all_to_all(rows.reshape(GROUPS, part, WIDTH), ('y', 'z'), split_axis=...  17 us
    pallas_call x5, Pallas kernels, scores_call(): pl.pallas_call(kernel, out_shape=jax.tree.map(lambda dims: jax.ShapeDtype...  16 us
    all_to_all x1, blocking collectives, shards(): lax.all_to_all(jnp.broadcast_to(own[:, None], (Y, Z, CAP)).reshape(GROUPS...  15.2 us
    pallas_call x1, Pallas kernels, place(): pl.pallas_call(place_kernel, out_shape=(jax.ShapeDtypeStruct((GROUPS * PA...  5.55 us
    ppermute x2, starting transfers between devices, share(): e = lax.ppermute(own, ALL, swap)  5.35 us
    ppermute x3, starting transfers between devices, shards(): row = lax.ppermute(row, ALL, routes(lambda y, x, c, z: (y + j, x, c, z)))  4.89 us
    ppermute x4, starting transfers between devices, shards(): own = jnp.maximum(own, lax.ppermute(part, ALL, way))  4.3 us
  transfers between devices with their start and end apart: 17, of which 8 were waited for; matrix products, arithmetic and copies ran while one was open for 1% of the time, Pallas kernels for 12%

profile of v6, /device:TPU:1, one launch (start us, length us, event | category | flops | bytes accessed | tf_op | source)
XLA Modules:
  0.0 117.7 jit_solution(17954866616193152844)
XLA Ops:
  0.0 5.5 %place.1 = (bf16[4096,128]{1,0:T(8,128)(2,1)}, bf16[2048,128]{1,0:T(8,128)(2,1)}, s32[24,128]{1,0:T(8,128)}) custom-call(s32[24,128]{1,0:T(8,128)} %bitcast.27, bf16[3072,128]{1,0:T(8,128)(2,1)} %rows_any.1), custom_call_target="tpu_custom_call" | custom-call | tf_op jit(solution)/shard_map/place/pallas_call | solution.py:88
  5.6 12.2 %all-to-all-start = ((bf16[32,128,128]{2,1,0:T(8,128)(2,1)}), bf16[32,128,128]{2,1,0:T(8,128)(2,1)S(1)}, u32[]{:S(2)}, u32[]{:S(2)}) async-start(bf16[32,128,128]{2,1,0:T(8,128)(2,1)} %bitcast.33), calls=%async_computation | async-start | bytes 2097152 | tf_op jit(solution)/shard_map/all_to_all | solution.py:373
  18.8 1.3 %collective-permute-start = (f32[1,192]{1,0:T(1,128)S(1)}, f32[1,192]{1,0:T(1,128)S(1)}, u32[]{:S(2)}, u32[]{:S(2)}) collective-permute-start(f32[1,192]{1,0:T(1,128)S(1)} %get-tuple-element.34), channel_id=1, source_target_pairs={{0,64},{1,65},{2,66},{3,67},{4,68},{5,69},{6,70},{7,71},{8,72},{9,... | collective-permute-start | bytes 2312 | tf_op jit(solution)/shard_map/ppermute | solution.py:385
  20.1 2.4 %collective-permute-start.1 = (f32[1,192]{1,0:T(1,128)S(1)}, f32[1,192]{1,0:T(1,128)S(1)}, u32[]{:S(2)}, u32[]{:S(2)}) collective-permute-start(f32[1,192]{1,0:T(1,128)S(1)} %get-tuple-element.33), channel_id=1, source_target_pairs={{0,128},{1,129},{2,130},{3,131},{4,132},{5,133},{6,134},{7,135},{8... | collective-permute-start | bytes 2312 | tf_op jit(solution)/shard_map/ppermute | solution.py:385
  22.5 1.1 collective-permute-start.2
  25.8 16.6 %all-to-all-done = bf16[32,128,128]{2,1,0:T(8,128)(2,1)S(1)} async-done(((bf16[32,128,128]{2,1,0:T(8,128)(2,1)}), bf16[32,128,128]{2,1,0:T(8,128)(2,1)S(1)}, u32[]{:S(2)}, u32[]{:S(2)}) %all-to-all-start) | async-done | bytes 1048608 | tf_op jit(solution)/shard_map/all_to_all | solution.py:373
  42.4 1.6 %gather.8.o1 = bf16[528,1024]{1,0:T(8,128)(2,1)} custom-call(bf16[4096,128]{1,0:T(8,128)(2,1)S(1)} %bitcast.24, f32[1,512]{1,0:T(1,128)S(1)} %bitcast.32), custom_call_target="tpu_custom_call" | custom-call | tf_op jit(solution)/shard_map/gather/pallas_call | solution.py:191
  44.0 5.0 %collective-permute-start.4 = (bf16[528,1024]{1,0:T(8,128)(2,1)}, bf16[528,1024]{1,0:T(8,128)(2,1)}, u32[]{:S(2)}, u32[]{:S(2)}) collective-permute-start(bf16[528,1024]{1,0:T(8,128)(2,1)} %gather.8.o1), channel_id=1, source_target_pairs={{0,8},{1,9},{2,10},{3,11},{4,12},{5,13},{6,14},{7,15},{8,0},{9,1},... | collective-permute-start | bytes 3244040 | tf_op jit(solution)/shard_map/ppermute | solution.py:400
  48.9 2.5 %collective-permute-start.3 = (bf16[528,1024]{1,0:T(8,128)(2,1)}, bf16[528,1024]{1,0:T(8,128)(2,1)S(1)}, u32[]{:S(2)}, u32[]{:S(2)}) collective-permute-start(bf16[528,1024]{1,0:T(8,128)(2,1)} %gather.8.o1), channel_id=1, source_target_pairs={{0,16},{1,17},{2,18},{3,19},{4,20},{5,21},{6,22},{7,23},{8,56},{9,... | collective-permute-start | bytes 3244040 | tf_op jit(solution)/shard_map/ppermute | solution.py:398
  51.4 4.8 %all-to-all-start.1 = ((bf16[32,64,128]{2,1,0:T(8,128)(2,1)}), bf16[32,64,128]{2,1,0:T(8,128)(2,1)S(1)}, u32[]{:S(2)}, u32[]{:S(2)}) async-start(bf16[32,64,128]{2,1,0:T(8,128)(2,1)} %bitcast.13), calls=%async_computation.1 | async-start | bytes 1048576 | tf_op jit(solution)/shard_map/all_to_all | solution.py:373
  56.3 2.5 %own.1.before = f32[16,512]{1,0:T(8,128)S(1)} custom-call(s32[2]{0:T(128)S(1)} %pad_add_fusion.spots, bf16[528,1024]{1,0:T(8,128)(2,1)} %gather.8.o1, bf16[528,1024]{1,0:T(8,128)(2,1)} %collective-permute-done.4.e1), custom_call_target="tpu_custom_call" | custom-call | flops 1073741824 | bytes 4194304 | tf_op jit(solution)/shard_map/own/pallas_call | solution.py:322
  58.8 14.0 %all-to-all-done.1 = bf16[32,64,128]{2,1,0:T(8,128)(2,1)S(1)} async-done(((bf16[32,64,128]{2,1,0:T(8,128)(2,1)}), bf16[32,64,128]{2,1,0:T(8,128)(2,1)S(1)}, u32[]{:S(2)}, u32[]{:S(2)}) %all-to-all-start.1) | async-done | bytes 524320 | tf_op jit(solution)/shard_map/all_to_all | solution.py:373
  73.8 1.3 %collective-permute-start.5 = (bf16[272,1024]{1,0:T(8,128)(2,1)S(1)}, bf16[272,1024]{1,0:T(8,128)(2,1)S(1)}, u32[]{:S(2)}, u32[]{:S(2)}) collective-permute-start(bf16[272,1024]{1,0:T(8,128)(2,1)S(1)} %gather.9.o2), channel_id=1, source_target_pairs={{0,16},{1,17},{2,18},{3,19},{4,20},{5,21},{6,22},{7,23},{8,56},{9,... | collective-permute-start | bytes 1671176 | tf_op jit(solution)/shard_map/ppermute | solution.py:398
  76.4 4.9 %first.1.before = f32[16,512]{1,0:T(8,128)S(1)} custom-call(s32[2]{0:T(128)S(1)} %pad_add_fusion.spots, bf16[528,1024]{1,0:T(8,128)(2,1)} %gather.8.o1, bf16[528,1024]{1,0:T(8,128)(2,1)S(1)} %collective-permute-done.3.u1, bf16[528,1024]{1,0:T(8,128)(2,1)S(1)} %collective-permute-done.6.v1, bf16[528,1024]{1,0:T(8,128)(2,1)} %collective-permute-done.4.e1, ...), custom_call_target="tpu_custom_call" | custom-call | flops 1610612736 | bytes 4194304 | tf_op jit(solution)/shard_map/first/pallas_call | solution.py:322
  81.3 4.6 %second.1.before = f32[16,512]{1,0:T(8,128)S(1)} custom-call(s32[2]{0:T(128)S(1)} %pad_add_fusion.spots, bf16[528,1024]{1,0:T(8,128)(2,1)} %gather.8.o1, bf16[272,1024]{1,0:T(8,128)(2,1)S(1)} %gather.9.o2, bf16[528,1024]{1,0:T(8,128)(2,1)S(1)} %collective-permute-done.3.u1, bf16[528,1024]{1,0:T(8,128)(2,1)S(1)} %collective-permute-done.6.v1, ...), custom_call_target="tpu_custom_call" | custom-call | flops 1879048192 | bytes 4194304 | tf_op jit(solution)/shard_map/second/pallas_call | solution.py:322
  85.9 1.1 collective-permute-done.5.u2
  87.0 3.2 %collective-permute-start.10 = (bf16[272,1024]{1,0:T(8,128)(2,1)S(1)}, bf16[272,1024]{1,0:T(8,128)(2,1)S(1)}, u32[]{:S(2)}, u32[]{:S(2)}) collective-permute-start(bf16[272,1024]{1,0:T(8,128)(2,1)S(1)} %collective-permute-done.5.u2), channel_id=1, source_target_pairs={{0,8},{1,9},{2,10},{3,11},{4,12},{5,13},{6,14},{7,15},{8,0},{9,1},... | collective-permute-start | bytes 1671176 | tf_op jit(solution)/shard_map/ppermute | solution.py:402
  90.2 1.5 %third.1.before = f32[16,512]{1,0:T(8,128)S(1)} custom-call(s32[2]{0:T(128)S(1)} %pad_add_fusion.spots, bf16[272,1024]{1,0:T(8,128)(2,1)S(1)} %gather.9.o2, bf16[272,1024]{1,0:T(8,128)(2,1)S(1)} %collective-permute-done.5.u2, bf16[272,1024]{1,0:T(8,128)(2,1)S(1)} %collective-permute-done.9.v2, bf16[272,1024]{1,0:T(8,128)(2,1)S(1)} %collective-permute-done.7.e2, ...), custom_call_target="tpu_custom_call" | custom-call | flops 268435456 | bytes 4194304 | tf_op jit(solution)/shard_map/third/pallas_call | solution.py:322
  91.8 2.5 %fourth.1 = (f32[4,192]{1,0:T(4,128)S(1)}, f32[4,192]{1,0:T(4,128)S(1)}, f32[4,192]{1,0:T(4,128)S(1)}, f32[4,192]{1,0:T(4,128)S(1)}, f32[4,192]{1,0:T(4,128)S(1)}) custom-call(s32[2]{0:T(128)S(1)} %pad_add_fusion.spots, bf16[528,1024]{1,0:T(8,128)(2,1)S(1)} %collective-permute-done.3.u1, bf16[272,1024]{1,0:T(8,128)(2,1)S(1)} %collective-permute-done.5.u2, ...), custom_call_target="tpu_custom_call" | custom-call | flops 671088640 | bytes 4194304 | tf_op jit(solution)/shard_map/fourth/pallas_call | solution.py:322
  94.4 2.7 %collective-permute-start.12 = (f32[4,192]{1,0:T(4,128)S(1)}, f32[4,192]{1,0:T(4,128)S(1)}, u32[]{:S(2)}, u32[]{:S(2)}) collective-permute-start(f32[4,192]{1,0:T(4,128)S(1)} %get-tuple-element.28), channel_id=1, source_target_pairs={{0,16},{1,17},{2,18},{3,19},{4,20},{5,21},{6,22},{7,23},{8,56},{9,... | collective-permute-start | bytes 9224 | tf_op jit(solution)/shard_map/ppermute | solution.py:427
  97.1 1.6 %collective-permute-start.14 = (f32[4,192]{1,0:T(4,128)S(1)}, f32[4,192]{1,0:T(4,128)S(1)}, u32[]{:S(2)}, u32[]{:S(2)}) collective-permute-start(f32[4,192]{1,0:T(4,128)S(1)} %get-tuple-element.30), channel_id=1, source_target_pairs={{0,24},{1,25},{2,26},{3,27},{4,28},{5,29},{6,30},{7,31},{8,48},{9,... | collective-permute-start | bytes 9224 | tf_op jit(solution)/shard_map/ppermute | solution.py:427
  98.6 2.7 %collective-permute-done.14 = f32[4,192]{1,0:T(4,128)S(1)} collective-permute-done((f32[4,192]{1,0:T(4,128)S(1)}, f32[4,192]{1,0:T(4,128)S(1)}, u32[]{:S(2)}, u32[]{:S(2)}) %collective-permute-start.14) | collective-permute-done | bytes 3104 | tf_op jit(solution)/shard_map/ppermute | solution.py:427
  101.4 15.2 %all_to_all.21 = f32[32,1,192]{2,1,0:T(1,128)S(1)} all-to-all(f32[32,1,192]{2,1,0:T(1,128)S(1)} %all_to_all.15), channel_id=1, replica_groups=mesh['y'=4,'x'=4,'core'=2,'z'=8] {'y','z'}, dimensions={0} | all-to-all | bytes 49152 | tf_op jit(solution)/shard_map/all_to_all | solution.py:428
  116.6 1.1 answer.1
  (40 shorter events, 5.7 us)
Async XLA Ops:
  5.6 12.3 %copy-start = (s32[3072]{0:T(1024)S(1)}, s32[3072]{0:T(1024)}, u32[]{:S(2)}) copy-start(s32[3072]{0:T(1024)} %param.4) | copy-start | bytes 36868
  5.6 12.3 %copy-start.1 = (s32[24,128]{1,0:T(8,128)S(1)}, s32[24,128]{1,0:T(8,128)}, u32[]{:S(2)}) copy-start(s32[24,128]{1,0:T(8,128)} %get-tuple-element.18.slot_ref) | copy-start | bytes 36868
  5.6 12.3 %copy-start.2 = (s32[3072]{0:T(1024)S(1)}, s32[3072]{0:T(1024)}, u32[]{:S(2)}) copy-start(s32[3072]{0:T(1024)} %param.5) | copy-start | bytes 36868
  5.6 36.8 %all-to-all-start = ((bf16[32,128,128]{2,1,0:T(8,128)(2,1)}), bf16[32,128,128]{2,1,0:T(8,128)(2,1)S(1)}, u32[]{:S(2)}, u32[]{:S(2)}) async-start(bf16[32,128,128]{2,1,0:T(8,128)(2,1)} %bitcast.33), calls=%async_computation | async-start | bytes 2097152 | tf_op jit(solution)/shard_map/all_to_all | solution.py:373
  18.8 4.9 %collective-permute-start = (f32[1,192]{1,0:T(1,128)S(1)}, f32[1,192]{1,0:T(1,128)S(1)}, u32[]{:S(2)}, u32[]{:S(2)}) collective-permute-start(f32[1,192]{1,0:T(1,128)S(1)} %get-tuple-element.34), channel_id=1, source_target_pairs={{0,64},{1,65},{2,66},{3,67},{4,68},{5,69},{6,70},{7,71},{8,72},{9,... | collective-permute-start | bytes 2312 | tf_op jit(solution)/shard_map/ppermute | solution.py:385
  20.1 4.2 %collective-permute-start.1 = (f32[1,192]{1,0:T(1,128)S(1)}, f32[1,192]{1,0:T(1,128)S(1)}, u32[]{:S(2)}, u32[]{:S(2)}) collective-permute-start(f32[1,192]{1,0:T(1,128)S(1)} %get-tuple-element.33), channel_id=1, source_target_pairs={{0,128},{1,129},{2,130},{3,131},{4,132},{5,133},{6,134},{7,135},{8... | collective-permute-start | bytes 2312 | tf_op jit(solution)/shard_map/ppermute | solution.py:385
  22.5 2.7 %collective-permute-start.2 = (f32[1,192]{1,0:T(1,128)S(1)}, f32[1,192]{1,0:T(1,128)S(1)}, u32[]{:S(2)}, u32[]{:S(2)}) collective-permute-start(f32[1,192]{1,0:T(1,128)S(1)} %get-tuple-element.32), channel_id=1, source_target_pairs={{0,192},{1,193},{2,194},{3,195},{4,196},{5,197},{6,198},{7,199},{8... | collective-permute-start | bytes 2312 | tf_op jit(solution)/shard_map/ppermute | solution.py:385
  44.0 12.4 %collective-permute-start.4 = (bf16[528,1024]{1,0:T(8,128)(2,1)}, bf16[528,1024]{1,0:T(8,128)(2,1)}, u32[]{:S(2)}, u32[]{:S(2)}) collective-permute-start(bf16[528,1024]{1,0:T(8,128)(2,1)} %gather.8.o1), channel_id=1, source_target_pairs={{0,8},{1,9},{2,10},{3,11},{4,12},{5,13},{6,14},{7,15},{8,0},{9,1},... | collective-permute-start | bytes 3244040 | tf_op jit(solution)/shard_map/ppermute | solution.py:400
  48.9 23.9 %collective-permute-start.3 = (bf16[528,1024]{1,0:T(8,128)(2,1)}, bf16[528,1024]{1,0:T(8,128)(2,1)S(1)}, u32[]{:S(2)}, u32[]{:S(2)}) collective-permute-start(bf16[528,1024]{1,0:T(8,128)(2,1)} %gather.8.o1), channel_id=1, source_target_pairs={{0,16},{1,17},{2,18},{3,19},{4,20},{5,21},{6,22},{7,23},{8,56},{9,... | collective-permute-start | bytes 3244040 | tf_op jit(solution)/shard_map/ppermute | solution.py:398
  51.4 21.4 %all-to-all-start.1 = ((bf16[32,64,128]{2,1,0:T(8,128)(2,1)}), bf16[32,64,128]{2,1,0:T(8,128)(2,1)S(1)}, u32[]{:S(2)}, u32[]{:S(2)}) async-start(bf16[32,64,128]{2,1,0:T(8,128)(2,1)} %bitcast.13), calls=%async_computation.1 | async-start | bytes 1048576 | tf_op jit(solution)/shard_map/all_to_all | solution.py:373
  56.3 20.1 %collective-permute-start.6 = (bf16[528,1024]{1,0:T(8,128)(2,1)}, bf16[528,1024]{1,0:T(8,128)(2,1)S(1)}, u32[]{:S(2)}, u32[]{:S(2)}) collective-permute-start(bf16[528,1024]{1,0:T(8,128)(2,1)} %gather.8.o1), channel_id=1, source_target_pairs={{0,48},{1,49},{2,50},{3,51},{4,52},{5,53},{6,54},{7,55},{8,24},{9,... | collective-permute-start | bytes 3244040 | tf_op jit(solution)/shard_map/ppermute | solution.py:399
  72.8 3.6 %collective-permute-start.8 = (bf16[528,1024]{1,0:T(8,128)(2,1)S(1)}, bf16[528,1024]{1,0:T(8,128)(2,1)}, u32[]{:S(2)}, u32[]{:S(2)}) collective-permute-start(bf16[528,1024]{1,0:T(8,128)(2,1)S(1)} %collective-permute-done.3.u1), channel_id=1, source_target_pairs={{0,8},{1,9},{2,10},{3,11},{4,12},{5,13},{6,14},{7,15},{8,0},{9,1},... | collective-permute-start | bytes 3244040 | tf_op jit(solution)/shard_map/ppermute | solution.py:402
  73.4 7.9 %collective-permute-start.7 = (bf16[272,1024]{1,0:T(8,128)(2,1)S(1)}, bf16[272,1024]{1,0:T(8,128)(2,1)S(1)}, u32[]{:S(2)}, u32[]{:S(2)}) collective-permute-start(bf16[272,1024]{1,0:T(8,128)(2,1)S(1)} %gather.9.o2), channel_id=1, source_target_pairs={{0,8},{1,9},{2,10},{3,11},{4,12},{5,13},{6,14},{7,15},{8,0},{9,1},... | collective-permute-start | bytes 1671176 | tf_op jit(solution)/shard_map/ppermute | solution.py:400
  73.8 13.2 %collective-permute-start.5 = (bf16[272,1024]{1,0:T(8,128)(2,1)S(1)}, bf16[272,1024]{1,0:T(8,128)(2,1)S(1)}, u32[]{:S(2)}, u32[]{:S(2)}) collective-permute-start(bf16[272,1024]{1,0:T(8,128)(2,1)S(1)} %gather.9.o2), channel_id=1, source_target_pairs={{0,16},{1,17},{2,18},{3,19},{4,20},{5,21},{6,22},{7,23},{8,56},{9,... | collective-permute-start | bytes 1671176 | tf_op jit(solution)/shard_map/ppermute | solution.py:398
  75.1 15.1 %collective-permute-start.9 = (bf16[272,1024]{1,0:T(8,128)(2,1)S(1)}, bf16[272,1024]{1,0:T(8,128)(2,1)S(1)}, u32[]{:S(2)}, u32[]{:S(2)}) collective-permute-start(bf16[272,1024]{1,0:T(8,128)(2,1)S(1)} %gather.9.o2), channel_id=1, source_target_pairs={{0,48},{1,49},{2,50},{3,51},{4,52},{5,53},{6,54},{7,55},{8,24},{9,... | collective-permute-start | bytes 1671176 | tf_op jit(solution)/shard_map/ppermute | solution.py:399
  87.0 4.8 %collective-permute-start.10 = (bf16[272,1024]{1,0:T(8,128)(2,1)S(1)}, bf16[272,1024]{1,0:T(8,128)(2,1)S(1)}, u32[]{:S(2)}, u32[]{:S(2)}) collective-permute-start(bf16[272,1024]{1,0:T(8,128)(2,1)S(1)} %collective-permute-done.5.u2), channel_id=1, source_target_pairs={{0,8},{1,9},{2,10},{3,11},{4,12},{5,13},{6,14},{7,15},{8,0},{9,1},... | collective-permute-start | bytes 1671176 | tf_op jit(solution)/shard_map/ppermute | solution.py:402
  94.3 4.3 %collective-permute-start.11 = (f32[4,192]{1,0:T(4,128)S(1)}, f32[4,192]{1,0:T(4,128)S(1)}, u32[]{:S(2)}, u32[]{:S(2)}) collective-permute-start(f32[4,192]{1,0:T(4,128)S(1)} %get-tuple-element.27), channel_id=1, source_target_pairs={{0,48},{1,49},{2,50},{3,51},{4,52},{5,53},{6,54},{7,55},{8,24},{9,... | collective-permute-start | bytes 9224 | tf_op jit(solution)/shard_map/ppermute | solution.py:427
  94.4 4.2 %collective-permute-start.12 = (f32[4,192]{1,0:T(4,128)S(1)}, f32[4,192]{1,0:T(4,128)S(1)}, u32[]{:S(2)}, u32[]{:S(2)}) collective-permute-start(f32[4,192]{1,0:T(4,128)S(1)} %get-tuple-element.28), channel_id=1, source_target_pairs={{0,16},{1,17},{2,18},{3,19},{4,20},{5,21},{6,22},{7,23},{8,56},{9,... | collective-permute-start | bytes 9224 | tf_op jit(solution)/shard_map/ppermute | solution.py:427
  97.1 1.6 %collective-permute-start.13 = (f32[4,192]{1,0:T(4,128)S(1)}, f32[4,192]{1,0:T(4,128)S(1)}, u32[]{:S(2)}, u32[]{:S(2)}) collective-permute-start(f32[4,192]{1,0:T(4,128)S(1)} %get-tuple-element.29), channel_id=1, source_target_pairs={{0,8},{1,9},{2,10},{3,11},{4,12},{5,13},{6,14},{7,15},{8,0},{9,1},... | collective-permute-start | bytes 9224 | tf_op jit(solution)/shard_map/ppermute | solution.py:427
  97.1 4.2 %collective-permute-start.14 = (f32[4,192]{1,0:T(4,128)S(1)}, f32[4,192]{1,0:T(4,128)S(1)}, u32[]{:S(2)}, u32[]{:S(2)}) collective-permute-start(f32[4,192]{1,0:T(4,128)S(1)} %get-tuple-element.30), channel_id=1, source_target_pairs={{0,24},{1,25},{2,26},{3,27},{4,28},{5,29},{6,30},{7,31},{8,48},{9,... | collective-permute-start | bytes 9224 | tf_op jit(solution)/shard_map/ppermute | solution.py:427

commit v7 on v6

--- a/solution.py
+++ b/solution.py
@@ -16,7 +16,6 @@
 WIDTH = 128
 PARTS = (128, 64)
 SIZES = (Y * 128, Y * 64)
-META = 16
 LINES = ROWS // 128
 ALL = ("y", "x", "core", "z")
 PARAMS = pltpu.CompilerParams(vmem_limit_bytes=40 * 2**20)
@@ -36,8 +35,16 @@
     return pairs
 
 
+def scatter_rows(spot_sm, wide_ref, out_ref):
+    @pl.loop(0, LINES)
+    def _(i):
+        for lane in range(128):
+            spot = spot_sm[i, lane]
+            out_ref[pl.ds(spot, 1), :] = wide_ref[pl.ds(i * 128 + lane, 1), :]
+
+
 def place_kernel(
-    ids_any, rows_any, first_ref, second_ref, slot_ref,
+    ids_any, rows_any, placed_ref, slot_ref,
     ids_ref, rows_ref, member_ref, wide_ref, out_ref, spot_ref, spot_sm, sems,
 ):
     ids_copy = pltpu.make_async_copy(ids_any, ids_ref, sems.at[0])
@@ -62,9 +69,7 @@
         within = within.astype(jnp.int32)
         slot_ref[pl.ds(i, 1), :] = line * CAP + within
         spot_ref[pl.ds(i, 1), :] = jnp.where(
-            within < PARTS[0],
-            line * PARTS[0] + within,
-            GROUPS * PARTS[0] + line * PARTS[1] + within - PARTS[0],
+            within < PARTS[0], line * PARTS[0] + within, GROUPS * PARTS[0]
         )
         carry = carry + part[:, 128:]
     copy = pltpu.make_async_copy(spot_ref, spot_sm, sems.at[2])
@@ -72,16 +77,8 @@
     rows_copy.wait()
     wide_ref[...] = rows_ref[...].astype(jnp.float32)
     copy.wait()
-
-    @pl.loop(0, LINES)
-    def _(i):
-        for lane in range(128):
-            spot = spot_sm[i, lane]
-            out_ref[pl.ds(spot, 1), :] = wide_ref[pl.ds(i * 128 + lane, 1), :]
-
-    split = GROUPS * PARTS[0]
-    first_ref[...] = out_ref[pl.ds(0, split), :].astype(jnp.bfloat16)
-    second_ref[...] = out_ref[pl.ds(split, GROUPS * PARTS[1]), :].astype(jnp.bfloat16)
+    scatter_rows(spot_sm, wide_ref, out_ref)
+    placed_ref[...] = out_ref[pl.ds(0, GROUPS * PARTS[0]), :].astype(jnp.bfloat16)
 
 
 def place(ids, rows):
@@ -89,17 +86,16 @@
         place_kernel,
         out_shape=(
             jax.ShapeDtypeStruct((GROUPS * PARTS[0], WIDTH), jnp.bfloat16),
-            jax.ShapeDtypeStruct((GROUPS * PARTS[1], WIDTH), jnp.bfloat16),
             jax.ShapeDtypeStruct((LINES, 128), jnp.int32),
         ),
         in_specs=[pl.BlockSpec(memory_space=pltpu.HBM)] * 2,
-        out_specs=(VMEM, VMEM, VMEM),
+        out_specs=(VMEM, VMEM),
         scratch_shapes=[
             pltpu.VMEM((LINES, 128), jnp.int32),
             pltpu.VMEM((ROWS, WIDTH), jnp.bfloat16),
             pltpu.VMEM((LINES * GROUPS, 128), jnp.bfloat16),
             pltpu.VMEM((ROWS, WIDTH), jnp.float32),
-            pltpu.VMEM((GROUPS * CAP, WIDTH), jnp.float32),
+            pltpu.VMEM((GROUPS * PARTS[0] + 8, WIDTH), jnp.float32),
             pltpu.VMEM((LINES, 128), jnp.int32),
             pltpu.SMEM((LINES, 128), jnp.int32),
             pltpu.SemaphoreType.DMA((3,)),
@@ -107,6 +103,41 @@
         compiler_params=pltpu.CompilerParams(vmem_limit_bytes=60 * 2**20),
         name="place",
     )(ids, rows)
+
+
+def place_rest_kernel(
+    ids_ref, slot_ref, rows_ref, placed_ref, wide_ref, out_ref, spot_ref, spot_sm, sem
+):
+    ids = ids_ref[...]
+    within = slot_ref[...] - ids * CAP
+    spot_ref[...] = jnp.where(
+        within < PARTS[0], GROUPS * PARTS[1], ids * PARTS[1] + within - PARTS[0]
+    )
+    copy = pltpu.make_async_copy(spot_ref, spot_sm, sem)
+    copy.start()
+    out_ref[...] = jnp.zeros_like(out_ref)
+    wide_ref[...] = rows_ref[...].astype(jnp.float32)
+    copy.wait()
+    scatter_rows(spot_sm, wide_ref, out_ref)
+    placed_ref[...] = out_ref[pl.ds(0, GROUPS * PARTS[1]), :].astype(jnp.bfloat16)
+
+
+def place_rest(ids, slots, rows):
+    return pl.pallas_call(
+        place_rest_kernel,
+        out_shape=jax.ShapeDtypeStruct((GROUPS * PARTS[1], WIDTH), jnp.bfloat16),
+        in_specs=[VMEM] * 3,
+        out_specs=VMEM,
+        scratch_shapes=[
+            pltpu.VMEM((ROWS, WIDTH), jnp.float32),
+            pltpu.VMEM((GROUPS * PARTS[1] + 8, WIDTH), jnp.float32),
+            pltpu.VMEM((LINES, 128), jnp.int32),
+            pltpu.SMEM((LINES, 128), jnp.int32),
+            pltpu.SemaphoreType.DMA,
+        ],
+        compiler_params=PARAMS,
+        name="place_rest",
+    )(ids, slots, rows)
 
 
 def ranks_kernel(ids_ref, slot_ref, orders_ref, table_ref):
@@ -165,62 +196,47 @@
     return jnp.concatenate(pieces, axis=0)
 
 
-def gather_kernel(size, in_ref, rank_ref, out_ref, meta_ref):
-    part = size // Y
+def part_of(ref):
+    return ref.shape[0] // GROUPS
+
+
+def size_of(ref):
+    return Y * part_of(ref)
+
+
+def rows_of(ref, start, count):
+    part = part_of(ref)
+    lines = []
+    for y in range(start // part, (start + count) // part):
+        pieces = [ref[pl.ds((y * Z + z) * part, part), :] for z in range(Z)]
+        lines.append(jnp.concatenate(pieces, axis=1))
+    return jnp.concatenate(lines, axis=0)
+
+
+def note(inverses, name, ref):
+    part = part_of(ref)
     cols = []
     for y in range(Y):
         total = jnp.zeros((part, WIDTH), jnp.float32)
         for z in range(Z):
-            piece = in_ref[pl.ds((y * Z + z) * part, part), :]
-            out_ref[pl.ds(y * part, part), pl.ds(z * WIDTH, WIDTH)] = piece
-            wide = piece.astype(jnp.float32)
+            wide = ref[pl.ds((y * Z + z) * part, part), :].astype(jnp.float32)
             total = total + wide * wide
         cols.append(lax.rsqrt(jnp.sum(total, axis=1, keepdims=True) + 1e-06))
-    inverse = to_row(jnp.concatenate(cols, axis=0))
-    high = inverse.astype(jnp.bfloat16).astype(jnp.float32)
-    middle = (inverse - high).astype(jnp.bfloat16).astype(jnp.float32)
-    rank = rank_ref[...].astype(jnp.int32)
-    lines = (high, middle, inverse - high - middle, rank & 255, (rank >> 8) & 255, rank >> 16)
-    meta_ref[...] = jnp.zeros_like(meta_ref)
-    for i, line in enumerate(lines):
-        meta_ref[pl.ds(i, 1), pl.ds(0, size)] = line.astype(jnp.float32)
-    out_ref[pl.ds(size, META), :] = meta_ref[...].astype(jnp.bfloat16)
-
-
-def gather(size, arrived, rank):
-    return pl.pallas_call(
-        functools.partial(gather_kernel, size),
-        out_shape=jax.ShapeDtypeStruct((size + META, Z * WIDTH), jnp.bfloat16),
-        in_specs=[VMEM] * 2,
-        out_specs=VMEM,
-        scratch_shapes=[pltpu.VMEM((META, Z * WIDTH), jnp.float32)],
-        compiler_params=PARAMS,
-        name="gather",
-    )(arrived, rank)
-
-
-def size_of(ref):
-    return ref.shape[0] - META
-
-
-def row_meta(ref):
-    size = size_of(ref)
-    meta = ref[pl.ds(size, META), pl.ds(0, size)].astype(jnp.float32)
-    rank = meta[3:4] + 256.0 * meta[4:5] + 65536.0 * meta[5:6]
-    return meta[0:1] + meta[1:2] + meta[2:3], jnp.where(rank > 0, rank, never_order)
-
-
-def meet(best, p_name, p_ref, others):
+    inverses[pl.ds(name, 1), pl.ds(0, Y * part)] = to_row(jnp.concatenate(cols, axis=0))
+
+
+def meet(best, inverses, ranks, p_name, p_ref, others):
     size = size_of(p_ref)
-    inv_p, rank_p = (to_col(row) for row in row_meta(p_ref))
+    at = (pl.ds(p_name, 1), pl.ds(0, size))
+    inv_p, rank_p = to_col(inverses[at]), to_col(ranks[at])
     p_best = jnp.full((size, 128), low, jnp.float32)
     for q_name, q_ref in others:
-        inv_q, rank_q = row_meta(q_ref)
         q_best = []
         for j in range(0, size_of(q_ref), 256):
-            s = dot_rows(p_ref[pl.ds(0, size), :], q_ref[pl.ds(j, 256), :])
-            s = s * inv_p * inv_q[:, j : j + 256]
-            earlier = rank_q[:, j : j + 256] < rank_p
+            at = (pl.ds(q_name, 1), pl.ds(j, 256))
+            s = dot_rows(rows_of(p_ref, 0, size), rows_of(q_ref, j, 256))
+            s = s * inv_p * inverses[at]
+            earlier = ranks[at] < rank_p
             mine = jnp.where(earlier, s, low)
             p_best = jnp.maximum(p_best, jnp.maximum(mine[:, :128], mine[:, 128:]))
             if q_name != p_name:
@@ -238,72 +254,99 @@
 O1, O2, U1, U2, V1, V2, E1, E2, W1, W2 = range(10)
 
 
-def own_kernel(spots, o1, e1, best):
+def own_kernel(spots, ranks, o1, e1, best, inverses):
     best[...] = jnp.full_like(best, -1.0)
-    meet(best, O1, o1, [(O1, o1)])
+    inverses[...] = jnp.zeros_like(inverses)
+    note(inverses, O1, o1)
+    note(inverses, E1, e1)
+    meet(best, inverses, ranks, O1, o1, [(O1, o1)])
 
     @pl.when(spots[0] == 0)
     def _():
-        meet(best, O1, o1, [(E1, e1)])
-
-
-def first_kernel(spots, o1, u1, v1, e1, w1, before, best):
+        meet(best, inverses, ranks, O1, o1, [(E1, e1)])
+
+
+def first_kernel(spots, ranks, o1, u1, v1, e1, w1, before, known, best, inverses):
     best[...] = before[...]
-    meet(best, O1, o1, [(U1, u1)])
+    inverses[...] = known[...]
+    note(inverses, U1, u1)
+    note(inverses, V1, v1)
+    note(inverses, W1, w1)
+    meet(best, inverses, ranks, O1, o1, [(U1, u1)])
 
     @pl.when(spots[0] == 0)
     def _():
-        meet(best, E1, e1, [(V1, v1)])
+        meet(best, inverses, ranks, E1, e1, [(V1, v1)])
 
     @pl.when(spots[0] != 0)
     def _():
-        meet(best, E1, e1, [(U1, u1)])
+        meet(best, inverses, ranks, E1, e1, [(U1, u1)])
 
     @pl.when(spots[1] != 0)
     def _():
-        meet(best, U1, u1, [(V1, v1)])
+        meet(best, inverses, ranks, U1, u1, [(V1, v1)])
 
     @pl.when(spots[1] == 0)
     def _():
-        meet(best, U1, u1, [(W1, w1)])
-
-
-def second_kernel(spots, o1, o2, u1, v1, e1, e2, before, best):
+        meet(best, inverses, ranks, U1, u1, [(W1, w1)])
+
+
+def second_kernel(spots, ranks, o1, o2, u1, v1, e1, e2, before, known, best, inverses):
     best[...] = before[...]
-    meet(best, O2, o2, [(O1, o1), (O2, o2), (U1, u1), (V1, v1)])
-    meet(best, E2, e2, [(O1, o1), (U1, u1), (V1, v1)])
+    inverses[...] = known[...]
+    note(inverses, O2, o2)
+    note(inverses, E2, e2)
+    meet(best, inverses, ranks, O2, o2, [(O1, o1), (O2, o2), (U1, u1), (V1, v1)])
+    meet(best, inverses, ranks, E2, e2, [(O1, o1), (U1, u1), (V1, v1)])
 
     @pl.when(spots[0] != 0)
     def _():
-        meet(best, O2, o2, [(E2, e2)])
-
-
-def third_kernel(spots, o2, u2, v2, e2, before, best):
+        meet(best, inverses, ranks, O2, o2, [(E2, e2)])
+
+
+def third_kernel(spots, ranks, o2, u2, v2, e2, before, known, best, inverses):
     best[...] = before[...]
-    meet(best, O2, o2, [(U2, u2)])
+    inverses[...] = known[...]
+    note(inverses, U2, u2)
+    note(inverses, V2, v2)
+    meet(best, inverses, ranks, O2, o2, [(U2, u2)])
 
     @pl.when(spots[0] == 0)
     def _():
-        meet(best, E2, e2, [(V2, v2)])
+        meet(best, inverses, ranks, E2, e2, [(V2, v2)])
 
     @pl.when(spots[0] != 0)
     def _():
-        meet(best, E2, e2, [(U2, u2)])
-
-
-def fourth_kernel(spots, u1, u2, v1, v2, w1, w2, before, *refs):
-    *outs, best = refs
+        meet(best, inverses, ranks, E2, e2, [(U2, u2)])
+
+
+def fourth_kernel(spots, ranks, before, known, u1, u2, v1, v2, w1, w2, *refs):
+    *outs, best, inverses, near1, near2, far1, far2, sems = refs
     best[...] = before[...]
+    inverses[...] = known[...]
+
+    def opposite(name1, other1, name2, other2):
+        pairs = ((u2, near2), (other2, far2), (u1, near1), (other1, far1))
+        copies = [pltpu.make_async_copy(*pair, sems.at[i]) for i, pair in enumerate(pairs)]
+        for copy in copies:
+            copy.start()
+        copies[0].wait()
+        copies[1].wait()
+        if name2 == W2:
+            note(inverses, W2, far2)
+        meet(best, inverses, ranks, U2, near2, [(name2, far2)])
+        copies[2].wait()
+        meet(best, inverses, ranks, name2, far2, [(U1, near1)])
+        copies[3].wait()
+        meet(best, inverses, ranks, U2, near2, [(name1, far1)])
 
     @pl.when(spots[1] != 0)
     def _():
-        meet(best, V2, v2, [(U1, u1)])
-        meet(best, U2, u2, [(V1, v1), (V2, v2)])
+        opposite(V1, v1, V2, v2)
 
     @pl.when(spots[1] == 0)
     def _():
-        meet(best, W2, w2, [(U1, u1)])
-        meet(best, U2, u2, [(W1, w1), (W2, w2)])
+        opposite(W1, w1, W2, w2)
 
     for i, out in enumerate(outs):
         for y in range(Y):
@@ -318,11 +361,13 @@
     return isinstance(item, tuple) and isinstance(item[0], int)
 
 
-def scores_call(kernel, units, inputs, out, scratch, name):
+def scores_call(kernel, units, inputs, out, scratch, name, loose=0):
     return pl.pallas_call(
         kernel,
         out_shape=jax.tree.map(lambda dims: jax.ShapeDtypeStruct(dims, jnp.float32), out, is_leaf=is_dims),
-        in_specs=[SMEM] + [VMEM] * (len(inputs) - 1),
+        in_specs=[SMEM]
+        + [VMEM] * (len(inputs) - 1 - loose)
+        + [pl.BlockSpec(memory_space=pl.ANY)] * loose,
         out_specs=jax.tree.map(lambda _: VMEM, out, is_leaf=is_dims),
         scratch_shapes=scratch,
         compiler_params=PARAMS,
@@ -367,14 +412,20 @@
 
 def shards(embeds, cluster_ids, orders):
     y, x, core, z = (lax.axis_index(name) for name in ALL)
-    ids = cluster_ids.reshape(LINES, 128)
-    *placed, slots = place(ids, embeds)
-    arrived = [
-        lax.all_to_all(
+    swap = routes(lambda y, x, c, z: (y, x, 1 - c, z))
+    ahead = routes(lambda y, x, c, z: (y, x + 1 - 2 * c, c, z))
+    behind = routes(lambda y, x, c, z: (y, x - 1 + 2 * c, c, z))
+
+    def bring(rows):
+        part = rows.shape[0] // GROUPS
+        return lax.all_to_all(
             rows.reshape(GROUPS, part, WIDTH), ("y", "z"), split_axis=0, concat_axis=0, tiled=True
         ).reshape(GROUPS * part, WIDTH)
-        for rows, part in zip(placed, PARTS)
-    ]
+
+    ids = cluster_ids.reshape(LINES, 128)
+    placed1, slots = place(ids, embeds)
+    o1 = bring(placed1)
+    placed2 = place_rest(ids, slots, embeds)
 
     table = ranks(ids, slots, orders.reshape(LINES, 128)).reshape(Y, Z, CAP)
     table = lax.dynamic_index_in_dim(table, z, 1, keepdims=False)
@@ -384,15 +435,28 @@
         if j:
             row = lax.ppermute(row, ALL, routes(lambda y, x, c, z: (y + j, x, c, z)))
         rank_parts.append(row)
-    member_ranks = jnp.concatenate(rank_parts)[(y - jnp.arange(Y)) % Y]
-    rank1 = member_ranks[:, : PARTS[0]].reshape(1, SIZES[0])
-    rank2 = member_ranks[:, PARTS[0] :].reshape(1, SIZES[1])
-
+    own_ranks = jnp.concatenate(rank_parts)[(y - jnp.arange(Y)) % Y]
+    own_ranks = jnp.where(own_ranks > 0, own_ranks, never_order)
+    own_ranks = jnp.stack(
+        [
+            own_ranks[:, : PARTS[0]].reshape(SIZES[0]),
+            jnp.pad(own_ranks[:, PARTS[0] :].reshape(SIZES[1]), (0, SIZES[0] - SIZES[1])),
+        ]
+    )
+    near_ranks = lax.ppermute(own_ranks, ALL, ahead)
+    member_ranks = jnp.concatenate(
+        [
+            own_ranks,
+            near_ranks,
+            lax.ppermute(own_ranks, ALL, behind),
+            lax.ppermute(own_ranks, ALL, swap),
+            lax.ppermute(near_ranks, ALL, swap),
+            jnp.zeros((6, SIZES[0]), jnp.float32),
+        ]
+    )
     spots = jnp.stack([core, ((x < X // 2) == (core == 0)).astype(jnp.int32)]).astype(jnp.int32)
-
-    swap = routes(lambda y, x, c, z: (y, x, 1 - c, z))
-    ahead = routes(lambda y, x, c, z: (y, x + 1 - 2 * c, c, z))
-    behind = routes(lambda y, x, c, z: (y, x - 1 + 2 * c, c, z))
+    o1, placed2, member_ranks, spots = lax.optimization_barrier((o1, placed2, member_ranks, spots))
+    o2 = bring(placed2)
 
     def share(own, after):
         u = lax.ppermute(own, ALL, ahead)
@@ -402,25 +466,35 @@
         return (u, v, e, lax.ppermute(u, ALL, swap), *after)
 
     wide = (16, SIZES[0])
-    o1 = gather(SIZES[0], arrived[0], rank1)
-    u1, v1, e1, w1, best, later = share(
-        o1,
-        lambda e: (scores_call(own_kernel, 8, (spots, o1, e), wide, [], "own"), arrived[1]),
-    )
-    o2 = gather(SIZES[1], later, rank2)
+
+    def score(kernel, units, blocks, state, name):
+        return scores_call(
+            kernel, units, (spots, member_ranks, *blocks, *state), [wide, wide], [], name
+        )
+
+    u1, v1, e1, w1, *state, o2 = share(
+        o1, lambda e: (*score(own_kernel, 8, (o1, e), (), "own"), o2)
+    )
 
     def before_arrival(e2):
-        first = scores_call(
-            first_kernel, 12, (spots, o1, u1, v1, e1, w1, best), wide, [], "first"
-        )
-        inputs = (spots, o1, o2, u1, v1, e1, e2, first)
-        return (scores_call(second_kernel, 14, inputs, wide, [], "second"),)
-
-    u2, v2, e2, w2, best = share(o2, before_arrival)
-    best = scores_call(third_kernel, 2, (spots, o2, u2, v2, e2, best), wide, [], "third")
+        first = score(first_kernel, 12, (o1, u1, v1, e1, w1), state, "first")
+        return score(second_kernel, 14, (o1, o2, u1, v1, e1, e2), first, "second")
+
+    u2, v2, e2, w2, *known = share(o2, before_arrival)
+    best, inverses = score(third_kernel, 2, (o2, u2, v2, e2), known, "third")
     own, *others = scores_call(
-        fourth_kernel, 5, (spots, u1, u2, v1, v2, w1, w2, best), [(Y, CAP)] * 5,
-        [pltpu.VMEM(wide, jnp.float32)], "fourth",
+        fourth_kernel, 5, (spots, member_ranks, best, inverses, u1, u2, v1, v2, w1, w2),
+        [(Y, CAP)] * 5,
+        [
+            pltpu.VMEM(wide, jnp.float32),
+            pltpu.VMEM(wide, jnp.float32),
+            pltpu.VMEM((GROUPS * PARTS[0], WIDTH), jnp.bfloat16),
+            pltpu.VMEM((GROUPS * PARTS[1], WIDTH), jnp.bfloat16),
+            pltpu.VMEM((GROUPS * PARTS[0], WIDTH), jnp.bfloat16),
+            pltpu.VMEM((GROUPS * PARTS[1], WIDTH), jnp.bfloat16),
+            pltpu.SemaphoreType.DMA((4,)),
+        ],
+        "fourth", 6,
     )
     across = routes(lambda y, x, c, z: (y, x + 1 - 2 * c, 1 - c, z))
     for part, way in zip(others, (behind, ahead, swap, across)):

time: 118 us -> 116 us (0.983)
  waiting for transfers between devices: 37.1 us -> 23.9 us
  starting transfers between devices: 38.9 us -> 46.4 us
  Pallas kernels: 25.5 us -> 27.8 us
    all_to_all x2, waiting for transfers between devices: 30.5 us -> 17.8 us  [bring(): lax.all_to_all(rows.reshape(GROUPS, part, WIDTH), ('y', 'z'), split_axis=...]
    ppermute x0 -> x4, starting transfers between devices: none -> 7.56 us  [the longest x1 3.42 us: shards(): lax.ppermute(own_ranks, ALL, swap)]
    pallas_call x2 -> x1, Pallas kernels: 1.92 us -> 4.21 us  [place_rest(): pl.pallas_call(place_rest_kernel, out_shape=jax.ShapeDtypeStruct((GROUPS...]
  transfers between devices with their start and end apart: 17 -> 21, of which waited for: 8 -> 7; matrix products, arithmetic and copies ran while one was open for 1% -> 1% of each run, Pallas kernels for 12% -> 16%
where the time goes in v7:
time: 116 us; the launch traced here: 115 us
  starting transfers between devices  46.4 us (40%)
  Pallas kernels  27.8 us (24%)
  waiting for transfers between devices  23.9 us (21%)
  blocking collectives  15 us (13%)
  local copies, waits for them, and re-layouts  1.48 us (1%)
    all_to_all x2, waiting for transfers between devices, bring(): lax.all_to_all(rows.reshape(GROUPS, part, WIDTH), ('y', 'z'), split_axis=...  17.8 us
    all_to_all x2, starting transfers between devices, bring(): lax.all_to_all(rows.reshape(GROUPS, part, WIDTH), ('y', 'z'), split_axis=...  17.1 us
    pallas_call x5, Pallas kernels, scores_call(): pl.pallas_call(kernel, out_shape=jax.tree.map(lambda dims: jax.ShapeDtype...  16.1 us
    all_to_all x1, blocking collectives, shards(): lax.all_to_all(jnp.broadcast_to(own[:, None], (Y, Z, CAP)).reshape(GROUPS...  15 us
    pallas_call x1, Pallas kernels, place(): pl.pallas_call(place_kernel, out_shape=(jax.ShapeDtypeStruct((GROUPS * PA...  5.4 us
    ppermute x2, starting transfers between devices, share(): e = lax.ppermute(own, ALL, swap)  5.27 us
    ppermute x3, starting transfers between devices, shards(): row = lax.ppermute(row, ALL, routes(lambda y, x, c, z: (y + j, x, c, z)))  4.82 us
    pallas_call x1, Pallas kernels, place_rest(): pl.pallas_call(place_rest_kernel, out_shape=jax.ShapeDtypeStruct((GROUPS...  4.21 us
  transfers between devices with their start and end apart: 21, of which 7 were waited for; matrix products, arithmetic and copies ran while one was open for 1% of the time, Pallas kernels for 16%

profile of v7, /device:TPU:1, one launch (start us, length us, event | category | flops | bytes accessed | tf_op | source)
XLA Modules:
  0.0 115.0 jit_solution(15839592331950366277)
XLA Ops:
  0.0 5.4 %place.1 = (bf16[4096,128]{1,0:T(8,128)(2,1)}, s32[24,128]{1,0:T(8,128)}) custom-call(s32[24,128]{1,0:T(8,128)} %bitcast.30, bf16[3072,128]{1,0:T(8,128)(2,1)} %rows_ref.1), custom_call_target="tpu_custom_call" | custom-call | tf_op jit(solution)/shard_map/place/pallas_call | solution.py:85
  5.4 12.3 %all-to-all-start = ((bf16[32,128,128]{2,1,0:T(8,128)(2,1)}), bf16[32,128,128]{2,1,0:T(8,128)(2,1)}, u32[]{:S(2)}, u32[]{:S(2)}) async-start(bf16[32,128,128]{2,1,0:T(8,128)(2,1)} %bitcast.37), calls=%async_computation | async-start | bytes 2097152 | tf_op jit(solution)/shard_map/all_to_all | solution.py:421
  19.4 1.2 %collective-permute-start = (f32[1,192]{1,0:T(1,128)S(1)}, f32[1,192]{1,0:T(1,128)S(1)}, u32[]{:S(2)}, u32[]{:S(2)}) collective-permute-start(f32[1,192]{1,0:T(1,128)S(1)} %get-tuple-element.60), channel_id=1, source_target_pairs={{0,64},{1,65},{2,66},{3,67},{4,68},{5,69},{6,70},{7,71},{8,72},{9,... | collective-permute-start | bytes 2312 | tf_op jit(solution)/shard_map/ppermute | solution.py:436
  20.7 2.4 %collective-permute-start.1 = (f32[1,192]{1,0:T(1,128)S(1)}, f32[1,192]{1,0:T(1,128)S(1)}, u32[]{:S(2)}, u32[]{:S(2)}) collective-permute-start(f32[1,192]{1,0:T(1,128)S(1)} %get-tuple-element.59), channel_id=1, source_target_pairs={{0,128},{1,129},{2,130},{3,131},{4,132},{5,133},{6,134},{7,135},{8... | collective-permute-start | bytes 2312 | tf_op jit(solution)/shard_map/ppermute | solution.py:436
  26.5 2.6 %collective-permute-start.3 = (f32[2,512]{1,0:T(2,128)S(1)}, f32[2,512]{1,0:T(2,128)S(1)}, u32[]{:S(2)}, u32[]{:S(2)}) collective-permute-start(f32[2,512]{1,0:T(2,128)S(1)} %pad_maximum_fusion.1), channel_id=1, source_target_pairs={{0,16},{1,17},{2,18},{3,19},{4,20},{5,21},{6,22},{7,23},{8,56},{9,... | collective-permute-start | bytes 12296 | tf_op jit(solution)/shard_map/ppermute | solution.py:446
  29.1 3.4 %collective-permute-start.5 = (f32[2,512]{1,0:T(2,128)S(1)}, f32[2,512]{1,0:T(2,128)S(1)}, u32[]{:S(2)}, u32[]{:S(2)}) collective-permute-start(f32[2,512]{1,0:T(2,128)S(1)} %pad_maximum_fusion.1), channel_id=1, source_target_pairs={{0,8},{1,9},{2,10},{3,11},{4,12},{5,13},{6,14},{7,15},{8,0},{9,1},... | collective-permute-start | bytes 12296 | tf_op jit(solution)/shard_map/ppermute | solution.py:452
  32.5 1.6 %collective-permute-start.6 = (f32[2,512]{1,0:T(2,128)S(1)}, f32[2,512]{1,0:T(2,128)S(1)}, u32[]{:S(2)}, u32[]{:S(2)}) collective-permute-start(f32[2,512]{1,0:T(2,128)S(1)} %collective-permute-done.3), channel_id=1, source_target_pairs={{0,8},{1,9},{2,10},{3,11},{4,12},{5,13},{6,14},{7,15},{8,0},{9,1},... | collective-permute-start | bytes 12296 | tf_op jit(solution)/shard_map/ppermute | solution.py:453
  34.2 4.2 %place_rest.1 = bf16[2048,128]{1,0:T(8,128)(2,1)} custom-call(s32[24,128]{1,0:T(8,128)S(1)} %bitcast.32, s32[24,128]{1,0:T(8,128)S(1)} %copy-done.2, bf16[3072,128]{1,0:T(8,128)(2,1)S(1)} %copy-done), custom_call_target="tpu_custom_call" | custom-call | tf_op jit(solution)/shard_map/place_rest/pallas_call | solution.py:126
  38.5 3.8 %all-to-all-done = bf16[32,128,128]{2,1,0:T(8,128)(2,1)} async-done(((bf16[32,128,128]{2,1,0:T(8,128)(2,1)}), bf16[32,128,128]{2,1,0:T(8,128)(2,1)}, u32[]{:S(2)}, u32[]{:S(2)}) %all-to-all-start) | async-done | bytes 1048608 | tf_op jit(solution)/shard_map/all_to_all | solution.py:421
  42.3 5.0 %collective-permute-start.8 = (bf16[4096,128]{1,0:T(8,128)(2,1)}, bf16[4096,128]{1,0:T(8,128)(2,1)}, u32[]{:S(2)}, u32[]{:S(2)}) collective-permute-start(bf16[4096,128]{1,0:T(8,128)(2,1)} %bitcast.2.o1), channel_id=1, source_target_pairs={{0,8},{1,9},{2,10},{3,11},{4,12},{5,13},{6,14},{7,15},{8,0},{9,1},... | collective-permute-start | bytes 3145736 | tf_op jit(solution)/shard_map/ppermute | solution.py:464
  47.3 2.5 %collective-permute-start.7 = (bf16[4096,128]{1,0:T(8,128)(2,1)}, bf16[4096,128]{1,0:T(8,128)(2,1)S(1)}, u32[]{:S(2)}, u32[]{:S(2)}) collective-permute-start(bf16[4096,128]{1,0:T(8,128)(2,1)} %bitcast.2.o1), channel_id=1, source_target_pairs={{0,16},{1,17},{2,18},{3,19},{4,20},{5,21},{6,22},{7,23},{8,56},{9,... | collective-permute-start | bytes 3145736 | tf_op jit(solution)/shard_map/ppermute | solution.py:462
  49.8 4.8 %all-to-all-start.1 = ((bf16[32,64,128]{2,1,0:T(8,128)(2,1)}), bf16[32,64,128]{2,1,0:T(8,128)(2,1)S(1)}, u32[]{:S(2)}, u32[]{:S(2)}) async-start(bf16[32,64,128]{2,1,0:T(8,128)(2,1)} %bitcast.14), calls=%async_computation.1 | async-start | bytes 1048576 | tf_op jit(solution)/shard_map/all_to_all | solution.py:421
  54.7 2.5 %own.1 = (f32[16,512]{1,0:T(8,128)S(1)}, f32[16,512]{1,0:T(8,128)S(1)}) custom-call(s32[2]{0:T(128)S(1)} %pad_add_fusion.spots, f32[16,512]{1,0:T(8,128)S(1)} %concatenate.8.ranks, bf16[4096,128]{1,0:T(8,128)(2,1)} %bitcast.2.o1, bf16[4096,128]{1,0:T(8,128)(2,1)} %collective-permute-done.8.e1), custom_call_target="tpu_custom_call" | custom-call | flops 1073741824 | bytes 4194304 | tf_op jit(solution)/shard_map/own/pallas_call | solution.py:365
  57.2 13.9 %all-to-all-done.1 = bf16[32,64,128]{2,1,0:T(8,128)(2,1)S(1)} async-done(((bf16[32,64,128]{2,1,0:T(8,128)(2,1)}), bf16[32,64,128]{2,1,0:T(8,128)(2,1)S(1)}, u32[]{:S(2)}, u32[]{:S(2)}) %all-to-all-start.1) | async-done | bytes 524320 | tf_op jit(solution)/shard_map/all_to_all | solution.py:421
  71.7 1.2 %collective-permute-start.9 = (bf16[2048,128]{1,0:T(8,128)(2,1)S(1)}, bf16[2048,128]{1,0:T(8,128)(2,1)S(1)}, u32[]{:S(2)}, u32[]{:S(2)}) collective-permute-start(bf16[2048,128]{1,0:T(8,128)(2,1)S(1)} %bitcast.26), channel_id=1, source_target_pairs={{0,16},{1,17},{2,18},{3,19},{4,20},{5,21},{6,22},{7,23},{8,56},{9,... | collective-permute-start | bytes 1572872 | tf_op jit(solution)/shard_map/ppermute | solution.py:462
  74.1 4.9 %first.1 = (f32[16,512]{1,0:T(8,128)S(1)}, f32[16,512]{1,0:T(8,128)S(1)}) custom-call(s32[2]{0:T(128)S(1)} %pad_add_fusion.spots, f32[16,512]{1,0:T(8,128)S(1)} %concatenate.8.ranks, bf16[4096,128]{1,0:T(8,128)(2,1)} %bitcast.2.o1, bf16[4096,128]{1,0:T(8,128)(2,1)S(1)} %collective-permute-done.7.u1, bf16[4096,128]{1,0:T(8,128)(2,1)S(1)} %collective-permute-done.10.v1, ...), custom_call_target="tpu_custom_call" | custom-call | flops 1610612736 | bytes 4194304 | tf_op jit(solution)/shard_map/first/pallas_call | solution.py:365
  79.0 4.3 %second.1 = (f32[16,512]{1,0:T(8,128)S(1)}, f32[16,512]{1,0:T(8,128)S(1)}) custom-call(s32[2]{0:T(128)S(1)} %pad_add_fusion.spots, f32[16,512]{1,0:T(8,128)S(1)} %concatenate.8.ranks, bf16[4096,128]{1,0:T(8,128)(2,1)} %bitcast.2.o1, bf16[2048,128]{1,0:T(8,128)(2,1)S(1)} %bitcast.28, bf16[4096,128]{1,0:T(8,128)(2,1)S(1)} %collective-permute-done.7.u1, ...), custom_call_target="tpu_custom_call" | custom-call | flops 1879048192 | bytes 4194304 | tf_op jit(solution)/shard_map/second/pallas_call | solution.py:365
  84.2 3.3 %collective-permute-start.14 = (bf16[2048,128]{1,0:T(8,128)(2,1)S(1)}, bf16[2048,128]{1,0:T(8,128)(2,1)S(1)}, u32[]{:S(2)}, u32[]{:S(2)}) collective-permute-start(bf16[2048,128]{1,0:T(8,128)(2,1)S(1)} %collective-permute-done.9.u2), channel_id=1, source_target_pairs={{0,8},{1,9},{2,10},{3,11},{4,12},{5,13},{6,14},{7,15},{8,0},{9,1},... | collective-permute-start | bytes 1572872 | tf_op jit(solution)/shard_map/ppermute | solution.py:466
  87.4 1.5 %third.1 = (f32[16,512]{1,0:T(8,128)S(1)}, f32[16,512]{1,0:T(8,128)S(1)}) custom-call(s32[2]{0:T(128)S(1)} %pad_add_fusion.spots, f32[16,512]{1,0:T(8,128)S(1)} %concatenate.8.ranks, bf16[2048,128]{1,0:T(8,128)(2,1)S(1)} %bitcast.29, bf16[2048,128]{1,0:T(8,128)(2,1)S(1)} %collective-permute-done.9.u2, bf16[2048,128]{1,0:T(8,128)(2,1)S(1)} %collective-permute-done.13.v2, ...), custom_call_target="tpu_custom_call" | custom-call | flops 268435456 | bytes 4194304 | tf_op jit(solution)/shard_map/third/pallas_call | solution.py:365
  89.0 2.8 %fourth.1 = (f32[4,192]{1,0:T(4,128)S(1)}, f32[4,192]{1,0:T(4,128)S(1)}, f32[4,192]{1,0:T(4,128)S(1)}, f32[4,192]{1,0:T(4,128)S(1)}, f32[4,192]{1,0:T(4,128)S(1)}) custom-call(s32[2]{0:T(128)S(1)} %pad_add_fusion.spots, f32[16,512]{1,0:T(8,128)S(1)} %concatenate.8.ranks, f32[16,512]{1,0:T(8,128)S(1)} %get-tuple-element.50.before, ...), custom_call_target="tpu_custom_call" | custom-call | flops 671088640 | bytes 4194304 | tf_op jit(solution)/shard_map/fourth/pallas_call | solution.py:365
  91.9 2.7 %collective-permute-start.16 = (f32[4,192]{1,0:T(4,128)S(1)}, f32[4,192]{1,0:T(4,128)S(1)}, u32[]{:S(2)}, u32[]{:S(2)}) collective-permute-start(f32[4,192]{1,0:T(4,128)S(1)} %get-tuple-element.54), channel_id=1, source_target_pairs={{0,16},{1,17},{2,18},{3,19},{4,20},{5,21},{6,22},{7,23},{8,56},{9,... | collective-permute-start | bytes 9224 | tf_op jit(solution)/shard_map/ppermute | solution.py:501
  94.6 1.4 %collective-permute-start.18 = (f32[4,192]{1,0:T(4,128)S(1)}, f32[4,192]{1,0:T(4,128)S(1)}, u32[]{:S(2)}, u32[]{:S(2)}) collective-permute-start(f32[4,192]{1,0:T(4,128)S(1)} %get-tuple-element.56), channel_id=1, source_target_pairs={{0,24},{1,25},{2,26},{3,27},{4,28},{5,29},{6,30},{7,31},{8,48},{9,... | collective-permute-start | bytes 9224 | tf_op jit(solution)/shard_map/ppermute | solution.py:501
  96.0 2.8 %collective-permute-done.18 = f32[4,192]{1,0:T(4,128)S(1)} collective-permute-done((f32[4,192]{1,0:T(4,128)S(1)}, f32[4,192]{1,0:T(4,128)S(1)}, u32[]{:S(2)}, u32[]{:S(2)}) %collective-permute-start.18) | collective-permute-done | bytes 3104 | tf_op jit(solution)/shard_map/ppermute | solution.py:501
  98.9 15.0 %all_to_all.21 = f32[32,1,192]{2,1,0:T(1,128)S(1)} all-to-all(f32[32,1,192]{2,1,0:T(1,128)S(1)} %all_to_all.15), channel_id=1, replica_groups=mesh['y'=4,'x'=4,'core'=2,'z'=8] {'y','z'}, dimensions={0} | all-to-all | bytes 49152 | tf_op jit(solution)/shard_map/all_to_all | solution.py:502
  (54 shorter events, 9.1 us)
Async XLA Ops:
  5.4 28.8 %copy-start = (bf16[3072,128]{1,0:T(8,128)(2,1)S(1)}, bf16[3072,128]{1,0:T(8,128)(2,1)}, u32[]{:S(2)}) copy-start(bf16[3072,128]{1,0:T(8,128)(2,1)} %rows_ref.1) | copy-start | bytes 2359300
  5.4 36.9 %all-to-all-start = ((bf16[32,128,128]{2,1,0:T(8,128)(2,1)}), bf16[32,128,128]{2,1,0:T(8,128)(2,1)}, u32[]{:S(2)}, u32[]{:S(2)}) async-start(bf16[32,128,128]{2,1,0:T(8,128)(2,1)} %bitcast.37), calls=%async_computation | async-start | bytes 2097152 | tf_op jit(solution)/shard_map/all_to_all | solution.py:421
  17.8 0.7 copy-start.2
  17.8 0.7 copy-start.1
  19.4 4.8 %collective-permute-start = (f32[1,192]{1,0:T(1,128)S(1)}, f32[1,192]{1,0:T(1,128)S(1)}, u32[]{:S(2)}, u32[]{:S(2)}) collective-permute-start(f32[1,192]{1,0:T(1,128)S(1)} %get-tuple-element.60), channel_id=1, source_target_pairs={{0,64},{1,65},{2,66},{3,67},{4,68},{5,69},{6,70},{7,71},{8,72},{9,... | collective-permute-start | bytes 2312 | tf_op jit(solution)/shard_map/ppermute | solution.py:436
  20.7 4.0 %collective-permute-start.1 = (f32[1,192]{1,0:T(1,128)S(1)}, f32[1,192]{1,0:T(1,128)S(1)}, u32[]{:S(2)}, u32[]{:S(2)}) collective-permute-start(f32[1,192]{1,0:T(1,128)S(1)} %get-tuple-element.59), channel_id=1, source_target_pairs={{0,128},{1,129},{2,130},{3,131},{4,132},{5,133},{6,134},{7,135},{8... | collective-permute-start | bytes 2312 | tf_op jit(solution)/shard_map/ppermute | solution.py:436
  23.1 2.7 %collective-permute-start.2 = (f32[1,192]{1,0:T(1,128)S(1)}, f32[1,192]{1,0:T(1,128)S(1)}, u32[]{:S(2)}, u32[]{:S(2)}) collective-permute-start(f32[1,192]{1,0:T(1,128)S(1)} %get-tuple-element.58), channel_id=1, source_target_pairs={{0,192},{1,193},{2,194},{3,195},{4,196},{5,197},{6,198},{7,199},{8... | collective-permute-start | bytes 2312 | tf_op jit(solution)/shard_map/ppermute | solution.py:436
  26.5 6.0 %collective-permute-start.3 = (f32[2,512]{1,0:T(2,128)S(1)}, f32[2,512]{1,0:T(2,128)S(1)}, u32[]{:S(2)}, u32[]{:S(2)}) collective-permute-start(f32[2,512]{1,0:T(2,128)S(1)} %pad_maximum_fusion.1), channel_id=1, source_target_pairs={{0,16},{1,17},{2,18},{3,19},{4,20},{5,21},{6,22},{7,23},{8,56},{9,... | collective-permute-start | bytes 12296 | tf_op jit(solution)/shard_map/ppermute | solution.py:446
  29.1 9.3 %collective-permute-start.4 = (f32[2,512]{1,0:T(2,128)S(1)}, f32[2,512]{1,0:T(2,128)S(1)}, u32[]{:S(2)}, u32[]{:S(2)}) collective-permute-start(f32[2,512]{1,0:T(2,128)S(1)} %pad_maximum_fusion.1), channel_id=1, source_target_pairs={{0,48},{1,49},{2,50},{3,51},{4,52},{5,53},{6,54},{7,55},{8,24},{9,... | collective-permute-start | bytes 12296 | tf_op jit(solution)/shard_map/ppermute | solution.py:451
  29.1 9.3 %collective-permute-start.5 = (f32[2,512]{1,0:T(2,128)S(1)}, f32[2,512]{1,0:T(2,128)S(1)}, u32[]{:S(2)}, u32[]{:S(2)}) collective-permute-start(f32[2,512]{1,0:T(2,128)S(1)} %pad_maximum_fusion.1), channel_id=1, source_target_pairs={{0,8},{1,9},{2,10},{3,11},{4,12},{5,13},{6,14},{7,15},{8,0},{9,1},... | collective-permute-start | bytes 12296 | tf_op jit(solution)/shard_map/ppermute | solution.py:452
  32.5 5.9 %collective-permute-start.6 = (f32[2,512]{1,0:T(2,128)S(1)}, f32[2,512]{1,0:T(2,128)S(1)}, u32[]{:S(2)}, u32[]{:S(2)}) collective-permute-start(f32[2,512]{1,0:T(2,128)S(1)} %collective-permute-done.3), channel_id=1, source_target_pairs={{0,8},{1,9},{2,10},{3,11},{4,12},{5,13},{6,14},{7,15},{8,0},{9,1},... | collective-permute-start | bytes 12296 | tf_op jit(solution)/shard_map/ppermute | solution.py:453
  42.3 12.3 %collective-permute-start.8 = (bf16[4096,128]{1,0:T(8,128)(2,1)}, bf16[4096,128]{1,0:T(8,128)(2,1)}, u32[]{:S(2)}, u32[]{:S(2)}) collective-permute-start(bf16[4096,128]{1,0:T(8,128)(2,1)} %bitcast.2.o1), channel_id=1, source_target_pairs={{0,8},{1,9},{2,10},{3,11},{4,12},{5,13},{6,14},{7,15},{8,0},{9,1},... | collective-permute-start | bytes 3145736 | tf_op jit(solution)/shard_map/ppermute | solution.py:464
  47.3 23.9 %collective-permute-start.7 = (bf16[4096,128]{1,0:T(8,128)(2,1)}, bf16[4096,128]{1,0:T(8,128)(2,1)S(1)}, u32[]{:S(2)}, u32[]{:S(2)}) collective-permute-start(bf16[4096,128]{1,0:T(8,128)(2,1)} %bitcast.2.o1), channel_id=1, source_target_pairs={{0,16},{1,17},{2,18},{3,19},{4,20},{5,21},{6,22},{7,23},{8,56},{9,... | collective-permute-start | bytes 3145736 | tf_op jit(solution)/shard_map/ppermute | solution.py:462
  49.8 21.4 %all-to-all-start.1 = ((bf16[32,64,128]{2,1,0:T(8,128)(2,1)}), bf16[32,64,128]{2,1,0:T(8,128)(2,1)S(1)}, u32[]{:S(2)}, u32[]{:S(2)}) async-start(bf16[32,64,128]{2,1,0:T(8,128)(2,1)} %bitcast.14), calls=%async_computation.1 | async-start | bytes 1048576 | tf_op jit(solution)/shard_map/all_to_all | solution.py:421
  54.6 19.5 %collective-permute-start.10 = (bf16[4096,128]{1,0:T(8,128)(2,1)}, bf16[4096,128]{1,0:T(8,128)(2,1)S(1)}, u32[]{:S(2)}, u32[]{:S(2)}) collective-permute-start(bf16[4096,128]{1,0:T(8,128)(2,1)} %bitcast.2.o1), channel_id=1, source_target_pairs={{0,48},{1,49},{2,50},{3,51},{4,52},{5,53},{6,54},{7,55},{8,24},{9,... | collective-permute-start | bytes 3145736 | tf_op jit(solution)/shard_map/ppermute | solution.py:463
  71.2 2.9 %collective-permute-start.12 = (bf16[4096,128]{1,0:T(8,128)(2,1)S(1)}, bf16[4096,128]{1,0:T(8,128)(2,1)S(1)}, u32[]{:S(2)}, u32[]{:S(2)}) collective-permute-start(bf16[4096,128]{1,0:T(8,128)(2,1)S(1)} %collective-permute-done.7.u1), channel_id=1, source_target_pairs={{0,8},{1,9},{2,10},{3,11},{4,12},{5,13},{6,14},{7,15},{8,0},{9,1},... | collective-permute-start | bytes 3145736 | tf_op jit(solution)/shard_map/ppermute | solution.py:466
  71.4 7.6 %collective-permute-start.11 = (bf16[2048,128]{1,0:T(8,128)(2,1)S(1)}, bf16[2048,128]{1,0:T(8,128)(2,1)S(1)}, u32[]{:S(2)}, u32[]{:S(2)}) collective-permute-start(bf16[2048,128]{1,0:T(8,128)(2,1)S(1)} %bitcast.25), channel_id=1, source_target_pairs={{0,8},{1,9},{2,10},{3,11},{4,12},{5,13},{6,14},{7,15},{8,0},{9,1},... | collective-permute-start | bytes 1572872 | tf_op jit(solution)/shard_map/ppermute | solution.py:464
  71.7 12.5 %collective-permute-start.9 = (bf16[2048,128]{1,0:T(8,128)(2,1)S(1)}, bf16[2048,128]{1,0:T(8,128)(2,1)S(1)}, u32[]{:S(2)}, u32[]{:S(2)}) collective-permute-start(bf16[2048,128]{1,0:T(8,128)(2,1)S(1)} %bitcast.26), channel_id=1, source_target_pairs={{0,16},{1,17},{2,18},{3,19},{4,20},{5,21},{6,22},{7,23},{8,56},{9,... | collective-permute-start | bytes 1572872 | tf_op jit(solution)/shard_map/ppermute | solution.py:462
  72.9 14.6 %collective-permute-start.13 = (bf16[2048,128]{1,0:T(8,128)(2,1)S(1)}, bf16[2048,128]{1,0:T(8,128)(2,1)S(1)}, u32[]{:S(2)}, u32[]{:S(2)}) collective-permute-start(bf16[2048,128]{1,0:T(8,128)(2,1)S(1)} %bitcast.27), channel_id=1, source_target_pairs={{0,48},{1,49},{2,50},{3,51},{4,52},{5,53},{6,54},{7,55},{8,24},{9,... | collective-permute-start | bytes 1572872 | tf_op jit(solution)/shard_map/ppermute | solution.py:463
  84.2 4.8 %collective-permute-start.14 = (bf16[2048,128]{1,0:T(8,128)(2,1)S(1)}, bf16[2048,128]{1,0:T(8,128)(2,1)S(1)}, u32[]{:S(2)}, u32[]{:S(2)}) collective-permute-start(bf16[2048,128]{1,0:T(8,128)(2,1)S(1)} %collective-permute-done.9.u2), channel_id=1, source_target_pairs={{0,8},{1,9},{2,10},{3,11},{4,12},{5,13},{6,14},{7,15},{8,0},{9,1},... | collective-permute-start | bytes 1572872 | tf_op jit(solution)/shard_map/ppermute | solution.py:466
  91.8 4.2 %collective-permute-start.15 = (f32[4,192]{1,0:T(4,128)S(1)}, f32[4,192]{1,0:T(4,128)S(1)}, u32[]{:S(2)}, u32[]{:S(2)}) collective-permute-start(f32[4,192]{1,0:T(4,128)S(1)} %get-tuple-element.53), channel_id=1, source_target_pairs={{0,48},{1,49},{2,50},{3,51},{4,52},{5,53},{6,54},{7,55},{8,24},{9,... | collective-permute-start | bytes 9224 | tf_op jit(solution)/shard_map/ppermute | solution.py:501
  91.9 4.1 %collective-permute-start.16 = (f32[4,192]{1,0:T(4,128)S(1)}, f32[4,192]{1,0:T(4,128)S(1)}, u32[]{:S(2)}, u32[]{:S(2)}) collective-permute-start(f32[4,192]{1,0:T(4,128)S(1)} %get-tuple-element.54), channel_id=1, source_target_pairs={{0,16},{1,17},{2,18},{3,19},{4,20},{5,21},{6,22},{7,23},{8,56},{9,... | collective-permute-start | bytes 9224 | tf_op jit(solution)/shard_map/ppermute | solution.py:501
  94.6 1.4 %collective-permute-start.17 = (f32[4,192]{1,0:T(4,128)S(1)}, f32[4,192]{1,0:T(4,128)S(1)}, u32[]{:S(2)}, u32[]{:S(2)}) collective-permute-start(f32[4,192]{1,0:T(4,128)S(1)} %get-tuple-element.55), channel_id=1, source_target_pairs={{0,8},{1,9},{2,10},{3,11},{4,12},{5,13},{6,14},{7,15},{8,0},{9,1},... | collective-permute-start | bytes 9224 | tf_op jit(solution)/shard_map/ppermute | solution.py:501
  94.6 4.2 %collective-permute-start.18 = (f32[4,192]{1,0:T(4,128)S(1)}, f32[4,192]{1,0:T(4,128)S(1)}, u32[]{:S(2)}, u32[]{:S(2)}) collective-permute-start(f32[4,192]{1,0:T(4,128)S(1)} %get-tuple-element.56), channel_id=1, source_target_pairs={{0,24},{1,25},{2,26},{3,27},{4,28},{5,29},{6,30},{7,31},{8,48},{9,... | collective-permute-start | bytes 9224 | tf_op jit(solution)/shard_map/ppermute | solution.py:501
  (1 other events, 0.7 us)

commit v8 on v7

--- a/solution.py
+++ b/solution.py
@@ -304,7 +304,16 @@
         meet(best, inverses, ranks, O2, o2, [(E2, e2)])
 
 
-def third_kernel(spots, ranks, o2, u2, v2, e2, before, known, best, inverses):
+def give(best, name, out):
+    for y in range(Y):
+        at = pl.ds(y, 1)
+        out[at, pl.ds(0, PARTS[0])] = best[pl.ds(name, 1), pl.ds(y * PARTS[0], PARTS[0])]
+        pair = best[pl.ds(name + 1, 1), pl.ds(y // 2 * 128, 128)]
+        pair = pltpu.roll(pair, 64, 1) if y % 2 else pair
+        out[at, pl.ds(PARTS[0], PARTS[1])] = pair[:, : PARTS[1]]
+
+
+def third_kernel(spots, ranks, o2, u2, v2, e2, before, known, best, inverses, e_best):
     best[...] = before[...]
     inverses[...] = known[...]
     note(inverses, U2, u2)
@@ -319,55 +328,42 @@
     def _():
         meet(best, inverses, ranks, E2, e2, [(U2, u2)])
 
-
-def fourth_kernel(spots, ranks, before, known, u1, u2, v1, v2, w1, w2, *refs):
-    *outs, best, inverses, near1, near2, far1, far2, sems = refs
+    give(best, E1, e_best)
+
+
+def fourth_kernel(
+    spots, ranks, u1, u2, v1, v2, w1, w2, before, known, o_best, u_best, v_best, w_best,
+    best, inverses,
+):
     best[...] = before[...]
     inverses[...] = known[...]
 
-    def opposite(name1, other1, name2, other2):
-        pairs = ((u2, near2), (other2, far2), (u1, near1), (other1, far1))
-        copies = [pltpu.make_async_copy(*pair, sems.at[i]) for i, pair in enumerate(pairs)]
-        for copy in copies:
-            copy.start()
-        copies[0].wait()
-        copies[1].wait()
-        if name2 == W2:
-            note(inverses, W2, far2)
-        meet(best, inverses, ranks, U2, near2, [(name2, far2)])
-        copies[2].wait()
-        meet(best, inverses, ranks, name2, far2, [(U1, near1)])
-        copies[3].wait()
-        meet(best, inverses, ranks, U2, near2, [(name1, far1)])
-
     @pl.when(spots[1] != 0)
     def _():
-        opposite(V1, v1, V2, v2)
+        meet(best, inverses, ranks, V2, v2, [(U1, u1)])
+        meet(best, inverses, ranks, U2, u2, [(V1, v1), (V2, v2)])
 
     @pl.when(spots[1] == 0)
     def _():
-        opposite(W1, w1, W2, w2)
-
-    for i, out in enumerate(outs):
-        for y in range(Y):
-            at = pl.ds(y, 1)
-            out[at, pl.ds(0, PARTS[0])] = best[pl.ds(2 * i, 1), pl.ds(y * PARTS[0], PARTS[0])]
-            pair = best[pl.ds(2 * i + 1, 1), pl.ds(y // 2 * 128, 128)]
-            pair = pltpu.roll(pair, 64, 1) if y % 2 else pair
-            out[at, pl.ds(PARTS[0], PARTS[1])] = pair[:, : PARTS[1]]
+        note(inverses, W2, w2)
+        meet(best, inverses, ranks, W2, w2, [(U1, u1)])
+        meet(best, inverses, ranks, U2, u2, [(W1, w1), (W2, w2)])
+
+    give(best, O1, o_best)
+    give(best, U1, u_best)
+    give(best, V1, v_best)
+    give(best, W1, w_best)
 
 
 def is_dims(item):
     return isinstance(item, tuple) and isinstance(item[0], int)
 
 
-def scores_call(kernel, units, inputs, out, scratch, name, loose=0):
+def scores_call(kernel, units, inputs, out, scratch, name):
     return pl.pallas_call(
         kernel,
         out_shape=jax.tree.map(lambda dims: jax.ShapeDtypeStruct(dims, jnp.float32), out, is_leaf=is_dims),
-        in_specs=[SMEM]
-        + [VMEM] * (len(inputs) - 1 - loose)
-        + [pl.BlockSpec(memory_space=pl.ANY)] * loose,
+        in_specs=[SMEM] + [VMEM] * (len(inputs) - 1),
         out_specs=jax.tree.map(lambda _: VMEM, out, is_leaf=is_dims),
         scratch_shapes=scratch,
         compiler_params=PARAMS,
@@ -467,10 +463,9 @@
 
     wide = (16, SIZES[0])
 
-    def score(kernel, units, blocks, state, name):
-        return scores_call(
-            kernel, units, (spots, member_ranks, *blocks, *state), [wide, wide], [], name
-        )
+    def score(kernel, units, blocks, state, name, out=(wide, wide), scratch=()):
+        inputs = (spots, member_ranks, *blocks, *state)
+        return scores_call(kernel, units, inputs, list(out), list(scratch), name)
 
     u1, v1, e1, w1, *state, o2 = share(
         o1, lambda e: (*score(own_kernel, 8, (o1, e), (), "own"), o2)
@@ -481,24 +476,18 @@
         return score(second_kernel, 14, (o1, o2, u1, v1, e1, e2), first, "second")
 
     u2, v2, e2, w2, *known = share(o2, before_arrival)
-    best, inverses = score(third_kernel, 2, (o2, u2, v2, e2), known, "third")
-    own, *others = scores_call(
-        fourth_kernel, 5, (spots, member_ranks, best, inverses, u1, u2, v1, v2, w1, w2),
-        [(Y, CAP)] * 5,
-        [
-            pltpu.VMEM(wide, jnp.float32),
-            pltpu.VMEM(wide, jnp.float32),
-            pltpu.VMEM((GROUPS * PARTS[0], WIDTH), jnp.bfloat16),
-            pltpu.VMEM((GROUPS * PARTS[1], WIDTH), jnp.bfloat16),
-            pltpu.VMEM((GROUPS * PARTS[0], WIDTH), jnp.bfloat16),
-            pltpu.VMEM((GROUPS * PARTS[1], WIDTH), jnp.bfloat16),
-            pltpu.SemaphoreType.DMA((4,)),
-        ],
-        "fourth", 6,
-    )
     across = routes(lambda y, x, c, z: (y, x + 1 - 2 * c, 1 - c, z))
-    for part, way in zip(others, (behind, ahead, swap, across)):
+    *known, e_best = score(
+        third_kernel, 2, (o2, u2, v2, e2), known, "third", (wide, wide, (Y, CAP))
+    )
+    from_core = lax.ppermute(e_best, ALL, swap)
+    own, *others = score(
+        fourth_kernel, 5, (u1, u2, v1, v2, w1, w2), known, "fourth", [(Y, CAP)] * 4,
+        [pltpu.VMEM(wide, jnp.float32)] * 2,
+    )
+    for part, way in zip(others, (behind, ahead, across)):
         own = jnp.maximum(own, lax.ppermute(part, ALL, way))
+    own = jnp.maximum(own, from_core)
     table = lax.all_to_all(
         jnp.broadcast_to(own[:, None], (Y, Z, CAP)).reshape(GROUPS, CAP),
         ("y", "z"), split_axis=0, concat_axis=0, tiled=True,

time: 116 us -> 115 us (level)
    ppermute x4 -> x3, starting transfers between devices: 4.17 us -> 4.37 us  [shards(): own = jnp.maximum(own, lax.ppermute(part, ALL, way))]
    ppermute x4 -> x3, waiting for transfers between devices: 2.82 us -> 2.82 us  [shards(): own = jnp.maximum(own, lax.ppermute(part, ALL, way))]
  transfers between devices with their start and end apart: 21 -> 21, of which waited for: 7 -> 7; matrix products, arithmetic and copies ran while one was open for 1% -> 1% of each run, Pallas kernels for 16% -> 18%
where the time goes in v8:
time: 115 us; the launch traced here: 114 us
  starting transfers between devices  46.7 us (41%)
  Pallas kernels  26.8 us (23%)
  waiting for transfers between devices  23.9 us (21%)
  blocking collectives  14.9 us (13%)
  local copies, waits for them, and re-layouts  1.48 us (1%)
    all_to_all x2, waiting for transfers between devices, bring(): lax.all_to_all(rows.reshape(GROUPS, part, WIDTH), ('y', 'z'), split_axis=...  17.8 us
    all_to_all x2, starting transfers between devices, bring(): lax.all_to_all(rows.reshape(GROUPS, part, WIDTH), ('y', 'z'), split_axis=...  17.1 us
    pallas_call x5, Pallas kernels, scores_call(): pl.pallas_call(kernel, out_shape=jax.tree.map(lambda dims: jax.ShapeDtype...  15.2 us
    all_to_all x1, blocking collectives, shards(): lax.all_to_all(jnp.broadcast_to(own[:, None], (Y, Z, CAP)).reshape(GROUPS...  14.9 us
    pallas_call x1, Pallas kernels, place(): pl.pallas_call(place_kernel, out_shape=(jax.ShapeDtypeStruct((GROUPS * PA...  5.4 us
    ppermute x2, starting transfers between devices, share(): e = lax.ppermute(own, ALL, swap)  5.27 us
    ppermute x3, starting transfers between devices, shards(): row = lax.ppermute(row, ALL, routes(lambda y, x, c, z: (y + j, x, c, z)))  4.81 us
    ppermute x3, starting transfers between devices, shards(): own = jnp.maximum(own, lax.ppermute(part, ALL, way))  4.37 us
  transfers between devices with their start and end apart: 21, of which 7 were waited for; matrix products, arithmetic and copies ran while one was open for 1% of the time, Pallas kernels for 18%

profile of v8, /device:TPU:1, one launch (start us, length us, event | category | flops | bytes accessed | tf_op | source)
XLA Modules:
  0.0 114.2 jit_solution(9869393265255821874)
XLA Ops:
  0.0 5.4 %place.1 = (bf16[4096,128]{1,0:T(8,128)(2,1)}, s32[24,128]{1,0:T(8,128)}) custom-call(s32[24,128]{1,0:T(8,128)} %bitcast.30, bf16[3072,128]{1,0:T(8,128)(2,1)} %rows_ref.1), custom_call_target="tpu_custom_call" | custom-call | tf_op jit(solution)/shard_map/place/pallas_call | solution.py:85
  5.4 12.3 %all-to-all-start = ((bf16[32,128,128]{2,1,0:T(8,128)(2,1)}), bf16[32,128,128]{2,1,0:T(8,128)(2,1)}, u32[]{:S(2)}, u32[]{:S(2)}) async-start(bf16[32,128,128]{2,1,0:T(8,128)(2,1)} %bitcast.37), calls=%async_computation | async-start | bytes 2097152 | tf_op jit(solution)/shard_map/all_to_all | solution.py:417
  19.4 1.2 %collective-permute-start = (f32[1,192]{1,0:T(1,128)S(1)}, f32[1,192]{1,0:T(1,128)S(1)}, u32[]{:S(2)}, u32[]{:S(2)}) collective-permute-start(f32[1,192]{1,0:T(1,128)S(1)} %get-tuple-element.60), channel_id=1, source_target_pairs={{0,64},{1,65},{2,66},{3,67},{4,68},{5,69},{6,70},{7,71},{8,72},{9,... | collective-permute-start | bytes 2312 | tf_op jit(solution)/shard_map/ppermute | solution.py:432
  20.7 2.4 %collective-permute-start.1 = (f32[1,192]{1,0:T(1,128)S(1)}, f32[1,192]{1,0:T(1,128)S(1)}, u32[]{:S(2)}, u32[]{:S(2)}) collective-permute-start(f32[1,192]{1,0:T(1,128)S(1)} %get-tuple-element.59), channel_id=1, source_target_pairs={{0,128},{1,129},{2,130},{3,131},{4,132},{5,133},{6,134},{7,135},{8... | collective-permute-start | bytes 2312 | tf_op jit(solution)/shard_map/ppermute | solution.py:432
  26.5 2.6 %collective-permute-start.3 = (f32[2,512]{1,0:T(2,128)S(1)}, f32[2,512]{1,0:T(2,128)S(1)}, u32[]{:S(2)}, u32[]{:S(2)}) collective-permute-start(f32[2,512]{1,0:T(2,128)S(1)} %pad_maximum_fusion.1), channel_id=1, source_target_pairs={{0,16},{1,17},{2,18},{3,19},{4,20},{5,21},{6,22},{7,23},{8,56},{9,... | collective-permute-start | bytes 12296 | tf_op jit(solution)/shard_map/ppermute | solution.py:442
  29.1 3.4 %collective-permute-start.5 = (f32[2,512]{1,0:T(2,128)S(1)}, f32[2,512]{1,0:T(2,128)S(1)}, u32[]{:S(2)}, u32[]{:S(2)}) collective-permute-start(f32[2,512]{1,0:T(2,128)S(1)} %pad_maximum_fusion.1), channel_id=1, source_target_pairs={{0,8},{1,9},{2,10},{3,11},{4,12},{5,13},{6,14},{7,15},{8,0},{9,1},... | collective-permute-start | bytes 12296 | tf_op jit(solution)/shard_map/ppermute | solution.py:448
  32.5 1.6 %collective-permute-start.6 = (f32[2,512]{1,0:T(2,128)S(1)}, f32[2,512]{1,0:T(2,128)S(1)}, u32[]{:S(2)}, u32[]{:S(2)}) collective-permute-start(f32[2,512]{1,0:T(2,128)S(1)} %collective-permute-done.3), channel_id=1, source_target_pairs={{0,8},{1,9},{2,10},{3,11},{4,12},{5,13},{6,14},{7,15},{8,0},{9,1},... | collective-permute-start | bytes 12296 | tf_op jit(solution)/shard_map/ppermute | solution.py:449
  34.2 4.2 %place_rest.1 = bf16[2048,128]{1,0:T(8,128)(2,1)} custom-call(s32[24,128]{1,0:T(8,128)S(1)} %bitcast.32, s32[24,128]{1,0:T(8,128)S(1)} %copy-done.2, bf16[3072,128]{1,0:T(8,128)(2,1)S(1)} %copy-done), custom_call_target="tpu_custom_call" | custom-call | tf_op jit(solution)/shard_map/place_rest/pallas_call | solution.py:126
  38.5 3.8 %all-to-all-done = bf16[32,128,128]{2,1,0:T(8,128)(2,1)} async-done(((bf16[32,128,128]{2,1,0:T(8,128)(2,1)}), bf16[32,128,128]{2,1,0:T(8,128)(2,1)}, u32[]{:S(2)}, u32[]{:S(2)}) %all-to-all-start) | async-done | bytes 1048608 | tf_op jit(solution)/shard_map/all_to_all | solution.py:417
  42.3 5.0 %collective-permute-start.8 = (bf16[4096,128]{1,0:T(8,128)(2,1)}, bf16[4096,128]{1,0:T(8,128)(2,1)}, u32[]{:S(2)}, u32[]{:S(2)}) collective-permute-start(bf16[4096,128]{1,0:T(8,128)(2,1)} %bitcast.2.o1), channel_id=1, source_target_pairs={{0,8},{1,9},{2,10},{3,11},{4,12},{5,13},{6,14},{7,15},{8,0},{9,1},... | collective-permute-start | bytes 3145736 | tf_op jit(solution)/shard_map/ppermute | solution.py:460
  47.3 2.5 %collective-permute-start.7 = (bf16[4096,128]{1,0:T(8,128)(2,1)}, bf16[4096,128]{1,0:T(8,128)(2,1)S(1)}, u32[]{:S(2)}, u32[]{:S(2)}) collective-permute-start(bf16[4096,128]{1,0:T(8,128)(2,1)} %bitcast.2.o1), channel_id=1, source_target_pairs={{0,16},{1,17},{2,18},{3,19},{4,20},{5,21},{6,22},{7,23},{8,56},{9,... | collective-permute-start | bytes 3145736 | tf_op jit(solution)/shard_map/ppermute | solution.py:458
  49.8 4.8 %all-to-all-start.1 = ((bf16[32,64,128]{2,1,0:T(8,128)(2,1)}), bf16[32,64,128]{2,1,0:T(8,128)(2,1)S(1)}, u32[]{:S(2)}, u32[]{:S(2)}) async-start(bf16[32,64,128]{2,1,0:T(8,128)(2,1)} %bitcast.14), calls=%async_computation.1 | async-start | bytes 1048576 | tf_op jit(solution)/shard_map/all_to_all | solution.py:417
  54.7 2.5 %own.1 = (f32[16,512]{1,0:T(8,128)S(1)}, f32[16,512]{1,0:T(8,128)S(1)}) custom-call(s32[2]{0:T(128)S(1)} %pad_add_fusion.spots, f32[16,512]{1,0:T(8,128)S(1)} %concatenate.8.ranks, bf16[4096,128]{1,0:T(8,128)(2,1)} %bitcast.2.o1, bf16[4096,128]{1,0:T(8,128)(2,1)} %collective-permute-done.8.e1), custom_call_target="tpu_custom_call" | custom-call | flops 1073741824 | bytes 4194304 | tf_op jit(solution)/shard_map/own/pallas_call | solution.py:363
  57.2 13.9 %all-to-all-done.1 = bf16[32,64,128]{2,1,0:T(8,128)(2,1)S(1)} async-done(((bf16[32,64,128]{2,1,0:T(8,128)(2,1)}), bf16[32,64,128]{2,1,0:T(8,128)(2,1)S(1)}, u32[]{:S(2)}, u32[]{:S(2)}) %all-to-all-start.1) | async-done | bytes 524320 | tf_op jit(solution)/shard_map/all_to_all | solution.py:417
  71.7 1.2 %collective-permute-start.9 = (bf16[2048,128]{1,0:T(8,128)(2,1)S(1)}, bf16[2048,128]{1,0:T(8,128)(2,1)S(1)}, u32[]{:S(2)}, u32[]{:S(2)}) collective-permute-start(bf16[2048,128]{1,0:T(8,128)(2,1)S(1)} %bitcast.26), channel_id=1, source_target_pairs={{0,16},{1,17},{2,18},{3,19},{4,20},{5,21},{6,22},{7,23},{8,56},{9,... | collective-permute-start | bytes 1572872 | tf_op jit(solution)/shard_map/ppermute | solution.py:458
  74.1 4.9 %first.1 = (f32[16,512]{1,0:T(8,128)S(1)}, f32[16,512]{1,0:T(8,128)S(1)}) custom-call(s32[2]{0:T(128)S(1)} %pad_add_fusion.spots, f32[16,512]{1,0:T(8,128)S(1)} %concatenate.8.ranks, bf16[4096,128]{1,0:T(8,128)(2,1)} %bitcast.2.o1, bf16[4096,128]{1,0:T(8,128)(2,1)S(1)} %collective-permute-done.7.u1, bf16[4096,128]{1,0:T(8,128)(2,1)S(1)} %collective-permute-done.10.v1, ...), custom_call_target="tpu_custom_call" | custom-call | flops 1610612736 | bytes 4194304 | tf_op jit(solution)/shard_map/first/pallas_call | solution.py:363
  79.0 4.3 %second.1 = (f32[16,512]{1,0:T(8,128)S(1)}, f32[16,512]{1,0:T(8,128)S(1)}) custom-call(s32[2]{0:T(128)S(1)} %pad_add_fusion.spots, f32[16,512]{1,0:T(8,128)S(1)} %concatenate.8.ranks, bf16[4096,128]{1,0:T(8,128)(2,1)} %bitcast.2.o1, bf16[2048,128]{1,0:T(8,128)(2,1)S(1)} %bitcast.28, bf16[4096,128]{1,0:T(8,128)(2,1)S(1)} %collective-permute-done.7.u1, ...), custom_call_target="tpu_custom_call" | custom-call | flops 1879048192 | bytes 4194304 | tf_op jit(solution)/shard_map/second/pallas_call | solution.py:363
  84.2 3.3 %collective-permute-start.14 = (bf16[2048,128]{1,0:T(8,128)(2,1)S(1)}, bf16[2048,128]{1,0:T(8,128)(2,1)S(1)}, u32[]{:S(2)}, u32[]{:S(2)}) collective-permute-start(bf16[2048,128]{1,0:T(8,128)(2,1)S(1)} %collective-permute-done.9.u2), channel_id=1, source_target_pairs={{0,8},{1,9},{2,10},{3,11},{4,12},{5,13},{6,14},{7,15},{8,0},{9,1},... | collective-permute-start | bytes 1572872 | tf_op jit(solution)/shard_map/ppermute | solution.py:462
  87.4 1.6 %third.1 = (f32[16,512]{1,0:T(8,128)S(1)}, f32[16,512]{1,0:T(8,128)S(1)}, f32[4,192]{1,0:T(4,128)S(1)}) custom-call(s32[2]{0:T(128)S(1)} %pad_add_fusion.spots, f32[16,512]{1,0:T(8,128)S(1)} %concatenate.8.ranks, bf16[2048,128]{1,0:T(8,128)(2,1)S(1)} %bitcast.29, bf16[2048,128]{1,0:T(8,128)(2,1)S(1)} %collective-permute-done.9.u2, ...), custom_call_target="tpu_custom_call" | custom-call | flops 268435456 | bytes 4194304 | tf_op jit(solution)/shard_map/third/pallas_call | solution.py:363
  89.1 1.8 %fourth.1 = (f32[4,192]{1,0:T(4,128)S(1)}, f32[4,192]{1,0:T(4,128)S(1)}, f32[4,192]{1,0:T(4,128)S(1)}, f32[4,192]{1,0:T(4,128)S(1)}) custom-call(s32[2]{0:T(128)S(1)} %pad_add_fusion.spots, f32[16,512]{1,0:T(8,128)S(1)} %concatenate.8.ranks, bf16[4096,128]{1,0:T(8,128)(2,1)S(1)} %collective-permute-done.7.u1, ...), custom_call_target="tpu_custom_call" | custom-call | flops 671088640 | bytes 4194304 | tf_op jit(solution)/shard_map/fourth/pallas_call | solution.py:363
  91.2 2.7 %collective-permute-start.16 = (f32[4,192]{1,0:T(4,128)S(1)}, f32[4,192]{1,0:T(4,128)S(1)}, u32[]{:S(2)}, u32[]{:S(2)}) collective-permute-start(f32[4,192]{1,0:T(4,128)S(1)} %get-tuple-element.54), channel_id=1, source_target_pairs={{0,16},{1,17},{2,18},{3,19},{4,20},{5,21},{6,22},{7,23},{8,56},{9,... | collective-permute-start | bytes 9224 | tf_op jit(solution)/shard_map/ppermute | solution.py:489
  93.9 1.4 %collective-permute-start.17 = (f32[4,192]{1,0:T(4,128)S(1)}, f32[4,192]{1,0:T(4,128)S(1)}, u32[]{:S(2)}, u32[]{:S(2)}) collective-permute-start(f32[4,192]{1,0:T(4,128)S(1)} %get-tuple-element.55), channel_id=1, source_target_pairs={{0,24},{1,25},{2,26},{3,27},{4,28},{5,29},{6,30},{7,31},{8,48},{9,... | collective-permute-start | bytes 9224 | tf_op jit(solution)/shard_map/ppermute | solution.py:489
  95.3 2.8 %collective-permute-done.17 = f32[4,192]{1,0:T(4,128)S(1)} collective-permute-done((f32[4,192]{1,0:T(4,128)S(1)}, f32[4,192]{1,0:T(4,128)S(1)}, u32[]{:S(2)}, u32[]{:S(2)}) %collective-permute-start.17) | collective-permute-done | bytes 3104 | tf_op jit(solution)/shard_map/ppermute | solution.py:489
  98.2 14.9 %all_to_all.21 = f32[32,1,192]{2,1,0:T(1,128)S(1)} all-to-all(f32[32,1,192]{2,1,0:T(1,128)S(1)} %all_to_all.15), channel_id=1, replica_groups=mesh['y'=4,'x'=4,'core'=2,'z'=8] {'y','z'}, dimensions={0} | all-to-all | bytes 49152 | tf_op jit(solution)/shard_map/all_to_all | solution.py:491
  (54 shorter events, 9.3 us)
Async XLA Ops:
  5.4 28.8 %copy-start = (bf16[3072,128]{1,0:T(8,128)(2,1)S(1)}, bf16[3072,128]{1,0:T(8,128)(2,1)}, u32[]{:S(2)}) copy-start(bf16[3072,128]{1,0:T(8,128)(2,1)} %rows_ref.1) | copy-start | bytes 2359300
  5.4 36.9 %all-to-all-start = ((bf16[32,128,128]{2,1,0:T(8,128)(2,1)}), bf16[32,128,128]{2,1,0:T(8,128)(2,1)}, u32[]{:S(2)}, u32[]{:S(2)}) async-start(bf16[32,128,128]{2,1,0:T(8,128)(2,1)} %bitcast.37), calls=%async_computation | async-start | bytes 2097152 | tf_op jit(solution)/shard_map/all_to_all | solution.py:417
  17.8 0.7 copy-start.2
  17.8 0.7 copy-start.1
  19.4 4.8 %collective-permute-start = (f32[1,192]{1,0:T(1,128)S(1)}, f32[1,192]{1,0:T(1,128)S(1)}, u32[]{:S(2)}, u32[]{:S(2)}) collective-permute-start(f32[1,192]{1,0:T(1,128)S(1)} %get-tuple-element.60), channel_id=1, source_target_pairs={{0,64},{1,65},{2,66},{3,67},{4,68},{5,69},{6,70},{7,71},{8,72},{9,... | collective-permute-start | bytes 2312 | tf_op jit(solution)/shard_map/ppermute | solution.py:432
  20.7 4.0 %collective-permute-start.1 = (f32[1,192]{1,0:T(1,128)S(1)}, f32[1,192]{1,0:T(1,128)S(1)}, u32[]{:S(2)}, u32[]{:S(2)}) collective-permute-start(f32[1,192]{1,0:T(1,128)S(1)} %get-tuple-element.59), channel_id=1, source_target_pairs={{0,128},{1,129},{2,130},{3,131},{4,132},{5,133},{6,134},{7,135},{8... | collective-permute-start | bytes 2312 | tf_op jit(solution)/shard_map/ppermute | solution.py:432
  23.1 2.7 %collective-permute-start.2 = (f32[1,192]{1,0:T(1,128)S(1)}, f32[1,192]{1,0:T(1,128)S(1)}, u32[]{:S(2)}, u32[]{:S(2)}) collective-permute-start(f32[1,192]{1,0:T(1,128)S(1)} %get-tuple-element.58), channel_id=1, source_target_pairs={{0,192},{1,193},{2,194},{3,195},{4,196},{5,197},{6,198},{7,199},{8... | collective-permute-start | bytes 2312 | tf_op jit(solution)/shard_map/ppermute | solution.py:432
  26.5 6.0 %collective-permute-start.3 = (f32[2,512]{1,0:T(2,128)S(1)}, f32[2,512]{1,0:T(2,128)S(1)}, u32[]{:S(2)}, u32[]{:S(2)}) collective-permute-start(f32[2,512]{1,0:T(2,128)S(1)} %pad_maximum_fusion.1), channel_id=1, source_target_pairs={{0,16},{1,17},{2,18},{3,19},{4,20},{5,21},{6,22},{7,23},{8,56},{9,... | collective-permute-start | bytes 12296 | tf_op jit(solution)/shard_map/ppermute | solution.py:442
  29.1 9.3 %collective-permute-start.4 = (f32[2,512]{1,0:T(2,128)S(1)}, f32[2,512]{1,0:T(2,128)S(1)}, u32[]{:S(2)}, u32[]{:S(2)}) collective-permute-start(f32[2,512]{1,0:T(2,128)S(1)} %pad_maximum_fusion.1), channel_id=1, source_target_pairs={{0,48},{1,49},{2,50},{3,51},{4,52},{5,53},{6,54},{7,55},{8,24},{9,... | collective-permute-start | bytes 12296 | tf_op jit(solution)/shard_map/ppermute | solution.py:447
  29.1 9.3 %collective-permute-start.5 = (f32[2,512]{1,0:T(2,128)S(1)}, f32[2,512]{1,0:T(2,128)S(1)}, u32[]{:S(2)}, u32[]{:S(2)}) collective-permute-start(f32[2,512]{1,0:T(2,128)S(1)} %pad_maximum_fusion.1), channel_id=1, source_target_pairs={{0,8},{1,9},{2,10},{3,11},{4,12},{5,13},{6,14},{7,15},{8,0},{9,1},... | collective-permute-start | bytes 12296 | tf_op jit(solution)/shard_map/ppermute | solution.py:448
  32.5 5.9 %collective-permute-start.6 = (f32[2,512]{1,0:T(2,128)S(1)}, f32[2,512]{1,0:T(2,128)S(1)}, u32[]{:S(2)}, u32[]{:S(2)}) collective-permute-start(f32[2,512]{1,0:T(2,128)S(1)} %collective-permute-done.3), channel_id=1, source_target_pairs={{0,8},{1,9},{2,10},{3,11},{4,12},{5,13},{6,14},{7,15},{8,0},{9,1},... | collective-permute-start | bytes 12296 | tf_op jit(solution)/shard_map/ppermute | solution.py:449
  42.3 12.3 %collective-permute-start.8 = (bf16[4096,128]{1,0:T(8,128)(2,1)}, bf16[4096,128]{1,0:T(8,128)(2,1)}, u32[]{:S(2)}, u32[]{:S(2)}) collective-permute-start(bf16[4096,128]{1,0:T(8,128)(2,1)} %bitcast.2.o1), channel_id=1, source_target_pairs={{0,8},{1,9},{2,10},{3,11},{4,12},{5,13},{6,14},{7,15},{8,0},{9,1},... | collective-permute-start | bytes 3145736 | tf_op jit(solution)/shard_map/ppermute | solution.py:460
  47.3 23.9 %collective-permute-start.7 = (bf16[4096,128]{1,0:T(8,128)(2,1)}, bf16[4096,128]{1,0:T(8,128)(2,1)S(1)}, u32[]{:S(2)}, u32[]{:S(2)}) collective-permute-start(bf16[4096,128]{1,0:T(8,128)(2,1)} %bitcast.2.o1), channel_id=1, source_target_pairs={{0,16},{1,17},{2,18},{3,19},{4,20},{5,21},{6,22},{7,23},{8,56},{9,... | collective-permute-start | bytes 3145736 | tf_op jit(solution)/shard_map/ppermute | solution.py:458
  49.8 21.4 %all-to-all-start.1 = ((bf16[32,64,128]{2,1,0:T(8,128)(2,1)}), bf16[32,64,128]{2,1,0:T(8,128)(2,1)S(1)}, u32[]{:S(2)}, u32[]{:S(2)}) async-start(bf16[32,64,128]{2,1,0:T(8,128)(2,1)} %bitcast.14), calls=%async_computation.1 | async-start | bytes 1048576 | tf_op jit(solution)/shard_map/all_to_all | solution.py:417
  54.6 19.5 %collective-permute-start.10 = (bf16[4096,128]{1,0:T(8,128)(2,1)}, bf16[4096,128]{1,0:T(8,128)(2,1)S(1)}, u32[]{:S(2)}, u32[]{:S(2)}) collective-permute-start(bf16[4096,128]{1,0:T(8,128)(2,1)} %bitcast.2.o1), channel_id=1, source_target_pairs={{0,48},{1,49},{2,50},{3,51},{4,52},{5,53},{6,54},{7,55},{8,24},{9,... | collective-permute-start | bytes 3145736 | tf_op jit(solution)/shard_map/ppermute | solution.py:459
  71.2 2.9 %collective-permute-start.12 = (bf16[4096,128]{1,0:T(8,128)(2,1)S(1)}, bf16[4096,128]{1,0:T(8,128)(2,1)S(1)}, u32[]{:S(2)}, u32[]{:S(2)}) collective-permute-start(bf16[4096,128]{1,0:T(8,128)(2,1)S(1)} %collective-permute-done.7.u1), channel_id=1, source_target_pairs={{0,8},{1,9},{2,10},{3,11},{4,12},{5,13},{6,14},{7,15},{8,0},{9,1},... | collective-permute-start | bytes 3145736 | tf_op jit(solution)/shard_map/ppermute | solution.py:462
  71.4 7.6 %collective-permute-start.11 = (bf16[2048,128]{1,0:T(8,128)(2,1)S(1)}, bf16[2048,128]{1,0:T(8,128)(2,1)S(1)}, u32[]{:S(2)}, u32[]{:S(2)}) collective-permute-start(bf16[2048,128]{1,0:T(8,128)(2,1)S(1)} %bitcast.25), channel_id=1, source_target_pairs={{0,8},{1,9},{2,10},{3,11},{4,12},{5,13},{6,14},{7,15},{8,0},{9,1},... | collective-permute-start | bytes 1572872 | tf_op jit(solution)/shard_map/ppermute | solution.py:460
  71.7 12.5 %collective-permute-start.9 = (bf16[2048,128]{1,0:T(8,128)(2,1)S(1)}, bf16[2048,128]{1,0:T(8,128)(2,1)S(1)}, u32[]{:S(2)}, u32[]{:S(2)}) collective-permute-start(bf16[2048,128]{1,0:T(8,128)(2,1)S(1)} %bitcast.26), channel_id=1, source_target_pairs={{0,16},{1,17},{2,18},{3,19},{4,20},{5,21},{6,22},{7,23},{8,56},{9,... | collective-permute-start | bytes 1572872 | tf_op jit(solution)/shard_map/ppermute | solution.py:458
  72.9 14.6 %collective-permute-start.13 = (bf16[2048,128]{1,0:T(8,128)(2,1)S(1)}, bf16[2048,128]{1,0:T(8,128)(2,1)S(1)}, u32[]{:S(2)}, u32[]{:S(2)}) collective-permute-start(bf16[2048,128]{1,0:T(8,128)(2,1)S(1)} %bitcast.27), channel_id=1, source_target_pairs={{0,48},{1,49},{2,50},{3,51},{4,52},{5,53},{6,54},{7,55},{8,24},{9,... | collective-permute-start | bytes 1572872 | tf_op jit(solution)/shard_map/ppermute | solution.py:459
  84.2 4.9 %collective-permute-start.14 = (bf16[2048,128]{1,0:T(8,128)(2,1)S(1)}, bf16[2048,128]{1,0:T(8,128)(2,1)S(1)}, u32[]{:S(2)}, u32[]{:S(2)}) collective-permute-start(bf16[2048,128]{1,0:T(8,128)(2,1)S(1)} %collective-permute-done.9.u2), channel_id=1, source_target_pairs={{0,8},{1,9},{2,10},{3,11},{4,12},{5,13},{6,14},{7,15},{8,0},{9,1},... | collective-permute-start | bytes 1572872 | tf_op jit(solution)/shard_map/ppermute | solution.py:462
  89.0 6.3 %collective-permute-start.18 = (f32[4,192]{1,0:T(4,128)S(1)}, f32[4,192]{1,0:T(4,128)S(1)}, u32[]{:S(2)}, u32[]{:S(2)}) collective-permute-start(f32[4,192]{1,0:T(4,128)S(1)} %get-tuple-element.56), channel_id=1, source_target_pairs={{0,8},{1,9},{2,10},{3,11},{4,12},{5,13},{6,14},{7,15},{8,0},{9,1},... | collective-permute-start | bytes 9224 | tf_op jit(solution)/shard_map/ppermute | solution.py:483
  90.9 4.4 %collective-permute-start.15 = (f32[4,192]{1,0:T(4,128)S(1)}, f32[4,192]{1,0:T(4,128)S(1)}, u32[]{:S(2)}, u32[]{:S(2)}) collective-permute-start(f32[4,192]{1,0:T(4,128)S(1)} %get-tuple-element.53), channel_id=1, source_target_pairs={{0,48},{1,49},{2,50},{3,51},{4,52},{5,53},{6,54},{7,55},{8,24},{9,... | collective-permute-start | bytes 9224 | tf_op jit(solution)/shard_map/ppermute | solution.py:489
  91.2 4.1 %collective-permute-start.16 = (f32[4,192]{1,0:T(4,128)S(1)}, f32[4,192]{1,0:T(4,128)S(1)}, u32[]{:S(2)}, u32[]{:S(2)}) collective-permute-start(f32[4,192]{1,0:T(4,128)S(1)} %get-tuple-element.54), channel_id=1, source_target_pairs={{0,16},{1,17},{2,18},{3,19},{4,20},{5,21},{6,22},{7,23},{8,56},{9,... | collective-permute-start | bytes 9224 | tf_op jit(solution)/shard_map/ppermute | solution.py:489
  93.9 4.2 %collective-permute-start.17 = (f32[4,192]{1,0:T(4,128)S(1)}, f32[4,192]{1,0:T(4,128)S(1)}, u32[]{:S(2)}, u32[]{:S(2)}) collective-permute-start(f32[4,192]{1,0:T(4,128)S(1)} %get-tuple-element.55), channel_id=1, source_target_pairs={{0,24},{1,25},{2,26},{3,27},{4,28},{5,29},{6,30},{7,31},{8,48},{9,... | collective-permute-start | bytes 9224 | tf_op jit(solution)/shard_map/ppermute | solution.py:489
  (1 other events, 0.7 us)

commit v9 on v8

--- a/solution.py
+++ b/solution.py
@@ -313,45 +313,50 @@
         out[at, pl.ds(PARTS[0], PARTS[1])] = pair[:, : PARTS[1]]
 
 
-def third_kernel(spots, ranks, o2, u2, v2, e2, before, known, best, inverses, e_best):
+def third_kernel(spots, ranks, o2, u2, e2, v1, w1, before, known, best, inverses):
     best[...] = before[...]
     inverses[...] = known[...]
     note(inverses, U2, u2)
-    note(inverses, V2, v2)
-    meet(best, inverses, ranks, O2, o2, [(U2, u2)])
-
-    @pl.when(spots[0] == 0)
-    def _():
-        meet(best, inverses, ranks, E2, e2, [(V2, v2)])
+    meet(best, inverses, ranks, U2, u2, [(O2, o2)])
 
     @pl.when(spots[0] != 0)
     def _():
-        meet(best, inverses, ranks, E2, e2, [(U2, u2)])
-
-    give(best, E1, e_best)
+        meet(best, inverses, ranks, U2, u2, [(E2, e2)])
+
+    @pl.when(spots[1] != 0)
+    def _():
+        meet(best, inverses, ranks, U2, u2, [(V1, v1)])
+
+    @pl.when(spots[1] == 0)
+    def _():
+        meet(best, inverses, ranks, U2, u2, [(W1, w1)])
 
 
 def fourth_kernel(
-    spots, ranks, u1, u2, v1, v2, w1, w2, before, known, o_best, u_best, v_best, w_best,
+    spots, ranks, u1, u2, v2, e2, w2, before, known, o_best, u_best, v_best, e_best, w_best,
     best, inverses,
 ):
     best[...] = before[...]
     inverses[...] = known[...]
+    note(inverses, V2, v2)
+
+    @pl.when(spots[0] == 0)
+    def _():
+        meet(best, inverses, ranks, V2, v2, [(E2, e2)])
 
     @pl.when(spots[1] != 0)
     def _():
-        meet(best, inverses, ranks, V2, v2, [(U1, u1)])
-        meet(best, inverses, ranks, U2, u2, [(V1, v1), (V2, v2)])
+        meet(best, inverses, ranks, V2, v2, [(U1, u1), (U2, u2)])
 
     @pl.when(spots[1] == 0)
     def _():
         note(inverses, W2, w2)
-        meet(best, inverses, ranks, W2, w2, [(U1, u1)])
-        meet(best, inverses, ranks, U2, u2, [(W1, w1), (W2, w2)])
+        meet(best, inverses, ranks, W2, w2, [(U1, u1), (U2, u2)])
 
     give(best, O1, o_best)
     give(best, U1, u_best)
     give(best, V1, v_best)
+    give(best, E1, e_best)
     give(best, W1, w_best)
 
 
@@ -454,40 +459,37 @@
     o1, placed2, member_ranks, spots = lax.optimization_barrier((o1, placed2, member_ranks, spots))
     o2 = bring(placed2)
 
-    def share(own, after):
-        u = lax.ppermute(own, ALL, ahead)
-        v = lax.ppermute(own, ALL, behind)
-        e = lax.ppermute(own, ALL, swap)
-        u, *after = lax.optimization_barrier((u, *after(e)))
-        return (u, v, e, lax.ppermute(u, ALL, swap), *after)
-
     wide = (16, SIZES[0])
 
     def score(kernel, units, blocks, state, name, out=(wide, wide), scratch=()):
         inputs = (spots, member_ranks, *blocks, *state)
         return scores_call(kernel, units, inputs, list(out), list(scratch), name)
 
-    u1, v1, e1, w1, *state, o2 = share(
-        o1, lambda e: (*score(own_kernel, 8, (o1, e), (), "own"), o2)
-    )
-
-    def before_arrival(e2):
-        first = score(first_kernel, 12, (o1, u1, v1, e1, w1), state, "first")
-        return score(second_kernel, 14, (o1, o2, u1, v1, e1, e2), first, "second")
-
-    u2, v2, e2, w2, *known = share(o2, before_arrival)
-    across = routes(lambda y, x, c, z: (y, x + 1 - 2 * c, 1 - c, z))
-    *known, e_best = score(
-        third_kernel, 2, (o2, u2, v2, e2), known, "third", (wide, wide, (Y, CAP))
-    )
-    from_core = lax.ppermute(e_best, ALL, swap)
+    u1 = lax.ppermute(o1, ALL, ahead)
+    v1 = lax.ppermute(o1, ALL, behind)
+    e1 = lax.ppermute(o1, ALL, swap)
+    state = score(own_kernel, 8, (o1, e1), (), "own")
+    u1, o2, *state = lax.optimization_barrier((u1, o2, *state))
+    w1 = lax.ppermute(u1, ALL, swap)
+
+    u2 = lax.ppermute(o2, ALL, ahead)
+    e2 = lax.ppermute(o2, ALL, swap)
+    state = score(first_kernel, 12, (o1, u1, v1, e1, w1), state, "first")
+    o2, *state = lax.optimization_barrier((o2, *state))
+    v2 = lax.ppermute(o2, ALL, behind)
+    state = score(second_kernel, 14, (o1, o2, u1, v1, e1, e2), state, "second")
+    u2, *state = lax.optimization_barrier((u2, *state))
+    w2 = lax.ppermute(u2, ALL, swap)
+    state = score(third_kernel, 4, (o2, u2, e2, v1, w1), state, "third")
+    v2, *state = lax.optimization_barrier((v2, *state))
     own, *others = score(
-        fourth_kernel, 5, (u1, u2, v1, v2, w1, w2), known, "fourth", [(Y, CAP)] * 4,
+        fourth_kernel, 4, (u1, u2, v2, e2, w2), state, "fourth", [(Y, CAP)] * 5,
         [pltpu.VMEM(wide, jnp.float32)] * 2,
     )
-    for part, way in zip(others, (behind, ahead, across)):
+
+    across = routes(lambda y, x, c, z: (y, x + 1 - 2 * c, 1 - c, z))
+    for part, way in zip(others, (behind, ahead, swap, across)):
         own = jnp.maximum(own, lax.ppermute(part, ALL, way))
-    own = jnp.maximum(own, from_core)
     table = lax.all_to_all(
         jnp.broadcast_to(own[:, None], (Y, Z, CAP)).reshape(GROUPS, CAP),
         ("y", "z"), split_axis=0, concat_axis=0, tiled=True,

time: 115 us -> 114 us (level)
  waiting for transfers between devices: 23.9 us -> 22.3 us
  starting transfers between devices: 46.7 us -> 48.3 us
  blocking collectives: 14.9 us -> 13.4 us
    ppermute x3 -> x4, starting transfers between devices: 4.37 us -> 7.02 us  [shards(): own = jnp.maximum(own, lax.ppermute(part, ALL, way))]
    all_to_all x1, blocking collectives: 14.9 us -> 13.4 us  [shards(): lax.all_to_all(jnp.broadcast_to(own[:, None], (Y, Z, CAP)).reshape(GROUPS...]
    ppermute x3 -> x4, waiting for transfers between devices: 2.82 us -> 1.57 us  [shards(): own = jnp.maximum(own, lax.ppermute(part, ALL, way))]
    ppermute x9 -> x8, starting transfers between devices: 12.8 us -> 11.9 us  [the longest x1 4.97 us: shards(): e1 = lax.ppermute(o1, ALL, swap)]
  transfers between devices with their start and end apart: 21 -> 21, of which waited for: 7 -> 6; matrix products, arithmetic and copies ran while one was open for 1% -> 1% of each run, Pallas kernels for 18% -> 17%
where the time goes in v9:
time: 114 us
  starting transfers between devices  48.3 us (42%)
  Pallas kernels  27.7 us (24%)
  waiting for transfers between devices  22.3 us (20%)
  blocking collectives  13.4 us (12%)
  local copies, waits for them, and re-layouts  1.48 us (1%)
    all_to_all x2, waiting for transfers between devices, bring(): lax.all_to_all(rows.reshape(GROUPS, part, WIDTH), ('y', 'z'), split_axis=...  18.1 us
    all_to_all x2, starting transfers between devices, bring(): lax.all_to_all(rows.reshape(GROUPS, part, WIDTH), ('y', 'z'), split_axis=...  17 us
    pallas_call x5, Pallas kernels, scores_call(): pl.pallas_call(kernel, out_shape=jax.tree.map(lambda dims: jax.ShapeDtype...  16.1 us
    all_to_all x1, blocking collectives, shards(): lax.all_to_all(jnp.broadcast_to(own[:, None], (Y, Z, CAP)).reshape(GROUPS...  13.4 us
    ppermute x4, starting transfers between devices, shards(): own = jnp.maximum(own, lax.ppermute(part, ALL, way))  7.02 us
    pallas_call x1, Pallas kernels, place(): pl.pallas_call(place_kernel, out_shape=(jax.ShapeDtypeStruct((GROUPS * PA...  5.4 us
    ppermute x1, starting transfers between devices, shards(): e1 = lax.ppermute(o1, ALL, swap)  4.97 us
    ppermute x3, starting transfers between devices, shards(): row = lax.ppermute(row, ALL, routes(lambda y, x, c, z: (y + j, x, c, z)))  4.89 us
  transfers between devices with their start and end apart: 21, of which 6 were waited for; matrix products, arithmetic and copies ran while one was open for 1% of the time, Pallas kernels for 17%

profile of v9, /device:TPU:1, one launch (start us, length us, event | category | flops | bytes accessed | tf_op | source)
XLA Modules:
  0.0 113.6 jit_solution(18167374577356871908)
XLA Ops:
  0.0 5.4 %place.1 = (bf16[4096,128]{1,0:T(8,128)(2,1)}, s32[24,128]{1,0:T(8,128)}) custom-call(s32[24,128]{1,0:T(8,128)} %bitcast.36, bf16[3072,128]{1,0:T(8,128)(2,1)} %rows_ref.1), custom_call_target="tpu_custom_call" | custom-call | tf_op jit(solution)/shard_map/place/pallas_call | solution.py:85
  5.4 12.2 %all-to-all-start = ((bf16[32,128,128]{2,1,0:T(8,128)(2,1)}), bf16[32,128,128]{2,1,0:T(8,128)(2,1)S(1)}, u32[]{:S(2)}, u32[]{:S(2)}) async-start(bf16[32,128,128]{2,1,0:T(8,128)(2,1)} %bitcast.43), calls=%async_computation | async-start | bytes 2097152 | tf_op jit(solution)/shard_map/all_to_all | solution.py:422
  19.3 1.3 %collective-permute-start = (f32[1,192]{1,0:T(1,128)S(1)}, f32[1,192]{1,0:T(1,128)S(1)}, u32[]{:S(2)}, u32[]{:S(2)}) collective-permute-start(f32[1,192]{1,0:T(1,128)S(1)} %get-tuple-element.72), channel_id=1, source_target_pairs={{0,64},{1,65},{2,66},{3,67},{4,68},{5,69},{6,70},{7,71},{8,72},{9,... | collective-permute-start | bytes 2312 | tf_op jit(solution)/shard_map/ppermute | solution.py:437
  20.6 2.4 %collective-permute-start.1 = (f32[1,192]{1,0:T(1,128)S(1)}, f32[1,192]{1,0:T(1,128)S(1)}, u32[]{:S(2)}, u32[]{:S(2)}) collective-permute-start(f32[1,192]{1,0:T(1,128)S(1)} %get-tuple-element.71), channel_id=1, source_target_pairs={{0,128},{1,129},{2,130},{3,131},{4,132},{5,133},{6,134},{7,135},{8... | collective-permute-start | bytes 2312 | tf_op jit(solution)/shard_map/ppermute | solution.py:437
  26.5 2.6 %collective-permute-start.3 = (f32[2,512]{1,0:T(2,128)S(1)}, f32[2,512]{1,0:T(2,128)S(1)}, u32[]{:S(2)}, u32[]{:S(2)}) collective-permute-start(f32[2,512]{1,0:T(2,128)S(1)} %pad_maximum_fusion.1), channel_id=1, source_target_pairs={{0,16},{1,17},{2,18},{3,19},{4,20},{5,21},{6,22},{7,23},{8,56},{9,... | collective-permute-start | bytes 12296 | tf_op jit(solution)/shard_map/ppermute | solution.py:447
  29.0 3.4 %collective-permute-start.5 = (f32[2,512]{1,0:T(2,128)S(1)}, f32[2,512]{1,0:T(2,128)S(1)}, u32[]{:S(2)}, u32[]{:S(2)}) collective-permute-start(f32[2,512]{1,0:T(2,128)S(1)} %pad_maximum_fusion.1), channel_id=1, source_target_pairs={{0,8},{1,9},{2,10},{3,11},{4,12},{5,13},{6,14},{7,15},{8,0},{9,1},... | collective-permute-start | bytes 12296 | tf_op jit(solution)/shard_map/ppermute | solution.py:453
  32.4 1.6 %collective-permute-start.6 = (f32[2,512]{1,0:T(2,128)S(1)}, f32[2,512]{1,0:T(2,128)S(1)}, u32[]{:S(2)}, u32[]{:S(2)}) collective-permute-start(f32[2,512]{1,0:T(2,128)S(1)} %collective-permute-done.3), channel_id=1, source_target_pairs={{0,8},{1,9},{2,10},{3,11},{4,12},{5,13},{6,14},{7,15},{8,0},{9,1},... | collective-permute-start | bytes 12296 | tf_op jit(solution)/shard_map/ppermute | solution.py:454
  34.1 4.2 %place_rest.1 = bf16[2048,128]{1,0:T(8,128)(2,1)} custom-call(s32[24,128]{1,0:T(8,128)S(1)} %bitcast.38, s32[24,128]{1,0:T(8,128)S(1)} %copy-done.2, bf16[3072,128]{1,0:T(8,128)(2,1)S(1)} %copy-done), custom_call_target="tpu_custom_call" | custom-call | tf_op jit(solution)/shard_map/place_rest/pallas_call | solution.py:126
  38.4 3.8 %all-to-all-done = bf16[32,128,128]{2,1,0:T(8,128)(2,1)S(1)} async-done(((bf16[32,128,128]{2,1,0:T(8,128)(2,1)}), bf16[32,128,128]{2,1,0:T(8,128)(2,1)S(1)}, u32[]{:S(2)}, u32[]{:S(2)}) %all-to-all-start) | async-done | bytes 1048608 | tf_op jit(solution)/shard_map/all_to_all | solution.py:422
  42.2 5.0 %collective-permute-start.8 = (bf16[4096,128]{1,0:T(8,128)(2,1)S(1)}, bf16[4096,128]{1,0:T(8,128)(2,1)}, u32[]{:S(2)}, u32[]{:S(2)}) collective-permute-start(bf16[4096,128]{1,0:T(8,128)(2,1)S(1)} %bitcast.30), channel_id=1, source_target_pairs={{0,8},{1,9},{2,10},{3,11},{4,12},{5,13},{6,14},{7,15},{8,0},{9,1},... | collective-permute-start | bytes 3145736 | tf_op jit(solution)/shard_map/ppermute | solution.py:470
  47.2 2.5 %collective-permute-start.7 = (bf16[4096,128]{1,0:T(8,128)(2,1)S(1)}, bf16[4096,128]{1,0:T(8,128)(2,1)S(1)}, u32[]{:S(2)}, u32[]{:S(2)}) collective-permute-start(bf16[4096,128]{1,0:T(8,128)(2,1)S(1)} %bitcast.31), channel_id=1, source_target_pairs={{0,16},{1,17},{2,18},{3,19},{4,20},{5,21},{6,22},{7,23},{8,56},{9,... | collective-permute-start | bytes 3145736 | tf_op jit(solution)/shard_map/ppermute | solution.py:468
  49.7 4.8 %all-to-all-start.1 = ((bf16[32,64,128]{2,1,0:T(8,128)(2,1)}), bf16[32,64,128]{2,1,0:T(8,128)(2,1)S(1)}, u32[]{:S(2)}, u32[]{:S(2)}) async-start(bf16[32,64,128]{2,1,0:T(8,128)(2,1)} %bitcast.14), calls=%async_computation.1 | async-start | bytes 1048576 | tf_op jit(solution)/shard_map/all_to_all | solution.py:422
  54.6 2.2 %own.1 = (f32[16,512]{1,0:T(8,128)S(1)}, f32[16,512]{1,0:T(8,128)S(1)}) custom-call(s32[2]{0:T(128)S(1)} %pad_add_fusion.spots, f32[16,512]{1,0:T(8,128)S(1)} %concatenate.8.ranks, bf16[4096,128]{1,0:T(8,128)(2,1)S(1)} %bitcast.33, bf16[4096,128]{1,0:T(8,128)(2,1)} %collective-permute-done.8.e1), custom_call_target="tpu_custom_call" | custom-call | flops 1073741824 | bytes 4194304 | tf_op jit(solution)/shard_map/own/pallas_call | solution.py:368
  56.8 14.3 %all-to-all-done.1 = bf16[32,64,128]{2,1,0:T(8,128)(2,1)S(1)} async-done(((bf16[32,64,128]{2,1,0:T(8,128)(2,1)}), bf16[32,64,128]{2,1,0:T(8,128)(2,1)S(1)}, u32[]{:S(2)}, u32[]{:S(2)}) %all-to-all-start.1) | async-done | bytes 524320 | tf_op jit(solution)/shard_map/all_to_all | solution.py:422
  73.9 4.9 %first.1 = (f32[16,512]{1,0:T(8,128)S(1)}, f32[16,512]{1,0:T(8,128)S(1)}) custom-call(s32[2]{0:T(128)S(1)} %pad_add_fusion.spots, f32[16,512]{1,0:T(8,128)S(1)} %concatenate.8.ranks, bf16[4096,128]{1,0:T(8,128)(2,1)S(1)} %bitcast.34, bf16[4096,128]{1,0:T(8,128)(2,1)S(1)} %collective-permute-done.7.u1, bf16[4096,128]{1,0:T(8,128)(2,1)} %collective-permute-done.10.v1, ...), custom_call_target="tpu_custom_call" | custom-call | flops 1610612736 | bytes 4194304 | tf_op jit(solution)/shard_map/first/pallas_call | solution.py:368
  79.0 4.3 %second.1 = (f32[16,512]{1,0:T(8,128)S(1)}, f32[16,512]{1,0:T(8,128)S(1)}) custom-call(s32[2]{0:T(128)S(1)} %pad_add_fusion.spots, f32[16,512]{1,0:T(8,128)S(1)} %concatenate.8.ranks, bf16[4096,128]{1,0:T(8,128)(2,1)S(1)} %bitcast.35, bf16[2048,128]{1,0:T(8,128)(2,1)S(1)} %bitcast.28, bf16[4096,128]{1,0:T(8,128)(2,1)S(1)} %collective-permute-done.7.u1, ...), custom_call_target="tpu_custom_call" | custom-call | flops 1879048192 | bytes 4194304 | tf_op jit(solution)/shard_map/second/pallas_call | solution.py:368
  83.3 2.5 %collective-permute-start.14 = (bf16[2048,128]{1,0:T(8,128)(2,1)S(1)}, bf16[2048,128]{1,0:T(8,128)(2,1)S(1)}, u32[]{:S(2)}, u32[]{:S(2)}) collective-permute-start(bf16[2048,128]{1,0:T(8,128)(2,1)S(1)} %collective-permute-done.9.u2), channel_id=1, source_target_pairs={{0,8},{1,9},{2,10},{3,11},{4,12},{5,13},{6,14},{7,15},{8,0},{9,1},... | collective-permute-start | bytes 1572872 | tf_op jit(solution)/shard_map/ppermute | solution.py:482
  85.8 3.0 %third.1 = (f32[16,512]{1,0:T(8,128)S(1)}, f32[16,512]{1,0:T(8,128)S(1)}) custom-call(s32[2]{0:T(128)S(1)} %pad_add_fusion.spots, f32[16,512]{1,0:T(8,128)S(1)} %concatenate.8.ranks, bf16[2048,128]{1,0:T(8,128)(2,1)S(1)} %bitcast.29, bf16[2048,128]{1,0:T(8,128)(2,1)S(1)} %collective-permute-done.9.u2, bf16[2048,128]{1,0:T(8,128)(2,1)S(1)} %collective-permute-done.12.e2, ...), custom_call_target="tpu_custom_call" | custom-call | flops 536870912 | bytes 4194304 | tf_op jit(solution)/shard_map/third/pallas_call | solution.py:368
  88.7 1.7 %fourth.1 = (f32[4,192]{1,0:T(4,128)S(1)}, f32[4,192]{1,0:T(4,128)S(1)}, f32[4,192]{1,0:T(4,128)S(1)}, f32[4,192]{1,0:T(4,128)S(1)}, f32[4,192]{1,0:T(4,128)S(1)}) custom-call(s32[2]{0:T(128)S(1)} %pad_add_fusion.spots, f32[16,512]{1,0:T(8,128)S(1)} %concatenate.8.ranks, bf16[4096,128]{1,0:T(8,128)(2,1)S(1)} %collective-permute-done.7.u1, ...), custom_call_target="tpu_custom_call" | custom-call | flops 536870912 | bytes 4194304 | tf_op jit(solution)/shard_map/fourth/pallas_call | solution.py:368
  90.7 2.7 %collective-permute-start.16 = (f32[4,192]{1,0:T(4,128)S(1)}, f32[4,192]{1,0:T(4,128)S(1)}, u32[]{:S(2)}, u32[]{:S(2)}) collective-permute-start(f32[4,192]{1,0:T(4,128)S(1)} %get-tuple-element.66), channel_id=1, source_target_pairs={{0,16},{1,17},{2,18},{3,19},{4,20},{5,21},{6,22},{7,23},{8,56},{9,... | collective-permute-start | bytes 9224 | tf_op jit(solution)/shard_map/ppermute | solution.py:492
  93.4 1.3 %collective-permute-start.17 = (f32[4,192]{1,0:T(4,128)S(1)}, f32[4,192]{1,0:T(4,128)S(1)}, u32[]{:S(2)}, u32[]{:S(2)}) collective-permute-start(f32[4,192]{1,0:T(4,128)S(1)} %get-tuple-element.67), channel_id=1, source_target_pairs={{0,8},{1,9},{2,10},{3,11},{4,12},{5,13},{6,14},{7,15},{8,0},{9,1},... | collective-permute-start | bytes 9224 | tf_op jit(solution)/shard_map/ppermute | solution.py:492
  94.6 2.8 %collective-permute-start.18 = (f32[4,192]{1,0:T(4,128)S(1)}, f32[4,192]{1,0:T(4,128)S(1)}, u32[]{:S(2)}, u32[]{:S(2)}) collective-permute-start(f32[4,192]{1,0:T(4,128)S(1)} %get-tuple-element.68), channel_id=1, source_target_pairs={{0,24},{1,25},{2,26},{3,27},{4,28},{5,29},{6,30},{7,31},{8,48},{9,... | collective-permute-start | bytes 9224 | tf_op jit(solution)/shard_map/ppermute | solution.py:492
  97.5 1.6 %collective-permute-done.18 = f32[4,192]{1,0:T(4,128)S(1)} collective-permute-done((f32[4,192]{1,0:T(4,128)S(1)}, f32[4,192]{1,0:T(4,128)S(1)}, u32[]{:S(2)}, u32[]{:S(2)}) %collective-permute-start.18) | collective-permute-done | bytes 3104 | tf_op jit(solution)/shard_map/ppermute | solution.py:492
  99.1 13.4 %all_to_all.21 = f32[32,1,192]{2,1,0:T(1,128)S(1)} all-to-all(f32[32,1,192]{2,1,0:T(1,128)S(1)} %all_to_all.15), channel_id=1, replica_groups=mesh['y'=4,'x'=4,'core'=2,'z'=8] {'y','z'}, dimensions={0} | all-to-all | bytes 49152 | tf_op jit(solution)/shard_map/all_to_all | solution.py:493
  (54 shorter events, 9.7 us)
Async XLA Ops:
  5.4 28.7 %copy-start = (bf16[3072,128]{1,0:T(8,128)(2,1)S(1)}, bf16[3072,128]{1,0:T(8,128)(2,1)}, u32[]{:S(2)}) copy-start(bf16[3072,128]{1,0:T(8,128)(2,1)} %rows_ref.1) | copy-start | bytes 2359300
  5.4 36.8 %all-to-all-start = ((bf16[32,128,128]{2,1,0:T(8,128)(2,1)}), bf16[32,128,128]{2,1,0:T(8,128)(2,1)S(1)}, u32[]{:S(2)}, u32[]{:S(2)}) async-start(bf16[32,128,128]{2,1,0:T(8,128)(2,1)} %bitcast.43), calls=%async_computation | async-start | bytes 2097152 | tf_op jit(solution)/shard_map/all_to_all | solution.py:422
  17.7 0.7 copy-start.2
  17.7 0.7 copy-start.1
  19.3 4.9 %collective-permute-start = (f32[1,192]{1,0:T(1,128)S(1)}, f32[1,192]{1,0:T(1,128)S(1)}, u32[]{:S(2)}, u32[]{:S(2)}) collective-permute-start(f32[1,192]{1,0:T(1,128)S(1)} %get-tuple-element.72), channel_id=1, source_target_pairs={{0,64},{1,65},{2,66},{3,67},{4,68},{5,69},{6,70},{7,71},{8,72},{9,... | collective-permute-start | bytes 2312 | tf_op jit(solution)/shard_map/ppermute | solution.py:437
  20.6 4.0 %collective-permute-start.1 = (f32[1,192]{1,0:T(1,128)S(1)}, f32[1,192]{1,0:T(1,128)S(1)}, u32[]{:S(2)}, u32[]{:S(2)}) collective-permute-start(f32[1,192]{1,0:T(1,128)S(1)} %get-tuple-element.71), channel_id=1, source_target_pairs={{0,128},{1,129},{2,130},{3,131},{4,132},{5,133},{6,134},{7,135},{8... | collective-permute-start | bytes 2312 | tf_op jit(solution)/shard_map/ppermute | solution.py:437
  23.1 2.7 %collective-permute-start.2 = (f32[1,192]{1,0:T(1,128)S(1)}, f32[1,192]{1,0:T(1,128)S(1)}, u32[]{:S(2)}, u32[]{:S(2)}) collective-permute-start(f32[1,192]{1,0:T(1,128)S(1)} %get-tuple-element.70), channel_id=1, source_target_pairs={{0,192},{1,193},{2,194},{3,195},{4,196},{5,197},{6,198},{7,199},{8... | collective-permute-start | bytes 2312 | tf_op jit(solution)/shard_map/ppermute | solution.py:437
  26.5 6.0 %collective-permute-start.3 = (f32[2,512]{1,0:T(2,128)S(1)}, f32[2,512]{1,0:T(2,128)S(1)}, u32[]{:S(2)}, u32[]{:S(2)}) collective-permute-start(f32[2,512]{1,0:T(2,128)S(1)} %pad_maximum_fusion.1), channel_id=1, source_target_pairs={{0,16},{1,17},{2,18},{3,19},{4,20},{5,21},{6,22},{7,23},{8,56},{9,... | collective-permute-start | bytes 12296 | tf_op jit(solution)/shard_map/ppermute | solution.py:447
  29.0 9.3 %collective-permute-start.4 = (f32[2,512]{1,0:T(2,128)S(1)}, f32[2,512]{1,0:T(2,128)S(1)}, u32[]{:S(2)}, u32[]{:S(2)}) collective-permute-start(f32[2,512]{1,0:T(2,128)S(1)} %pad_maximum_fusion.1), channel_id=1, source_target_pairs={{0,48},{1,49},{2,50},{3,51},{4,52},{5,53},{6,54},{7,55},{8,24},{9,... | collective-permute-start | bytes 12296 | tf_op jit(solution)/shard_map/ppermute | solution.py:452
  29.0 9.3 %collective-permute-start.5 = (f32[2,512]{1,0:T(2,128)S(1)}, f32[2,512]{1,0:T(2,128)S(1)}, u32[]{:S(2)}, u32[]{:S(2)}) collective-permute-start(f32[2,512]{1,0:T(2,128)S(1)} %pad_maximum_fusion.1), channel_id=1, source_target_pairs={{0,8},{1,9},{2,10},{3,11},{4,12},{5,13},{6,14},{7,15},{8,0},{9,1},... | collective-permute-start | bytes 12296 | tf_op jit(solution)/shard_map/ppermute | solution.py:453
  32.4 5.9 %collective-permute-start.6 = (f32[2,512]{1,0:T(2,128)S(1)}, f32[2,512]{1,0:T(2,128)S(1)}, u32[]{:S(2)}, u32[]{:S(2)}) collective-permute-start(f32[2,512]{1,0:T(2,128)S(1)} %collective-permute-done.3), channel_id=1, source_target_pairs={{0,8},{1,9},{2,10},{3,11},{4,12},{5,13},{6,14},{7,15},{8,0},{9,1},... | collective-permute-start | bytes 12296 | tf_op jit(solution)/shard_map/ppermute | solution.py:454
  42.2 12.3 %collective-permute-start.8 = (bf16[4096,128]{1,0:T(8,128)(2,1)S(1)}, bf16[4096,128]{1,0:T(8,128)(2,1)}, u32[]{:S(2)}, u32[]{:S(2)}) collective-permute-start(bf16[4096,128]{1,0:T(8,128)(2,1)S(1)} %bitcast.30), channel_id=1, source_target_pairs={{0,8},{1,9},{2,10},{3,11},{4,12},{5,13},{6,14},{7,15},{8,0},{9,1},... | collective-permute-start | bytes 3145736 | tf_op jit(solution)/shard_map/ppermute | solution.py:470
  47.2 23.9 %collective-permute-start.7 = (bf16[4096,128]{1,0:T(8,128)(2,1)S(1)}, bf16[4096,128]{1,0:T(8,128)(2,1)S(1)}, u32[]{:S(2)}, u32[]{:S(2)}) collective-permute-start(bf16[4096,128]{1,0:T(8,128)(2,1)S(1)} %bitcast.31), channel_id=1, source_target_pairs={{0,16},{1,17},{2,18},{3,19},{4,20},{5,21},{6,22},{7,23},{8,56},{9,... | collective-permute-start | bytes 3145736 | tf_op jit(solution)/shard_map/ppermute | solution.py:468
  49.7 21.4 %all-to-all-start.1 = ((bf16[32,64,128]{2,1,0:T(8,128)(2,1)}), bf16[32,64,128]{2,1,0:T(8,128)(2,1)S(1)}, u32[]{:S(2)}, u32[]{:S(2)}) async-start(bf16[32,64,128]{2,1,0:T(8,128)(2,1)} %bitcast.14), calls=%async_computation.1 | async-start | bytes 1048576 | tf_op jit(solution)/shard_map/all_to_all | solution.py:422
  54.5 19.4 %collective-permute-start.10 = (bf16[4096,128]{1,0:T(8,128)(2,1)S(1)}, bf16[4096,128]{1,0:T(8,128)(2,1)}, u32[]{:S(2)}, u32[]{:S(2)}) collective-permute-start(bf16[4096,128]{1,0:T(8,128)(2,1)S(1)} %bitcast.32), channel_id=1, source_target_pairs={{0,48},{1,49},{2,50},{3,51},{4,52},{5,53},{6,54},{7,55},{8,24},{9,... | collective-permute-start | bytes 3145736 | tf_op jit(solution)/shard_map/ppermute | solution.py:469
  71.1 2.8 %collective-permute-start.11 = (bf16[4096,128]{1,0:T(8,128)(2,1)S(1)}, bf16[4096,128]{1,0:T(8,128)(2,1)S(1)}, u32[]{:S(2)}, u32[]{:S(2)}) collective-permute-start(bf16[4096,128]{1,0:T(8,128)(2,1)S(1)} %collective-permute-done.7.u1), channel_id=1, source_target_pairs={{0,8},{1,9},{2,10},{3,11},{4,12},{5,13},{6,14},{7,15},{8,0},{9,1},... | collective-permute-start | bytes 3145736 | tf_op jit(solution)/shard_map/ppermute | solution.py:473
  71.3 7.7 %collective-permute-start.12 = (bf16[2048,128]{1,0:T(8,128)(2,1)S(1)}, bf16[2048,128]{1,0:T(8,128)(2,1)S(1)}, u32[]{:S(2)}, u32[]{:S(2)}) collective-permute-start(bf16[2048,128]{1,0:T(8,128)(2,1)S(1)} %bitcast.25), channel_id=1, source_target_pairs={{0,8},{1,9},{2,10},{3,11},{4,12},{5,13},{6,14},{7,15},{8,0},{9,1},... | collective-permute-start | bytes 1572872 | tf_op jit(solution)/shard_map/ppermute | solution.py:476
  71.6 11.7 %collective-permute-start.9 = (bf16[2048,128]{1,0:T(8,128)(2,1)S(1)}, bf16[2048,128]{1,0:T(8,128)(2,1)S(1)}, u32[]{:S(2)}, u32[]{:S(2)}) collective-permute-start(bf16[2048,128]{1,0:T(8,128)(2,1)S(1)} %bitcast.26), channel_id=1, source_target_pairs={{0,16},{1,17},{2,18},{3,19},{4,20},{5,21},{6,22},{7,23},{8,56},{9,... | collective-permute-start | bytes 1572872 | tf_op jit(solution)/shard_map/ppermute | solution.py:475
  78.8 10.0 %collective-permute-start.13 = (bf16[2048,128]{1,0:T(8,128)(2,1)S(1)}, bf16[2048,128]{1,0:T(8,128)(2,1)S(1)}, u32[]{:S(2)}, u32[]{:S(2)}) collective-permute-start(bf16[2048,128]{1,0:T(8,128)(2,1)S(1)} %bitcast.27), channel_id=1, source_target_pairs={{0,48},{1,49},{2,50},{3,51},{4,52},{5,53},{6,54},{7,55},{8,24},{9,... | collective-permute-start | bytes 1572872 | tf_op jit(solution)/shard_map/ppermute | solution.py:479
  83.3 5.4 %collective-permute-start.14 = (bf16[2048,128]{1,0:T(8,128)(2,1)S(1)}, bf16[2048,128]{1,0:T(8,128)(2,1)S(1)}, u32[]{:S(2)}, u32[]{:S(2)}) collective-permute-start(bf16[2048,128]{1,0:T(8,128)(2,1)S(1)} %collective-permute-done.9.u2), channel_id=1, source_target_pairs={{0,8},{1,9},{2,10},{3,11},{4,12},{5,13},{6,14},{7,15},{8,0},{9,1},... | collective-permute-start | bytes 1572872 | tf_op jit(solution)/shard_map/ppermute | solution.py:482
  90.4 7.0 %collective-permute-start.15 = (f32[4,192]{1,0:T(4,128)S(1)}, f32[4,192]{1,0:T(4,128)S(1)}, u32[]{:S(2)}, u32[]{:S(2)}) collective-permute-start(f32[4,192]{1,0:T(4,128)S(1)} %get-tuple-element.65), channel_id=1, source_target_pairs={{0,48},{1,49},{2,50},{3,51},{4,52},{5,53},{6,54},{7,55},{8,24},{9,... | collective-permute-start | bytes 9224 | tf_op jit(solution)/shard_map/ppermute | solution.py:492
  90.7 6.8 %collective-permute-start.16 = (f32[4,192]{1,0:T(4,128)S(1)}, f32[4,192]{1,0:T(4,128)S(1)}, u32[]{:S(2)}, u32[]{:S(2)}) collective-permute-start(f32[4,192]{1,0:T(4,128)S(1)} %get-tuple-element.66), channel_id=1, source_target_pairs={{0,16},{1,17},{2,18},{3,19},{4,20},{5,21},{6,22},{7,23},{8,56},{9,... | collective-permute-start | bytes 9224 | tf_op jit(solution)/shard_map/ppermute | solution.py:492
  93.4 4.1 %collective-permute-start.17 = (f32[4,192]{1,0:T(4,128)S(1)}, f32[4,192]{1,0:T(4,128)S(1)}, u32[]{:S(2)}, u32[]{:S(2)}) collective-permute-start(f32[4,192]{1,0:T(4,128)S(1)} %get-tuple-element.67), channel_id=1, source_target_pairs={{0,8},{1,9},{2,10},{3,11},{4,12},{5,13},{6,14},{7,15},{8,0},{9,1},... | collective-permute-start | bytes 9224 | tf_op jit(solution)/shard_map/ppermute | solution.py:492
  94.6 4.4 %collective-permute-start.18 = (f32[4,192]{1,0:T(4,128)S(1)}, f32[4,192]{1,0:T(4,128)S(1)}, u32[]{:S(2)}, u32[]{:S(2)}) collective-permute-start(f32[4,192]{1,0:T(4,128)S(1)} %get-tuple-element.68), channel_id=1, source_target_pairs={{0,24},{1,25},{2,26},{3,27},{4,28},{5,29},{6,30},{7,31},{8,48},{9,... | collective-permute-start | bytes 9224 | tf_op jit(solution)/shard_map/ppermute | solution.py:492
  (1 other events, 0.7 us)

commit v10 on v9

--- a/solution.py
+++ b/solution.py
@@ -266,29 +266,34 @@
         meet(best, inverses, ranks, O1, o1, [(E1, e1)])
 
 
-def first_kernel(spots, ranks, o1, u1, v1, e1, w1, before, known, best, inverses):
+def near_kernel(spots, ranks, o1, u1, e1, before, known, best, inverses):
     best[...] = before[...]
     inverses[...] = known[...]
     note(inverses, U1, u1)
+    meet(best, inverses, ranks, U1, u1, [(O1, o1)])
+
+    @pl.when(spots[0] != 0)
+    def _():
+        meet(best, inverses, ranks, U1, u1, [(E1, e1)])
+
+
+def first_kernel(spots, ranks, u1, v1, e1, w1, before, known, best, inverses):
+    best[...] = before[...]
+    inverses[...] = known[...]
     note(inverses, V1, v1)
     note(inverses, W1, w1)
-    meet(best, inverses, ranks, O1, o1, [(U1, u1)])
 
     @pl.when(spots[0] == 0)
     def _():
-        meet(best, inverses, ranks, E1, e1, [(V1, v1)])
-
-    @pl.when(spots[0] != 0)
-    def _():
-        meet(best, inverses, ranks, E1, e1, [(U1, u1)])
+        meet(best, inverses, ranks, V1, v1, [(E1, e1)])
 
     @pl.when(spots[1] != 0)
     def _():
-        meet(best, inverses, ranks, U1, u1, [(V1, v1)])
+        meet(best, inverses, ranks, V1, v1, [(U1, u1)])
 
     @pl.when(spots[1] == 0)
     def _():
-        meet(best, inverses, ranks, U1, u1, [(W1, w1)])
+        meet(best, inverses, ranks, W1, w1, [(U1, u1)])
 
 
 def second_kernel(spots, ranks, o1, o2, u1, v1, e1, e2, before, known, best, inverses):
@@ -466,15 +471,17 @@
         return scores_call(kernel, units, inputs, list(out), list(scratch), name)
 
     u1 = lax.ppermute(o1, ALL, ahead)
-    v1 = lax.ppermute(o1, ALL, behind)
     e1 = lax.ppermute(o1, ALL, swap)
     state = score(own_kernel, 8, (o1, e1), (), "own")
-    u1, o2, *state = lax.optimization_barrier((u1, o2, *state))
+    o1, *state = lax.optimization_barrier((o1, *state))
+    v1 = lax.ppermute(o1, ALL, behind)
     w1 = lax.ppermute(u1, ALL, swap)
+    state = score(near_kernel, 6, (o1, u1, e1), state, "near")
+    o2, *state = lax.optimization_barrier((o2, *state))
 
     u2 = lax.ppermute(o2, ALL, ahead)
     e2 = lax.ppermute(o2, ALL, swap)
-    state = score(first_kernel, 12, (o1, u1, v1, e1, w1), state, "first")
+    state = score(first_kernel, 6, (u1, v1, e1, w1), state, "first")
     o2, *state = lax.optimization_barrier((o2, *state))
     v2 = lax.ppermute(o2, ALL, behind)
     state = score(second_kernel, 14, (o1, o2, u1, v1, e1, e2), state, "second")

time: 114 us -> 117 us (1.026)
  waiting for transfers between devices: 22.3 us -> 18.4 us
  blocking collectives: 13.4 us -> 16.6 us
  starting transfers between devices: 48.3 us -> 51.1 us
    all_to_all x2, waiting for transfers between devices: 18.1 us -> 6.69 us  [bring(): lax.all_to_all(rows.reshape(GROUPS, part, WIDTH), ('y', 'z'), split_axis=...]
    ppermute x1, waiting for transfers between devices: 0.01 us -> 7.58 us  [shards(): u1 = lax.ppermute(o1, ALL, ahead)]
    all_to_all x1, blocking collectives: 13.4 us -> 16.6 us  [shards(): lax.all_to_all(jnp.broadcast_to(own[:, None], (Y, Z, CAP)).reshape(GROUPS...]
    ppermute x1, starting transfers between devices: 0.21 us -> 1.99 us  [shards(): w1 = lax.ppermute(u1, ALL, swap)]
    pallas_call x5 -> x6, Pallas kernels: 16.1 us -> 16.6 us  [scores_call(): pl.pallas_call(kernel, out_shape=jax.tree.map(lambda dims: jax.ShapeDtype...]
  transfers between devices with their start and end apart: 21 -> 21, of which waited for: 6 -> 7; matrix products, arithmetic and copies ran while one was open for 1% -> 1% of each run, Pallas kernels for 17% -> 16%
where the time goes in v10:
time: 117 us; the launch traced here: 116 us
  starting transfers between devices  51.1 us (44%)
  Pallas kernels  27.4 us (23%)
  waiting for transfers between devices  18.4 us (16%)
  blocking collectives  16.6 us (14%)
  local copies, waits for them, and re-layouts  2.26 us (2%)
    all_to_all x2, starting transfers between devices, bring(): lax.all_to_all(rows.reshape(GROUPS, part, WIDTH), ('y', 'z'), split_axis=...  17.1 us
    all_to_all x1, blocking collectives, shards(): lax.all_to_all(jnp.broadcast_to(own[:, None], (Y, Z, CAP)).reshape(GROUPS...  16.6 us
    pallas_call x6, Pallas kernels, scores_call(): pl.pallas_call(kernel, out_shape=jax.tree.map(lambda dims: jax.ShapeDtype...  16.6 us
    ppermute x1, waiting for transfers between devices, shards(): u1 = lax.ppermute(o1, ALL, ahead)  7.58 us
    ppermute x4, starting transfers between devices, shards(): own = jnp.maximum(own, lax.ppermute(part, ALL, way))  6.75 us
    all_to_all x2, waiting for transfers between devices, bring(): lax.all_to_all(rows.reshape(GROUPS, part, WIDTH), ('y', 'z'), split_axis=...  6.69 us
    pallas_call x1, Pallas kernels, place(): pl.pallas_call(place_kernel, out_shape=(jax.ShapeDtypeStruct((GROUPS * PA...  5.41 us
    ppermute x1, starting transfers between devices, shards(): e1 = lax.ppermute(o1, ALL, swap)  4.97 us
  transfers between devices with their start and end apart: 21, of which 7 were waited for; matrix products, arithmetic and copies ran while one was open for 1% of the time, Pallas kernels for 16%

profile of v10, /device:TPU:1, one launch (start us, length us, event | category | flops | bytes accessed | tf_op | source)
XLA Modules:
  0.0 116.2 jit_solution(3468632863897780434)
XLA Ops:
  0.0 5.4 %place.1 = (bf16[4096,128]{1,0:T(8,128)(2,1)}, s32[24,128]{1,0:T(8,128)}) custom-call(s32[24,128]{1,0:T(8,128)} %bitcast.32, bf16[3072,128]{1,0:T(8,128)(2,1)} %rows_ref.1), custom_call_target="tpu_custom_call" | custom-call | tf_op jit(solution)/shard_map/place/pallas_call | solution.py:85
  5.4 12.2 %all-to-all-start = ((bf16[32,128,128]{2,1,0:T(8,128)(2,1)}), bf16[32,128,128]{2,1,0:T(8,128)(2,1)S(1)}, u32[]{:S(2)}, u32[]{:S(2)}) async-start(bf16[32,128,128]{2,1,0:T(8,128)(2,1)} %bitcast.39), calls=%async_computation | async-start | bytes 2097152 | tf_op jit(solution)/shard_map/all_to_all | solution.py:427
  20.6 2.4 %collective-permute-start.1 = (f32[1,192]{1,0:T(1,128)S(1)}, f32[1,192]{1,0:T(1,128)S(1)}, u32[]{:S(2)}, u32[]{:S(2)}) collective-permute-start(f32[1,192]{1,0:T(1,128)S(1)} %get-tuple-element.79), channel_id=1, source_target_pairs={{0,128},{1,129},{2,130},{3,131},{4,132},{5,133},{6,134},{7,135},{8... | collective-permute-start | bytes 2312 | tf_op jit(solution)/shard_map/ppermute | solution.py:442
  26.5 2.6 %collective-permute-start.3 = (f32[2,512]{1,0:T(2,128)S(1)}, f32[2,512]{1,0:T(2,128)S(1)}, u32[]{:S(2)}, u32[]{:S(2)}) collective-permute-start(f32[2,512]{1,0:T(2,128)S(1)} %pad_maximum_fusion.1), channel_id=1, source_target_pairs={{0,16},{1,17},{2,18},{3,19},{4,20},{5,21},{6,22},{7,23},{8,56},{9,... | collective-permute-start | bytes 12296 | tf_op jit(solution)/shard_map/ppermute | solution.py:452
  29.0 3.4 %collective-permute-start.5 = (f32[2,512]{1,0:T(2,128)S(1)}, f32[2,512]{1,0:T(2,128)S(1)}, u32[]{:S(2)}, u32[]{:S(2)}) collective-permute-start(f32[2,512]{1,0:T(2,128)S(1)} %pad_maximum_fusion.1), channel_id=1, source_target_pairs={{0,8},{1,9},{2,10},{3,11},{4,12},{5,13},{6,14},{7,15},{8,0},{9,1},... | collective-permute-start | bytes 12296 | tf_op jit(solution)/shard_map/ppermute | solution.py:458
  32.4 1.6 %collective-permute-start.6 = (f32[2,512]{1,0:T(2,128)S(1)}, f32[2,512]{1,0:T(2,128)S(1)}, u32[]{:S(2)}, u32[]{:S(2)}) collective-permute-start(f32[2,512]{1,0:T(2,128)S(1)} %collective-permute-done.3), channel_id=1, source_target_pairs={{0,8},{1,9},{2,10},{3,11},{4,12},{5,13},{6,14},{7,15},{8,0},{9,1},... | collective-permute-start | bytes 12296 | tf_op jit(solution)/shard_map/ppermute | solution.py:459
  34.1 3.4 %place_rest.1 = bf16[2048,128]{1,0:T(8,128)(2,1)S(1)} custom-call(s32[24,128]{1,0:T(8,128)S(1)} %bitcast.34, s32[24,128]{1,0:T(8,128)S(1)} %copy-done.3, bf16[3072,128]{1,0:T(8,128)(2,1)S(1)} %copy-done), custom_call_target="tpu_custom_call" | custom-call | tf_op jit(solution)/shard_map/place_rest/pallas_call | solution.py:126
  38.4 3.9 %all-to-all-done = bf16[32,128,128]{2,1,0:T(8,128)(2,1)S(1)} async-done(((bf16[32,128,128]{2,1,0:T(8,128)(2,1)}), bf16[32,128,128]{2,1,0:T(8,128)(2,1)S(1)}, u32[]{:S(2)}, u32[]{:S(2)}) %all-to-all-start) | async-done | bytes 1048608 | tf_op jit(solution)/shard_map/all_to_all | solution.py:427
  42.2 5.0 %collective-permute-start.8 = (bf16[4096,128]{1,0:T(8,128)(2,1)S(1)}, bf16[4096,128]{1,0:T(8,128)(2,1)S(1)}, u32[]{:S(2)}, u32[]{:S(2)}) collective-permute-start(bf16[4096,128]{1,0:T(8,128)(2,1)S(1)} %bitcast.25), channel_id=1, source_target_pairs={{0,8},{1,9},{2,10},{3,11},{4,12},{5,13},{6,14},{7,15},{8,0},{9,1},... | collective-permute-start | bytes 3145736 | tf_op jit(solution)/shard_map/ppermute | solution.py:474
  47.2 2.5 %collective-permute-start.7 = (bf16[4096,128]{1,0:T(8,128)(2,1)S(1)}, bf16[4096,128]{1,0:T(8,128)(2,1)S(1)}, u32[]{:S(2)}, u32[]{:S(2)}) collective-permute-start(bf16[4096,128]{1,0:T(8,128)(2,1)S(1)} %bitcast.26), channel_id=1, source_target_pairs={{0,16},{1,17},{2,18},{3,19},{4,20},{5,21},{6,22},{7,23},{8,56},{9,... | collective-permute-start | bytes 3145736 | tf_op jit(solution)/shard_map/ppermute | solution.py:473
  49.7 4.9 %all-to-all-start.1 = ((bf16[32,64,128]{2,1,0:T(8,128)(2,1)}), bf16[32,64,128]{2,1,0:T(8,128)(2,1)}, u32[]{:S(2)}, u32[]{:S(2)}) async-start(bf16[32,64,128]{2,1,0:T(8,128)(2,1)} %bitcast.31), calls=%async_computation.1 | async-start | bytes 1048576 | tf_op jit(solution)/shard_map/all_to_all | solution.py:427
  56.3 7.6 %collective-permute-done.7.u1 = bf16[4096,128]{1,0:T(8,128)(2,1)S(1)} collective-permute-done((bf16[4096,128]{1,0:T(8,128)(2,1)S(1)}, bf16[4096,128]{1,0:T(8,128)(2,1)S(1)}, u32[]{:S(2)}, u32[]{:S(2)}) %collective-permute-start.7) | collective-permute-done | bytes 1048608 | tf_op jit(solution)/shard_map/ppermute | solution.py:473
  63.8 2.0 %collective-permute-start.11 = (bf16[4096,128]{1,0:T(8,128)(2,1)S(1)}, bf16[4096,128]{1,0:T(8,128)(2,1)}, u32[]{:S(2)}, u32[]{:S(2)}) collective-permute-start(bf16[4096,128]{1,0:T(8,128)(2,1)S(1)} %collective-permute-done.7.u1), channel_id=1, source_target_pairs={{0,8},{1,9},{2,10},{3,11},{4,12},{5,13},{6,14},{7,15},{8,0},{9,1},... | collective-permute-start | bytes 3145736 | tf_op jit(solution)/shard_map/ppermute | solution.py:478
  65.8 2.5 %near.1 = (f32[16,512]{1,0:T(8,128)S(1)}, f32[16,512]{1,0:T(8,128)S(1)}) custom-call(s32[2]{0:T(128)S(1)} %pad_add_fusion.spots, f32[16,512]{1,0:T(8,128)S(1)} %concatenate.8.ranks, bf16[4096,128]{1,0:T(8,128)(2,1)S(1)} %bitcast.29, bf16[4096,128]{1,0:T(8,128)(2,1)S(1)} %collective-permute-done.7.u1, bf16[4096,128]{1,0:T(8,128)(2,1)S(1)} %collective-permute-done.8.e1, ...), custom_call_target="tpu_custom_call" | custom-call | flops 805306368 | bytes 4194304 | tf_op jit(solution)/shard_map/near/pallas_call | solution.py:373
  68.3 2.8 %all-to-all-done.1 = bf16[32,64,128]{2,1,0:T(8,128)(2,1)} async-done(((bf16[32,64,128]{2,1,0:T(8,128)(2,1)}), bf16[32,64,128]{2,1,0:T(8,128)(2,1)}, u32[]{:S(2)}, u32[]{:S(2)}) %all-to-all-start.1) | async-done | bytes 524320 | tf_op jit(solution)/shard_map/all_to_all | solution.py:427
  73.9 3.1 %first.1 = (f32[16,512]{1,0:T(8,128)S(1)}, f32[16,512]{1,0:T(8,128)S(1)}) custom-call(s32[2]{0:T(128)S(1)} %pad_add_fusion.spots, f32[16,512]{1,0:T(8,128)S(1)} %concatenate.8.ranks, bf16[4096,128]{1,0:T(8,128)(2,1)S(1)} %collective-permute-done.7.u1, bf16[4096,128]{1,0:T(8,128)(2,1)} %collective-permute-done.10.v1, ...), custom_call_target="tpu_custom_call" | custom-call | flops 805306368 | bytes 4194304 | tf_op jit(solution)/shard_map/first/pallas_call | solution.py:373
  77.0 4.1 %second.1 = (f32[16,512]{1,0:T(8,128)S(1)}, f32[16,512]{1,0:T(8,128)S(1)}) custom-call(s32[2]{0:T(128)S(1)} %pad_add_fusion.spots, f32[16,512]{1,0:T(8,128)S(1)} %concatenate.8.ranks, bf16[4096,128]{1,0:T(8,128)(2,1)S(1)} %bitcast.30, bf16[2048,128]{1,0:T(8,128)(2,1)} %bitcast.15.o2, bf16[4096,128]{1,0:T(8,128)(2,1)S(1)} %collective-permute-done.7.u1, ...), custom_call_target="tpu_custom_call" | custom-call | flops 1879048192 | bytes 4194304 | tf_op jit(solution)/shard_map/second/pallas_call | solution.py:373
  81.2 3.5 %collective-permute-start.14 = (bf16[2048,128]{1,0:T(8,128)(2,1)S(1)}, bf16[2048,128]{1,0:T(8,128)(2,1)S(1)}, u32[]{:S(2)}, u32[]{:S(2)}) collective-permute-start(bf16[2048,128]{1,0:T(8,128)(2,1)S(1)} %collective-permute-done.9.u2), channel_id=1, source_target_pairs={{0,8},{1,9},{2,10},{3,11},{4,12},{5,13},{6,14},{7,15},{8,0},{9,1},... | collective-permute-start | bytes 1572872 | tf_op jit(solution)/shard_map/ppermute | solution.py:489
  84.7 3.4 %third.1 = (f32[16,512]{1,0:T(8,128)S(1)}, f32[16,512]{1,0:T(8,128)S(1)}) custom-call(s32[2]{0:T(128)S(1)} %pad_add_fusion.spots, f32[16,512]{1,0:T(8,128)S(1)} %concatenate.8.ranks, bf16[2048,128]{1,0:T(8,128)(2,1)} %bitcast.15.o2, bf16[2048,128]{1,0:T(8,128)(2,1)S(1)} %collective-permute-done.9.u2, bf16[2048,128]{1,0:T(8,128)(2,1)S(1)} %collective-permute-done.12.e2, ...), custom_call_target="tpu_custom_call" | custom-call | flops 536870912 | bytes 4194304 | tf_op jit(solution)/shard_map/third/pallas_call | solution.py:373
  88.1 1.9 %fourth.1 = (f32[4,192]{1,0:T(4,128)S(1)}, f32[4,192]{1,0:T(4,128)S(1)}, f32[4,192]{1,0:T(4,128)S(1)}, f32[4,192]{1,0:T(4,128)S(1)}, f32[4,192]{1,0:T(4,128)S(1)}) custom-call(s32[2]{0:T(128)S(1)} %pad_add_fusion.spots, f32[16,512]{1,0:T(8,128)S(1)} %concatenate.8.ranks, bf16[4096,128]{1,0:T(8,128)(2,1)S(1)} %collective-permute-done.7.u1, ...), custom_call_target="tpu_custom_call" | custom-call | flops 536870912 | bytes 4194304 | tf_op jit(solution)/shard_map/fourth/pallas_call | solution.py:373
  90.1 2.7 %collective-permute-start.16 = (f32[4,192]{1,0:T(4,128)S(1)}, f32[4,192]{1,0:T(4,128)S(1)}, u32[]{:S(2)}, u32[]{:S(2)}) collective-permute-start(f32[4,192]{1,0:T(4,128)S(1)} %get-tuple-element.74), channel_id=1, source_target_pairs={{0,16},{1,17},{2,18},{3,19},{4,20},{5,21},{6,22},{7,23},{8,56},{9,... | collective-permute-start | bytes 9224 | tf_op jit(solution)/shard_map/ppermute | solution.py:499
  94.0 2.8 %collective-permute-start.18 = (f32[4,192]{1,0:T(4,128)S(1)}, f32[4,192]{1,0:T(4,128)S(1)}, u32[]{:S(2)}, u32[]{:S(2)}) collective-permute-start(f32[4,192]{1,0:T(4,128)S(1)} %get-tuple-element.76), channel_id=1, source_target_pairs={{0,24},{1,25},{2,26},{3,27},{4,28},{5,29},{6,30},{7,31},{8,48},{9,... | collective-permute-start | bytes 9224 | tf_op jit(solution)/shard_map/ppermute | solution.py:499
  96.8 1.6 %collective-permute-done.18 = f32[4,192]{1,0:T(4,128)S(1)} collective-permute-done((f32[4,192]{1,0:T(4,128)S(1)}, f32[4,192]{1,0:T(4,128)S(1)}, u32[]{:S(2)}, u32[]{:S(2)}) %collective-permute-start.18) | collective-permute-done | bytes 3104 | tf_op jit(solution)/shard_map/ppermute | solution.py:499
  98.4 16.6 %all_to_all.21 = f32[32,1,192]{2,1,0:T(1,128)S(1)} all-to-all(f32[32,1,192]{2,1,0:T(1,128)S(1)} %all_to_all.15), channel_id=1, replica_groups=mesh['y'=4,'x'=4,'core'=2,'z'=8] {'y','z'}, dimensions={0} | all-to-all | bytes 49152 | tf_op jit(solution)/shard_map/all_to_all | solution.py:500
  (57 shorter events, 14.1 us)
Async XLA Ops:
  5.4 28.7 %copy-start = (bf16[3072,128]{1,0:T(8,128)(2,1)S(1)}, bf16[3072,128]{1,0:T(8,128)(2,1)}, u32[]{:S(2)}) copy-start(bf16[3072,128]{1,0:T(8,128)(2,1)} %rows_ref.1) | copy-start | bytes 2359300
  5.4 36.8 %all-to-all-start = ((bf16[32,128,128]{2,1,0:T(8,128)(2,1)}), bf16[32,128,128]{2,1,0:T(8,128)(2,1)S(1)}, u32[]{:S(2)}, u32[]{:S(2)}) async-start(bf16[32,128,128]{2,1,0:T(8,128)(2,1)} %bitcast.39), calls=%async_computation | async-start | bytes 2097152 | tf_op jit(solution)/shard_map/all_to_all | solution.py:427
  17.7 0.7 copy-start.2
  19.3 4.9 %collective-permute-start = (f32[1,192]{1,0:T(1,128)S(1)}, f32[1,192]{1,0:T(1,128)S(1)}, u32[]{:S(2)}, u32[]{:S(2)}) collective-permute-start(f32[1,192]{1,0:T(1,128)S(1)} %get-tuple-element.80), channel_id=1, source_target_pairs={{0,64},{1,65},{2,66},{3,67},{4,68},{5,69},{6,70},{7,71},{8,72},{9,... | collective-permute-start | bytes 2312 | tf_op jit(solution)/shard_map/ppermute | solution.py:442
  20.6 4.0 %collective-permute-start.1 = (f32[1,192]{1,0:T(1,128)S(1)}, f32[1,192]{1,0:T(1,128)S(1)}, u32[]{:S(2)}, u32[]{:S(2)}) collective-permute-start(f32[1,192]{1,0:T(1,128)S(1)} %get-tuple-element.79), channel_id=1, source_target_pairs={{0,128},{1,129},{2,130},{3,131},{4,132},{5,133},{6,134},{7,135},{8... | collective-permute-start | bytes 2312 | tf_op jit(solution)/shard_map/ppermute | solution.py:442
  23.1 2.7 %collective-permute-start.2 = (f32[1,192]{1,0:T(1,128)S(1)}, f32[1,192]{1,0:T(1,128)S(1)}, u32[]{:S(2)}, u32[]{:S(2)}) collective-permute-start(f32[1,192]{1,0:T(1,128)S(1)} %get-tuple-element.78), channel_id=1, source_target_pairs={{0,192},{1,193},{2,194},{3,195},{4,196},{5,197},{6,198},{7,199},{8... | collective-permute-start | bytes 2312 | tf_op jit(solution)/shard_map/ppermute | solution.py:442
  26.5 6.0 %collective-permute-start.3 = (f32[2,512]{1,0:T(2,128)S(1)}, f32[2,512]{1,0:T(2,128)S(1)}, u32[]{:S(2)}, u32[]{:S(2)}) collective-permute-start(f32[2,512]{1,0:T(2,128)S(1)} %pad_maximum_fusion.1), channel_id=1, source_target_pairs={{0,16},{1,17},{2,18},{3,19},{4,20},{5,21},{6,22},{7,23},{8,56},{9,... | collective-permute-start | bytes 12296 | tf_op jit(solution)/shard_map/ppermute | solution.py:452
  29.0 9.3 %collective-permute-start.4 = (f32[2,512]{1,0:T(2,128)S(1)}, f32[2,512]{1,0:T(2,128)S(1)}, u32[]{:S(2)}, u32[]{:S(2)}) collective-permute-start(f32[2,512]{1,0:T(2,128)S(1)} %pad_maximum_fusion.1), channel_id=1, source_target_pairs={{0,48},{1,49},{2,50},{3,51},{4,52},{5,53},{6,54},{7,55},{8,24},{9,... | collective-permute-start | bytes 12296 | tf_op jit(solution)/shard_map/ppermute | solution.py:457
  29.0 9.3 %collective-permute-start.5 = (f32[2,512]{1,0:T(2,128)S(1)}, f32[2,512]{1,0:T(2,128)S(1)}, u32[]{:S(2)}, u32[]{:S(2)}) collective-permute-start(f32[2,512]{1,0:T(2,128)S(1)} %pad_maximum_fusion.1), channel_id=1, source_target_pairs={{0,8},{1,9},{2,10},{3,11},{4,12},{5,13},{6,14},{7,15},{8,0},{9,1},... | collective-permute-start | bytes 12296 | tf_op jit(solution)/shard_map/ppermute | solution.py:458
  32.4 5.9 %collective-permute-start.6 = (f32[2,512]{1,0:T(2,128)S(1)}, f32[2,512]{1,0:T(2,128)S(1)}, u32[]{:S(2)}, u32[]{:S(2)}) collective-permute-start(f32[2,512]{1,0:T(2,128)S(1)} %collective-permute-done.3), channel_id=1, source_target_pairs={{0,8},{1,9},{2,10},{3,11},{4,12},{5,13},{6,14},{7,15},{8,0},{9,1},... | collective-permute-start | bytes 12296 | tf_op jit(solution)/shard_map/ppermute | solution.py:459
  37.5 0.8 copy-start.1
  42.2 12.4 %collective-permute-start.8 = (bf16[4096,128]{1,0:T(8,128)(2,1)S(1)}, bf16[4096,128]{1,0:T(8,128)(2,1)S(1)}, u32[]{:S(2)}, u32[]{:S(2)}) collective-permute-start(bf16[4096,128]{1,0:T(8,128)(2,1)S(1)} %bitcast.25), channel_id=1, source_target_pairs={{0,8},{1,9},{2,10},{3,11},{4,12},{5,13},{6,14},{7,15},{8,0},{9,1},... | collective-permute-start | bytes 3145736 | tf_op jit(solution)/shard_map/ppermute | solution.py:474
  47.2 16.6 %collective-permute-start.7 = (bf16[4096,128]{1,0:T(8,128)(2,1)S(1)}, bf16[4096,128]{1,0:T(8,128)(2,1)S(1)}, u32[]{:S(2)}, u32[]{:S(2)}) collective-permute-start(bf16[4096,128]{1,0:T(8,128)(2,1)S(1)} %bitcast.26), channel_id=1, source_target_pairs={{0,16},{1,17},{2,18},{3,19},{4,20},{5,21},{6,22},{7,23},{8,56},{9,... | collective-permute-start | bytes 3145736 | tf_op jit(solution)/shard_map/ppermute | solution.py:473
  49.7 21.5 %all-to-all-start.1 = ((bf16[32,64,128]{2,1,0:T(8,128)(2,1)}), bf16[32,64,128]{2,1,0:T(8,128)(2,1)}, u32[]{:S(2)}, u32[]{:S(2)}) async-start(bf16[32,64,128]{2,1,0:T(8,128)(2,1)} %bitcast.31), calls=%async_computation.1 | async-start | bytes 1048576 | tf_op jit(solution)/shard_map/all_to_all | solution.py:427
  56.2 17.7 %collective-permute-start.10 = (bf16[4096,128]{1,0:T(8,128)(2,1)S(1)}, bf16[4096,128]{1,0:T(8,128)(2,1)}, u32[]{:S(2)}, u32[]{:S(2)}) collective-permute-start(bf16[4096,128]{1,0:T(8,128)(2,1)S(1)} %bitcast.28), channel_id=1, source_target_pairs={{0,48},{1,49},{2,50},{3,51},{4,52},{5,53},{6,54},{7,55},{8,24},{9,... | collective-permute-start | bytes 3145736 | tf_op jit(solution)/shard_map/ppermute | solution.py:477
  63.8 10.0 %collective-permute-start.11 = (bf16[4096,128]{1,0:T(8,128)(2,1)S(1)}, bf16[4096,128]{1,0:T(8,128)(2,1)}, u32[]{:S(2)}, u32[]{:S(2)}) collective-permute-start(bf16[4096,128]{1,0:T(8,128)(2,1)S(1)} %collective-permute-done.7.u1), channel_id=1, source_target_pairs={{0,8},{1,9},{2,10},{3,11},{4,12},{5,13},{6,14},{7,15},{8,0},{9,1},... | collective-permute-start | bytes 3145736 | tf_op jit(solution)/shard_map/ppermute | solution.py:478
  71.2 5.9 %collective-permute-start.12 = (bf16[2048,128]{1,0:T(8,128)(2,1)}, bf16[2048,128]{1,0:T(8,128)(2,1)S(1)}, u32[]{:S(2)}, u32[]{:S(2)}) collective-permute-start(bf16[2048,128]{1,0:T(8,128)(2,1)} %bitcast.15.o2), channel_id=1, source_target_pairs={{0,8},{1,9},{2,10},{3,11},{4,12},{5,13},{6,14},{7,15},{8,0},{9,1},... | collective-permute-start | bytes 1572872 | tf_op jit(solution)/shard_map/ppermute | solution.py:483
  71.4 9.8 %collective-permute-start.9 = (bf16[2048,128]{1,0:T(8,128)(2,1)}, bf16[2048,128]{1,0:T(8,128)(2,1)S(1)}, u32[]{:S(2)}, u32[]{:S(2)}) collective-permute-start(bf16[2048,128]{1,0:T(8,128)(2,1)} %bitcast.15.o2), channel_id=1, source_target_pairs={{0,16},{1,17},{2,18},{3,19},{4,20},{5,21},{6,22},{7,23},{8,56},{9,... | collective-permute-start | bytes 1572872 | tf_op jit(solution)/shard_map/ppermute | solution.py:482
  76.9 11.2 %collective-permute-start.13 = (bf16[2048,128]{1,0:T(8,128)(2,1)}, bf16[2048,128]{1,0:T(8,128)(2,1)S(1)}, u32[]{:S(2)}, u32[]{:S(2)}) collective-permute-start(bf16[2048,128]{1,0:T(8,128)(2,1)} %bitcast.15.o2), channel_id=1, source_target_pairs={{0,48},{1,49},{2,50},{3,51},{4,52},{5,53},{6,54},{7,55},{8,24},{9,... | collective-permute-start | bytes 1572872 | tf_op jit(solution)/shard_map/ppermute | solution.py:486
  81.2 7.0 %collective-permute-start.14 = (bf16[2048,128]{1,0:T(8,128)(2,1)S(1)}, bf16[2048,128]{1,0:T(8,128)(2,1)S(1)}, u32[]{:S(2)}, u32[]{:S(2)}) collective-permute-start(bf16[2048,128]{1,0:T(8,128)(2,1)S(1)} %collective-permute-done.9.u2), channel_id=1, source_target_pairs={{0,8},{1,9},{2,10},{3,11},{4,12},{5,13},{6,14},{7,15},{8,0},{9,1},... | collective-permute-start | bytes 1572872 | tf_op jit(solution)/shard_map/ppermute | solution.py:489
  90.0 6.8 %collective-permute-start.15 = (f32[4,192]{1,0:T(4,128)S(1)}, f32[4,192]{1,0:T(4,128)S(1)}, u32[]{:S(2)}, u32[]{:S(2)}) collective-permute-start(f32[4,192]{1,0:T(4,128)S(1)} %get-tuple-element.73), channel_id=1, source_target_pairs={{0,48},{1,49},{2,50},{3,51},{4,52},{5,53},{6,54},{7,55},{8,24},{9,... | collective-permute-start | bytes 9224 | tf_op jit(solution)/shard_map/ppermute | solution.py:499
  90.1 6.7 %collective-permute-start.16 = (f32[4,192]{1,0:T(4,128)S(1)}, f32[4,192]{1,0:T(4,128)S(1)}, u32[]{:S(2)}, u32[]{:S(2)}) collective-permute-start(f32[4,192]{1,0:T(4,128)S(1)} %get-tuple-element.74), channel_id=1, source_target_pairs={{0,16},{1,17},{2,18},{3,19},{4,20},{5,21},{6,22},{7,23},{8,56},{9,... | collective-permute-start | bytes 9224 | tf_op jit(solution)/shard_map/ppermute | solution.py:499
  92.7 4.1 %collective-permute-start.17 = (f32[4,192]{1,0:T(4,128)S(1)}, f32[4,192]{1,0:T(4,128)S(1)}, u32[]{:S(2)}, u32[]{:S(2)}) collective-permute-start(f32[4,192]{1,0:T(4,128)S(1)} %get-tuple-element.75), channel_id=1, source_target_pairs={{0,8},{1,9},{2,10},{3,11},{4,12},{5,13},{6,14},{7,15},{8,0},{9,1},... | collective-permute-start | bytes 9224 | tf_op jit(solution)/shard_map/ppermute | solution.py:499
  94.0 4.4 %collective-permute-start.18 = (f32[4,192]{1,0:T(4,128)S(1)}, f32[4,192]{1,0:T(4,128)S(1)}, u32[]{:S(2)}, u32[]{:S(2)}) collective-permute-start(f32[4,192]{1,0:T(4,128)S(1)} %get-tuple-element.76), channel_id=1, source_target_pairs={{0,24},{1,25},{2,26},{3,27},{4,28},{5,29},{6,30},{7,31},{8,48},{9,... | collective-permute-start | bytes 9224 | tf_op jit(solution)/shard_map/ppermute | solution.py:499
  (2 other events, 1.4 us)

commit v11 on v9

--- a/solution.py
+++ b/solution.py
@@ -225,25 +225,42 @@
     inverses[pl.ds(name, 1), pl.ds(0, Y * part)] = to_row(jnp.concatenate(cols, axis=0))
 
 
-def meet(best, inverses, ranks, p_name, p_ref, others):
-    size = size_of(p_ref)
-    at = (pl.ds(p_name, 1), pl.ds(0, size))
-    inv_p, rank_p = to_col(inverses[at]), to_col(ranks[at])
-    p_best = jnp.full((size, 128), low, jnp.float32)
+def meet(best, inverses, ranks, ps, others):
+    sizes = [size_of(ref) for _, ref in ps]
+    inv_p, rank_p = (
+        jnp.concatenate(
+            [to_col(rows[pl.ds(name, 1), pl.ds(0, size)]) for (name, _), size in zip(ps, sizes)]
+        )
+        for rows in (inverses, ranks)
+    )
+    p_best = jnp.full((sum(sizes), 128), low, jnp.float32)
     for q_name, q_ref in others:
         q_best = []
         for j in range(0, size_of(q_ref), 256):
             at = (pl.ds(q_name, 1), pl.ds(j, 256))
-            s = dot_rows(rows_of(p_ref, 0, size), rows_of(q_ref, j, 256))
+            p = jnp.concatenate([rows_of(ref, 0, size) for (_, ref), size in zip(ps, sizes)])
+            s = dot_rows(p, rows_of(q_ref, j, 256))
             s = s * inv_p * inverses[at]
             earlier = ranks[at] < rank_p
             mine = jnp.where(earlier, s, low)
             p_best = jnp.maximum(p_best, jnp.maximum(mine[:, :128], mine[:, 128:]))
-            if q_name != p_name:
+            if q_name != ps[0][0]:
                 q_best.append(jnp.max(jnp.where(earlier, low, s), axis=0, keepdims=True))
         if q_best:
             record(best, q_name, jnp.concatenate(q_best, axis=1))
-    record(best, p_name, to_row(jnp.max(p_best, axis=1, keepdims=True)))
+    start = 0
+    for (name, _), size in zip(ps, sizes):
+        record(best, name, to_row(jnp.max(p_best[start : start + size], axis=1, keepdims=True)))
+        start += size
+
+
+def by_place(spots, run):
+    for core in range(2):
+        for side in range(2):
+
+            @pl.when((spots[0] == core) & (spots[1] == side))
+            def _():
+                run(core, side)
 
 
 def record(best, name, row):
@@ -259,49 +276,61 @@
     inverses[...] = jnp.zeros_like(inverses)
     note(inverses, O1, o1)
     note(inverses, E1, e1)
-    meet(best, inverses, ranks, O1, o1, [(O1, o1)])
 
     @pl.when(spots[0] == 0)
     def _():
-        meet(best, inverses, ranks, O1, o1, [(E1, e1)])
-
-
-def first_kernel(spots, ranks, o1, u1, v1, e1, w1, before, known, best, inverses):
+        meet(best, inverses, ranks, [(O1, o1)], [(O1, o1), (E1, e1)])
+
+    @pl.when(spots[0] != 0)
+    def _():
+        meet(best, inverses, ranks, [(O1, o1)], [(O1, o1)])
+
+
+def near_kernel(spots, ranks, o1, u1, e1, before, known, best, inverses):
     best[...] = before[...]
     inverses[...] = known[...]
     note(inverses, U1, u1)
+
+    @pl.when(spots[0] == 0)
+    def _():
+        meet(best, inverses, ranks, [(U1, u1)], [(O1, o1)])
+
+    @pl.when(spots[0] != 0)
+    def _():
+        meet(best, inverses, ranks, [(U1, u1)], [(O1, o1), (E1, e1)])
+
+
+def second_kernel(spots, ranks, o1, o2, u1, v1, e1, e2, w1, before, known, best, inverses):
+    best[...] = before[...]
+    inverses[...] = known[...]
     note(inverses, V1, v1)
     note(inverses, W1, w1)
-    meet(best, inverses, ranks, O1, o1, [(U1, u1)])
-
-    @pl.when(spots[0] == 0)
-    def _():
-        meet(best, inverses, ranks, E1, e1, [(V1, v1)])
-
-    @pl.when(spots[0] != 0)
-    def _():
-        meet(best, inverses, ranks, E1, e1, [(U1, u1)])
-
-    @pl.when(spots[1] != 0)
-    def _():
-        meet(best, inverses, ranks, U1, u1, [(V1, v1)])
-
-    @pl.when(spots[1] == 0)
-    def _():
-        meet(best, inverses, ranks, U1, u1, [(W1, w1)])
-
-
-def second_kernel(spots, ranks, o1, o2, u1, v1, e1, e2, before, known, best, inverses):
+    note(inverses, O2, o2)
+    note(inverses, E2, e2)
+    meet(best, inverses, ranks, [(O2, o2), (E2, e2)], [(O1, o1), (U1, u1), (V1, v1)])
+
+    def run(core, side):
+        meet(best, inverses, ranks, [(O2, o2)], [(O2, o2)] + [(E2, e2)] * core)
+        if side:
+            meet(best, inverses, ranks, [(V1, v1)], [(E1, e1)] * (1 - core) + [(U1, u1)])
+        else:
+            if core == 0:
+                meet(best, inverses, ranks, [(V1, v1)], [(E1, e1)])
+            meet(best, inverses, ranks, [(W1, w1)], [(U1, u1)])
+
+    by_place(spots, run)
+
+
+def third_kernel(spots, ranks, o2, u2, e2, v1, w1, before, known, best, inverses):
     best[...] = before[...]
     inverses[...] = known[...]
-    note(inverses, O2, o2)
-    note(inverses, E2, e2)
-    meet(best, inverses, ranks, O2, o2, [(O1, o1), (O2, o2), (U1, u1), (V1, v1)])
-    meet(best, inverses, ranks, E2, e2, [(O1, o1), (U1, u1), (V1, v1)])
-
-    @pl.when(spots[0] != 0)
-    def _():
-        meet(best, inverses, ranks, O2, o2, [(E2, e2)])
+    note(inverses, U2, u2)
+
+    def run(core, side):
+        others = [(O2, o2), (V1, v1) if side else (W1, w1)] + [(E2, e2)] * core
+        meet(best, inverses, ranks, [(U2, u2)], others)
+
+    by_place(spots, run)
 
 
 def give(best, name, out):
@@ -313,25 +342,6 @@
         out[at, pl.ds(PARTS[0], PARTS[1])] = pair[:, : PARTS[1]]
 
 
-def third_kernel(spots, ranks, o2, u2, e2, v1, w1, before, known, best, inverses):
-    best[...] = before[...]
-    inverses[...] = known[...]
-    note(inverses, U2, u2)
-    meet(best, inverses, ranks, U2, u2, [(O2, o2)])
-
-    @pl.when(spots[0] != 0)
-    def _():
-        meet(best, inverses, ranks, U2, u2, [(E2, e2)])
-
-    @pl.when(spots[1] != 0)
-    def _():
-        meet(best, inverses, ranks, U2, u2, [(V1, v1)])
-
-    @pl.when(spots[1] == 0)
-    def _():
-        meet(best, inverses, ranks, U2, u2, [(W1, w1)])
-
-
 def fourth_kernel(
     spots, ranks, u1, u2, v2, e2, w2, before, known, o_best, u_best, v_best, e_best, w_best,
     best, inverses,
@@ -340,18 +350,17 @@
     inverses[...] = known[...]
     note(inverses, V2, v2)
 
-    @pl.when(spots[0] == 0)
-    def _():
-        meet(best, inverses, ranks, V2, v2, [(E2, e2)])
-
-    @pl.when(spots[1] != 0)
-    def _():
-        meet(best, inverses, ranks, V2, v2, [(U1, u1), (U2, u2)])
-
-    @pl.when(spots[1] == 0)
-    def _():
-        note(inverses, W2, w2)
-        meet(best, inverses, ranks, W2, w2, [(U1, u1), (U2, u2)])
+    def run(core, side):
+        if side:
+            others = [(E2, e2)] * (1 - core) + [(U1, u1), (U2, u2)]
+            meet(best, inverses, ranks, [(V2, v2)], others)
+        else:
+            note(inverses, W2, w2)
+            if core == 0:
+                meet(best, inverses, ranks, [(V2, v2)], [(E2, e2)])
+            meet(best, inverses, ranks, [(W2, w2)], [(U1, u1), (U2, u2)])
+
+    by_place(spots, run)
 
     give(best, O1, o_best)
     give(best, U1, u_best)
@@ -469,15 +478,16 @@
     v1 = lax.ppermute(o1, ALL, behind)
     e1 = lax.ppermute(o1, ALL, swap)
     state = score(own_kernel, 8, (o1, e1), (), "own")
-    u1, o2, *state = lax.optimization_barrier((u1, o2, *state))
+    u1, *state = lax.optimization_barrier((u1, *state))
     w1 = lax.ppermute(u1, ALL, swap)
+    o2, *state = lax.optimization_barrier((o2, *state))
 
     u2 = lax.ppermute(o2, ALL, ahead)
     e2 = lax.ppermute(o2, ALL, swap)
-    state = score(first_kernel, 12, (o1, u1, v1, e1, w1), state, "first")
+    state = score(near_kernel, 6, (o1, u1, e1), state, "near")
     o2, *state = lax.optimization_barrier((o2, *state))
     v2 = lax.ppermute(o2, ALL, behind)
-    state = score(second_kernel, 14, (o1, o2, u1, v1, e1, e2), state, "second")
+    state = score(second_kernel, 20, (o1, o2, u1, v1, e1, e2, w1), state, "second")
     u2, *state = lax.optimization_barrier((u2, *state))
     w2 = lax.ppermute(u2, ALL, swap)
     state = score(third_kernel, 4, (o2, u2, e2, v1, w1), state, "third")

time: 114 us -> 112 us (0.982)
  starting transfers between devices: 48.3 us -> 46.6 us
  waiting for transfers between devices: 22.3 us -> 20.8 us
    all_to_all x2, waiting for transfers between devices: 18.1 us -> 7.4 us  [bring(): lax.all_to_all(rows.reshape(GROUPS, part, WIDTH), ('y', 'z'), split_axis=...]
    ppermute x1, waiting for transfers between devices: 0.01 us -> 9.2 us  [shards(): u1 = lax.ppermute(o1, ALL, ahead)]
    ppermute x4, starting transfers between devices: 7.02 us -> 4.72 us  [shards(): own = jnp.maximum(own, lax.ppermute(part, ALL, way))]
  transfers between devices with their start and end apart: 21 -> 21, of which waited for: 6 -> 7; matrix products, arithmetic and copies ran while one was open for 1% -> 1% of each run, Pallas kernels for 17% -> 17%
where the time goes in v11:
time: 112 us; the launch traced here: 111 us
  starting transfers between devices  46.6 us (42%)
  Pallas kernels  27.4 us (24%)
  waiting for transfers between devices  20.8 us (19%)
  blocking collectives  14.4 us (13%)
  local copies, waits for them, and re-layouts  1.48 us (1%)
    all_to_all x2, starting transfers between devices, bring(): lax.all_to_all(rows.reshape(GROUPS, part, WIDTH), ('y', 'z'), split_axis=...  17 us
    pallas_call x5, Pallas kernels, scores_call(): pl.pallas_call(kernel, out_shape=jax.tree.map(lambda dims: jax.ShapeDtype...  15.8 us
    all_to_all x1, blocking collectives, shards(): lax.all_to_all(jnp.broadcast_to(own[:, None], (Y, Z, CAP)).reshape(GROUPS...  14.4 us
    ppermute x1, waiting for transfers between devices, shards(): u1 = lax.ppermute(o1, ALL, ahead)  9.2 us
    all_to_all x2, waiting for transfers between devices, bring(): lax.all_to_all(rows.reshape(GROUPS, part, WIDTH), ('y', 'z'), split_axis=...  7.4 us
    pallas_call x1, Pallas kernels, place(): pl.pallas_call(place_kernel, out_shape=(jax.ShapeDtypeStruct((GROUPS * PA...  5.4 us
    ppermute x1, starting transfers between devices, shards(): e1 = lax.ppermute(o1, ALL, swap)  4.97 us
    ppermute x3, starting transfers between devices, shards(): row = lax.ppermute(row, ALL, routes(lambda y, x, c, z: (y + j, x, c, z)))  4.89 us
  transfers between devices with their start and end apart: 21, of which 7 were waited for; matrix products, arithmetic and copies ran while one was open for 1% of the time, Pallas kernels for 17%

profile of v11, /device:TPU:1, one launch (start us, length us, event | category | flops | bytes accessed | tf_op | source)
XLA Modules:
  0.0 111.2 jit_solution(6919993157564955511)
XLA Ops:
  0.0 5.4 %place.1 = (bf16[4096,128]{1,0:T(8,128)(2,1)}, s32[24,128]{1,0:T(8,128)}) custom-call(s32[24,128]{1,0:T(8,128)} %bitcast.36, bf16[3072,128]{1,0:T(8,128)(2,1)} %rows_ref.1), custom_call_target="tpu_custom_call" | custom-call | tf_op jit(solution)/shard_map/place/pallas_call | solution.py:85
  5.4 12.2 %all-to-all-start = ((bf16[32,128,128]{2,1,0:T(8,128)(2,1)}), bf16[32,128,128]{2,1,0:T(8,128)(2,1)S(1)}, u32[]{:S(2)}, u32[]{:S(2)}) async-start(bf16[32,128,128]{2,1,0:T(8,128)(2,1)} %bitcast.43), calls=%async_computation | async-start | bytes 2097152 | tf_op jit(solution)/shard_map/all_to_all | solution.py:431
  20.6 2.4 %collective-permute-start.1 = (f32[1,192]{1,0:T(1,128)S(1)}, f32[1,192]{1,0:T(1,128)S(1)}, u32[]{:S(2)}, u32[]{:S(2)}) collective-permute-start(f32[1,192]{1,0:T(1,128)S(1)} %get-tuple-element.75), channel_id=1, source_target_pairs={{0,128},{1,129},{2,130},{3,131},{4,132},{5,133},{6,134},{7,135},{8... | collective-permute-start | bytes 2312 | tf_op jit(solution)/shard_map/ppermute | solution.py:446
  26.5 2.6 %collective-permute-start.3 = (f32[2,512]{1,0:T(2,128)S(1)}, f32[2,512]{1,0:T(2,128)S(1)}, u32[]{:S(2)}, u32[]{:S(2)}) collective-permute-start(f32[2,512]{1,0:T(2,128)S(1)} %pad_maximum_fusion.1), channel_id=1, source_target_pairs={{0,16},{1,17},{2,18},{3,19},{4,20},{5,21},{6,22},{7,23},{8,56},{9,... | collective-permute-start | bytes 12296 | tf_op jit(solution)/shard_map/ppermute | solution.py:456
  29.0 3.4 %collective-permute-start.5 = (f32[2,512]{1,0:T(2,128)S(1)}, f32[2,512]{1,0:T(2,128)S(1)}, u32[]{:S(2)}, u32[]{:S(2)}) collective-permute-start(f32[2,512]{1,0:T(2,128)S(1)} %pad_maximum_fusion.1), channel_id=1, source_target_pairs={{0,8},{1,9},{2,10},{3,11},{4,12},{5,13},{6,14},{7,15},{8,0},{9,1},... | collective-permute-start | bytes 12296 | tf_op jit(solution)/shard_map/ppermute | solution.py:462
  32.4 1.6 %collective-permute-start.6 = (f32[2,512]{1,0:T(2,128)S(1)}, f32[2,512]{1,0:T(2,128)S(1)}, u32[]{:S(2)}, u32[]{:S(2)}) collective-permute-start(f32[2,512]{1,0:T(2,128)S(1)} %collective-permute-done.3), channel_id=1, source_target_pairs={{0,8},{1,9},{2,10},{3,11},{4,12},{5,13},{6,14},{7,15},{8,0},{9,1},... | collective-permute-start | bytes 12296 | tf_op jit(solution)/shard_map/ppermute | solution.py:463
  34.1 4.2 %place_rest.1 = bf16[2048,128]{1,0:T(8,128)(2,1)} custom-call(s32[24,128]{1,0:T(8,128)S(1)} %bitcast.38, s32[24,128]{1,0:T(8,128)S(1)} %copy-done.2, bf16[3072,128]{1,0:T(8,128)(2,1)S(1)} %copy-done), custom_call_target="tpu_custom_call" | custom-call | tf_op jit(solution)/shard_map/place_rest/pallas_call | solution.py:126
  38.4 3.8 %all-to-all-done = bf16[32,128,128]{2,1,0:T(8,128)(2,1)S(1)} async-done(((bf16[32,128,128]{2,1,0:T(8,128)(2,1)}), bf16[32,128,128]{2,1,0:T(8,128)(2,1)S(1)}, u32[]{:S(2)}, u32[]{:S(2)}) %all-to-all-start) | async-done | bytes 1048608 | tf_op jit(solution)/shard_map/all_to_all | solution.py:431
  42.2 5.0 %collective-permute-start.8 = (bf16[4096,128]{1,0:T(8,128)(2,1)S(1)}, bf16[4096,128]{1,0:T(8,128)(2,1)}, u32[]{:S(2)}, u32[]{:S(2)}) collective-permute-start(bf16[4096,128]{1,0:T(8,128)(2,1)S(1)} %bitcast.25), channel_id=1, source_target_pairs={{0,8},{1,9},{2,10},{3,11},{4,12},{5,13},{6,14},{7,15},{8,0},{9,1},... | collective-permute-start | bytes 3145736 | tf_op jit(solution)/shard_map/ppermute | solution.py:479
  47.2 2.5 %collective-permute-start.7 = (bf16[4096,128]{1,0:T(8,128)(2,1)S(1)}, bf16[4096,128]{1,0:T(8,128)(2,1)S(1)}, u32[]{:S(2)}, u32[]{:S(2)}) collective-permute-start(bf16[4096,128]{1,0:T(8,128)(2,1)S(1)} %bitcast.26), channel_id=1, source_target_pairs={{0,16},{1,17},{2,18},{3,19},{4,20},{5,21},{6,22},{7,23},{8,56},{9,... | collective-permute-start | bytes 3145736 | tf_op jit(solution)/shard_map/ppermute | solution.py:477
  49.7 4.8 %all-to-all-start.1 = ((bf16[32,64,128]{2,1,0:T(8,128)(2,1)}), bf16[32,64,128]{2,1,0:T(8,128)(2,1)S(1)}, u32[]{:S(2)}, u32[]{:S(2)}) async-start(bf16[32,64,128]{2,1,0:T(8,128)(2,1)} %bitcast.14), calls=%async_computation.1 | async-start | bytes 1048576 | tf_op jit(solution)/shard_map/all_to_all | solution.py:431
  54.6 2.7 %own.1 = (f32[16,512]{1,0:T(8,128)S(1)}, f32[16,512]{1,0:T(8,128)S(1)}) custom-call(s32[2]{0:T(128)S(1)} %pad_add_fusion.spots, f32[16,512]{1,0:T(8,128)S(1)} %concatenate.8.ranks, bf16[4096,128]{1,0:T(8,128)(2,1)S(1)} %bitcast.28, bf16[4096,128]{1,0:T(8,128)(2,1)} %collective-permute-done.8.e1), custom_call_target="tpu_custom_call" | custom-call | flops 1073741824 | bytes 4194304 | tf_op jit(solution)/shard_map/own/pallas_call | solution.py:377
  57.3 9.2 %collective-permute-done.7.u1 = bf16[4096,128]{1,0:T(8,128)(2,1)S(1)} collective-permute-done((bf16[4096,128]{1,0:T(8,128)(2,1)S(1)}, bf16[4096,128]{1,0:T(8,128)(2,1)S(1)}, u32[]{:S(2)}, u32[]{:S(2)}) %collective-permute-start.7) | collective-permute-done | bytes 1048608 | tf_op jit(solution)/shard_map/ppermute | solution.py:477
  67.5 3.6 %all-to-all-done.1 = bf16[32,64,128]{2,1,0:T(8,128)(2,1)S(1)} async-done(((bf16[32,64,128]{2,1,0:T(8,128)(2,1)}), bf16[32,64,128]{2,1,0:T(8,128)(2,1)S(1)}, u32[]{:S(2)}, u32[]{:S(2)}) %all-to-all-start.1) | async-done | bytes 524320 | tf_op jit(solution)/shard_map/all_to_all | solution.py:431
  71.3 1.5 %collective-permute-start.9 = (bf16[2048,128]{1,0:T(8,128)(2,1)S(1)}, bf16[2048,128]{1,0:T(8,128)(2,1)S(1)}, u32[]{:S(2)}, u32[]{:S(2)}) collective-permute-start(bf16[2048,128]{1,0:T(8,128)(2,1)S(1)} %bitcast.32), channel_id=1, source_target_pairs={{0,16},{1,17},{2,18},{3,19},{4,20},{5,21},{6,22},{7,23},{8,56},{9,... | collective-permute-start | bytes 1572872 | tf_op jit(solution)/shard_map/ppermute | solution.py:485
  72.8 3.1 %near.1 = (f32[16,512]{1,0:T(8,128)S(1)}, f32[16,512]{1,0:T(8,128)S(1)}) custom-call(s32[2]{0:T(128)S(1)} %pad_add_fusion.spots, f32[16,512]{1,0:T(8,128)S(1)} %concatenate.8.ranks, bf16[4096,128]{1,0:T(8,128)(2,1)S(1)} %bitcast.29, bf16[4096,128]{1,0:T(8,128)(2,1)S(1)} %collective-permute-done.7.u1, bf16[4096,128]{1,0:T(8,128)(2,1)} %collective-permute-done.8.e1, ...), custom_call_target="tpu_custom_call" | custom-call | flops 805306368 | bytes 4194304 | tf_op jit(solution)/shard_map/near/pallas_call | solution.py:377
  76.0 5.5 %second.1 = (f32[16,512]{1,0:T(8,128)S(1)}, f32[16,512]{1,0:T(8,128)S(1)}) custom-call(s32[2]{0:T(128)S(1)} %pad_add_fusion.spots, f32[16,512]{1,0:T(8,128)S(1)} %concatenate.8.ranks, bf16[4096,128]{1,0:T(8,128)(2,1)S(1)} %bitcast.30, bf16[2048,128]{1,0:T(8,128)(2,1)S(1)} %bitcast.34, bf16[4096,128]{1,0:T(8,128)(2,1)S(1)} %collective-permute-done.7.u1, ...), custom_call_target="tpu_custom_call" | custom-call | flops 2684354560 | bytes 4194304 | tf_op jit(solution)/shard_map/second/pallas_call | solution.py:377
  81.5 2.2 %collective-permute-start.14 = (bf16[2048,128]{1,0:T(8,128)(2,1)S(1)}, bf16[2048,128]{1,0:T(8,128)(2,1)S(1)}, u32[]{:S(2)}, u32[]{:S(2)}) collective-permute-start(bf16[2048,128]{1,0:T(8,128)(2,1)S(1)} %collective-permute-done.9.u2), channel_id=1, source_target_pairs={{0,8},{1,9},{2,10},{3,11},{4,12},{5,13},{6,14},{7,15},{8,0},{9,1},... | collective-permute-start | bytes 1572872 | tf_op jit(solution)/shard_map/ppermute | solution.py:492
  83.7 2.8 %third.1 = (f32[16,512]{1,0:T(8,128)S(1)}, f32[16,512]{1,0:T(8,128)S(1)}) custom-call(s32[2]{0:T(128)S(1)} %pad_add_fusion.spots, f32[16,512]{1,0:T(8,128)S(1)} %concatenate.8.ranks, bf16[2048,128]{1,0:T(8,128)(2,1)S(1)} %bitcast.35, bf16[2048,128]{1,0:T(8,128)(2,1)S(1)} %collective-permute-done.9.u2, bf16[2048,128]{1,0:T(8,128)(2,1)S(1)} %collective-permute-done.11.e2, ...), custom_call_target="tpu_custom_call" | custom-call | flops 536870912 | bytes 4194304 | tf_op jit(solution)/shard_map/third/pallas_call | solution.py:377
  86.9 1.7 %fourth.1 = (f32[4,192]{1,0:T(4,128)S(1)}, f32[4,192]{1,0:T(4,128)S(1)}, f32[4,192]{1,0:T(4,128)S(1)}, f32[4,192]{1,0:T(4,128)S(1)}, f32[4,192]{1,0:T(4,128)S(1)}) custom-call(s32[2]{0:T(128)S(1)} %pad_add_fusion.spots, f32[16,512]{1,0:T(8,128)S(1)} %concatenate.8.ranks, bf16[4096,128]{1,0:T(8,128)(2,1)S(1)} %collective-permute-done.7.u1, ...), custom_call_target="tpu_custom_call" | custom-call | flops 536870912 | bytes 4194304 | tf_op jit(solution)/shard_map/fourth/pallas_call | solution.py:377
  88.6 2.7 %collective-permute-start.16 = (f32[4,192]{1,0:T(4,128)S(1)}, f32[4,192]{1,0:T(4,128)S(1)}, u32[]{:S(2)}, u32[]{:S(2)}) collective-permute-start(f32[4,192]{1,0:T(4,128)S(1)} %get-tuple-element.70), channel_id=1, source_target_pairs={{0,16},{1,17},{2,18},{3,19},{4,20},{5,21},{6,22},{7,23},{8,56},{9,... | collective-permute-start | bytes 9224 | tf_op jit(solution)/shard_map/ppermute | solution.py:502
  91.3 2.0 %collective-permute-start.18 = (f32[4,192]{1,0:T(4,128)S(1)}, f32[4,192]{1,0:T(4,128)S(1)}, u32[]{:S(2)}, u32[]{:S(2)}) collective-permute-start(f32[4,192]{1,0:T(4,128)S(1)} %get-tuple-element.72), channel_id=1, source_target_pairs={{0,24},{1,25},{2,26},{3,27},{4,28},{5,29},{6,30},{7,31},{8,48},{9,... | collective-permute-start | bytes 9224 | tf_op jit(solution)/shard_map/ppermute | solution.py:502
  93.3 2.2 %collective-permute-done.18 = f32[4,192]{1,0:T(4,128)S(1)} collective-permute-done((f32[4,192]{1,0:T(4,128)S(1)}, f32[4,192]{1,0:T(4,128)S(1)}, u32[]{:S(2)}, u32[]{:S(2)}) %collective-permute-start.18) | collective-permute-done | bytes 3104 | tf_op jit(solution)/shard_map/ppermute | solution.py:502
  95.6 14.4 %all_to_all.21 = f32[32,1,192]{2,1,0:T(1,128)S(1)} all-to-all(f32[32,1,192]{2,1,0:T(1,128)S(1)} %all_to_all.15), channel_id=1, replica_groups=mesh['y'=4,'x'=4,'core'=2,'z'=8] {'y','z'}, dimensions={0} | all-to-all | bytes 49152 | tf_op jit(solution)/shard_map/all_to_all | solution.py:503
  (54 shorter events, 9.5 us)
Async XLA Ops:
  5.4 28.7 %copy-start = (bf16[3072,128]{1,0:T(8,128)(2,1)S(1)}, bf16[3072,128]{1,0:T(8,128)(2,1)}, u32[]{:S(2)}) copy-start(bf16[3072,128]{1,0:T(8,128)(2,1)} %rows_ref.1) | copy-start | bytes 2359300
  5.4 36.8 %all-to-all-start = ((bf16[32,128,128]{2,1,0:T(8,128)(2,1)}), bf16[32,128,128]{2,1,0:T(8,128)(2,1)S(1)}, u32[]{:S(2)}, u32[]{:S(2)}) async-start(bf16[32,128,128]{2,1,0:T(8,128)(2,1)} %bitcast.43), calls=%async_computation | async-start | bytes 2097152 | tf_op jit(solution)/shard_map/all_to_all | solution.py:431
  17.7 0.7 copy-start.2
  17.7 0.7 copy-start.1
  19.3 4.9 %collective-permute-start = (f32[1,192]{1,0:T(1,128)S(1)}, f32[1,192]{1,0:T(1,128)S(1)}, u32[]{:S(2)}, u32[]{:S(2)}) collective-permute-start(f32[1,192]{1,0:T(1,128)S(1)} %get-tuple-element.76), channel_id=1, source_target_pairs={{0,64},{1,65},{2,66},{3,67},{4,68},{5,69},{6,70},{7,71},{8,72},{9,... | collective-permute-start | bytes 2312 | tf_op jit(solution)/shard_map/ppermute | solution.py:446
  20.6 4.0 %collective-permute-start.1 = (f32[1,192]{1,0:T(1,128)S(1)}, f32[1,192]{1,0:T(1,128)S(1)}, u32[]{:S(2)}, u32[]{:S(2)}) collective-permute-start(f32[1,192]{1,0:T(1,128)S(1)} %get-tuple-element.75), channel_id=1, source_target_pairs={{0,128},{1,129},{2,130},{3,131},{4,132},{5,133},{6,134},{7,135},{8... | collective-permute-start | bytes 2312 | tf_op jit(solution)/shard_map/ppermute | solution.py:446
  23.1 2.7 %collective-permute-start.2 = (f32[1,192]{1,0:T(1,128)S(1)}, f32[1,192]{1,0:T(1,128)S(1)}, u32[]{:S(2)}, u32[]{:S(2)}) collective-permute-start(f32[1,192]{1,0:T(1,128)S(1)} %get-tuple-element.74), channel_id=1, source_target_pairs={{0,192},{1,193},{2,194},{3,195},{4,196},{5,197},{6,198},{7,199},{8... | collective-permute-start | bytes 2312 | tf_op jit(solution)/shard_map/ppermute | solution.py:446
  26.5 6.0 %collective-permute-start.3 = (f32[2,512]{1,0:T(2,128)S(1)}, f32[2,512]{1,0:T(2,128)S(1)}, u32[]{:S(2)}, u32[]{:S(2)}) collective-permute-start(f32[2,512]{1,0:T(2,128)S(1)} %pad_maximum_fusion.1), channel_id=1, source_target_pairs={{0,16},{1,17},{2,18},{3,19},{4,20},{5,21},{6,22},{7,23},{8,56},{9,... | collective-permute-start | bytes 12296 | tf_op jit(solution)/shard_map/ppermute | solution.py:456
  29.0 9.3 %collective-permute-start.4 = (f32[2,512]{1,0:T(2,128)S(1)}, f32[2,512]{1,0:T(2,128)S(1)}, u32[]{:S(2)}, u32[]{:S(2)}) collective-permute-start(f32[2,512]{1,0:T(2,128)S(1)} %pad_maximum_fusion.1), channel_id=1, source_target_pairs={{0,48},{1,49},{2,50},{3,51},{4,52},{5,53},{6,54},{7,55},{8,24},{9,... | collective-permute-start | bytes 12296 | tf_op jit(solution)/shard_map/ppermute | solution.py:461
  29.0 9.3 %collective-permute-start.5 = (f32[2,512]{1,0:T(2,128)S(1)}, f32[2,512]{1,0:T(2,128)S(1)}, u32[]{:S(2)}, u32[]{:S(2)}) collective-permute-start(f32[2,512]{1,0:T(2,128)S(1)} %pad_maximum_fusion.1), channel_id=1, source_target_pairs={{0,8},{1,9},{2,10},{3,11},{4,12},{5,13},{6,14},{7,15},{8,0},{9,1},... | collective-permute-start | bytes 12296 | tf_op jit(solution)/shard_map/ppermute | solution.py:462
  32.4 5.9 %collective-permute-start.6 = (f32[2,512]{1,0:T(2,128)S(1)}, f32[2,512]{1,0:T(2,128)S(1)}, u32[]{:S(2)}, u32[]{:S(2)}) collective-permute-start(f32[2,512]{1,0:T(2,128)S(1)} %collective-permute-done.3), channel_id=1, source_target_pairs={{0,8},{1,9},{2,10},{3,11},{4,12},{5,13},{6,14},{7,15},{8,0},{9,1},... | collective-permute-start | bytes 12296 | tf_op jit(solution)/shard_map/ppermute | solution.py:463
  42.2 12.3 %collective-permute-start.8 = (bf16[4096,128]{1,0:T(8,128)(2,1)S(1)}, bf16[4096,128]{1,0:T(8,128)(2,1)}, u32[]{:S(2)}, u32[]{:S(2)}) collective-permute-start(bf16[4096,128]{1,0:T(8,128)(2,1)S(1)} %bitcast.25), channel_id=1, source_target_pairs={{0,8},{1,9},{2,10},{3,11},{4,12},{5,13},{6,14},{7,15},{8,0},{9,1},... | collective-permute-start | bytes 3145736 | tf_op jit(solution)/shard_map/ppermute | solution.py:479
  47.2 19.3 %collective-permute-start.7 = (bf16[4096,128]{1,0:T(8,128)(2,1)S(1)}, bf16[4096,128]{1,0:T(8,128)(2,1)S(1)}, u32[]{:S(2)}, u32[]{:S(2)}) collective-permute-start(bf16[4096,128]{1,0:T(8,128)(2,1)S(1)} %bitcast.26), channel_id=1, source_target_pairs={{0,16},{1,17},{2,18},{3,19},{4,20},{5,21},{6,22},{7,23},{8,56},{9,... | collective-permute-start | bytes 3145736 | tf_op jit(solution)/shard_map/ppermute | solution.py:477
  49.7 21.4 %all-to-all-start.1 = ((bf16[32,64,128]{2,1,0:T(8,128)(2,1)}), bf16[32,64,128]{2,1,0:T(8,128)(2,1)S(1)}, u32[]{:S(2)}, u32[]{:S(2)}) async-start(bf16[32,64,128]{2,1,0:T(8,128)(2,1)} %bitcast.14), calls=%async_computation.1 | async-start | bytes 1048576 | tf_op jit(solution)/shard_map/all_to_all | solution.py:431
  54.5 21.5 %collective-permute-start.10 = (bf16[4096,128]{1,0:T(8,128)(2,1)S(1)}, bf16[4096,128]{1,0:T(8,128)(2,1)}, u32[]{:S(2)}, u32[]{:S(2)}) collective-permute-start(bf16[4096,128]{1,0:T(8,128)(2,1)S(1)} %bitcast.27), channel_id=1, source_target_pairs={{0,48},{1,49},{2,50},{3,51},{4,52},{5,53},{6,54},{7,55},{8,24},{9,... | collective-permute-start | bytes 3145736 | tf_op jit(solution)/shard_map/ppermute | solution.py:478
  66.5 9.5 %collective-permute-start.12 = (bf16[4096,128]{1,0:T(8,128)(2,1)S(1)}, bf16[4096,128]{1,0:T(8,128)(2,1)}, u32[]{:S(2)}, u32[]{:S(2)}) collective-permute-start(bf16[4096,128]{1,0:T(8,128)(2,1)S(1)} %collective-permute-done.7.u1), channel_id=1, source_target_pairs={{0,8},{1,9},{2,10},{3,11},{4,12},{5,13},{6,14},{7,15},{8,0},{9,1},... | collective-permute-start | bytes 3145736 | tf_op jit(solution)/shard_map/ppermute | solution.py:482
  71.1 4.9 %collective-permute-start.11 = (bf16[2048,128]{1,0:T(8,128)(2,1)S(1)}, bf16[2048,128]{1,0:T(8,128)(2,1)S(1)}, u32[]{:S(2)}, u32[]{:S(2)}) collective-permute-start(bf16[2048,128]{1,0:T(8,128)(2,1)S(1)} %bitcast.31), channel_id=1, source_target_pairs={{0,8},{1,9},{2,10},{3,11},{4,12},{5,13},{6,14},{7,15},{8,0},{9,1},... | collective-permute-start | bytes 1572872 | tf_op jit(solution)/shard_map/ppermute | solution.py:486
  71.3 10.3 %collective-permute-start.9 = (bf16[2048,128]{1,0:T(8,128)(2,1)S(1)}, bf16[2048,128]{1,0:T(8,128)(2,1)S(1)}, u32[]{:S(2)}, u32[]{:S(2)}) collective-permute-start(bf16[2048,128]{1,0:T(8,128)(2,1)S(1)} %bitcast.32), channel_id=1, source_target_pairs={{0,16},{1,17},{2,18},{3,19},{4,20},{5,21},{6,22},{7,23},{8,56},{9,... | collective-permute-start | bytes 1572872 | tf_op jit(solution)/shard_map/ppermute | solution.py:485
  75.9 11.0 %collective-permute-start.13 = (bf16[2048,128]{1,0:T(8,128)(2,1)S(1)}, bf16[2048,128]{1,0:T(8,128)(2,1)S(1)}, u32[]{:S(2)}, u32[]{:S(2)}) collective-permute-start(bf16[2048,128]{1,0:T(8,128)(2,1)S(1)} %bitcast.33), channel_id=1, source_target_pairs={{0,48},{1,49},{2,50},{3,51},{4,52},{5,53},{6,54},{7,55},{8,24},{9,... | collective-permute-start | bytes 1572872 | tf_op jit(solution)/shard_map/ppermute | solution.py:489
  81.5 5.4 %collective-permute-start.14 = (bf16[2048,128]{1,0:T(8,128)(2,1)S(1)}, bf16[2048,128]{1,0:T(8,128)(2,1)S(1)}, u32[]{:S(2)}, u32[]{:S(2)}) collective-permute-start(bf16[2048,128]{1,0:T(8,128)(2,1)S(1)} %collective-permute-done.9.u2), channel_id=1, source_target_pairs={{0,8},{1,9},{2,10},{3,11},{4,12},{5,13},{6,14},{7,15},{8,0},{9,1},... | collective-permute-start | bytes 1572872 | tf_op jit(solution)/shard_map/ppermute | solution.py:492
  88.6 4.7 %collective-permute-start.15 = (f32[4,192]{1,0:T(4,128)S(1)}, f32[4,192]{1,0:T(4,128)S(1)}, u32[]{:S(2)}, u32[]{:S(2)}) collective-permute-start(f32[4,192]{1,0:T(4,128)S(1)} %get-tuple-element.69), channel_id=1, source_target_pairs={{0,48},{1,49},{2,50},{3,51},{4,52},{5,53},{6,54},{7,55},{8,24},{9,... | collective-permute-start | bytes 9224 | tf_op jit(solution)/shard_map/ppermute | solution.py:502
  88.6 4.7 %collective-permute-start.16 = (f32[4,192]{1,0:T(4,128)S(1)}, f32[4,192]{1,0:T(4,128)S(1)}, u32[]{:S(2)}, u32[]{:S(2)}) collective-permute-start(f32[4,192]{1,0:T(4,128)S(1)} %get-tuple-element.70), channel_id=1, source_target_pairs={{0,16},{1,17},{2,18},{3,19},{4,20},{5,21},{6,22},{7,23},{8,56},{9,... | collective-permute-start | bytes 9224 | tf_op jit(solution)/shard_map/ppermute | solution.py:502
  91.3 2.0 %collective-permute-start.17 = (f32[4,192]{1,0:T(4,128)S(1)}, f32[4,192]{1,0:T(4,128)S(1)}, u32[]{:S(2)}, u32[]{:S(2)}) collective-permute-start(f32[4,192]{1,0:T(4,128)S(1)} %get-tuple-element.71), channel_id=1, source_target_pairs={{0,8},{1,9},{2,10},{3,11},{4,12},{5,13},{6,14},{7,15},{8,0},{9,1},... | collective-permute-start | bytes 9224 | tf_op jit(solution)/shard_map/ppermute | solution.py:502
  91.3 4.2 %collective-permute-start.18 = (f32[4,192]{1,0:T(4,128)S(1)}, f32[4,192]{1,0:T(4,128)S(1)}, u32[]{:S(2)}, u32[]{:S(2)}) collective-permute-start(f32[4,192]{1,0:T(4,128)S(1)} %get-tuple-element.72), channel_id=1, source_target_pairs={{0,24},{1,25},{2,26},{3,27},{4,28},{5,29},{6,30},{7,31},{8,48},{9,... | collective-permute-start | bytes 9224 | tf_op jit(solution)/shard_map/ppermute | solution.py:502
  (1 other events, 0.7 us)

commit v12 on v11

--- a/solution.py
+++ b/solution.py
@@ -333,9 +333,9 @@
     by_place(spots, run)
 
 
-def give(best, name, out):
+def give(best, name, out, start):
     for y in range(Y):
-        at = pl.ds(y, 1)
+        at = pl.ds(start + y, 1)
         out[at, pl.ds(0, PARTS[0])] = best[pl.ds(name, 1), pl.ds(y * PARTS[0], PARTS[0])]
         pair = best[pl.ds(name + 1, 1), pl.ds(y // 2 * 128, 128)]
         pair = pltpu.roll(pair, 64, 1) if y % 2 else pair
@@ -343,8 +343,7 @@
 
 
 def fourth_kernel(
-    spots, ranks, u1, u2, v2, e2, w2, before, known, o_best, u_best, v_best, e_best, w_best,
-    best, inverses,
+    spots, ranks, u1, u2, v2, e2, w2, before, known, mine, others, v_best, best, inverses
 ):
     best[...] = before[...]
     inverses[...] = known[...]
@@ -362,11 +361,11 @@
 
     by_place(spots, run)
 
-    give(best, O1, o_best)
-    give(best, U1, u_best)
-    give(best, V1, v_best)
-    give(best, E1, e_best)
-    give(best, W1, w_best)
+    give(best, O1, mine, 0)
+    give(best, U1, mine, Y)
+    give(best, E1, others, 0)
+    give(best, W1, others, Y)
+    give(best, V1, v_best, 0)
 
 
 def is_dims(item):
@@ -492,14 +491,14 @@
     w2 = lax.ppermute(u2, ALL, swap)
     state = score(third_kernel, 4, (o2, u2, e2, v1, w1), state, "third")
     v2, *state = lax.optimization_barrier((v2, *state))
-    own, *others = score(
-        fourth_kernel, 4, (u1, u2, v2, e2, w2), state, "fourth", [(Y, CAP)] * 5,
-        [pltpu.VMEM(wide, jnp.float32)] * 2,
-    )
-
-    across = routes(lambda y, x, c, z: (y, x + 1 - 2 * c, 1 - c, z))
-    for part, way in zip(others, (behind, ahead, swap, across)):
-        own = jnp.maximum(own, lax.ppermute(part, ALL, way))
+    mine, others, v_best = score(
+        fourth_kernel, 4, (u1, u2, v2, e2, w2), state, "fourth",
+        [(2 * Y, CAP), (2 * Y, CAP), (Y, CAP)], [pltpu.VMEM(wide, jnp.float32)] * 2,
+    )
+    v_best = lax.ppermute(v_best, ALL, ahead)
+    mine = jnp.maximum(mine, lax.ppermute(others, ALL, swap))
+    own = jnp.maximum(mine[:Y], v_best)
+    own = jnp.maximum(own, lax.ppermute(mine[Y:], ALL, behind))
     table = lax.all_to_all(
         jnp.broadcast_to(own[:, None], (Y, Z, CAP)).reshape(GROUPS, CAP),
         ("y", "z"), split_axis=0, concat_axis=0, tiled=True,

time: 112 us -> 111 us (level)
  starting transfers between devices: 46.6 us -> 43.8 us
  waiting for transfers between devices: 20.8 us -> 22 us
    ppermute x4 -> x3, starting transfers between devices: 4.72 us -> 1.68 us  [the longest x1 1.56 us: shards(): v_best = lax.ppermute(v_best, ALL, ahead)]
    ppermute x4 -> x3, waiting for transfers between devices: 2.22 us -> 3.66 us  [the longest x1 2.78 us: shards(): own = jnp.maximum(own, lax.ppermute(mine[Y:], ALL, behind))]
  transfers between devices with their start and end apart: 21 -> 20, of which waited for: 7 -> 8; matrix products, arithmetic and copies ran while one was open for 1% -> 1% of each run, Pallas kernels for 17% -> 18%
where the time goes in v12:
time: 111 us; the launch traced here: 109 us
  starting transfers between devices  43.8 us (39%)
  Pallas kernels  27.5 us (25%)
  waiting for transfers between devices  22 us (20%)
  blocking collectives  14 us (13%)
  local copies, waits for them, and re-layouts  1.49 us (1%)
    all_to_all x2, starting transfers between devices, bring(): lax.all_to_all(rows.reshape(GROUPS, part, WIDTH), ('y', 'z'), split_axis=...  17 us
    pallas_call x5, Pallas kernels, scores_call(): pl.pallas_call(kernel, out_shape=jax.tree.map(lambda dims: jax.ShapeDtype...  15.8 us
    all_to_all x1, blocking collectives, shards(): lax.all_to_all(jnp.broadcast_to(own[:, None], (Y, Z, CAP)).reshape(GROUPS...  14 us
    ppermute x1, waiting for transfers between devices, shards(): u1 = lax.ppermute(o1, ALL, ahead)  9.21 us
    all_to_all x2, waiting for transfers between devices, bring(): lax.all_to_all(rows.reshape(GROUPS, part, WIDTH), ('y', 'z'), split_axis=...  7.39 us
    pallas_call x1, Pallas kernels, place(): pl.pallas_call(place_kernel, out_shape=(jax.ShapeDtypeStruct((GROUPS * PA...  5.41 us
    ppermute x1, starting transfers between devices, shards(): e1 = lax.ppermute(o1, ALL, swap)  4.97 us
    ppermute x3, starting transfers between devices, shards(): row = lax.ppermute(row, ALL, routes(lambda y, x, c, z: (y + j, x, c, z)))  4.89 us
  transfers between devices with their start and end apart: 20, of which 8 were waited for; matrix products, arithmetic and copies ran while one was open for 1% of the time, Pallas kernels for 18%

profile of v12, /device:TPU:1, one launch (start us, length us, event | category | flops | bytes accessed | tf_op | source)
XLA Modules:
  0.0 109.2 jit_solution(15746684838508610247)
XLA Ops:
  0.0 5.4 %place.1 = (bf16[4096,128]{1,0:T(8,128)(2,1)}, s32[24,128]{1,0:T(8,128)}) custom-call(s32[24,128]{1,0:T(8,128)} %bitcast.36, bf16[3072,128]{1,0:T(8,128)(2,1)} %rows_ref.1), custom_call_target="tpu_custom_call" | custom-call | tf_op jit(solution)/shard_map/place/pallas_call | solution.py:85
  5.4 12.2 %all-to-all-start = ((bf16[32,128,128]{2,1,0:T(8,128)(2,1)}), bf16[32,128,128]{2,1,0:T(8,128)(2,1)S(1)}, u32[]{:S(2)}, u32[]{:S(2)}) async-start(bf16[32,128,128]{2,1,0:T(8,128)(2,1)} %bitcast.43), calls=%async_computation | async-start | bytes 2097152 | tf_op jit(solution)/shard_map/all_to_all | solution.py:430
  19.3 1.3 %collective-permute-start = (f32[1,192]{1,0:T(1,128)S(1)}, f32[1,192]{1,0:T(1,128)S(1)}, u32[]{:S(2)}, u32[]{:S(2)}) collective-permute-start(f32[1,192]{1,0:T(1,128)S(1)} %get-tuple-element.72), channel_id=1, source_target_pairs={{0,64},{1,65},{2,66},{3,67},{4,68},{5,69},{6,70},{7,71},{8,72},{9,... | collective-permute-start | bytes 2312 | tf_op jit(solution)/shard_map/ppermute | solution.py:445
  20.6 2.4 %collective-permute-start.1 = (f32[1,192]{1,0:T(1,128)S(1)}, f32[1,192]{1,0:T(1,128)S(1)}, u32[]{:S(2)}, u32[]{:S(2)}) collective-permute-start(f32[1,192]{1,0:T(1,128)S(1)} %get-tuple-element.71), channel_id=1, source_target_pairs={{0,128},{1,129},{2,130},{3,131},{4,132},{5,133},{6,134},{7,135},{8... | collective-permute-start | bytes 2312 | tf_op jit(solution)/shard_map/ppermute | solution.py:445
  26.2 2.6 %collective-permute-start.3 = (f32[2,512]{1,0:T(2,128)S(1)}, f32[2,512]{1,0:T(2,128)S(1)}, u32[]{:S(2)}, u32[]{:S(2)}) collective-permute-start(f32[2,512]{1,0:T(2,128)S(1)} %pad_maximum_fusion.1), channel_id=1, source_target_pairs={{0,16},{1,17},{2,18},{3,19},{4,20},{5,21},{6,22},{7,23},{8,56},{9,... | collective-permute-start | bytes 12296 | tf_op jit(solution)/shard_map/ppermute | solution.py:455
  28.7 3.7 %collective-permute-start.5 = (f32[2,512]{1,0:T(2,128)S(1)}, f32[2,512]{1,0:T(2,128)S(1)}, u32[]{:S(2)}, u32[]{:S(2)}) collective-permute-start(f32[2,512]{1,0:T(2,128)S(1)} %pad_maximum_fusion.1), channel_id=1, source_target_pairs={{0,8},{1,9},{2,10},{3,11},{4,12},{5,13},{6,14},{7,15},{8,0},{9,1},... | collective-permute-start | bytes 12296 | tf_op jit(solution)/shard_map/ppermute | solution.py:461
  32.4 1.6 %collective-permute-start.6 = (f32[2,512]{1,0:T(2,128)S(1)}, f32[2,512]{1,0:T(2,128)S(1)}, u32[]{:S(2)}, u32[]{:S(2)}) collective-permute-start(f32[2,512]{1,0:T(2,128)S(1)} %collective-permute-done.3), channel_id=1, source_target_pairs={{0,8},{1,9},{2,10},{3,11},{4,12},{5,13},{6,14},{7,15},{8,0},{9,1},... | collective-permute-start | bytes 12296 | tf_op jit(solution)/shard_map/ppermute | solution.py:462
  34.1 4.2 %place_rest.1 = bf16[2048,128]{1,0:T(8,128)(2,1)} custom-call(s32[24,128]{1,0:T(8,128)S(1)} %bitcast.38, s32[24,128]{1,0:T(8,128)S(1)} %copy-done.2, bf16[3072,128]{1,0:T(8,128)(2,1)S(1)} %copy-done), custom_call_target="tpu_custom_call" | custom-call | tf_op jit(solution)/shard_map/place_rest/pallas_call | solution.py:126
  38.4 3.8 %all-to-all-done = bf16[32,128,128]{2,1,0:T(8,128)(2,1)S(1)} async-done(((bf16[32,128,128]{2,1,0:T(8,128)(2,1)}), bf16[32,128,128]{2,1,0:T(8,128)(2,1)S(1)}, u32[]{:S(2)}, u32[]{:S(2)}) %all-to-all-start) | async-done | bytes 1048608 | tf_op jit(solution)/shard_map/all_to_all | solution.py:430
  42.2 5.0 %collective-permute-start.8 = (bf16[4096,128]{1,0:T(8,128)(2,1)S(1)}, bf16[4096,128]{1,0:T(8,128)(2,1)}, u32[]{:S(2)}, u32[]{:S(2)}) collective-permute-start(bf16[4096,128]{1,0:T(8,128)(2,1)S(1)} %bitcast.25), channel_id=1, source_target_pairs={{0,8},{1,9},{2,10},{3,11},{4,12},{5,13},{6,14},{7,15},{8,0},{9,1},... | collective-permute-start | bytes 3145736 | tf_op jit(solution)/shard_map/ppermute | solution.py:478
  47.2 2.5 %collective-permute-start.7 = (bf16[4096,128]{1,0:T(8,128)(2,1)S(1)}, bf16[4096,128]{1,0:T(8,128)(2,1)S(1)}, u32[]{:S(2)}, u32[]{:S(2)}) collective-permute-start(bf16[4096,128]{1,0:T(8,128)(2,1)S(1)} %bitcast.26), channel_id=1, source_target_pairs={{0,16},{1,17},{2,18},{3,19},{4,20},{5,21},{6,22},{7,23},{8,56},{9,... | collective-permute-start | bytes 3145736 | tf_op jit(solution)/shard_map/ppermute | solution.py:476
  49.7 4.8 %all-to-all-start.1 = ((bf16[32,64,128]{2,1,0:T(8,128)(2,1)}), bf16[32,64,128]{2,1,0:T(8,128)(2,1)S(1)}, u32[]{:S(2)}, u32[]{:S(2)}) async-start(bf16[32,64,128]{2,1,0:T(8,128)(2,1)} %bitcast.14), calls=%async_computation.1 | async-start | bytes 1048576 | tf_op jit(solution)/shard_map/all_to_all | solution.py:430
  54.6 2.7 %own.1 = (f32[16,512]{1,0:T(8,128)S(1)}, f32[16,512]{1,0:T(8,128)S(1)}) custom-call(s32[2]{0:T(128)S(1)} %pad_add_fusion.spots, f32[16,512]{1,0:T(8,128)S(1)} %concatenate.8.ranks, bf16[4096,128]{1,0:T(8,128)(2,1)S(1)} %bitcast.28, bf16[4096,128]{1,0:T(8,128)(2,1)} %collective-permute-done.8.e1), custom_call_target="tpu_custom_call" | custom-call | flops 1073741824 | bytes 4194304 | tf_op jit(solution)/shard_map/own/pallas_call | solution.py:376
  57.3 9.2 %collective-permute-done.7.u1 = bf16[4096,128]{1,0:T(8,128)(2,1)S(1)} collective-permute-done((bf16[4096,128]{1,0:T(8,128)(2,1)S(1)}, bf16[4096,128]{1,0:T(8,128)(2,1)S(1)}, u32[]{:S(2)}, u32[]{:S(2)}) %collective-permute-start.7) | collective-permute-done | bytes 1048608 | tf_op jit(solution)/shard_map/ppermute | solution.py:476
  67.5 3.6 %all-to-all-done.1 = bf16[32,64,128]{2,1,0:T(8,128)(2,1)S(1)} async-done(((bf16[32,64,128]{2,1,0:T(8,128)(2,1)}), bf16[32,64,128]{2,1,0:T(8,128)(2,1)S(1)}, u32[]{:S(2)}, u32[]{:S(2)}) %all-to-all-start.1) | async-done | bytes 524320 | tf_op jit(solution)/shard_map/all_to_all | solution.py:430
  71.3 1.5 %collective-permute-start.9 = (bf16[2048,128]{1,0:T(8,128)(2,1)S(1)}, bf16[2048,128]{1,0:T(8,128)(2,1)S(1)}, u32[]{:S(2)}, u32[]{:S(2)}) collective-permute-start(bf16[2048,128]{1,0:T(8,128)(2,1)S(1)} %bitcast.32), channel_id=1, source_target_pairs={{0,16},{1,17},{2,18},{3,19},{4,20},{5,21},{6,22},{7,23},{8,56},{9,... | collective-permute-start | bytes 1572872 | tf_op jit(solution)/shard_map/ppermute | solution.py:484
  72.8 3.1 %near.1 = (f32[16,512]{1,0:T(8,128)S(1)}, f32[16,512]{1,0:T(8,128)S(1)}) custom-call(s32[2]{0:T(128)S(1)} %pad_add_fusion.spots, f32[16,512]{1,0:T(8,128)S(1)} %concatenate.8.ranks, bf16[4096,128]{1,0:T(8,128)(2,1)S(1)} %bitcast.29, bf16[4096,128]{1,0:T(8,128)(2,1)S(1)} %collective-permute-done.7.u1, bf16[4096,128]{1,0:T(8,128)(2,1)} %collective-permute-done.8.e1, ...), custom_call_target="tpu_custom_call" | custom-call | flops 805306368 | bytes 4194304 | tf_op jit(solution)/shard_map/near/pallas_call | solution.py:376
  76.0 5.5 %second.1 = (f32[16,512]{1,0:T(8,128)S(1)}, f32[16,512]{1,0:T(8,128)S(1)}) custom-call(s32[2]{0:T(128)S(1)} %pad_add_fusion.spots, f32[16,512]{1,0:T(8,128)S(1)} %concatenate.8.ranks, bf16[4096,128]{1,0:T(8,128)(2,1)S(1)} %bitcast.30, bf16[2048,128]{1,0:T(8,128)(2,1)S(1)} %bitcast.34, bf16[4096,128]{1,0:T(8,128)(2,1)S(1)} %collective-permute-done.7.u1, ...), custom_call_target="tpu_custom_call" | custom-call | flops 2684354560 | bytes 4194304 | tf_op jit(solution)/shard_map/second/pallas_call | solution.py:376
  81.5 2.1 %collective-permute-start.14 = (bf16[2048,128]{1,0:T(8,128)(2,1)S(1)}, bf16[2048,128]{1,0:T(8,128)(2,1)S(1)}, u32[]{:S(2)}, u32[]{:S(2)}) collective-permute-start(bf16[2048,128]{1,0:T(8,128)(2,1)S(1)} %collective-permute-done.9.u2), channel_id=1, source_target_pairs={{0,8},{1,9},{2,10},{3,11},{4,12},{5,13},{6,14},{7,15},{8,0},{9,1},... | collective-permute-start | bytes 1572872 | tf_op jit(solution)/shard_map/ppermute | solution.py:491
  83.7 2.8 %third.1 = (f32[16,512]{1,0:T(8,128)S(1)}, f32[16,512]{1,0:T(8,128)S(1)}) custom-call(s32[2]{0:T(128)S(1)} %pad_add_fusion.spots, f32[16,512]{1,0:T(8,128)S(1)} %concatenate.8.ranks, bf16[2048,128]{1,0:T(8,128)(2,1)S(1)} %bitcast.35, bf16[2048,128]{1,0:T(8,128)(2,1)S(1)} %collective-permute-done.9.u2, bf16[2048,128]{1,0:T(8,128)(2,1)S(1)} %collective-permute-done.11.e2, ...), custom_call_target="tpu_custom_call" | custom-call | flops 536870912 | bytes 4194304 | tf_op jit(solution)/shard_map/third/pallas_call | solution.py:376
  86.9 1.7 %fourth.1 = (f32[8,192]{1,0:T(8,128)S(1)}, f32[8,192]{1,0:T(8,128)S(1)}, f32[4,192]{1,0:T(4,128)S(1)}) custom-call(s32[2]{0:T(128)S(1)} %pad_add_fusion.spots, f32[16,512]{1,0:T(8,128)S(1)} %concatenate.8.ranks, bf16[4096,128]{1,0:T(8,128)(2,1)S(1)} %collective-permute-done.7.u1, bf16[2048,128]{1,0:T(8,128)(2,1)S(1)} %collective-permute-done.9.u2, ...), custom_call_target="tpu_custom_call" | custom-call | flops 536870912 | bytes 4194304 | tf_op jit(solution)/shard_map/fourth/pallas_call | solution.py:376
  88.6 1.6 %collective-permute-start.16 = (f32[4,192]{1,0:T(4,128)S(1)}, f32[4,192]{1,0:T(4,128)S(1)}, u32[]{:S(2)}, u32[]{:S(2)}) collective-permute-start(f32[4,192]{1,0:T(4,128)S(1)} %get-tuple-element.68), channel_id=1, source_target_pairs={{0,16},{1,17},{2,18},{3,19},{4,20},{5,21},{6,22},{7,23},{8,56},{9,... | collective-permute-start | bytes 9224 | tf_op jit(solution)/shard_map/ppermute | solution.py:498
  91.2 2.8 %collective-permute-done.17 = f32[4,192]{1,0:T(4,128)S(1)} collective-permute-done((f32[4,192]{1,0:T(4,128)S(1)}, f32[4,192]{1,0:T(4,128)S(1)}, u32[]{:S(2)}, u32[]{:S(2)}) %collective-permute-start.17) | collective-permute-done | bytes 3104 | tf_op jit(solution)/shard_map/ppermute | solution.py:501
  94.0 14.0 %all_to_all.21 = f32[32,1,192]{2,1,0:T(1,128)S(1)} all-to-all(f32[32,1,192]{2,1,0:T(1,128)S(1)} %all_to_all.15), channel_id=1, replica_groups=mesh['y'=4,'x'=4,'core'=2,'z'=8] {'y','z'}, dimensions={0} | all-to-all | bytes 49152 | tf_op jit(solution)/shard_map/all_to_all | solution.py:502
  (54 shorter events, 8.9 us)
Async XLA Ops:
  5.4 28.7 %copy-start = (bf16[3072,128]{1,0:T(8,128)(2,1)S(1)}, bf16[3072,128]{1,0:T(8,128)(2,1)}, u32[]{:S(2)}) copy-start(bf16[3072,128]{1,0:T(8,128)(2,1)} %rows_ref.1) | copy-start | bytes 2359300
  5.4 36.8 %all-to-all-start = ((bf16[32,128,128]{2,1,0:T(8,128)(2,1)}), bf16[32,128,128]{2,1,0:T(8,128)(2,1)S(1)}, u32[]{:S(2)}, u32[]{:S(2)}) async-start(bf16[32,128,128]{2,1,0:T(8,128)(2,1)} %bitcast.43), calls=%async_computation | async-start | bytes 2097152 | tf_op jit(solution)/shard_map/all_to_all | solution.py:430
  17.6 0.7 copy-start.3
  17.7 0.7 copy-start.2
  17.7 0.7 copy-start.1
  19.3 4.9 %collective-permute-start = (f32[1,192]{1,0:T(1,128)S(1)}, f32[1,192]{1,0:T(1,128)S(1)}, u32[]{:S(2)}, u32[]{:S(2)}) collective-permute-start(f32[1,192]{1,0:T(1,128)S(1)} %get-tuple-element.72), channel_id=1, source_target_pairs={{0,64},{1,65},{2,66},{3,67},{4,68},{5,69},{6,70},{7,71},{8,72},{9,... | collective-permute-start | bytes 2312 | tf_op jit(solution)/shard_map/ppermute | solution.py:445
  20.6 4.0 %collective-permute-start.1 = (f32[1,192]{1,0:T(1,128)S(1)}, f32[1,192]{1,0:T(1,128)S(1)}, u32[]{:S(2)}, u32[]{:S(2)}) collective-permute-start(f32[1,192]{1,0:T(1,128)S(1)} %get-tuple-element.71), channel_id=1, source_target_pairs={{0,128},{1,129},{2,130},{3,131},{4,132},{5,133},{6,134},{7,135},{8... | collective-permute-start | bytes 2312 | tf_op jit(solution)/shard_map/ppermute | solution.py:445
  23.1 2.4 %collective-permute-start.2 = (f32[1,192]{1,0:T(1,128)S(1)}, f32[1,192]{1,0:T(1,128)S(1)}, u32[]{:S(2)}, u32[]{:S(2)}) collective-permute-start(f32[1,192]{1,0:T(1,128)S(1)} %get-tuple-element.70), channel_id=1, source_target_pairs={{0,192},{1,193},{2,194},{3,195},{4,196},{5,197},{6,198},{7,199},{8... | collective-permute-start | bytes 2312 | tf_op jit(solution)/shard_map/ppermute | solution.py:445
  26.2 6.3 %collective-permute-start.3 = (f32[2,512]{1,0:T(2,128)S(1)}, f32[2,512]{1,0:T(2,128)S(1)}, u32[]{:S(2)}, u32[]{:S(2)}) collective-permute-start(f32[2,512]{1,0:T(2,128)S(1)} %pad_maximum_fusion.1), channel_id=1, source_target_pairs={{0,16},{1,17},{2,18},{3,19},{4,20},{5,21},{6,22},{7,23},{8,56},{9,... | collective-permute-start | bytes 12296 | tf_op jit(solution)/shard_map/ppermute | solution.py:455
  28.7 9.6 %collective-permute-start.4 = (f32[2,512]{1,0:T(2,128)S(1)}, f32[2,512]{1,0:T(2,128)S(1)}, u32[]{:S(2)}, u32[]{:S(2)}) collective-permute-start(f32[2,512]{1,0:T(2,128)S(1)} %pad_maximum_fusion.1), channel_id=1, source_target_pairs={{0,48},{1,49},{2,50},{3,51},{4,52},{5,53},{6,54},{7,55},{8,24},{9,... | collective-permute-start | bytes 12296 | tf_op jit(solution)/shard_map/ppermute | solution.py:460
  28.7 9.6 %collective-permute-start.5 = (f32[2,512]{1,0:T(2,128)S(1)}, f32[2,512]{1,0:T(2,128)S(1)}, u32[]{:S(2)}, u32[]{:S(2)}) collective-permute-start(f32[2,512]{1,0:T(2,128)S(1)} %pad_maximum_fusion.1), channel_id=1, source_target_pairs={{0,8},{1,9},{2,10},{3,11},{4,12},{5,13},{6,14},{7,15},{8,0},{9,1},... | collective-permute-start | bytes 12296 | tf_op jit(solution)/shard_map/ppermute | solution.py:461
  32.4 5.9 %collective-permute-start.6 = (f32[2,512]{1,0:T(2,128)S(1)}, f32[2,512]{1,0:T(2,128)S(1)}, u32[]{:S(2)}, u32[]{:S(2)}) collective-permute-start(f32[2,512]{1,0:T(2,128)S(1)} %collective-permute-done.3), channel_id=1, source_target_pairs={{0,8},{1,9},{2,10},{3,11},{4,12},{5,13},{6,14},{7,15},{8,0},{9,1},... | collective-permute-start | bytes 12296 | tf_op jit(solution)/shard_map/ppermute | solution.py:462
  42.2 12.3 %collective-permute-start.8 = (bf16[4096,128]{1,0:T(8,128)(2,1)S(1)}, bf16[4096,128]{1,0:T(8,128)(2,1)}, u32[]{:S(2)}, u32[]{:S(2)}) collective-permute-start(bf16[4096,128]{1,0:T(8,128)(2,1)S(1)} %bitcast.25), channel_id=1, source_target_pairs={{0,8},{1,9},{2,10},{3,11},{4,12},{5,13},{6,14},{7,15},{8,0},{9,1},... | collective-permute-start | bytes 3145736 | tf_op jit(solution)/shard_map/ppermute | solution.py:478
  47.2 19.3 %collective-permute-start.7 = (bf16[4096,128]{1,0:T(8,128)(2,1)S(1)}, bf16[4096,128]{1,0:T(8,128)(2,1)S(1)}, u32[]{:S(2)}, u32[]{:S(2)}) collective-permute-start(bf16[4096,128]{1,0:T(8,128)(2,1)S(1)} %bitcast.26), channel_id=1, source_target_pairs={{0,16},{1,17},{2,18},{3,19},{4,20},{5,21},{6,22},{7,23},{8,56},{9,... | collective-permute-start | bytes 3145736 | tf_op jit(solution)/shard_map/ppermute | solution.py:476
  49.7 21.4 %all-to-all-start.1 = ((bf16[32,64,128]{2,1,0:T(8,128)(2,1)}), bf16[32,64,128]{2,1,0:T(8,128)(2,1)S(1)}, u32[]{:S(2)}, u32[]{:S(2)}) async-start(bf16[32,64,128]{2,1,0:T(8,128)(2,1)} %bitcast.14), calls=%async_computation.1 | async-start | bytes 1048576 | tf_op jit(solution)/shard_map/all_to_all | solution.py:430
  54.5 21.5 %collective-permute-start.10 = (bf16[4096,128]{1,0:T(8,128)(2,1)S(1)}, bf16[4096,128]{1,0:T(8,128)(2,1)}, u32[]{:S(2)}, u32[]{:S(2)}) collective-permute-start(bf16[4096,128]{1,0:T(8,128)(2,1)S(1)} %bitcast.27), channel_id=1, source_target_pairs={{0,48},{1,49},{2,50},{3,51},{4,52},{5,53},{6,54},{7,55},{8,24},{9,... | collective-permute-start | bytes 3145736 | tf_op jit(solution)/shard_map/ppermute | solution.py:477
  66.5 9.5 %collective-permute-start.12 = (bf16[4096,128]{1,0:T(8,128)(2,1)S(1)}, bf16[4096,128]{1,0:T(8,128)(2,1)}, u32[]{:S(2)}, u32[]{:S(2)}) collective-permute-start(bf16[4096,128]{1,0:T(8,128)(2,1)S(1)} %collective-permute-done.7.u1), channel_id=1, source_target_pairs={{0,8},{1,9},{2,10},{3,11},{4,12},{5,13},{6,14},{7,15},{8,0},{9,1},... | collective-permute-start | bytes 3145736 | tf_op jit(solution)/shard_map/ppermute | solution.py:481
  71.1 4.9 %collective-permute-start.11 = (bf16[2048,128]{1,0:T(8,128)(2,1)S(1)}, bf16[2048,128]{1,0:T(8,128)(2,1)S(1)}, u32[]{:S(2)}, u32[]{:S(2)}) collective-permute-start(bf16[2048,128]{1,0:T(8,128)(2,1)S(1)} %bitcast.31), channel_id=1, source_target_pairs={{0,8},{1,9},{2,10},{3,11},{4,12},{5,13},{6,14},{7,15},{8,0},{9,1},... | collective-permute-start | bytes 1572872 | tf_op jit(solution)/shard_map/ppermute | solution.py:485
  71.3 10.3 %collective-permute-start.9 = (bf16[2048,128]{1,0:T(8,128)(2,1)S(1)}, bf16[2048,128]{1,0:T(8,128)(2,1)S(1)}, u32[]{:S(2)}, u32[]{:S(2)}) collective-permute-start(bf16[2048,128]{1,0:T(8,128)(2,1)S(1)} %bitcast.32), channel_id=1, source_target_pairs={{0,16},{1,17},{2,18},{3,19},{4,20},{5,21},{6,22},{7,23},{8,56},{9,... | collective-permute-start | bytes 1572872 | tf_op jit(solution)/shard_map/ppermute | solution.py:484
  75.9 11.0 %collective-permute-start.13 = (bf16[2048,128]{1,0:T(8,128)(2,1)S(1)}, bf16[2048,128]{1,0:T(8,128)(2,1)S(1)}, u32[]{:S(2)}, u32[]{:S(2)}) collective-permute-start(bf16[2048,128]{1,0:T(8,128)(2,1)S(1)} %bitcast.33), channel_id=1, source_target_pairs={{0,48},{1,49},{2,50},{3,51},{4,52},{5,53},{6,54},{7,55},{8,24},{9,... | collective-permute-start | bytes 1572872 | tf_op jit(solution)/shard_map/ppermute | solution.py:488
  81.5 5.4 %collective-permute-start.14 = (bf16[2048,128]{1,0:T(8,128)(2,1)S(1)}, bf16[2048,128]{1,0:T(8,128)(2,1)S(1)}, u32[]{:S(2)}, u32[]{:S(2)}) collective-permute-start(bf16[2048,128]{1,0:T(8,128)(2,1)S(1)} %collective-permute-done.9.u2), channel_id=1, source_target_pairs={{0,8},{1,9},{2,10},{3,11},{4,12},{5,13},{6,14},{7,15},{8,0},{9,1},... | collective-permute-start | bytes 1572872 | tf_op jit(solution)/shard_map/ppermute | solution.py:491
  88.6 1.6 %collective-permute-start.15 = (f32[8,192]{1,0:T(8,128)S(1)}, f32[8,192]{1,0:T(8,128)S(1)}, u32[]{:S(2)}, u32[]{:S(2)}) collective-permute-start(f32[8,192]{1,0:T(8,128)S(1)} %get-tuple-element.67), channel_id=1, source_target_pairs={{0,8},{1,9},{2,10},{3,11},{4,12},{5,13},{6,14},{7,15},{8,0},{9,1},... | collective-permute-start | bytes 18440 | tf_op jit(solution)/shard_map/ppermute | solution.py:499
  88.6 2.5 %collective-permute-start.16 = (f32[4,192]{1,0:T(4,128)S(1)}, f32[4,192]{1,0:T(4,128)S(1)}, u32[]{:S(2)}, u32[]{:S(2)}) collective-permute-start(f32[4,192]{1,0:T(4,128)S(1)} %get-tuple-element.68), channel_id=1, source_target_pairs={{0,16},{1,17},{2,18},{3,19},{4,20},{5,21},{6,22},{7,23},{8,56},{9,... | collective-permute-start | bytes 9224 | tf_op jit(solution)/shard_map/ppermute | solution.py:498
  90.2 3.7 %collective-permute-start.17 = (f32[4,192]{1,0:T(4,128)S(1)}, f32[4,192]{1,0:T(4,128)S(1)}, u32[]{:S(2)}, u32[]{:S(2)}) collective-permute-start(f32[4,192]{1,0:T(4,128)S(1)} %slice.21), channel_id=1, source_target_pairs={{0,48},{1,49},{2,50},{3,51},{4,52},{5,53},{6,54},{7,55},{8,24},{9,... | collective-permute-start | bytes 9224 | tf_op jit(solution)/shard_map/ppermute | solution.py:501

commit v13 on v12

--- a/solution.py
+++ b/solution.py
@@ -35,8 +35,8 @@
     return pairs
 
 
-def scatter_rows(spot_sm, wide_ref, out_ref):
-    @pl.loop(0, LINES)
+def scatter_rows(spot_sm, wide_ref, out_ref, first, last):
+    @pl.loop(first, last)
     def _(i):
         for lane in range(128):
             spot = spot_sm[i, lane]
@@ -57,27 +57,34 @@
     weights = ((r < c) | (c >= 128)).astype(jnp.float32).astype(jnp.bfloat16)
     group = lax.broadcasted_iota(jnp.int32, (GROUPS, 128), 0)
     ids_copy.wait()
-    for i in range(LINES):
-        hit = group == ids_ref[pl.ds(i, 1), :]
-        member_ref[pl.ds(i * GROUPS, GROUPS), :] = hit.astype(jnp.float32).astype(jnp.bfloat16)
-    counts = jnp.dot(member_ref[...], weights, preferred_element_type=jnp.float32)
     carry = jnp.zeros((GROUPS, 128), jnp.float32)
-    for i in range(LINES):
-        part = counts[i * GROUPS : (i + 1) * GROUPS]
-        line = ids_ref[pl.ds(i, 1), :]
-        within = jnp.sum(jnp.where(group == line, part[:, :128] + carry, 0.0), axis=0, keepdims=True)
-        within = within.astype(jnp.int32)
-        slot_ref[pl.ds(i, 1), :] = line * CAP + within
-        spot_ref[pl.ds(i, 1), :] = jnp.where(
-            within < PARTS[0], line * PARTS[0] + within, GROUPS * PARTS[0]
-        )
-        carry = carry + part[:, 128:]
-    copy = pltpu.make_async_copy(spot_ref, spot_sm, sems.at[2])
-    copy.start()
+    copies = []
+    for piece in range(LINES // 8):
+        lines = range(piece * 8, piece * 8 + 8)
+        for i in lines:
+            hit = group == ids_ref[pl.ds(i, 1), :]
+            member_ref[pl.ds(i * GROUPS, GROUPS), :] = hit.astype(jnp.float32).astype(jnp.bfloat16)
+        members = member_ref[pl.ds(piece * 8 * GROUPS, 8 * GROUPS), :]
+        counts = jnp.dot(members, weights, preferred_element_type=jnp.float32)
+        for at, i in enumerate(lines):
+            part = counts[at * GROUPS : (at + 1) * GROUPS]
+            line = ids_ref[pl.ds(i, 1), :]
+            within = jnp.sum(
+                jnp.where(group == line, part[:, :128] + carry, 0.0), axis=0, keepdims=True
+            ).astype(jnp.int32)
+            slot_ref[pl.ds(i, 1), :] = line * CAP + within
+            spot_ref[pl.ds(i, 1), :] = jnp.where(
+                within < PARTS[0], line * PARTS[0] + within, GROUPS * PARTS[0]
+            )
+            carry = carry + part[:, 128:]
+        rows = pl.ds(piece * 8, 8)
+        copies.append(pltpu.make_async_copy(spot_ref.at[rows], spot_sm.at[rows], sems.at[2 + piece]))
+        copies[piece].start()
     rows_copy.wait()
     wide_ref[...] = rows_ref[...].astype(jnp.float32)
-    copy.wait()
-    scatter_rows(spot_sm, wide_ref, out_ref)
+    for piece, copy in enumerate(copies):
+        copy.wait()
+        scatter_rows(spot_sm, wide_ref, out_ref, piece * 8, piece * 8 + 8)
     placed_ref[...] = out_ref[pl.ds(0, GROUPS * PARTS[0]), :].astype(jnp.bfloat16)
 
 
@@ -98,7 +105,7 @@
             pltpu.VMEM((GROUPS * PARTS[0] + 8, WIDTH), jnp.float32),
             pltpu.VMEM((LINES, 128), jnp.int32),
             pltpu.SMEM((LINES, 128), jnp.int32),
-            pltpu.SemaphoreType.DMA((3,)),
+            pltpu.SemaphoreType.DMA((2 + LINES // 8,)),
         ],
         compiler_params=pltpu.CompilerParams(vmem_limit_bytes=60 * 2**20),
         name="place",
@@ -118,7 +125,7 @@
     out_ref[...] = jnp.zeros_like(out_ref)
     wide_ref[...] = rows_ref[...].astype(jnp.float32)
     copy.wait()
-    scatter_rows(spot_sm, wide_ref, out_ref)
+    scatter_rows(spot_sm, wide_ref, out_ref, 0, LINES)
     placed_ref[...] = out_ref[pl.ds(0, GROUPS * PARTS[1]), :].astype(jnp.bfloat16)
 
 
@@ -396,16 +403,21 @@
     pieces = jnp.concatenate([high, middle, small], axis=0)
     group = lax.broadcasted_iota(jnp.int32, (3 * GROUPS, 128), 0) & (GROUPS - 1)
     place_in = lax.broadcasted_iota(jnp.int32, (CAP, 128), 0)
-    for i in range(LINES):
-        ids = ids_ref[pl.ds(i, 1), :]
-        within = slot_ref[pl.ds(i, 1), :] - ids * CAP
-        member = (group == ids).astype(jnp.float32).astype(jnp.bfloat16)
+    for first in range(0, LINES, 4):
+        lines = range(first, first + 4)
+        member = jnp.concatenate(
+            [(group == ids_ref[pl.ds(i, 1), :]).astype(jnp.float32) for i in lines], axis=1
+        ).astype(jnp.bfloat16)
         found = lax.dot_general(
             pieces, member, (((0,), (0,)), ((), ())), preferred_element_type=jnp.float32
         )
-        out_ref[pl.ds(i, 1), :] = jnp.sum(
-            jnp.where(place_in == within, found, 0.0), axis=0, keepdims=True
-        )
+        for at, i in enumerate(lines):
+            within = slot_ref[pl.ds(i, 1), :] - ids_ref[pl.ds(i, 1), :] * CAP
+            out_ref[pl.ds(i, 1), :] = jnp.sum(
+                jnp.where(place_in == within, found[:, at * 128 : (at + 1) * 128], 0.0),
+                axis=0,
+                keepdims=True,
+            )
 
 
 def answer(ids, slots, table):

time: 111 us -> 110 us (level)
  no operation moved by 1% of the time
where the time goes in v13:
time: 110 us; the launch traced here: 109 us
  starting transfers between devices  43.5 us (40%)
  Pallas kernels  27.4 us (25%)
  waiting for transfers between devices  22.1 us (20%)
  blocking collectives  14 us (13%)
  local copies, waits for them, and re-layouts  1.49 us (1%)
    all_to_all x2, starting transfers between devices, bring(): lax.all_to_all(rows.reshape(GROUPS, part, WIDTH), ('y', 'z'), split_axis=...  17 us
    pallas_call x5, Pallas kernels, scores_call(): pl.pallas_call(kernel, out_shape=jax.tree.map(lambda dims: jax.ShapeDtype...  16 us
    all_to_all x1, blocking collectives, shards(): lax.all_to_all(jnp.broadcast_to(own[:, None], (Y, Z, CAP)).reshape(GROUPS...  14 us
    ppermute x1, waiting for transfers between devices, shards(): u1 = lax.ppermute(o1, ALL, ahead)  9.02 us
    all_to_all x2, waiting for transfers between devices, bring(): lax.all_to_all(rows.reshape(GROUPS, part, WIDTH), ('y', 'z'), split_axis=...  7.39 us
    pallas_call x1, Pallas kernels, place(): pl.pallas_call(place_kernel, out_shape=(jax.ShapeDtypeStruct((GROUPS * PA...  5.18 us
    ppermute x1, starting transfers between devices, shards(): e1 = lax.ppermute(o1, ALL, swap)  4.97 us
    ppermute x3, starting transfers between devices, shards(): row = lax.ppermute(row, ALL, routes(lambda y, x, c, z: (y + j, x, c, z)))  4.89 us
  transfers between devices with their start and end apart: 20, of which 8 were waited for; matrix products, arithmetic and copies ran while one was open for 1% of the time, Pallas kernels for 18%

profile of v13, /device:TPU:1, one launch (start us, length us, event | category | flops | bytes accessed | tf_op | source)
XLA Modules:
  0.0 108.9 jit_solution(5036739422843849223)
XLA Ops:
  0.0 5.2 %place.1 = (bf16[4096,128]{1,0:T(8,128)(2,1)}, s32[24,128]{1,0:T(8,128)}) custom-call(s32[24,128]{1,0:T(8,128)} %bitcast.36, bf16[3072,128]{1,0:T(8,128)(2,1)} %rows_ref.1), custom_call_target="tpu_custom_call" | custom-call | tf_op jit(solution)/shard_map/place/pallas_call | solution.py:92
  5.2 12.2 %all-to-all-start = ((bf16[32,128,128]{2,1,0:T(8,128)(2,1)}), bf16[32,128,128]{2,1,0:T(8,128)(2,1)S(1)}, u32[]{:S(2)}, u32[]{:S(2)}) async-start(bf16[32,128,128]{2,1,0:T(8,128)(2,1)} %bitcast.43), calls=%async_computation | async-start | bytes 2097152 | tf_op jit(solution)/shard_map/all_to_all | solution.py:442
  19.1 1.3 %collective-permute-start = (f32[1,192]{1,0:T(1,128)S(1)}, f32[1,192]{1,0:T(1,128)S(1)}, u32[]{:S(2)}, u32[]{:S(2)}) collective-permute-start(f32[1,192]{1,0:T(1,128)S(1)} %get-tuple-element.72), channel_id=1, source_target_pairs={{0,64},{1,65},{2,66},{3,67},{4,68},{5,69},{6,70},{7,71},{8,72},{9,... | collective-permute-start | bytes 2312 | tf_op jit(solution)/shard_map/ppermute | solution.py:457
  20.4 2.4 %collective-permute-start.1 = (f32[1,192]{1,0:T(1,128)S(1)}, f32[1,192]{1,0:T(1,128)S(1)}, u32[]{:S(2)}, u32[]{:S(2)}) collective-permute-start(f32[1,192]{1,0:T(1,128)S(1)} %get-tuple-element.71), channel_id=1, source_target_pairs={{0,128},{1,129},{2,130},{3,131},{4,132},{5,133},{6,134},{7,135},{8... | collective-permute-start | bytes 2312 | tf_op jit(solution)/shard_map/ppermute | solution.py:457
  26.3 2.6 %collective-permute-start.3 = (f32[2,512]{1,0:T(2,128)S(1)}, f32[2,512]{1,0:T(2,128)S(1)}, u32[]{:S(2)}, u32[]{:S(2)}) collective-permute-start(f32[2,512]{1,0:T(2,128)S(1)} %pad_maximum_fusion.1), channel_id=1, source_target_pairs={{0,16},{1,17},{2,18},{3,19},{4,20},{5,21},{6,22},{7,23},{8,56},{9,... | collective-permute-start | bytes 12296 | tf_op jit(solution)/shard_map/ppermute | solution.py:467
  28.8 3.4 %collective-permute-start.5 = (f32[2,512]{1,0:T(2,128)S(1)}, f32[2,512]{1,0:T(2,128)S(1)}, u32[]{:S(2)}, u32[]{:S(2)}) collective-permute-start(f32[2,512]{1,0:T(2,128)S(1)} %pad_maximum_fusion.1), channel_id=1, source_target_pairs={{0,8},{1,9},{2,10},{3,11},{4,12},{5,13},{6,14},{7,15},{8,0},{9,1},... | collective-permute-start | bytes 12296 | tf_op jit(solution)/shard_map/ppermute | solution.py:473
  32.2 1.6 %collective-permute-start.6 = (f32[2,512]{1,0:T(2,128)S(1)}, f32[2,512]{1,0:T(2,128)S(1)}, u32[]{:S(2)}, u32[]{:S(2)}) collective-permute-start(f32[2,512]{1,0:T(2,128)S(1)} %collective-permute-done.3), channel_id=1, source_target_pairs={{0,8},{1,9},{2,10},{3,11},{4,12},{5,13},{6,14},{7,15},{8,0},{9,1},... | collective-permute-start | bytes 12296 | tf_op jit(solution)/shard_map/ppermute | solution.py:474
  33.9 4.2 %place_rest.1 = bf16[2048,128]{1,0:T(8,128)(2,1)} custom-call(s32[24,128]{1,0:T(8,128)S(1)} %bitcast.38, s32[24,128]{1,0:T(8,128)S(1)} %copy-done.2, bf16[3072,128]{1,0:T(8,128)(2,1)S(1)} %copy-done), custom_call_target="tpu_custom_call" | custom-call | tf_op jit(solution)/shard_map/place_rest/pallas_call | solution.py:133
  38.2 3.8 %all-to-all-done = bf16[32,128,128]{2,1,0:T(8,128)(2,1)S(1)} async-done(((bf16[32,128,128]{2,1,0:T(8,128)(2,1)}), bf16[32,128,128]{2,1,0:T(8,128)(2,1)S(1)}, u32[]{:S(2)}, u32[]{:S(2)}) %all-to-all-start) | async-done | bytes 1048608 | tf_op jit(solution)/shard_map/all_to_all | solution.py:442
  42.0 5.0 %collective-permute-start.8 = (bf16[4096,128]{1,0:T(8,128)(2,1)S(1)}, bf16[4096,128]{1,0:T(8,128)(2,1)}, u32[]{:S(2)}, u32[]{:S(2)}) collective-permute-start(bf16[4096,128]{1,0:T(8,128)(2,1)S(1)} %bitcast.25), channel_id=1, source_target_pairs={{0,8},{1,9},{2,10},{3,11},{4,12},{5,13},{6,14},{7,15},{8,0},{9,1},... | collective-permute-start | bytes 3145736 | tf_op jit(solution)/shard_map/ppermute | solution.py:490
  47.0 2.5 %collective-permute-start.7 = (bf16[4096,128]{1,0:T(8,128)(2,1)S(1)}, bf16[4096,128]{1,0:T(8,128)(2,1)S(1)}, u32[]{:S(2)}, u32[]{:S(2)}) collective-permute-start(bf16[4096,128]{1,0:T(8,128)(2,1)S(1)} %bitcast.26), channel_id=1, source_target_pairs={{0,16},{1,17},{2,18},{3,19},{4,20},{5,21},{6,22},{7,23},{8,56},{9,... | collective-permute-start | bytes 3145736 | tf_op jit(solution)/shard_map/ppermute | solution.py:488
  49.5 4.8 %all-to-all-start.1 = ((bf16[32,64,128]{2,1,0:T(8,128)(2,1)}), bf16[32,64,128]{2,1,0:T(8,128)(2,1)S(1)}, u32[]{:S(2)}, u32[]{:S(2)}) async-start(bf16[32,64,128]{2,1,0:T(8,128)(2,1)} %bitcast.14), calls=%async_computation.1 | async-start | bytes 1048576 | tf_op jit(solution)/shard_map/all_to_all | solution.py:442
  54.4 2.9 %own.1 = (f32[16,512]{1,0:T(8,128)S(1)}, f32[16,512]{1,0:T(8,128)S(1)}) custom-call(s32[2]{0:T(128)S(1)} %pad_add_fusion.spots, f32[16,512]{1,0:T(8,128)S(1)} %concatenate.8.ranks, bf16[4096,128]{1,0:T(8,128)(2,1)S(1)} %bitcast.28, bf16[4096,128]{1,0:T(8,128)(2,1)} %collective-permute-done.8.e1), custom_call_target="tpu_custom_call" | custom-call | flops 1073741824 | bytes 4194304 | tf_op jit(solution)/shard_map/own/pallas_call | solution.py:383
  57.2 9.0 %collective-permute-done.7.u1 = bf16[4096,128]{1,0:T(8,128)(2,1)S(1)} collective-permute-done((bf16[4096,128]{1,0:T(8,128)(2,1)S(1)}, bf16[4096,128]{1,0:T(8,128)(2,1)S(1)}, u32[]{:S(2)}, u32[]{:S(2)}) %collective-permute-start.7) | collective-permute-done | bytes 1048608 | tf_op jit(solution)/shard_map/ppermute | solution.py:488
  67.3 3.6 %all-to-all-done.1 = bf16[32,64,128]{2,1,0:T(8,128)(2,1)S(1)} async-done(((bf16[32,64,128]{2,1,0:T(8,128)(2,1)}), bf16[32,64,128]{2,1,0:T(8,128)(2,1)S(1)}, u32[]{:S(2)}, u32[]{:S(2)}) %all-to-all-start.1) | async-done | bytes 524320 | tf_op jit(solution)/shard_map/all_to_all | solution.py:442
  71.0 1.5 %collective-permute-start.9 = (bf16[2048,128]{1,0:T(8,128)(2,1)S(1)}, bf16[2048,128]{1,0:T(8,128)(2,1)S(1)}, u32[]{:S(2)}, u32[]{:S(2)}) collective-permute-start(bf16[2048,128]{1,0:T(8,128)(2,1)S(1)} %bitcast.32), channel_id=1, source_target_pairs={{0,16},{1,17},{2,18},{3,19},{4,20},{5,21},{6,22},{7,23},{8,56},{9,... | collective-permute-start | bytes 1572872 | tf_op jit(solution)/shard_map/ppermute | solution.py:496
  72.5 3.1 %near.1 = (f32[16,512]{1,0:T(8,128)S(1)}, f32[16,512]{1,0:T(8,128)S(1)}) custom-call(s32[2]{0:T(128)S(1)} %pad_add_fusion.spots, f32[16,512]{1,0:T(8,128)S(1)} %concatenate.8.ranks, bf16[4096,128]{1,0:T(8,128)(2,1)S(1)} %bitcast.29, bf16[4096,128]{1,0:T(8,128)(2,1)S(1)} %collective-permute-done.7.u1, bf16[4096,128]{1,0:T(8,128)(2,1)} %collective-permute-done.8.e1, ...), custom_call_target="tpu_custom_call" | custom-call | flops 805306368 | bytes 4194304 | tf_op jit(solution)/shard_map/near/pallas_call | solution.py:383
  75.8 5.5 %second.1 = (f32[16,512]{1,0:T(8,128)S(1)}, f32[16,512]{1,0:T(8,128)S(1)}) custom-call(s32[2]{0:T(128)S(1)} %pad_add_fusion.spots, f32[16,512]{1,0:T(8,128)S(1)} %concatenate.8.ranks, bf16[4096,128]{1,0:T(8,128)(2,1)S(1)} %bitcast.30, bf16[2048,128]{1,0:T(8,128)(2,1)S(1)} %bitcast.34, bf16[4096,128]{1,0:T(8,128)(2,1)S(1)} %collective-permute-done.7.u1, ...), custom_call_target="tpu_custom_call" | custom-call | flops 2684354560 | bytes 4194304 | tf_op jit(solution)/shard_map/second/pallas_call | solution.py:383
  81.3 2.1 %collective-permute-start.14 = (bf16[2048,128]{1,0:T(8,128)(2,1)S(1)}, bf16[2048,128]{1,0:T(8,128)(2,1)S(1)}, u32[]{:S(2)}, u32[]{:S(2)}) collective-permute-start(bf16[2048,128]{1,0:T(8,128)(2,1)S(1)} %collective-permute-done.9.u2), channel_id=1, source_target_pairs={{0,8},{1,9},{2,10},{3,11},{4,12},{5,13},{6,14},{7,15},{8,0},{9,1},... | collective-permute-start | bytes 1572872 | tf_op jit(solution)/shard_map/ppermute | solution.py:503
  83.4 2.8 %third.1 = (f32[16,512]{1,0:T(8,128)S(1)}, f32[16,512]{1,0:T(8,128)S(1)}) custom-call(s32[2]{0:T(128)S(1)} %pad_add_fusion.spots, f32[16,512]{1,0:T(8,128)S(1)} %concatenate.8.ranks, bf16[2048,128]{1,0:T(8,128)(2,1)S(1)} %bitcast.35, bf16[2048,128]{1,0:T(8,128)(2,1)S(1)} %collective-permute-done.9.u2, bf16[2048,128]{1,0:T(8,128)(2,1)S(1)} %collective-permute-done.11.e2, ...), custom_call_target="tpu_custom_call" | custom-call | flops 536870912 | bytes 4194304 | tf_op jit(solution)/shard_map/third/pallas_call | solution.py:383
  86.7 1.7 %fourth.1 = (f32[8,192]{1,0:T(8,128)S(1)}, f32[8,192]{1,0:T(8,128)S(1)}, f32[4,192]{1,0:T(4,128)S(1)}) custom-call(s32[2]{0:T(128)S(1)} %pad_add_fusion.spots, f32[16,512]{1,0:T(8,128)S(1)} %concatenate.8.ranks, bf16[4096,128]{1,0:T(8,128)(2,1)S(1)} %collective-permute-done.7.u1, bf16[2048,128]{1,0:T(8,128)(2,1)S(1)} %collective-permute-done.9.u2, ...), custom_call_target="tpu_custom_call" | custom-call | flops 536870912 | bytes 4194304 | tf_op jit(solution)/shard_map/fourth/pallas_call | solution.py:383
  88.4 1.5 %collective-permute-start.16 = (f32[4,192]{1,0:T(4,128)S(1)}, f32[4,192]{1,0:T(4,128)S(1)}, u32[]{:S(2)}, u32[]{:S(2)}) collective-permute-start(f32[4,192]{1,0:T(4,128)S(1)} %get-tuple-element.68), channel_id=1, source_target_pairs={{0,16},{1,17},{2,18},{3,19},{4,20},{5,21},{6,22},{7,23},{8,56},{9,... | collective-permute-start | bytes 9224 | tf_op jit(solution)/shard_map/ppermute | solution.py:510
  91.0 2.8 %collective-permute-done.17 = f32[4,192]{1,0:T(4,128)S(1)} collective-permute-done((f32[4,192]{1,0:T(4,128)S(1)}, f32[4,192]{1,0:T(4,128)S(1)}, u32[]{:S(2)}, u32[]{:S(2)}) %collective-permute-start.17) | collective-permute-done | bytes 3104 | tf_op jit(solution)/shard_map/ppermute | solution.py:513
  93.8 14.0 %all_to_all.21 = f32[32,1,192]{2,1,0:T(1,128)S(1)} all-to-all(f32[32,1,192]{2,1,0:T(1,128)S(1)} %all_to_all.15), channel_id=1, replica_groups=mesh['y'=4,'x'=4,'core'=2,'z'=8] {'y','z'}, dimensions={0} | all-to-all | bytes 49152 | tf_op jit(solution)/shard_map/all_to_all | solution.py:514
  (54 shorter events, 9.2 us)
Async XLA Ops:
  5.2 28.7 %copy-start = (bf16[3072,128]{1,0:T(8,128)(2,1)S(1)}, bf16[3072,128]{1,0:T(8,128)(2,1)}, u32[]{:S(2)}) copy-start(bf16[3072,128]{1,0:T(8,128)(2,1)} %rows_ref.1) | copy-start | bytes 2359300
  5.2 36.8 %all-to-all-start = ((bf16[32,128,128]{2,1,0:T(8,128)(2,1)}), bf16[32,128,128]{2,1,0:T(8,128)(2,1)S(1)}, u32[]{:S(2)}, u32[]{:S(2)}) async-start(bf16[32,128,128]{2,1,0:T(8,128)(2,1)} %bitcast.43), calls=%async_computation | async-start | bytes 2097152 | tf_op jit(solution)/shard_map/all_to_all | solution.py:442
  17.4 0.7 copy-start.3
  17.4 0.7 copy-start.2
  17.5 0.7 copy-start.1
  19.1 4.9 %collective-permute-start = (f32[1,192]{1,0:T(1,128)S(1)}, f32[1,192]{1,0:T(1,128)S(1)}, u32[]{:S(2)}, u32[]{:S(2)}) collective-permute-start(f32[1,192]{1,0:T(1,128)S(1)} %get-tuple-element.72), channel_id=1, source_target_pairs={{0,64},{1,65},{2,66},{3,67},{4,68},{5,69},{6,70},{7,71},{8,72},{9,... | collective-permute-start | bytes 2312 | tf_op jit(solution)/shard_map/ppermute | solution.py:457
  20.4 4.0 %collective-permute-start.1 = (f32[1,192]{1,0:T(1,128)S(1)}, f32[1,192]{1,0:T(1,128)S(1)}, u32[]{:S(2)}, u32[]{:S(2)}) collective-permute-start(f32[1,192]{1,0:T(1,128)S(1)} %get-tuple-element.71), channel_id=1, source_target_pairs={{0,128},{1,129},{2,130},{3,131},{4,132},{5,133},{6,134},{7,135},{8... | collective-permute-start | bytes 2312 | tf_op jit(solution)/shard_map/ppermute | solution.py:457
  22.8 2.7 %collective-permute-start.2 = (f32[1,192]{1,0:T(1,128)S(1)}, f32[1,192]{1,0:T(1,128)S(1)}, u32[]{:S(2)}, u32[]{:S(2)}) collective-permute-start(f32[1,192]{1,0:T(1,128)S(1)} %get-tuple-element.70), channel_id=1, source_target_pairs={{0,192},{1,193},{2,194},{3,195},{4,196},{5,197},{6,198},{7,199},{8... | collective-permute-start | bytes 2312 | tf_op jit(solution)/shard_map/ppermute | solution.py:457
  26.3 6.0 %collective-permute-start.3 = (f32[2,512]{1,0:T(2,128)S(1)}, f32[2,512]{1,0:T(2,128)S(1)}, u32[]{:S(2)}, u32[]{:S(2)}) collective-permute-start(f32[2,512]{1,0:T(2,128)S(1)} %pad_maximum_fusion.1), channel_id=1, source_target_pairs={{0,16},{1,17},{2,18},{3,19},{4,20},{5,21},{6,22},{7,23},{8,56},{9,... | collective-permute-start | bytes 12296 | tf_op jit(solution)/shard_map/ppermute | solution.py:467
  28.8 9.3 %collective-permute-start.4 = (f32[2,512]{1,0:T(2,128)S(1)}, f32[2,512]{1,0:T(2,128)S(1)}, u32[]{:S(2)}, u32[]{:S(2)}) collective-permute-start(f32[2,512]{1,0:T(2,128)S(1)} %pad_maximum_fusion.1), channel_id=1, source_target_pairs={{0,48},{1,49},{2,50},{3,51},{4,52},{5,53},{6,54},{7,55},{8,24},{9,... | collective-permute-start | bytes 12296 | tf_op jit(solution)/shard_map/ppermute | solution.py:472
  28.8 9.3 %collective-permute-start.5 = (f32[2,512]{1,0:T(2,128)S(1)}, f32[2,512]{1,0:T(2,128)S(1)}, u32[]{:S(2)}, u32[]{:S(2)}) collective-permute-start(f32[2,512]{1,0:T(2,128)S(1)} %pad_maximum_fusion.1), channel_id=1, source_target_pairs={{0,8},{1,9},{2,10},{3,11},{4,12},{5,13},{6,14},{7,15},{8,0},{9,1},... | collective-permute-start | bytes 12296 | tf_op jit(solution)/shard_map/ppermute | solution.py:473
  32.2 5.9 %collective-permute-start.6 = (f32[2,512]{1,0:T(2,128)S(1)}, f32[2,512]{1,0:T(2,128)S(1)}, u32[]{:S(2)}, u32[]{:S(2)}) collective-permute-start(f32[2,512]{1,0:T(2,128)S(1)} %collective-permute-done.3), channel_id=1, source_target_pairs={{0,8},{1,9},{2,10},{3,11},{4,12},{5,13},{6,14},{7,15},{8,0},{9,1},... | collective-permute-start | bytes 12296 | tf_op jit(solution)/shard_map/ppermute | solution.py:474
  42.0 12.3 %collective-permute-start.8 = (bf16[4096,128]{1,0:T(8,128)(2,1)S(1)}, bf16[4096,128]{1,0:T(8,128)(2,1)}, u32[]{:S(2)}, u32[]{:S(2)}) collective-permute-start(bf16[4096,128]{1,0:T(8,128)(2,1)S(1)} %bitcast.25), channel_id=1, source_target_pairs={{0,8},{1,9},{2,10},{3,11},{4,12},{5,13},{6,14},{7,15},{8,0},{9,1},... | collective-permute-start | bytes 3145736 | tf_op jit(solution)/shard_map/ppermute | solution.py:490
  47.0 19.3 %collective-permute-start.7 = (bf16[4096,128]{1,0:T(8,128)(2,1)S(1)}, bf16[4096,128]{1,0:T(8,128)(2,1)S(1)}, u32[]{:S(2)}, u32[]{:S(2)}) collective-permute-start(bf16[4096,128]{1,0:T(8,128)(2,1)S(1)} %bitcast.26), channel_id=1, source_target_pairs={{0,16},{1,17},{2,18},{3,19},{4,20},{5,21},{6,22},{7,23},{8,56},{9,... | collective-permute-start | bytes 3145736 | tf_op jit(solution)/shard_map/ppermute | solution.py:488
  49.5 21.4 %all-to-all-start.1 = ((bf16[32,64,128]{2,1,0:T(8,128)(2,1)}), bf16[32,64,128]{2,1,0:T(8,128)(2,1)S(1)}, u32[]{:S(2)}, u32[]{:S(2)}) async-start(bf16[32,64,128]{2,1,0:T(8,128)(2,1)} %bitcast.14), calls=%async_computation.1 | async-start | bytes 1048576 | tf_op jit(solution)/shard_map/all_to_all | solution.py:442
  54.3 21.5 %collective-permute-start.10 = (bf16[4096,128]{1,0:T(8,128)(2,1)S(1)}, bf16[4096,128]{1,0:T(8,128)(2,1)}, u32[]{:S(2)}, u32[]{:S(2)}) collective-permute-start(bf16[4096,128]{1,0:T(8,128)(2,1)S(1)} %bitcast.27), channel_id=1, source_target_pairs={{0,48},{1,49},{2,50},{3,51},{4,52},{5,53},{6,54},{7,55},{8,24},{9,... | collective-permute-start | bytes 3145736 | tf_op jit(solution)/shard_map/ppermute | solution.py:489
  66.3 9.5 %collective-permute-start.12 = (bf16[4096,128]{1,0:T(8,128)(2,1)S(1)}, bf16[4096,128]{1,0:T(8,128)(2,1)}, u32[]{:S(2)}, u32[]{:S(2)}) collective-permute-start(bf16[4096,128]{1,0:T(8,128)(2,1)S(1)} %collective-permute-done.7.u1), channel_id=1, source_target_pairs={{0,8},{1,9},{2,10},{3,11},{4,12},{5,13},{6,14},{7,15},{8,0},{9,1},... | collective-permute-start | bytes 3145736 | tf_op jit(solution)/shard_map/ppermute | solution.py:493
  70.8 4.9 %collective-permute-start.11 = (bf16[2048,128]{1,0:T(8,128)(2,1)S(1)}, bf16[2048,128]{1,0:T(8,128)(2,1)S(1)}, u32[]{:S(2)}, u32[]{:S(2)}) collective-permute-start(bf16[2048,128]{1,0:T(8,128)(2,1)S(1)} %bitcast.31), channel_id=1, source_target_pairs={{0,8},{1,9},{2,10},{3,11},{4,12},{5,13},{6,14},{7,15},{8,0},{9,1},... | collective-permute-start | bytes 1572872 | tf_op jit(solution)/shard_map/ppermute | solution.py:497
  71.0 10.3 %collective-permute-start.9 = (bf16[2048,128]{1,0:T(8,128)(2,1)S(1)}, bf16[2048,128]{1,0:T(8,128)(2,1)S(1)}, u32[]{:S(2)}, u32[]{:S(2)}) collective-permute-start(bf16[2048,128]{1,0:T(8,128)(2,1)S(1)} %bitcast.32), channel_id=1, source_target_pairs={{0,16},{1,17},{2,18},{3,19},{4,20},{5,21},{6,22},{7,23},{8,56},{9,... | collective-permute-start | bytes 1572872 | tf_op jit(solution)/shard_map/ppermute | solution.py:496
  75.7 11.0 %collective-permute-start.13 = (bf16[2048,128]{1,0:T(8,128)(2,1)S(1)}, bf16[2048,128]{1,0:T(8,128)(2,1)S(1)}, u32[]{:S(2)}, u32[]{:S(2)}) collective-permute-start(bf16[2048,128]{1,0:T(8,128)(2,1)S(1)} %bitcast.33), channel_id=1, source_target_pairs={{0,48},{1,49},{2,50},{3,51},{4,52},{5,53},{6,54},{7,55},{8,24},{9,... | collective-permute-start | bytes 1572872 | tf_op jit(solution)/shard_map/ppermute | solution.py:500
  81.3 5.4 %collective-permute-start.14 = (bf16[2048,128]{1,0:T(8,128)(2,1)S(1)}, bf16[2048,128]{1,0:T(8,128)(2,1)S(1)}, u32[]{:S(2)}, u32[]{:S(2)}) collective-permute-start(bf16[2048,128]{1,0:T(8,128)(2,1)S(1)} %collective-permute-done.9.u2), channel_id=1, source_target_pairs={{0,8},{1,9},{2,10},{3,11},{4,12},{5,13},{6,14},{7,15},{8,0},{9,1},... | collective-permute-start | bytes 1572872 | tf_op jit(solution)/shard_map/ppermute | solution.py:503
  88.4 1.6 %collective-permute-start.15 = (f32[8,192]{1,0:T(8,128)S(1)}, f32[8,192]{1,0:T(8,128)S(1)}, u32[]{:S(2)}, u32[]{:S(2)}) collective-permute-start(f32[8,192]{1,0:T(8,128)S(1)} %get-tuple-element.67), channel_id=1, source_target_pairs={{0,8},{1,9},{2,10},{3,11},{4,12},{5,13},{6,14},{7,15},{8,0},{9,1},... | collective-permute-start | bytes 18440 | tf_op jit(solution)/shard_map/ppermute | solution.py:511
  88.4 2.5 %collective-permute-start.16 = (f32[4,192]{1,0:T(4,128)S(1)}, f32[4,192]{1,0:T(4,128)S(1)}, u32[]{:S(2)}, u32[]{:S(2)}) collective-permute-start(f32[4,192]{1,0:T(4,128)S(1)} %get-tuple-element.68), channel_id=1, source_target_pairs={{0,16},{1,17},{2,18},{3,19},{4,20},{5,21},{6,22},{7,23},{8,56},{9,... | collective-permute-start | bytes 9224 | tf_op jit(solution)/shard_map/ppermute | solution.py:510
  90.0 3.7 %collective-permute-start.17 = (f32[4,192]{1,0:T(4,128)S(1)}, f32[4,192]{1,0:T(4,128)S(1)}, u32[]{:S(2)}, u32[]{:S(2)}) collective-permute-start(f32[4,192]{1,0:T(4,128)S(1)} %slice.21), channel_id=1, source_target_pairs={{0,48},{1,49},{2,50},{3,51},{4,52},{5,53},{6,54},{7,55},{8,24},{9,... | collective-permute-start | bytes 9224 | tf_op jit(solution)/shard_map/ppermute | solution.py:513

commit v14 on v13

--- a/solution.py
+++ b/solution.py
@@ -293,18 +293,11 @@
         meet(best, inverses, ranks, [(O1, o1)], [(O1, o1)])
 
 
-def near_kernel(spots, ranks, o1, u1, e1, before, known, best, inverses):
+def near_kernel(spots, ranks, o1, u1, before, known, best, inverses):
     best[...] = before[...]
     inverses[...] = known[...]
     note(inverses, U1, u1)
-
-    @pl.when(spots[0] == 0)
-    def _():
-        meet(best, inverses, ranks, [(U1, u1)], [(O1, o1)])
-
-    @pl.when(spots[0] != 0)
-    def _():
-        meet(best, inverses, ranks, [(U1, u1)], [(O1, o1), (E1, e1)])
+    meet(best, inverses, ranks, [(U1, u1)], [(O1, o1)])
 
 
 def second_kernel(spots, ranks, o1, o2, u1, v1, e1, e2, w1, before, known, best, inverses):
@@ -318,11 +311,13 @@
 
     def run(core, side):
         meet(best, inverses, ranks, [(O2, o2)], [(O2, o2)] + [(E2, e2)] * core)
-        if side:
-            meet(best, inverses, ranks, [(V1, v1)], [(E1, e1)] * (1 - core) + [(U1, u1)])
+        if core:
+            others = [(V1, v1) if side else (W1, w1), (E1, e1)]
+            meet(best, inverses, ranks, [(U1, u1)], others)
+        elif side:
+            meet(best, inverses, ranks, [(V1, v1)], [(E1, e1), (U1, u1)])
         else:
-            if core == 0:
-                meet(best, inverses, ranks, [(V1, v1)], [(E1, e1)])
+            meet(best, inverses, ranks, [(V1, v1)], [(E1, e1)])
             meet(best, inverses, ranks, [(W1, w1)], [(U1, u1)])
 
     by_place(spots, run)
@@ -495,7 +490,7 @@
 
     u2 = lax.ppermute(o2, ALL, ahead)
     e2 = lax.ppermute(o2, ALL, swap)
-    state = score(near_kernel, 6, (o1, u1, e1), state, "near")
+    state = score(near_kernel, 4, (o1, u1), state, "near")
     o2, *state = lax.optimization_barrier((o2, *state))
     v2 = lax.ppermute(o2, ALL, behind)
     state = score(second_kernel, 20, (o1, o2, u1, v1, e1, e2, w1), state, "second")

time: 110 us -> 112 us (1.018)
  waiting for transfers between devices: 22.1 us -> 23.7 us
    ppermute x1, waiting for transfers between devices: 0.01 us -> 1.77 us  [shards(): u2 = lax.ppermute(o2, ALL, ahead)]
  transfers between devices with their start and end apart: 20 -> 20, of which waited for: 8 -> 9; matrix products, arithmetic and copies ran while one was open for 1% -> 1% of each run, Pallas kernels for 18% -> 17%
where the time goes in v14:
time: 112 us; the launch traced here: 111 us
  starting transfers between devices  43.6 us (39%)
  Pallas kernels  26.6 us (24%)
  waiting for transfers between devices  23.7 us (21%)
  blocking collectives  14.8 us (13%)
  local copies, waits for them, and re-layouts  1.49 us (1%)
    all_to_all x2, starting transfers between devices, bring(): lax.all_to_all(rows.reshape(GROUPS, part, WIDTH), ('y', 'z'), split_axis=...  17 us
    pallas_call x5, Pallas kernels, scores_call(): pl.pallas_call(kernel, out_shape=jax.tree.map(lambda dims: jax.ShapeDtype...  15.2 us
    all_to_all x1, blocking collectives, shards(): lax.all_to_all(jnp.broadcast_to(own[:, None], (Y, Z, CAP)).reshape(GROUPS...  14.8 us
    ppermute x1, waiting for transfers between devices, shards(): u1 = lax.ppermute(o1, ALL, ahead)  9.02 us
    all_to_all x2, waiting for transfers between devices, bring(): lax.all_to_all(rows.reshape(GROUPS, part, WIDTH), ('y', 'z'), split_axis=...  7.39 us
    pallas_call x1, Pallas kernels, place(): pl.pallas_call(place_kernel, out_shape=(jax.ShapeDtypeStruct((GROUPS * PA...  5.18 us
    ppermute x1, starting transfers between devices, shards(): e1 = lax.ppermute(o1, ALL, swap)  4.97 us
    ppermute x3, starting transfers between devices, shards(): row = lax.ppermute(row, ALL, routes(lambda y, x, c, z: (y + j, x, c, z)))  4.89 us
  transfers between devices with their start and end apart: 20, of which 9 were waited for; matrix products, arithmetic and copies ran while one was open for 1% of the time, Pallas kernels for 17%

profile of v14, /device:TPU:1, one launch (start us, length us, event | category | flops | bytes accessed | tf_op | source)
XLA Modules:
  0.0 110.6 jit_solution(8476959149896570196)
XLA Ops:
  0.0 5.2 %place.1 = (bf16[4096,128]{1,0:T(8,128)(2,1)}, s32[24,128]{1,0:T(8,128)}) custom-call(s32[24,128]{1,0:T(8,128)} %bitcast.36, bf16[3072,128]{1,0:T(8,128)(2,1)} %rows_ref.1), custom_call_target="tpu_custom_call" | custom-call | tf_op jit(solution)/shard_map/place/pallas_call | solution.py:92
  5.2 12.2 %all-to-all-start = ((bf16[32,128,128]{2,1,0:T(8,128)(2,1)}), bf16[32,128,128]{2,1,0:T(8,128)(2,1)S(1)}, u32[]{:S(2)}, u32[]{:S(2)}) async-start(bf16[32,128,128]{2,1,0:T(8,128)(2,1)} %bitcast.43), calls=%async_computation | async-start | bytes 2097152 | tf_op jit(solution)/shard_map/all_to_all | solution.py:437
  19.1 1.3 %collective-permute-start = (f32[1,192]{1,0:T(1,128)S(1)}, f32[1,192]{1,0:T(1,128)S(1)}, u32[]{:S(2)}, u32[]{:S(2)}) collective-permute-start(f32[1,192]{1,0:T(1,128)S(1)} %get-tuple-element.72), channel_id=1, source_target_pairs={{0,64},{1,65},{2,66},{3,67},{4,68},{5,69},{6,70},{7,71},{8,72},{9,... | collective-permute-start | bytes 2312 | tf_op jit(solution)/shard_map/ppermute | solution.py:452
  20.4 2.4 %collective-permute-start.1 = (f32[1,192]{1,0:T(1,128)S(1)}, f32[1,192]{1,0:T(1,128)S(1)}, u32[]{:S(2)}, u32[]{:S(2)}) collective-permute-start(f32[1,192]{1,0:T(1,128)S(1)} %get-tuple-element.71), channel_id=1, source_target_pairs={{0,128},{1,129},{2,130},{3,131},{4,132},{5,133},{6,134},{7,135},{8... | collective-permute-start | bytes 2312 | tf_op jit(solution)/shard_map/ppermute | solution.py:452
  26.3 2.6 %collective-permute-start.3 = (f32[2,512]{1,0:T(2,128)S(1)}, f32[2,512]{1,0:T(2,128)S(1)}, u32[]{:S(2)}, u32[]{:S(2)}) collective-permute-start(f32[2,512]{1,0:T(2,128)S(1)} %pad_maximum_fusion.1), channel_id=1, source_target_pairs={{0,16},{1,17},{2,18},{3,19},{4,20},{5,21},{6,22},{7,23},{8,56},{9,... | collective-permute-start | bytes 12296 | tf_op jit(solution)/shard_map/ppermute | solution.py:462
  28.8 3.4 %collective-permute-start.5 = (f32[2,512]{1,0:T(2,128)S(1)}, f32[2,512]{1,0:T(2,128)S(1)}, u32[]{:S(2)}, u32[]{:S(2)}) collective-permute-start(f32[2,512]{1,0:T(2,128)S(1)} %pad_maximum_fusion.1), channel_id=1, source_target_pairs={{0,8},{1,9},{2,10},{3,11},{4,12},{5,13},{6,14},{7,15},{8,0},{9,1},... | collective-permute-start | bytes 12296 | tf_op jit(solution)/shard_map/ppermute | solution.py:468
  32.2 1.6 %collective-permute-start.6 = (f32[2,512]{1,0:T(2,128)S(1)}, f32[2,512]{1,0:T(2,128)S(1)}, u32[]{:S(2)}, u32[]{:S(2)}) collective-permute-start(f32[2,512]{1,0:T(2,128)S(1)} %collective-permute-done.3), channel_id=1, source_target_pairs={{0,8},{1,9},{2,10},{3,11},{4,12},{5,13},{6,14},{7,15},{8,0},{9,1},... | collective-permute-start | bytes 12296 | tf_op jit(solution)/shard_map/ppermute | solution.py:469
  33.9 4.2 %place_rest.1 = bf16[2048,128]{1,0:T(8,128)(2,1)} custom-call(s32[24,128]{1,0:T(8,128)S(1)} %bitcast.38, s32[24,128]{1,0:T(8,128)S(1)} %copy-done.2, bf16[3072,128]{1,0:T(8,128)(2,1)S(1)} %copy-done), custom_call_target="tpu_custom_call" | custom-call | tf_op jit(solution)/shard_map/place_rest/pallas_call | solution.py:133
  38.2 3.8 %all-to-all-done = bf16[32,128,128]{2,1,0:T(8,128)(2,1)S(1)} async-done(((bf16[32,128,128]{2,1,0:T(8,128)(2,1)}), bf16[32,128,128]{2,1,0:T(8,128)(2,1)S(1)}, u32[]{:S(2)}, u32[]{:S(2)}) %all-to-all-start) | async-done | bytes 1048608 | tf_op jit(solution)/shard_map/all_to_all | solution.py:437
  42.0 5.0 %collective-permute-start.8 = (bf16[4096,128]{1,0:T(8,128)(2,1)S(1)}, bf16[4096,128]{1,0:T(8,128)(2,1)}, u32[]{:S(2)}, u32[]{:S(2)}) collective-permute-start(bf16[4096,128]{1,0:T(8,128)(2,1)S(1)} %bitcast.25), channel_id=1, source_target_pairs={{0,8},{1,9},{2,10},{3,11},{4,12},{5,13},{6,14},{7,15},{8,0},{9,1},... | collective-permute-start | bytes 3145736 | tf_op jit(solution)/shard_map/ppermute | solution.py:485
  47.0 2.5 %collective-permute-start.7 = (bf16[4096,128]{1,0:T(8,128)(2,1)S(1)}, bf16[4096,128]{1,0:T(8,128)(2,1)S(1)}, u32[]{:S(2)}, u32[]{:S(2)}) collective-permute-start(bf16[4096,128]{1,0:T(8,128)(2,1)S(1)} %bitcast.26), channel_id=1, source_target_pairs={{0,16},{1,17},{2,18},{3,19},{4,20},{5,21},{6,22},{7,23},{8,56},{9,... | collective-permute-start | bytes 3145736 | tf_op jit(solution)/shard_map/ppermute | solution.py:483
  49.5 4.8 %all-to-all-start.1 = ((bf16[32,64,128]{2,1,0:T(8,128)(2,1)}), bf16[32,64,128]{2,1,0:T(8,128)(2,1)S(1)}, u32[]{:S(2)}, u32[]{:S(2)}) async-start(bf16[32,64,128]{2,1,0:T(8,128)(2,1)} %bitcast.14), calls=%async_computation.1 | async-start | bytes 1048576 | tf_op jit(solution)/shard_map/all_to_all | solution.py:437
  54.4 2.9 %own.1 = (f32[16,512]{1,0:T(8,128)S(1)}, f32[16,512]{1,0:T(8,128)S(1)}) custom-call(s32[2]{0:T(128)S(1)} %pad_add_fusion.spots, f32[16,512]{1,0:T(8,128)S(1)} %concatenate.8.ranks, bf16[4096,128]{1,0:T(8,128)(2,1)S(1)} %bitcast.28, bf16[4096,128]{1,0:T(8,128)(2,1)} %collective-permute-done.8.e1), custom_call_target="tpu_custom_call" | custom-call | flops 1073741824 | bytes 4194304 | tf_op jit(solution)/shard_map/own/pallas_call | solution.py:378
  57.2 9.0 %collective-permute-done.7.u1 = bf16[4096,128]{1,0:T(8,128)(2,1)S(1)} collective-permute-done((bf16[4096,128]{1,0:T(8,128)(2,1)S(1)}, bf16[4096,128]{1,0:T(8,128)(2,1)S(1)}, u32[]{:S(2)}, u32[]{:S(2)}) %collective-permute-start.7) | collective-permute-done | bytes 1048608 | tf_op jit(solution)/shard_map/ppermute | solution.py:483
  67.3 3.6 %all-to-all-done.1 = bf16[32,64,128]{2,1,0:T(8,128)(2,1)S(1)} async-done(((bf16[32,64,128]{2,1,0:T(8,128)(2,1)}), bf16[32,64,128]{2,1,0:T(8,128)(2,1)S(1)}, u32[]{:S(2)}, u32[]{:S(2)}) %all-to-all-start.1) | async-done | bytes 524320 | tf_op jit(solution)/shard_map/all_to_all | solution.py:437
  71.0 1.5 %collective-permute-start.9 = (bf16[2048,128]{1,0:T(8,128)(2,1)S(1)}, bf16[2048,128]{1,0:T(8,128)(2,1)S(1)}, u32[]{:S(2)}, u32[]{:S(2)}) collective-permute-start(bf16[2048,128]{1,0:T(8,128)(2,1)S(1)} %bitcast.32), channel_id=1, source_target_pairs={{0,16},{1,17},{2,18},{3,19},{4,20},{5,21},{6,22},{7,23},{8,56},{9,... | collective-permute-start | bytes 1572872 | tf_op jit(solution)/shard_map/ppermute | solution.py:491
  72.5 1.6 %near.1 = (f32[16,512]{1,0:T(8,128)S(1)}, f32[16,512]{1,0:T(8,128)S(1)}) custom-call(s32[2]{0:T(128)S(1)} %pad_add_fusion.spots, f32[16,512]{1,0:T(8,128)S(1)} %concatenate.8.ranks, bf16[4096,128]{1,0:T(8,128)(2,1)S(1)} %bitcast.29, bf16[4096,128]{1,0:T(8,128)(2,1)S(1)} %collective-permute-done.7.u1, f32[16,512]{1,0:T(8,128)S(1)} %get-tuple-element.49.before, ...), custom_call_target="tpu_custom_call" | custom-call | flops 536870912 | bytes 4194304 | tf_op jit(solution)/shard_map/near/pallas_call | solution.py:378
  74.2 6.1 %second.1 = (f32[16,512]{1,0:T(8,128)S(1)}, f32[16,512]{1,0:T(8,128)S(1)}) custom-call(s32[2]{0:T(128)S(1)} %pad_add_fusion.spots, f32[16,512]{1,0:T(8,128)S(1)} %concatenate.8.ranks, bf16[4096,128]{1,0:T(8,128)(2,1)S(1)} %bitcast.30, bf16[2048,128]{1,0:T(8,128)(2,1)S(1)} %bitcast.34, bf16[4096,128]{1,0:T(8,128)(2,1)S(1)} %collective-permute-done.7.u1, ...), custom_call_target="tpu_custom_call" | custom-call | flops 2684354560 | bytes 4194304 | tf_op jit(solution)/shard_map/second/pallas_call | solution.py:378
  80.3 1.8 %collective-permute-done.9.u2 = bf16[2048,128]{1,0:T(8,128)(2,1)S(1)} collective-permute-done((bf16[2048,128]{1,0:T(8,128)(2,1)S(1)}, bf16[2048,128]{1,0:T(8,128)(2,1)S(1)}, u32[]{:S(2)}, u32[]{:S(2)}) %collective-permute-start.9) | collective-permute-done | bytes 524320 | tf_op jit(solution)/shard_map/ppermute | solution.py:491
  82.1 2.8 %collective-permute-start.14 = (bf16[2048,128]{1,0:T(8,128)(2,1)S(1)}, bf16[2048,128]{1,0:T(8,128)(2,1)S(1)}, u32[]{:S(2)}, u32[]{:S(2)}) collective-permute-start(bf16[2048,128]{1,0:T(8,128)(2,1)S(1)} %collective-permute-done.9.u2), channel_id=1, source_target_pairs={{0,8},{1,9},{2,10},{3,11},{4,12},{5,13},{6,14},{7,15},{8,0},{9,1},... | collective-permute-start | bytes 1572872 | tf_op jit(solution)/shard_map/ppermute | solution.py:498
  84.9 3.0 %third.1 = (f32[16,512]{1,0:T(8,128)S(1)}, f32[16,512]{1,0:T(8,128)S(1)}) custom-call(s32[2]{0:T(128)S(1)} %pad_add_fusion.spots, f32[16,512]{1,0:T(8,128)S(1)} %concatenate.8.ranks, bf16[2048,128]{1,0:T(8,128)(2,1)S(1)} %bitcast.35, bf16[2048,128]{1,0:T(8,128)(2,1)S(1)} %collective-permute-done.9.u2, bf16[2048,128]{1,0:T(8,128)(2,1)S(1)} %collective-permute-done.11.e2, ...), custom_call_target="tpu_custom_call" | custom-call | flops 536870912 | bytes 4194304 | tf_op jit(solution)/shard_map/third/pallas_call | solution.py:378
  87.9 1.7 %fourth.1 = (f32[8,192]{1,0:T(8,128)S(1)}, f32[8,192]{1,0:T(8,128)S(1)}, f32[4,192]{1,0:T(4,128)S(1)}) custom-call(s32[2]{0:T(128)S(1)} %pad_add_fusion.spots, f32[16,512]{1,0:T(8,128)S(1)} %concatenate.8.ranks, bf16[4096,128]{1,0:T(8,128)(2,1)S(1)} %collective-permute-done.7.u1, bf16[2048,128]{1,0:T(8,128)(2,1)S(1)} %collective-permute-done.9.u2, ...), custom_call_target="tpu_custom_call" | custom-call | flops 536870912 | bytes 4194304 | tf_op jit(solution)/shard_map/fourth/pallas_call | solution.py:378
  92.2 2.4 %collective-permute-done.17 = f32[4,192]{1,0:T(4,128)S(1)} collective-permute-done((f32[4,192]{1,0:T(4,128)S(1)}, f32[4,192]{1,0:T(4,128)S(1)}, u32[]{:S(2)}, u32[]{:S(2)}) %collective-permute-start.17) | collective-permute-done | bytes 3104 | tf_op jit(solution)/shard_map/ppermute | solution.py:508
  94.7 14.8 %all_to_all.21 = f32[32,1,192]{2,1,0:T(1,128)S(1)} all-to-all(f32[32,1,192]{2,1,0:T(1,128)S(1)} %all_to_all.15), channel_id=1, replica_groups=mesh['y'=4,'x'=4,'core'=2,'z'=8] {'y','z'}, dimensions={0} | all-to-all | bytes 49152 | tf_op jit(solution)/shard_map/all_to_all | solution.py:509
  (54 shorter events, 10.3 us)
Async XLA Ops:
  5.2 28.7 %copy-start = (bf16[3072,128]{1,0:T(8,128)(2,1)S(1)}, bf16[3072,128]{1,0:T(8,128)(2,1)}, u32[]{:S(2)}) copy-start(bf16[3072,128]{1,0:T(8,128)(2,1)} %rows_ref.1) | copy-start | bytes 2359300
  5.2 36.8 %all-to-all-start = ((bf16[32,128,128]{2,1,0:T(8,128)(2,1)}), bf16[32,128,128]{2,1,0:T(8,128)(2,1)S(1)}, u32[]{:S(2)}, u32[]{:S(2)}) async-start(bf16[32,128,128]{2,1,0:T(8,128)(2,1)} %bitcast.43), calls=%async_computation | async-start | bytes 2097152 | tf_op jit(solution)/shard_map/all_to_all | solution.py:437
  17.4 0.7 copy-start.3
  17.4 0.7 copy-start.2
  17.5 0.7 copy-start.1
  19.1 4.9 %collective-permute-start = (f32[1,192]{1,0:T(1,128)S(1)}, f32[1,192]{1,0:T(1,128)S(1)}, u32[]{:S(2)}, u32[]{:S(2)}) collective-permute-start(f32[1,192]{1,0:T(1,128)S(1)} %get-tuple-element.72), channel_id=1, source_target_pairs={{0,64},{1,65},{2,66},{3,67},{4,68},{5,69},{6,70},{7,71},{8,72},{9,... | collective-permute-start | bytes 2312 | tf_op jit(solution)/shard_map/ppermute | solution.py:452
  20.4 4.0 %collective-permute-start.1 = (f32[1,192]{1,0:T(1,128)S(1)}, f32[1,192]{1,0:T(1,128)S(1)}, u32[]{:S(2)}, u32[]{:S(2)}) collective-permute-start(f32[1,192]{1,0:T(1,128)S(1)} %get-tuple-element.71), channel_id=1, source_target_pairs={{0,128},{1,129},{2,130},{3,131},{4,132},{5,133},{6,134},{7,135},{8... | collective-permute-start | bytes 2312 | tf_op jit(solution)/shard_map/ppermute | solution.py:452
  22.8 2.7 %collective-permute-start.2 = (f32[1,192]{1,0:T(1,128)S(1)}, f32[1,192]{1,0:T(1,128)S(1)}, u32[]{:S(2)}, u32[]{:S(2)}) collective-permute-start(f32[1,192]{1,0:T(1,128)S(1)} %get-tuple-element.70), channel_id=1, source_target_pairs={{0,192},{1,193},{2,194},{3,195},{4,196},{5,197},{6,198},{7,199},{8... | collective-permute-start | bytes 2312 | tf_op jit(solution)/shard_map/ppermute | solution.py:452
  26.3 6.0 %collective-permute-start.3 = (f32[2,512]{1,0:T(2,128)S(1)}, f32[2,512]{1,0:T(2,128)S(1)}, u32[]{:S(2)}, u32[]{:S(2)}) collective-permute-start(f32[2,512]{1,0:T(2,128)S(1)} %pad_maximum_fusion.1), channel_id=1, source_target_pairs={{0,16},{1,17},{2,18},{3,19},{4,20},{5,21},{6,22},{7,23},{8,56},{9,... | collective-permute-start | bytes 12296 | tf_op jit(solution)/shard_map/ppermute | solution.py:462
  28.8 9.3 %collective-permute-start.4 = (f32[2,512]{1,0:T(2,128)S(1)}, f32[2,512]{1,0:T(2,128)S(1)}, u32[]{:S(2)}, u32[]{:S(2)}) collective-permute-start(f32[2,512]{1,0:T(2,128)S(1)} %pad_maximum_fusion.1), channel_id=1, source_target_pairs={{0,48},{1,49},{2,50},{3,51},{4,52},{5,53},{6,54},{7,55},{8,24},{9,... | collective-permute-start | bytes 12296 | tf_op jit(solution)/shard_map/ppermute | solution.py:467
  28.8 9.3 %collective-permute-start.5 = (f32[2,512]{1,0:T(2,128)S(1)}, f32[2,512]{1,0:T(2,128)S(1)}, u32[]{:S(2)}, u32[]{:S(2)}) collective-permute-start(f32[2,512]{1,0:T(2,128)S(1)} %pad_maximum_fusion.1), channel_id=1, source_target_pairs={{0,8},{1,9},{2,10},{3,11},{4,12},{5,13},{6,14},{7,15},{8,0},{9,1},... | collective-permute-start | bytes 12296 | tf_op jit(solution)/shard_map/ppermute | solution.py:468
  32.2 5.9 %collective-permute-start.6 = (f32[2,512]{1,0:T(2,128)S(1)}, f32[2,512]{1,0:T(2,128)S(1)}, u32[]{:S(2)}, u32[]{:S(2)}) collective-permute-start(f32[2,512]{1,0:T(2,128)S(1)} %collective-permute-done.3), channel_id=1, source_target_pairs={{0,8},{1,9},{2,10},{3,11},{4,12},{5,13},{6,14},{7,15},{8,0},{9,1},... | collective-permute-start | bytes 12296 | tf_op jit(solution)/shard_map/ppermute | solution.py:469
  42.0 12.3 %collective-permute-start.8 = (bf16[4096,128]{1,0:T(8,128)(2,1)S(1)}, bf16[4096,128]{1,0:T(8,128)(2,1)}, u32[]{:S(2)}, u32[]{:S(2)}) collective-permute-start(bf16[4096,128]{1,0:T(8,128)(2,1)S(1)} %bitcast.25), channel_id=1, source_target_pairs={{0,8},{1,9},{2,10},{3,11},{4,12},{5,13},{6,14},{7,15},{8,0},{9,1},... | collective-permute-start | bytes 3145736 | tf_op jit(solution)/shard_map/ppermute | solution.py:485
  47.0 19.3 %collective-permute-start.7 = (bf16[4096,128]{1,0:T(8,128)(2,1)S(1)}, bf16[4096,128]{1,0:T(8,128)(2,1)S(1)}, u32[]{:S(2)}, u32[]{:S(2)}) collective-permute-start(bf16[4096,128]{1,0:T(8,128)(2,1)S(1)} %bitcast.26), channel_id=1, source_target_pairs={{0,16},{1,17},{2,18},{3,19},{4,20},{5,21},{6,22},{7,23},{8,56},{9,... | collective-permute-start | bytes 3145736 | tf_op jit(solution)/shard_map/ppermute | solution.py:483
  49.5 21.4 %all-to-all-start.1 = ((bf16[32,64,128]{2,1,0:T(8,128)(2,1)}), bf16[32,64,128]{2,1,0:T(8,128)(2,1)S(1)}, u32[]{:S(2)}, u32[]{:S(2)}) async-start(bf16[32,64,128]{2,1,0:T(8,128)(2,1)} %bitcast.14), calls=%async_computation.1 | async-start | bytes 1048576 | tf_op jit(solution)/shard_map/all_to_all | solution.py:437
  54.3 19.9 %collective-permute-start.10 = (bf16[4096,128]{1,0:T(8,128)(2,1)S(1)}, bf16[4096,128]{1,0:T(8,128)(2,1)}, u32[]{:S(2)}, u32[]{:S(2)}) collective-permute-start(bf16[4096,128]{1,0:T(8,128)(2,1)S(1)} %bitcast.27), channel_id=1, source_target_pairs={{0,48},{1,49},{2,50},{3,51},{4,52},{5,53},{6,54},{7,55},{8,24},{9,... | collective-permute-start | bytes 3145736 | tf_op jit(solution)/shard_map/ppermute | solution.py:484
  66.3 7.9 %collective-permute-start.12 = (bf16[4096,128]{1,0:T(8,128)(2,1)S(1)}, bf16[4096,128]{1,0:T(8,128)(2,1)}, u32[]{:S(2)}, u32[]{:S(2)}) collective-permute-start(bf16[4096,128]{1,0:T(8,128)(2,1)S(1)} %collective-permute-done.7.u1), channel_id=1, source_target_pairs={{0,8},{1,9},{2,10},{3,11},{4,12},{5,13},{6,14},{7,15},{8,0},{9,1},... | collective-permute-start | bytes 3145736 | tf_op jit(solution)/shard_map/ppermute | solution.py:488
  70.8 3.4 %collective-permute-start.11 = (bf16[2048,128]{1,0:T(8,128)(2,1)S(1)}, bf16[2048,128]{1,0:T(8,128)(2,1)S(1)}, u32[]{:S(2)}, u32[]{:S(2)}) collective-permute-start(bf16[2048,128]{1,0:T(8,128)(2,1)S(1)} %bitcast.31), channel_id=1, source_target_pairs={{0,8},{1,9},{2,10},{3,11},{4,12},{5,13},{6,14},{7,15},{8,0},{9,1},... | collective-permute-start | bytes 1572872 | tf_op jit(solution)/shard_map/ppermute | solution.py:492
  71.0 11.0 %collective-permute-start.9 = (bf16[2048,128]{1,0:T(8,128)(2,1)S(1)}, bf16[2048,128]{1,0:T(8,128)(2,1)S(1)}, u32[]{:S(2)}, u32[]{:S(2)}) collective-permute-start(bf16[2048,128]{1,0:T(8,128)(2,1)S(1)} %bitcast.32), channel_id=1, source_target_pairs={{0,16},{1,17},{2,18},{3,19},{4,20},{5,21},{6,22},{7,23},{8,56},{9,... | collective-permute-start | bytes 1572872 | tf_op jit(solution)/shard_map/ppermute | solution.py:491
  74.1 13.8 %collective-permute-start.13 = (bf16[2048,128]{1,0:T(8,128)(2,1)S(1)}, bf16[2048,128]{1,0:T(8,128)(2,1)S(1)}, u32[]{:S(2)}, u32[]{:S(2)}) collective-permute-start(bf16[2048,128]{1,0:T(8,128)(2,1)S(1)} %bitcast.33), channel_id=1, source_target_pairs={{0,48},{1,49},{2,50},{3,51},{4,52},{5,53},{6,54},{7,55},{8,24},{9,... | collective-permute-start | bytes 1572872 | tf_op jit(solution)/shard_map/ppermute | solution.py:495
  82.1 5.8 %collective-permute-start.14 = (bf16[2048,128]{1,0:T(8,128)(2,1)S(1)}, bf16[2048,128]{1,0:T(8,128)(2,1)S(1)}, u32[]{:S(2)}, u32[]{:S(2)}) collective-permute-start(bf16[2048,128]{1,0:T(8,128)(2,1)S(1)} %collective-permute-done.9.u2), channel_id=1, source_target_pairs={{0,8},{1,9},{2,10},{3,11},{4,12},{5,13},{6,14},{7,15},{8,0},{9,1},... | collective-permute-start | bytes 1572872 | tf_op jit(solution)/shard_map/ppermute | solution.py:498
  89.6 1.2 %collective-permute-start.15 = (f32[8,192]{1,0:T(8,128)S(1)}, f32[8,192]{1,0:T(8,128)S(1)}, u32[]{:S(2)}, u32[]{:S(2)}) collective-permute-start(f32[8,192]{1,0:T(8,128)S(1)} %get-tuple-element.67), channel_id=1, source_target_pairs={{0,8},{1,9},{2,10},{3,11},{4,12},{5,13},{6,14},{7,15},{8,0},{9,1},... | collective-permute-start | bytes 18440 | tf_op jit(solution)/shard_map/ppermute | solution.py:506
  89.7 2.5 %collective-permute-start.16 = (f32[4,192]{1,0:T(4,128)S(1)}, f32[4,192]{1,0:T(4,128)S(1)}, u32[]{:S(2)}, u32[]{:S(2)}) collective-permute-start(f32[4,192]{1,0:T(4,128)S(1)} %get-tuple-element.68), channel_id=1, source_target_pairs={{0,16},{1,17},{2,18},{3,19},{4,20},{5,21},{6,22},{7,23},{8,56},{9,... | collective-permute-start | bytes 9224 | tf_op jit(solution)/shard_map/ppermute | solution.py:505
  90.9 3.7 %collective-permute-start.17 = (f32[4,192]{1,0:T(4,128)S(1)}, f32[4,192]{1,0:T(4,128)S(1)}, u32[]{:S(2)}, u32[]{:S(2)}) collective-permute-start(f32[4,192]{1,0:T(4,128)S(1)} %slice.21), channel_id=1, source_target_pairs={{0,48},{1,49},{2,50},{3,51},{4,52},{5,53},{6,54},{7,55},{8,24},{9,... | collective-permute-start | bytes 9224 | tf_op jit(solution)/shard_map/ppermute | solution.py:508

commit v15 on v13

--- a/solution.py
+++ b/solution.py
@@ -284,13 +284,7 @@
     note(inverses, O1, o1)
     note(inverses, E1, e1)
 
-    @pl.when(spots[0] == 0)
-    def _():
-        meet(best, inverses, ranks, [(O1, o1)], [(O1, o1), (E1, e1)])
-
-    @pl.when(spots[0] != 0)
-    def _():
-        meet(best, inverses, ranks, [(O1, o1)], [(O1, o1)])
+    meet(best, inverses, ranks, [(O1, o1)], [(O1, o1)])
 
 
 def near_kernel(spots, ranks, o1, u1, e1, before, known, best, inverses):
@@ -300,7 +294,7 @@
 
     @pl.when(spots[0] == 0)
     def _():
-        meet(best, inverses, ranks, [(U1, u1)], [(O1, o1)])
+        meet(best, inverses, ranks, [(O1, o1)], [(U1, u1), (E1, e1)])
 
     @pl.when(spots[0] != 0)
     def _():

time: 110 us -> 110 us (level)
  transfers between devices with their start and end apart: 20 -> 20, of which waited for: 8 -> 7; matrix products, arithmetic and copies ran while one was open for 1% -> 1% of each run, Pallas kernels for 18% -> 17%
where the time goes in v15:
time: 110 us; the launch traced here: 109 us
  starting transfers between devices  43.8 us (40%)
  Pallas kernels  26.9 us (24%)
  waiting for transfers between devices  22.2 us (20%)
  blocking collectives  14.1 us (13%)
  local copies, waits for them, and re-layouts  1.49 us (1%)
    all_to_all x2, starting transfers between devices, bring(): lax.all_to_all(rows.reshape(GROUPS, part, WIDTH), ('y', 'z'), split_axis=...  17 us
    pallas_call x5, Pallas kernels, scores_call(): pl.pallas_call(kernel, out_shape=jax.tree.map(lambda dims: jax.ShapeDtype...  15.5 us
    all_to_all x1, blocking collectives, shards(): lax.all_to_all(jnp.broadcast_to(own[:, None], (Y, Z, CAP)).reshape(GROUPS...  14.1 us
    ppermute x1, waiting for transfers between devices, shards(): u1 = lax.ppermute(o1, ALL, ahead)  9.68 us
    all_to_all x2, waiting for transfers between devices, bring(): lax.all_to_all(rows.reshape(GROUPS, part, WIDTH), ('y', 'z'), split_axis=...  7.39 us
    pallas_call x1, Pallas kernels, place(): pl.pallas_call(place_kernel, out_shape=(jax.ShapeDtypeStruct((GROUPS * PA...  5.18 us
    ppermute x1, starting transfers between devices, shards(): e1 = lax.ppermute(o1, ALL, swap)  4.97 us
    ppermute x3, starting transfers between devices, shards(): row = lax.ppermute(row, ALL, routes(lambda y, x, c, z: (y + j, x, c, z)))  4.89 us
  transfers between devices with their start and end apart: 20, of which 7 were waited for; matrix products, arithmetic and copies ran while one was open for 1% of the time, Pallas kernels for 17%

profile of v15, /device:TPU:1, one launch (start us, length us, event | category | flops | bytes accessed | tf_op | source)
XLA Modules:
  0.0 109.1 jit_solution(4966833940951481983)
XLA Ops:
  0.0 5.2 %place.1 = (bf16[4096,128]{1,0:T(8,128)(2,1)}, s32[24,128]{1,0:T(8,128)}) custom-call(s32[24,128]{1,0:T(8,128)} %bitcast.36, bf16[3072,128]{1,0:T(8,128)(2,1)} %rows_ref.1), custom_call_target="tpu_custom_call" | custom-call | tf_op jit(solution)/shard_map/place/pallas_call | solution.py:92
  5.2 12.2 %all-to-all-start = ((bf16[32,128,128]{2,1,0:T(8,128)(2,1)}), bf16[32,128,128]{2,1,0:T(8,128)(2,1)S(1)}, u32[]{:S(2)}, u32[]{:S(2)}) async-start(bf16[32,128,128]{2,1,0:T(8,128)(2,1)} %bitcast.43), calls=%async_computation | async-start | bytes 2097152 | tf_op jit(solution)/shard_map/all_to_all | solution.py:436
  19.1 1.3 %collective-permute-start = (f32[1,192]{1,0:T(1,128)S(1)}, f32[1,192]{1,0:T(1,128)S(1)}, u32[]{:S(2)}, u32[]{:S(2)}) collective-permute-start(f32[1,192]{1,0:T(1,128)S(1)} %get-tuple-element.72), channel_id=1, source_target_pairs={{0,64},{1,65},{2,66},{3,67},{4,68},{5,69},{6,70},{7,71},{8,72},{9,... | collective-permute-start | bytes 2312 | tf_op jit(solution)/shard_map/ppermute | solution.py:451
  20.4 2.4 %collective-permute-start.1 = (f32[1,192]{1,0:T(1,128)S(1)}, f32[1,192]{1,0:T(1,128)S(1)}, u32[]{:S(2)}, u32[]{:S(2)}) collective-permute-start(f32[1,192]{1,0:T(1,128)S(1)} %get-tuple-element.71), channel_id=1, source_target_pairs={{0,128},{1,129},{2,130},{3,131},{4,132},{5,133},{6,134},{7,135},{8... | collective-permute-start | bytes 2312 | tf_op jit(solution)/shard_map/ppermute | solution.py:451
  26.3 2.6 %collective-permute-start.3 = (f32[2,512]{1,0:T(2,128)S(1)}, f32[2,512]{1,0:T(2,128)S(1)}, u32[]{:S(2)}, u32[]{:S(2)}) collective-permute-start(f32[2,512]{1,0:T(2,128)S(1)} %pad_maximum_fusion.1), channel_id=1, source_target_pairs={{0,16},{1,17},{2,18},{3,19},{4,20},{5,21},{6,22},{7,23},{8,56},{9,... | collective-permute-start | bytes 12296 | tf_op jit(solution)/shard_map/ppermute | solution.py:461
  28.8 3.4 %collective-permute-start.5 = (f32[2,512]{1,0:T(2,128)S(1)}, f32[2,512]{1,0:T(2,128)S(1)}, u32[]{:S(2)}, u32[]{:S(2)}) collective-permute-start(f32[2,512]{1,0:T(2,128)S(1)} %pad_maximum_fusion.1), channel_id=1, source_target_pairs={{0,8},{1,9},{2,10},{3,11},{4,12},{5,13},{6,14},{7,15},{8,0},{9,1},... | collective-permute-start | bytes 12296 | tf_op jit(solution)/shard_map/ppermute | solution.py:467
  32.2 1.6 %collective-permute-start.6 = (f32[2,512]{1,0:T(2,128)S(1)}, f32[2,512]{1,0:T(2,128)S(1)}, u32[]{:S(2)}, u32[]{:S(2)}) collective-permute-start(f32[2,512]{1,0:T(2,128)S(1)} %collective-permute-done.3), channel_id=1, source_target_pairs={{0,8},{1,9},{2,10},{3,11},{4,12},{5,13},{6,14},{7,15},{8,0},{9,1},... | collective-permute-start | bytes 12296 | tf_op jit(solution)/shard_map/ppermute | solution.py:468
  33.9 4.2 %place_rest.1 = bf16[2048,128]{1,0:T(8,128)(2,1)} custom-call(s32[24,128]{1,0:T(8,128)S(1)} %bitcast.38, s32[24,128]{1,0:T(8,128)S(1)} %copy-done.2, bf16[3072,128]{1,0:T(8,128)(2,1)S(1)} %copy-done), custom_call_target="tpu_custom_call" | custom-call | tf_op jit(solution)/shard_map/place_rest/pallas_call | solution.py:133
  38.2 3.8 %all-to-all-done = bf16[32,128,128]{2,1,0:T(8,128)(2,1)S(1)} async-done(((bf16[32,128,128]{2,1,0:T(8,128)(2,1)}), bf16[32,128,128]{2,1,0:T(8,128)(2,1)S(1)}, u32[]{:S(2)}, u32[]{:S(2)}) %all-to-all-start) | async-done | bytes 1048608 | tf_op jit(solution)/shard_map/all_to_all | solution.py:436
  42.0 5.0 %collective-permute-start.8 = (bf16[4096,128]{1,0:T(8,128)(2,1)S(1)}, bf16[4096,128]{1,0:T(8,128)(2,1)}, u32[]{:S(2)}, u32[]{:S(2)}) collective-permute-start(bf16[4096,128]{1,0:T(8,128)(2,1)S(1)} %bitcast.25), channel_id=1, source_target_pairs={{0,8},{1,9},{2,10},{3,11},{4,12},{5,13},{6,14},{7,15},{8,0},{9,1},... | collective-permute-start | bytes 3145736 | tf_op jit(solution)/shard_map/ppermute | solution.py:484
  47.0 2.5 %collective-permute-start.7 = (bf16[4096,128]{1,0:T(8,128)(2,1)S(1)}, bf16[4096,128]{1,0:T(8,128)(2,1)S(1)}, u32[]{:S(2)}, u32[]{:S(2)}) collective-permute-start(bf16[4096,128]{1,0:T(8,128)(2,1)S(1)} %bitcast.26), channel_id=1, source_target_pairs={{0,16},{1,17},{2,18},{3,19},{4,20},{5,21},{6,22},{7,23},{8,56},{9,... | collective-permute-start | bytes 3145736 | tf_op jit(solution)/shard_map/ppermute | solution.py:482
  49.5 4.8 %all-to-all-start.1 = ((bf16[32,64,128]{2,1,0:T(8,128)(2,1)}), bf16[32,64,128]{2,1,0:T(8,128)(2,1)S(1)}, u32[]{:S(2)}, u32[]{:S(2)}) async-start(bf16[32,64,128]{2,1,0:T(8,128)(2,1)} %bitcast.14), calls=%async_computation.1 | async-start | bytes 1048576 | tf_op jit(solution)/shard_map/all_to_all | solution.py:436
  54.4 2.2 %own.1 = (f32[16,512]{1,0:T(8,128)S(1)}, f32[16,512]{1,0:T(8,128)S(1)}) custom-call(s32[2]{0:T(128)S(1)} %pad_add_fusion.spots, f32[16,512]{1,0:T(8,128)S(1)} %concatenate.8.ranks, bf16[4096,128]{1,0:T(8,128)(2,1)S(1)} %bitcast.28, bf16[4096,128]{1,0:T(8,128)(2,1)} %collective-permute-done.8.e1), custom_call_target="tpu_custom_call" | custom-call | flops 1073741824 | bytes 4194304 | tf_op jit(solution)/shard_map/own/pallas_call | solution.py:377
  56.6 9.7 %collective-permute-done.7.u1 = bf16[4096,128]{1,0:T(8,128)(2,1)S(1)} collective-permute-done((bf16[4096,128]{1,0:T(8,128)(2,1)S(1)}, bf16[4096,128]{1,0:T(8,128)(2,1)S(1)}, u32[]{:S(2)}, u32[]{:S(2)}) %collective-permute-start.7) | collective-permute-done | bytes 1048608 | tf_op jit(solution)/shard_map/ppermute | solution.py:482
  67.3 3.6 %all-to-all-done.1 = bf16[32,64,128]{2,1,0:T(8,128)(2,1)S(1)} async-done(((bf16[32,64,128]{2,1,0:T(8,128)(2,1)}), bf16[32,64,128]{2,1,0:T(8,128)(2,1)S(1)}, u32[]{:S(2)}, u32[]{:S(2)}) %all-to-all-start.1) | async-done | bytes 524320 | tf_op jit(solution)/shard_map/all_to_all | solution.py:436
  71.0 1.5 %collective-permute-start.9 = (bf16[2048,128]{1,0:T(8,128)(2,1)S(1)}, bf16[2048,128]{1,0:T(8,128)(2,1)S(1)}, u32[]{:S(2)}, u32[]{:S(2)}) collective-permute-start(bf16[2048,128]{1,0:T(8,128)(2,1)S(1)} %bitcast.32), channel_id=1, source_target_pairs={{0,16},{1,17},{2,18},{3,19},{4,20},{5,21},{6,22},{7,23},{8,56},{9,... | collective-permute-start | bytes 1572872 | tf_op jit(solution)/shard_map/ppermute | solution.py:490
  72.5 3.1 %near.1 = (f32[16,512]{1,0:T(8,128)S(1)}, f32[16,512]{1,0:T(8,128)S(1)}) custom-call(s32[2]{0:T(128)S(1)} %pad_add_fusion.spots, f32[16,512]{1,0:T(8,128)S(1)} %concatenate.8.ranks, bf16[4096,128]{1,0:T(8,128)(2,1)S(1)} %bitcast.29, bf16[4096,128]{1,0:T(8,128)(2,1)S(1)} %collective-permute-done.7.u1, bf16[4096,128]{1,0:T(8,128)(2,1)} %collective-permute-done.8.e1, ...), custom_call_target="tpu_custom_call" | custom-call | flops 805306368 | bytes 4194304 | tf_op jit(solution)/shard_map/near/pallas_call | solution.py:377
  75.8 5.5 %second.1 = (f32[16,512]{1,0:T(8,128)S(1)}, f32[16,512]{1,0:T(8,128)S(1)}) custom-call(s32[2]{0:T(128)S(1)} %pad_add_fusion.spots, f32[16,512]{1,0:T(8,128)S(1)} %concatenate.8.ranks, bf16[4096,128]{1,0:T(8,128)(2,1)S(1)} %bitcast.30, bf16[2048,128]{1,0:T(8,128)(2,1)S(1)} %bitcast.34, bf16[4096,128]{1,0:T(8,128)(2,1)S(1)} %collective-permute-done.7.u1, ...), custom_call_target="tpu_custom_call" | custom-call | flops 2684354560 | bytes 4194304 | tf_op jit(solution)/shard_map/second/pallas_call | solution.py:377
  81.3 2.4 %collective-permute-start.14 = (bf16[2048,128]{1,0:T(8,128)(2,1)S(1)}, bf16[2048,128]{1,0:T(8,128)(2,1)S(1)}, u32[]{:S(2)}, u32[]{:S(2)}) collective-permute-start(bf16[2048,128]{1,0:T(8,128)(2,1)S(1)} %collective-permute-done.9.u2), channel_id=1, source_target_pairs={{0,8},{1,9},{2,10},{3,11},{4,12},{5,13},{6,14},{7,15},{8,0},{9,1},... | collective-permute-start | bytes 1572872 | tf_op jit(solution)/shard_map/ppermute | solution.py:497
  83.8 3.0 %third.1 = (f32[16,512]{1,0:T(8,128)S(1)}, f32[16,512]{1,0:T(8,128)S(1)}) custom-call(s32[2]{0:T(128)S(1)} %pad_add_fusion.spots, f32[16,512]{1,0:T(8,128)S(1)} %concatenate.8.ranks, bf16[2048,128]{1,0:T(8,128)(2,1)S(1)} %bitcast.35, bf16[2048,128]{1,0:T(8,128)(2,1)S(1)} %collective-permute-done.9.u2, bf16[2048,128]{1,0:T(8,128)(2,1)S(1)} %collective-permute-done.11.e2, ...), custom_call_target="tpu_custom_call" | custom-call | flops 536870912 | bytes 4194304 | tf_op jit(solution)/shard_map/third/pallas_call | solution.py:377
  86.8 1.7 %fourth.1 = (f32[8,192]{1,0:T(8,128)S(1)}, f32[8,192]{1,0:T(8,128)S(1)}, f32[4,192]{1,0:T(4,128)S(1)}) custom-call(s32[2]{0:T(128)S(1)} %pad_add_fusion.spots, f32[16,512]{1,0:T(8,128)S(1)} %concatenate.8.ranks, bf16[4096,128]{1,0:T(8,128)(2,1)S(1)} %collective-permute-done.7.u1, bf16[2048,128]{1,0:T(8,128)(2,1)S(1)} %collective-permute-done.9.u2, ...), custom_call_target="tpu_custom_call" | custom-call | flops 536870912 | bytes 4194304 | tf_op jit(solution)/shard_map/fourth/pallas_call | solution.py:377
  88.5 1.5 %collective-permute-start.16 = (f32[4,192]{1,0:T(4,128)S(1)}, f32[4,192]{1,0:T(4,128)S(1)}, u32[]{:S(2)}, u32[]{:S(2)}) collective-permute-start(f32[4,192]{1,0:T(4,128)S(1)} %get-tuple-element.68), channel_id=1, source_target_pairs={{0,16},{1,17},{2,18},{3,19},{4,20},{5,21},{6,22},{7,23},{8,56},{9,... | collective-permute-start | bytes 9224 | tf_op jit(solution)/shard_map/ppermute | solution.py:504
  91.0 2.7 %collective-permute-done.17 = f32[4,192]{1,0:T(4,128)S(1)} collective-permute-done((f32[4,192]{1,0:T(4,128)S(1)}, f32[4,192]{1,0:T(4,128)S(1)}, u32[]{:S(2)}, u32[]{:S(2)}) %collective-permute-start.17) | collective-permute-done | bytes 3104 | tf_op jit(solution)/shard_map/ppermute | solution.py:507
  93.8 14.1 %all_to_all.21 = f32[32,1,192]{2,1,0:T(1,128)S(1)} all-to-all(f32[32,1,192]{2,1,0:T(1,128)S(1)} %all_to_all.15), channel_id=1, replica_groups=mesh['y'=4,'x'=4,'core'=2,'z'=8] {'y','z'}, dimensions={0} | all-to-all | bytes 49152 | tf_op jit(solution)/shard_map/all_to_all | solution.py:508
  (54 shorter events, 8.8 us)
Async XLA Ops:
  5.2 28.7 %copy-start = (bf16[3072,128]{1,0:T(8,128)(2,1)S(1)}, bf16[3072,128]{1,0:T(8,128)(2,1)}, u32[]{:S(2)}) copy-start(bf16[3072,128]{1,0:T(8,128)(2,1)} %rows_ref.1) | copy-start | bytes 2359300
  5.2 36.8 %all-to-all-start = ((bf16[32,128,128]{2,1,0:T(8,128)(2,1)}), bf16[32,128,128]{2,1,0:T(8,128)(2,1)S(1)}, u32[]{:S(2)}, u32[]{:S(2)}) async-start(bf16[32,128,128]{2,1,0:T(8,128)(2,1)} %bitcast.43), calls=%async_computation | async-start | bytes 2097152 | tf_op jit(solution)/shard_map/all_to_all | solution.py:436
  17.4 0.7 copy-start.3
  17.4 0.7 copy-start.2
  17.5 0.7 copy-start.1
  19.1 4.9 %collective-permute-start = (f32[1,192]{1,0:T(1,128)S(1)}, f32[1,192]{1,0:T(1,128)S(1)}, u32[]{:S(2)}, u32[]{:S(2)}) collective-permute-start(f32[1,192]{1,0:T(1,128)S(1)} %get-tuple-element.72), channel_id=1, source_target_pairs={{0,64},{1,65},{2,66},{3,67},{4,68},{5,69},{6,70},{7,71},{8,72},{9,... | collective-permute-start | bytes 2312 | tf_op jit(solution)/shard_map/ppermute | solution.py:451
  20.4 4.0 %collective-permute-start.1 = (f32[1,192]{1,0:T(1,128)S(1)}, f32[1,192]{1,0:T(1,128)S(1)}, u32[]{:S(2)}, u32[]{:S(2)}) collective-permute-start(f32[1,192]{1,0:T(1,128)S(1)} %get-tuple-element.71), channel_id=1, source_target_pairs={{0,128},{1,129},{2,130},{3,131},{4,132},{5,133},{6,134},{7,135},{8... | collective-permute-start | bytes 2312 | tf_op jit(solution)/shard_map/ppermute | solution.py:451
  22.8 2.7 %collective-permute-start.2 = (f32[1,192]{1,0:T(1,128)S(1)}, f32[1,192]{1,0:T(1,128)S(1)}, u32[]{:S(2)}, u32[]{:S(2)}) collective-permute-start(f32[1,192]{1,0:T(1,128)S(1)} %get-tuple-element.70), channel_id=1, source_target_pairs={{0,192},{1,193},{2,194},{3,195},{4,196},{5,197},{6,198},{7,199},{8... | collective-permute-start | bytes 2312 | tf_op jit(solution)/shard_map/ppermute | solution.py:451
  26.3 6.0 %collective-permute-start.3 = (f32[2,512]{1,0:T(2,128)S(1)}, f32[2,512]{1,0:T(2,128)S(1)}, u32[]{:S(2)}, u32[]{:S(2)}) collective-permute-start(f32[2,512]{1,0:T(2,128)S(1)} %pad_maximum_fusion.1), channel_id=1, source_target_pairs={{0,16},{1,17},{2,18},{3,19},{4,20},{5,21},{6,22},{7,23},{8,56},{9,... | collective-permute-start | bytes 12296 | tf_op jit(solution)/shard_map/ppermute | solution.py:461
  28.8 9.3 %collective-permute-start.4 = (f32[2,512]{1,0:T(2,128)S(1)}, f32[2,512]{1,0:T(2,128)S(1)}, u32[]{:S(2)}, u32[]{:S(2)}) collective-permute-start(f32[2,512]{1,0:T(2,128)S(1)} %pad_maximum_fusion.1), channel_id=1, source_target_pairs={{0,48},{1,49},{2,50},{3,51},{4,52},{5,53},{6,54},{7,55},{8,24},{9,... | collective-permute-start | bytes 12296 | tf_op jit(solution)/shard_map/ppermute | solution.py:466
  28.8 9.3 %collective-permute-start.5 = (f32[2,512]{1,0:T(2,128)S(1)}, f32[2,512]{1,0:T(2,128)S(1)}, u32[]{:S(2)}, u32[]{:S(2)}) collective-permute-start(f32[2,512]{1,0:T(2,128)S(1)} %pad_maximum_fusion.1), channel_id=1, source_target_pairs={{0,8},{1,9},{2,10},{3,11},{4,12},{5,13},{6,14},{7,15},{8,0},{9,1},... | collective-permute-start | bytes 12296 | tf_op jit(solution)/shard_map/ppermute | solution.py:467
  32.2 5.9 %collective-permute-start.6 = (f32[2,512]{1,0:T(2,128)S(1)}, f32[2,512]{1,0:T(2,128)S(1)}, u32[]{:S(2)}, u32[]{:S(2)}) collective-permute-start(f32[2,512]{1,0:T(2,128)S(1)} %collective-permute-done.3), channel_id=1, source_target_pairs={{0,8},{1,9},{2,10},{3,11},{4,12},{5,13},{6,14},{7,15},{8,0},{9,1},... | collective-permute-start | bytes 12296 | tf_op jit(solution)/shard_map/ppermute | solution.py:468
  42.0 12.3 %collective-permute-start.8 = (bf16[4096,128]{1,0:T(8,128)(2,1)S(1)}, bf16[4096,128]{1,0:T(8,128)(2,1)}, u32[]{:S(2)}, u32[]{:S(2)}) collective-permute-start(bf16[4096,128]{1,0:T(8,128)(2,1)S(1)} %bitcast.25), channel_id=1, source_target_pairs={{0,8},{1,9},{2,10},{3,11},{4,12},{5,13},{6,14},{7,15},{8,0},{9,1},... | collective-permute-start | bytes 3145736 | tf_op jit(solution)/shard_map/ppermute | solution.py:484
  47.0 19.3 %collective-permute-start.7 = (bf16[4096,128]{1,0:T(8,128)(2,1)S(1)}, bf16[4096,128]{1,0:T(8,128)(2,1)S(1)}, u32[]{:S(2)}, u32[]{:S(2)}) collective-permute-start(bf16[4096,128]{1,0:T(8,128)(2,1)S(1)} %bitcast.26), channel_id=1, source_target_pairs={{0,16},{1,17},{2,18},{3,19},{4,20},{5,21},{6,22},{7,23},{8,56},{9,... | collective-permute-start | bytes 3145736 | tf_op jit(solution)/shard_map/ppermute | solution.py:482
  49.5 21.4 %all-to-all-start.1 = ((bf16[32,64,128]{2,1,0:T(8,128)(2,1)}), bf16[32,64,128]{2,1,0:T(8,128)(2,1)S(1)}, u32[]{:S(2)}, u32[]{:S(2)}) async-start(bf16[32,64,128]{2,1,0:T(8,128)(2,1)} %bitcast.14), calls=%async_computation.1 | async-start | bytes 1048576 | tf_op jit(solution)/shard_map/all_to_all | solution.py:436
  54.3 21.5 %collective-permute-start.10 = (bf16[4096,128]{1,0:T(8,128)(2,1)S(1)}, bf16[4096,128]{1,0:T(8,128)(2,1)}, u32[]{:S(2)}, u32[]{:S(2)}) collective-permute-start(bf16[4096,128]{1,0:T(8,128)(2,1)S(1)} %bitcast.27), channel_id=1, source_target_pairs={{0,48},{1,49},{2,50},{3,51},{4,52},{5,53},{6,54},{7,55},{8,24},{9,... | collective-permute-start | bytes 3145736 | tf_op jit(solution)/shard_map/ppermute | solution.py:483
  66.3 9.5 %collective-permute-start.12 = (bf16[4096,128]{1,0:T(8,128)(2,1)S(1)}, bf16[4096,128]{1,0:T(8,128)(2,1)}, u32[]{:S(2)}, u32[]{:S(2)}) collective-permute-start(bf16[4096,128]{1,0:T(8,128)(2,1)S(1)} %collective-permute-done.7.u1), channel_id=1, source_target_pairs={{0,8},{1,9},{2,10},{3,11},{4,12},{5,13},{6,14},{7,15},{8,0},{9,1},... | collective-permute-start | bytes 3145736 | tf_op jit(solution)/shard_map/ppermute | solution.py:487
  70.8 4.9 %collective-permute-start.11 = (bf16[2048,128]{1,0:T(8,128)(2,1)S(1)}, bf16[2048,128]{1,0:T(8,128)(2,1)S(1)}, u32[]{:S(2)}, u32[]{:S(2)}) collective-permute-start(bf16[2048,128]{1,0:T(8,128)(2,1)S(1)} %bitcast.31), channel_id=1, source_target_pairs={{0,8},{1,9},{2,10},{3,11},{4,12},{5,13},{6,14},{7,15},{8,0},{9,1},... | collective-permute-start | bytes 1572872 | tf_op jit(solution)/shard_map/ppermute | solution.py:491
  71.0 10.3 %collective-permute-start.9 = (bf16[2048,128]{1,0:T(8,128)(2,1)S(1)}, bf16[2048,128]{1,0:T(8,128)(2,1)S(1)}, u32[]{:S(2)}, u32[]{:S(2)}) collective-permute-start(bf16[2048,128]{1,0:T(8,128)(2,1)S(1)} %bitcast.32), channel_id=1, source_target_pairs={{0,16},{1,17},{2,18},{3,19},{4,20},{5,21},{6,22},{7,23},{8,56},{9,... | collective-permute-start | bytes 1572872 | tf_op jit(solution)/shard_map/ppermute | solution.py:490
  75.7 11.1 %collective-permute-start.13 = (bf16[2048,128]{1,0:T(8,128)(2,1)S(1)}, bf16[2048,128]{1,0:T(8,128)(2,1)S(1)}, u32[]{:S(2)}, u32[]{:S(2)}) collective-permute-start(bf16[2048,128]{1,0:T(8,128)(2,1)S(1)} %bitcast.33), channel_id=1, source_target_pairs={{0,48},{1,49},{2,50},{3,51},{4,52},{5,53},{6,54},{7,55},{8,24},{9,... | collective-permute-start | bytes 1572872 | tf_op jit(solution)/shard_map/ppermute | solution.py:494
  81.3 5.4 %collective-permute-start.14 = (bf16[2048,128]{1,0:T(8,128)(2,1)S(1)}, bf16[2048,128]{1,0:T(8,128)(2,1)S(1)}, u32[]{:S(2)}, u32[]{:S(2)}) collective-permute-start(bf16[2048,128]{1,0:T(8,128)(2,1)S(1)} %collective-permute-done.9.u2), channel_id=1, source_target_pairs={{0,8},{1,9},{2,10},{3,11},{4,12},{5,13},{6,14},{7,15},{8,0},{9,1},... | collective-permute-start | bytes 1572872 | tf_op jit(solution)/shard_map/ppermute | solution.py:497
  88.5 1.5 %collective-permute-start.15 = (f32[8,192]{1,0:T(8,128)S(1)}, f32[8,192]{1,0:T(8,128)S(1)}, u32[]{:S(2)}, u32[]{:S(2)}) collective-permute-start(f32[8,192]{1,0:T(8,128)S(1)} %get-tuple-element.67), channel_id=1, source_target_pairs={{0,8},{1,9},{2,10},{3,11},{4,12},{5,13},{6,14},{7,15},{8,0},{9,1},... | collective-permute-start | bytes 18440 | tf_op jit(solution)/shard_map/ppermute | solution.py:505
  88.5 2.5 %collective-permute-start.16 = (f32[4,192]{1,0:T(4,128)S(1)}, f32[4,192]{1,0:T(4,128)S(1)}, u32[]{:S(2)}, u32[]{:S(2)}) collective-permute-start(f32[4,192]{1,0:T(4,128)S(1)} %get-tuple-element.68), channel_id=1, source_target_pairs={{0,16},{1,17},{2,18},{3,19},{4,20},{5,21},{6,22},{7,23},{8,56},{9,... | collective-permute-start | bytes 9224 | tf_op jit(solution)/shard_map/ppermute | solution.py:504
  90.0 3.7 %collective-permute-start.17 = (f32[4,192]{1,0:T(4,128)S(1)}, f32[4,192]{1,0:T(4,128)S(1)}, u32[]{:S(2)}, u32[]{:S(2)}) collective-permute-start(f32[4,192]{1,0:T(4,128)S(1)} %slice.21), channel_id=1, source_target_pairs={{0,48},{1,49},{2,50},{3,51},{4,52},{5,53},{6,54},{7,55},{8,24},{9,... | collective-permute-start | bytes 9224 | tf_op jit(solution)/shard_map/ppermute | solution.py:507
